TPU v7x, 32 devices: a whole 2x2x4 slice. The times are simulated.
32 devices in a mesh: dp: 8 (over z, x), col: 4 (over y, core).
Axes of the slice: x: 2, y: 2, z: 4, core: 2. Of those that a mesh axis runs over, the one named last changes fastest.
Arguments:
- features: bfloat16 [100, 262144], P('col', 'dp'), may hold values from -6 to 6
- neighbors_one: int32 [5, 65536], P(None, 'dp'), may hold values from 0 to 32767, as said below
- present_one: int32 [5, 65536], P(None, 'dp'), may hold values 0 or 1
- neighbors_two: int32 [10, 16384], P(None, 'dp'), may hold values from 0 to 8191, as said below
- present_two: int32 [10, 16384], P(None, 'dp'), may hold values 0 or 1
- neighbors_three: int32 [15, 4096], P(None, 'dp'), may hold values from 0 to 2047, as said below
- present_three: int32 [15, 4096], P(None, 'dp'), may hold values 0 or 1
- labels: int32 [4096], P('dp'), may hold values from 0 to 46
- seed_weight: int32 [4096], P('dp'), may hold values from 0 to 1, as said below
- serve_rows: int32 [64, 8], P('dp'), may hold values from 0 to 511
- take_seed: int32 [64, 8], P('dp'), may hold values from 0 to 511
- fetch_live: int32 [64], P('dp'), may hold values from 0 to 8, as said below
- weight_one: float32 [2, 100, 256], P(None, 'col'), may hold values from -0.4375 to 0.4375
- weight_two: float32 [2, 256, 256], P(None, 'col'), may hold values from -4 to 4
- weight_three: float32 [2, 256, 47], P(None, 'col'), may hold values from -4 to 4
- hidden_bias: float32 [2, 256], P(None, 'col'), may hold values from -0.5 to 0.5
- head_bias: float32 [47], replicated, may hold values from -1 to 1
- first_one: float32 [2, 100, 256], P(None, 'col'), may hold values from -0.21875 to 0.21875
- first_two: float32 [2, 256, 256], P(None, 'col'), may hold values from -0.21875 to 0.21875
- first_three: float32 [2, 256, 47], P(None, 'col'), may hold values from -0.21875 to 0.21875
- first_hidden: float32 [2, 256], P(None, 'col'), may hold values from -0.75 to 0.75
- first_head: float32 [47], replicated, may hold values from -6 to 6
- second_one: float32 [2, 100, 256], P(None, 'col'), may hold values from 0.0001024 to 0.0004096
- second_two: float32 [2, 256, 256], P(None, 'col'), may hold values from 0.0001024 to 0.0004096
- second_three: float32 [2, 256, 47], P(None, 'col'), may hold values from 0.0001024 to 0.0004096
- second_hidden: float32 [2, 256], P(None, 'col'), may hold values from 0.0016384 to 0.0065536
- second_head: float32 [47], replicated, may hold values from 0.08192 to 0.32768
Outputs:
- new_weight_one: float32 [2, 100, 256], P(None, 'col')
- new_weight_two: float32 [2, 256, 256], P(None, 'col')
- new_weight_three: float32 [2, 256, 47], P(None, 'col')
- new_hidden_bias: float32 [2, 256], P(None, 'col')
- new_head_bias: float32 [47], replicated
- moment_one: float32 [2, 100, 256], P(None, 'col')
- moment_two: float32 [2, 256, 256], P(None, 'col')
- moment_three: float32 [2, 256, 47], P(None, 'col')
- moment_hidden: float32 [2, 256], P(None, 'col')
- moment_head: float32 [47], replicated
- square_one: float32 [2, 100, 256], P(None, 'col')
- square_two: float32 [2, 256, 256], P(None, 'col')
- square_three: float32 [2, 256, 47], P(None, 'col')
- square_hidden: float32 [2, 256], P(None, 'col')
- square_head: float32 [47], replicated
- layer_norms: float32 [2, 5], replicated
- loss_sum: float32 [], replicated
- seed_count: float32 [], replicated
Inputs may be any that keep to these rules, and one draw needn't show every extreme that they name: `seed_weight`: share of counted seeds rises from about a third on block 0 to all seeds on the last block. `fetch_live`: some owners serve all 8 slots to every block; the others a quarter to a half of them. `neighbors_one`: A node at row i of its block has its neighbors at rows of at least 4 i - 64 and below 4 i + 64 of the set below, within that block's rows. `neighbors_two`: A node at row i of its block has its neighbors at rows of at least 4 i - 64 and below 4 i + 64 of the set below, within that block's rows. `neighbors_three`: A seed at row i of its block has its neighbors at rows of at least 4 i - 64 and below 4 i + 64 of the set below, within that block's rows.
All inputs are finite; a program needn't handle non-finite values. No bound on the sum of `present_one` or of `present_two` or of `present_three` on one device may be relied on, other than what follows from the above.
Results may differ from a plain program's by a relative error of at most 0.012.
The roundings to bfloat16 on the way count: a program that leaves them out, or rounds other values in their place, can miss the bound.
Values may be sent and summed in bfloat16 or wider, within the bound.
No kernel may reach another device: no remote copies, remote signals or barrier semaphores. Data moves between devices by JAX's collectives and lax.ppermute only.
A program may use at most 64 MiB of HBM per device.

v0:
```python
import jax
import jax.numpy as jnp
from jax import lax
from jax.sharding import PartitionSpec as P

REACH = 64
STEP = 5


DIST_WEIGHT = 1.0
ROW_EPS = 1e-06
LEARN_RATE = 0.5
BETA_ONE = 0.9
BETA_TWO = 0.999
ADAM_EPS = 1e-06
DECAY_RATE = 0.01
EXACT = lax.Precision.HIGHEST


def window_plan(rows, below):
    block = min(512, rows)
    width = min(4 * block + 2 * REACH, below)
    return (block, rows // block, width)


def window_start(first_row, below, width):
    return jnp.clip(4 * first_row - REACH, 0, below - width)


def window_counts(links, valid, start, width):
    spots = jnp.arange(width, dtype=jnp.int32)[None, :]
    counts = jnp.zeros((links.shape[0], width), jnp.float32)
    for slot in range(links.shape[1]):
        counts = counts + valid[:, slot : slot + 1] * (
            links[:, slot : slot + 1] - start == spots
        ).astype(jnp.float32)
    return counts


def neighbor_mean(states, neighbor, present):
    rows = neighbor.shape[0]
    below = states.shape[0]
    block, count_blocks, width = window_plan(rows, below)
    valid = present.astype(jnp.float32)
    totals = jnp.maximum(jnp.sum(valid, 1), 1.0)

    def neighbor_one_block(index):
        first_row = index * block
        start = window_start(first_row, below, width)
        links = lax.dynamic_slice_in_dim(neighbor, first_row, block, 0)
        marks = lax.dynamic_slice_in_dim(valid, first_row, block, 0)
        counts = window_counts(links, marks, start, width)
        window = lax.dynamic_slice_in_dim(states, start, width, 0)
        return jnp.dot(counts, window, precision=EXACT, preferred_element_type=jnp.float32)

    sums = lax.map(neighbor_one_block, jnp.arange(count_blocks, dtype=jnp.int32)).reshape(
        rows, states.shape[1]
    )
    return (sums / totals[:, None], totals)


def layer_inputs(states, neighbor, present):
    rows = neighbor.shape[0]
    average, totals = neighbor_mean(states, neighbor, present)
    return (jnp.stack([states[:rows], average], 1).astype(jnp.bfloat16), totals)


def summed_columns(inputs, weight_low):
    partial_value = jnp.einsum(
        "nsk,skd->nd", inputs, weight_low, preferred_element_type=jnp.float32
    )
    return lax.psum_scatter(partial_value, "col", scatter_dimension=1, tiled=True)


def hidden_forward(states, neighbor, present, weight, bias):
    inputs, totals = layer_inputs(states, neighbor, present)
    weight_low = weight.astype(jnp.bfloat16)
    result = summed_columns(inputs, weight_low)
    result = result + bias
    active = jax.nn.silu(result)
    squares = lax.psum(jnp.sum(active * active, 1), "col")
    scale = lax.rsqrt(squares + ROW_EPS)
    return (active * scale[:, None], (inputs, totals, result, active, scale, None))


def spread_back(grad_inputs, totals, neighbor, present, prev_rows):
    rows = neighbor.shape[0]
    block, count_blocks, width = window_plan(rows, prev_rows)
    valid = present.astype(jnp.float32)
    scaled = grad_inputs[:, 1] / totals[:, None]
    grad_prev = jnp.pad(grad_inputs[:, 0], ((0, prev_rows - rows), (0, 0)))

    def spread_one_block(carry, index):
        first_row = index * block
        start = window_start(first_row, prev_rows, width)
        links = lax.dynamic_slice_in_dim(neighbor, first_row, block, 0)
        marks = lax.dynamic_slice_in_dim(valid, first_row, block, 0)
        counts = window_counts(links, marks, start, width)
        part = lax.dynamic_slice_in_dim(scaled, first_row, block, 0)
        added = lax.dot_general(
            counts,
            part,
            (((0,), (0,)), ((), ())),
            precision=EXACT,
            preferred_element_type=jnp.float32,
        )
        window = lax.dynamic_slice_in_dim(carry, start, width, 0)
        return (lax.dynamic_update_slice_in_dim(carry, window + added, start, 0), None)

    grad_prev, _ = lax.scan(spread_one_block, grad_prev, jnp.arange(count_blocks, dtype=jnp.int32))
    return grad_prev


def column_grads(inputs, grad_result, totals, neighbor, present, weight_low, prev_rows):
    grad_full = lax.all_gather(grad_result, "col", axis=1, tiled=True)
    grad_weight = jnp.einsum("nsk,nd->skd", inputs, grad_full, preferred_element_type=jnp.float32)
    grad_prev = None
    if prev_rows > 0:
        grad_inputs = jnp.einsum(
            "nd,skd->nsk", grad_full, weight_low, preferred_element_type=jnp.float32
        )
        grad_prev = spread_back(grad_inputs, totals, neighbor, present, prev_rows)
    return (grad_weight, grad_prev)


def hidden_backward(grad_states, saved, neighbor, present, weight_low, prev_rows):
    inputs, totals, result, active, scale, whole_inputs = saved
    inner = lax.psum(jnp.sum(grad_states * active, 1), "col")
    grad_active = scale[:, None] * grad_states - active * (scale**3 * inner)[:, None]
    sigma = jax.nn.sigmoid(result)
    grad_result = (grad_active * sigma * (1.0 + result * (1.0 - sigma))).astype(jnp.bfloat16)
    grad_bias = jnp.sum(grad_result.astype(jnp.float32), 0)
    grad_weight, grad_prev = column_grads(
        inputs, grad_result, totals, neighbor, present, weight_low, prev_rows
    )
    return (grad_weight, grad_bias, grad_prev)


def lamb_parts(weight, grad, first, second):
    first_new = BETA_ONE * first + (1.0 - BETA_ONE) * grad
    second_new = BETA_TWO * second + (1.0 - BETA_TWO) * grad * grad
    update = (
        first_new
        / (1.0 - BETA_ONE**STEP)
        / (jnp.sqrt(second_new / (1.0 - BETA_TWO**STEP)) + ADAM_EPS)
        + DECAY_RATE * weight
    )
    return (first_new, second_new, update, jnp.sum(weight * weight), jnp.sum(update * update))


def seed_picks(indices, seeds):
    return indices[:, :, None] == jnp.arange(seeds, dtype=jnp.int32)[None, None, :]


def shards(
    features,
    neighbors_one,
    present_one,
    neighbors_two,
    present_two,
    neighbors_three,
    present_three,
    labels,
    seed_weight,
    serve_rows,
    take_seed,
    fetch_live,
    weight_one,
    weight_two,
    weight_three,
    hidden_bias,
    head_bias,
    first_one,
    first_two,
    first_three,
    first_hidden,
    first_head,
    second_one,
    second_two,
    second_three,
    second_hidden,
    second_head,
):
    layer_weights = (weight_one, weight_two)
    wiring = ((neighbors_one.T, present_one.T), (neighbors_two.T, present_two.T))
    seed_links = neighbors_three.T
    seed_valid = present_three.T
    states = features.T.astype(jnp.float32)
    saved_all = []
    prev_sizes = []
    for section in range(2):
        prev_sizes.append(states.shape[0])
        states, saved = hidden_forward(
            states,
            wiring[section][0],
            wiring[section][1],
            layer_weights[section],
            hidden_bias[section],
        )
        saved_all.append(saved)
    head_low = weight_three.astype(jnp.bfloat16)
    head_inputs, head_totals = layer_inputs(states, seed_links, seed_valid)
    partial_value = jnp.einsum(
        "nsk,skc->nc", head_inputs, head_low, preferred_element_type=jnp.float32
    )
    logits = lax.psum(partial_value, "col") + head_bias
    highest = jnp.max(logits, 1, keepdims=True)
    expo = jnp.exp(logits - highest)
    totals = jnp.sum(expo, 1, keepdims=True)
    lse = highest[:, 0] + jnp.log(totals[:, 0])
    onehot = (labels[:, None] == jnp.arange(logits.shape[1])[None, :]).astype(jnp.float32)
    weighting = seed_weight.astype(jnp.float32)
    ce_total = jnp.sum(weighting * (lse - jnp.sum(onehot * logits, 1)))
    grad_logits = (weighting[:, None] * (expo / totals - onehot)).astype(jnp.bfloat16)
    seeds = labels.shape[0]
    embed = states[:seeds]
    serve_pick = seed_picks(serve_rows, seeds)
    take_pick = seed_picks(take_seed, seeds).astype(jnp.float32)
    sent = jnp.einsum(
        "osn,nk->osk",
        serve_pick.astype(jnp.bfloat16),
        embed.astype(jnp.bfloat16),
        preferred_element_type=jnp.float32,
    ).astype(jnp.bfloat16)
    fetched = lax.all_to_all(sent, "dp", split_axis=0, concat_axis=0, tiled=True).astype(
        jnp.float32
    )
    local_rows = jnp.einsum(
        "osn,nk->osk", take_pick, embed, precision=EXACT, preferred_element_type=jnp.float32
    )
    slots = take_seed.shape[1]
    alive = (jnp.arange(slots)[None, :] < fetch_live[:, None]).astype(jnp.float32)
    differ = local_rows - fetched
    dist_total = DIST_WEIGHT * jnp.sum(alive[:, :, None] * differ * differ)
    first_col = (lax.axis_index("col") == 0).astype(jnp.float32)
    loss_sum, seed_count = lax.psum(
        (first_col * ce_total + dist_total, first_col * jnp.sum(weighting)), ("dp", "col")
    )
    grad_local = 2.0 * DIST_WEIGHT * alive[:, :, None] * differ
    returned = lax.all_to_all(
        (-grad_local).astype(jnp.bfloat16), "dp", split_axis=0, concat_axis=0, tiled=True
    ).astype(jnp.float32)
    grad_head_weight = jnp.einsum(
        "nsk,nc->skc", head_inputs, grad_logits, preferred_element_type=jnp.float32
    )
    grad_head_bias = jnp.sum(grad_logits.astype(jnp.float32), 0)
    grad_head_inputs = jnp.einsum(
        "nc,skc->nsk", grad_logits, head_low, preferred_element_type=jnp.float32
    )
    grad_states = spread_back(
        grad_head_inputs, head_totals, seed_links, seed_valid, states.shape[0]
    )
    grad_seeds = jnp.einsum(
        "osn,osk->nk", take_pick, grad_local, precision=EXACT, preferred_element_type=jnp.float32
    )
    grad_seeds = grad_seeds + jnp.einsum(
        "osn,osk->nk",
        serve_pick.astype(jnp.float32),
        returned,
        precision=EXACT,
        preferred_element_type=jnp.float32,
    )
    grad_states = grad_states + jnp.pad(grad_seeds, ((0, states.shape[0] - seeds), (0, 0)))
    grads_weight = [None, None]
    grads_bias = [None, None]
    for section in (1, 0):
        needed = prev_sizes[section] if section > 0 else 0
        grad_weight, grad_bias, grad_states = hidden_backward(
            grad_states,
            saved_all[section],
            wiring[section][0],
            wiring[section][1],
            layer_weights[section].astype(jnp.bfloat16),
            needed,
        )
        grads_weight[section] = grad_weight
        grads_bias[section] = grad_bias
    grad_hidden = jnp.stack(grads_bias)
    grads = lax.psum(
        (grads_weight[0], grads_weight[1], grad_head_weight, grad_hidden, grad_head_bias), "dp"
    )
    params = (weight_one, weight_two, weight_three, hidden_bias, head_bias)
    firsts = (first_one, first_two, first_three, first_hidden, first_head)
    seconds = (second_one, second_two, second_three, second_hidden, second_head)
    parts = [lamb_parts(params[i], grads[i], firsts[i], seconds[i]) for i in range(5)]
    weight_sums, update_sums = lax.psum(
        (jnp.stack([item[3] for item in parts[:4]]), jnp.stack([item[4] for item in parts[:4]])),
        "col",
    )
    weight_norms = jnp.sqrt(jnp.concatenate([weight_sums, parts[4][3][None]]))
    update_norms = jnp.sqrt(jnp.concatenate([update_sums, parts[4][4][None]]))
    fresh = [
        params[i] - LEARN_RATE * (weight_norms[i] / update_norms[i]) * parts[i][2] for i in range(5)
    ]
    layer_norms = jnp.stack([weight_norms, update_norms])
    return (
        fresh[0],
        fresh[1],
        fresh[2],
        fresh[3],
        fresh[4],
        parts[0][0],
        parts[1][0],
        parts[2][0],
        parts[3][0],
        parts[4][0],
        parts[0][1],
        parts[1][1],
        parts[2][1],
        parts[3][1],
        parts[4][1],
        layer_norms,
        loss_sum,
        seed_count,
    )


def solution(mesh):
    return jax.shard_map(
        shards,
        mesh=mesh,
        in_specs=(
            P("col", "dp"),
            P(None, "dp"),
            P(None, "dp"),
            P(None, "dp"),
            P(None, "dp"),
            P(None, "dp"),
            P(None, "dp"),
            P("dp"),
            P("dp"),
            P("dp", None),
            P("dp", None),
            P("dp"),
            P(None, "col", None),
            P(None, "col", None),
            P(None, "col", None),
            P(None, "col"),
            P(),
            P(None, "col", None),
            P(None, "col", None),
            P(None, "col", None),
            P(None, "col"),
            P(),
            P(None, "col", None),
            P(None, "col", None),
            P(None, "col", None),
            P(None, "col"),
            P(),
        ),
        out_specs=(
            P(None, "col", None),
            P(None, "col", None),
            P(None, "col", None),
            P(None, "col"),
            P(),
            P(None, "col", None),
            P(None, "col", None),
            P(None, "col", None),
            P(None, "col"),
            P(),
            P(None, "col", None),
            P(None, "col", None),
            P(None, "col", None),
            P(None, "col"),
            P(),
            P(),
            P(),
            P(),
        ),
        check_vma=False,
    )
```

profile of v0, /device:TPU:0, one launch (start us, length us, event | category | flops | bytes accessed | tf_op | source)
XLA Modules:
  0.0 843.6 jit_solution(9199490216660687992)
XLA Ops:
  13.0 186.0 %while.44 = (s32[]{:T(128)}, f32[16,512,25]{1,0,2:T(8,128)S(1)}, s32[16]{0:T(128)S(1)}, s32[8192,5]{0,1:T(8,128)}, f32[8192,5]{0,1:T(8,128)S(1)}, /*index=5*/f32...) while((s32[]{:T(128)}, f32[16,512,25]{1,0,2:T(8,128)S(1)}, ...), condition=%wide.region_7.8_spmd, body=%wide.region_6.7_spmd.sunk | while | flops 349833728 | bytes 596847 | solution.py:56
  16.0 7.8 fusion.202
  39.3 7.8 fusion.202
  50.9 7.8 fusion.202
  74.1 7.8 fusion.202
  85.7 7.8 fusion.202
  120.6 7.8 fusion.202
  143.9 7.8 fusion.202
  167.2 7.8 fusion.202
  178.8 7.8 fusion.202
  207.4 73.6 %reduce-scatter.3.cloned.1.call-done = f32[8192,64]{0,1:T(8,128)} async-done(((f32[8192,256]{0,1:T(8,128)}), f32[8192,64]{0,1:T(8,128)}) %reduce-scatter.3.cloned.1.call-update) | async-done | bytes 2097168 | tf_op jit(solution)/shard_map/reduce_scatter | solution.py:72
  283.4 10.5 %psum.99 = f32[8192]{0:T(1024)S(1)} all-reduce(f32[8192]{0:T(1024)S(1)} %multiply_reduce_fusion.1), channel_id=1, replica_groups=mesh['dp'=8,'col'=4] {'col'}, use_global_device_ids=true, to_apply=%region_11.12 | all-reduce | flops 8192 | bytes 65536 | tf_op jit(solution)/shard_map/psum | solution.py:81
  296.3 59.2 %while.45 = (s32[]{:T(128)}, f32[4,512,64]{1,0,2:T(4,128)S(1)}, s32[4]{0:T(128)S(1)}, s32[2048,10]{0,1:T(8,128)}, f32[2048,10]{0,1:T(8,128)S(1)}, /*index=5*/f32...) while((s32[]{:T(128)}, f32[4,512,64]{1,0,2:T(4,128)S(1)}, ...), condition=%wide.region_13.14_spmd, body=%wide.region_12.13_spmd.sunk | while | flops 887952384 | bytes 1335807 | solution.py:56
  299.5 10.1 %fusion.205 = f32[1,512,64]{1,2,0:T(8,128)S(1)} fusion(f32[512]{0:T(512)S(1)} %bitcast.335, s32[512]{0:T(512)S(1)} %bitcast.315, f32[512]{0:T(512)S(1)} %bitcast.327, s32[512]{0:T(512)S(1)} %bitcast.307, f32[512]{0:T(512)S(1)} %bitcast.328, s32[512]{0:T(512)S(1)} %bitcast.308, f32[512]{0:T(512)S(1)} %bitcast.329, s32[512]{0:T(512)S(1)} %bitcast.309, ...), kind=kOutput, calls=%fused_computation.87.clone.1 | convolution fusion | flops 887947264 | bytes 729092 | tf_op jit(solution)/shard_map/while/body/eval_jaxpr/dot_general | solution.py:54
  314.2 10.1 %fusion.205 = f32[1,512,64]{1,2,0:T(8,128)S(1)} fusion(f32[512]{0:T(512)S(1)} %bitcast.335, s32[512]{0:T(512)S(1)} %bitcast.315, f32[512]{0:T(512)S(1)} %bitcast.327, s32[512]{0:T(512)S(1)} %bitcast.307, f32[512]{0:T(512)S(1)} %bitcast.328, s32[512]{0:T(512)S(1)} %bitcast.308, f32[512]{0:T(512)S(1)} %bitcast.329, s32[512]{0:T(512)S(1)} %bitcast.309, ...), kind=kOutput, calls=%fused_computation.87.clone.1 | convolution fusion | flops 887947264 | bytes 729092 | tf_op jit(solution)/shard_map/while/body/eval_jaxpr/dot_general | solution.py:54
  328.9 10.1 %fusion.205 = f32[1,512,64]{1,2,0:T(8,128)S(1)} fusion(f32[512]{0:T(512)S(1)} %bitcast.335, s32[512]{0:T(512)S(1)} %bitcast.315, f32[512]{0:T(512)S(1)} %bitcast.327, s32[512]{0:T(512)S(1)} %bitcast.307, f32[512]{0:T(512)S(1)} %bitcast.328, s32[512]{0:T(512)S(1)} %bitcast.308, f32[512]{0:T(512)S(1)} %bitcast.329, s32[512]{0:T(512)S(1)} %bitcast.309, ...), kind=kOutput, calls=%fused_computation.87.clone.1 | convolution fusion | flops 887947264 | bytes 729092 | tf_op jit(solution)/shard_map/while/body/eval_jaxpr/dot_general | solution.py:54
  343.6 10.1 %fusion.205 = f32[1,512,64]{1,2,0:T(8,128)S(1)} fusion(f32[512]{0:T(512)S(1)} %bitcast.335, s32[512]{0:T(512)S(1)} %bitcast.315, f32[512]{0:T(512)S(1)} %bitcast.327, s32[512]{0:T(512)S(1)} %bitcast.307, f32[512]{0:T(512)S(1)} %bitcast.328, s32[512]{0:T(512)S(1)} %bitcast.308, f32[512]{0:T(512)S(1)} %bitcast.329, s32[512]{0:T(512)S(1)} %bitcast.309, ...), kind=kOutput, calls=%fused_computation.87.clone.1 | convolution fusion | flops 887947264 | bytes 729092 | tf_op jit(solution)/shard_map/while/body/eval_jaxpr/dot_general | solution.py:54
  358.8 31.7 %reduce-scatter.5.cloned.1.call-done = f32[2048,64]{0,1:T(8,128)} async-done(((f32[2048,256]{0,1:T(8,128)}), f32[2048,64]{0,1:T(8,128)}) %reduce-scatter.5.cloned.1.call-update) | async-done | bytes 524304 | tf_op jit(solution)/shard_map/reduce_scatter | solution.py:72
  405.8 12.3 %fusion.127 = bf16[512,1,64]{0,2,1:T(8,128)(2,1)S(1)} fusion(f32[2048,64]{0,1:T(8,128)S(1)} %broadcast_multiply_fusion.1, f32[512]{0:T(512)S(1)} %broadcast_maximum_fusion.2, f32[512]{0:T(512)S(1)} %bitcast.362, s32[512]{0:T(512)S(1)} %bitcast.392, f32[512]{0:T(512)S(1)} %bitcast.364, s32[512]{0:T(512)S(1)} %bitcast.394, f32[512]{0:T(512)S(1)} %bitcast.366, ...), kind=kOutput, calls=%fused_computation.202 | convolution fusion | flops 851509248 | bytes 653312 | tf_op jit(solution)/shard_map/while/body/eval_jaxpr/dot_general | solution.py:54
  433.4 18.3 %all-reduce.10.cloned.1.call-done = f32[512,47]{0,1:T(8,128)} async-done(((f32[512,47]{0,1:T(8,128)}), f32[512,47]{0,1:T(8,128)}) %all-reduce.10.cloned.1.call-update) | async-done | bytes 96272 | tf_op jit(solution)/shard_map/psum | solution.py:206
  456.2 10.6 %multiply_reduce_fusion.2 = (f32[2048]{0:T(1024)S(1)}, f32[2048,64]{0,1:T(8,128)S(1)}) fusion(f32[2048,64]{0,1:T(8,128)S(1)} %copy-done.3, f32[64]{0:T(128)S(1)} %get-tuple-element.504, f32[512,64]{0,1:T(8,128)S(1)} %fusion.125, f32[512,2,64]{0,2,1:T(8,128)S(1)} %fusion.153, f32[512]{0:T(512)S(1)} %broadcast_maximum_fusion.2, f32[512]{0:T(512)S(1)} %bitcast.363, ...), kind=kOutput, calls=%fused_computation.220 | convolution fusion | flops 852654080 | bytes 1513984 | tf_op jit(solution)/shard_map/while/body/eval_jaxpr/dot_general | solution.py:100
  474.7 16.9 %all-gather.3.cloned.1.call-done = bf16[2048,256]{0,1:T(8,128)(2,1)} async-done(((bf16[2048,64]{0,1:T(8,128)(2,1)}), bf16[2048,256]{0,1:T(8,128)(2,1)}) %all-gather.3.cloned.1.call-update) | async-done | bytes 1048592 | tf_op jit(solution)/shard_map/all_gather | solution.py:115
  495.6 64.3 %while.46 = (s32[]{:T(128)}, f32[8192,64]{0,1:T(8,128)}, s32[4]{0:T(128)S(1)}, s32[2048,10]{0,1:T(8,128)}, f32[2048,10]{0,1:T(8,128)S(1)}, /*index=5*/f32[2048,6...) while((s32[]{:T(128)}, f32[8192,64]{0,1:T(8,128)}, ...), condition=%wide.region_25.26_spmd, body=%wide.region_24.25_spmd.sunk | while | flops 888091648 | bytes 2483199 | solution.py:110
  498.9 9.4 %fusion.208 = f32[2176,64]{0,1:T(8,128)S(1)} fusion(f32[512]{0:T(512)S(1)} %bitcast.345, s32[512]{0:T(512)S(1)} %bitcast.325, f32[512]{0:T(512)S(1)} %bitcast.337, s32[512]{0:T(512)S(1)} %bitcast.317, f32[512]{0:T(512)S(1)} %bitcast.338, s32[512]{0:T(512)S(1)} %bitcast.318, f32[512]{0:T(512)S(1)} %bitcast.339, s32[512]{0:T(512)S(1)} %bitcast.319, ...), kind=kOutput, calls=%fused_computation.132.clone.1 | convolution fusion | flops 888086528 | bytes 1286660 | tf_op jit(solution)/shard_map/while/body/eval_jaxpr/dot_general | solution.py:100
  514.9 9.4 %fusion.208 = f32[2176,64]{0,1:T(8,128)S(1)} fusion(f32[512]{0:T(512)S(1)} %bitcast.345, s32[512]{0:T(512)S(1)} %bitcast.325, f32[512]{0:T(512)S(1)} %bitcast.337, s32[512]{0:T(512)S(1)} %bitcast.317, f32[512]{0:T(512)S(1)} %bitcast.338, s32[512]{0:T(512)S(1)} %bitcast.318, f32[512]{0:T(512)S(1)} %bitcast.339, s32[512]{0:T(512)S(1)} %bitcast.319, ...), kind=kOutput, calls=%fused_computation.132.clone.1 | convolution fusion | flops 888086528 | bytes 1286660 | tf_op jit(solution)/shard_map/while/body/eval_jaxpr/dot_general | solution.py:100
  531.3 9.4 %fusion.208 = f32[2176,64]{0,1:T(8,128)S(1)} fusion(f32[512]{0:T(512)S(1)} %bitcast.345, s32[512]{0:T(512)S(1)} %bitcast.325, f32[512]{0:T(512)S(1)} %bitcast.337, s32[512]{0:T(512)S(1)} %bitcast.317, f32[512]{0:T(512)S(1)} %bitcast.338, s32[512]{0:T(512)S(1)} %bitcast.318, f32[512]{0:T(512)S(1)} %bitcast.339, s32[512]{0:T(512)S(1)} %bitcast.319, ...), kind=kOutput, calls=%fused_computation.132.clone.1 | convolution fusion | flops 888086528 | bytes 1286660 | tf_op jit(solution)/shard_map/while/body/eval_jaxpr/dot_general | solution.py:100
  547.7 9.4 %fusion.208 = f32[2176,64]{0,1:T(8,128)S(1)} fusion(f32[512]{0:T(512)S(1)} %bitcast.345, s32[512]{0:T(512)S(1)} %bitcast.325, f32[512]{0:T(512)S(1)} %bitcast.337, s32[512]{0:T(512)S(1)} %bitcast.317, f32[512]{0:T(512)S(1)} %bitcast.338, s32[512]{0:T(512)S(1)} %bitcast.318, f32[512]{0:T(512)S(1)} %bitcast.339, s32[512]{0:T(512)S(1)} %bitcast.319, ...), kind=kOutput, calls=%fused_computation.132.clone.1 | convolution fusion | flops 888086528 | bytes 1286660 | tf_op jit(solution)/shard_map/while/body/eval_jaxpr/dot_general | solution.py:100
  562.3 10.7 %psum.103 = f32[8192]{0:T(1024)S(1)} all-reduce(f32[8192]{0:T(1024)S(1)} %multiply_reduce_fusion), channel_id=1, replica_groups=mesh['dp'=8,'col'=4] {'col'}, use_global_device_ids=true, to_apply=%region_27.28 | all-reduce | flops 8192 | bytes 65536 | tf_op jit(solution)/shard_map/psum | solution.py:128
  586.7 26.7 %all-gather.5.cloned.1.call-done = bf16[8192,256]{0,1:T(8,128)(2,1)} async-done(((bf16[8192,64]{0,1:T(8,128)(2,1)}), bf16[8192,256]{0,1:T(8,128)(2,1)}) %all-gather.5.cloned.1.call-update) | async-done | bytes 4194320 | tf_op jit(solution)/shard_map/all_gather | solution.py:115
  617.6 69.7 %all-reduce.12.cloned.1.call-done = f32[2,64,256]{2,1,0:T(8,128)} async-done(((f32[2,64,256]{2,1,0:T(8,128)}), f32[2,64,256]{2,1,0:T(8,128)}) %all-reduce.12.cloned.1.call-update) | async-done | bytes 131088 | tf_op jit(solution)/shard_map/psum | solution.py:279
  689.0 72.1 %all-reduce.14.cloned.1.call-done = (f32[47]{0:T(128)}, f32[2,64]{1,0:T(2,128)}, f32[2,64,47]{1,2,0:T(8,128)}, f32[2,25,256]{2,1,0:T(8,128)}) async-done(((f32[47]{0:T(128)}, f32[2,64]{1,0:T(2,128)}, f32[2,64,47]{1,2,0:T(8,128)}, f32[2,25,256]{2,1,0:T(8,128)}), (f32[47]{0:T(128)}, f32[2,64]{1,0:T(2,128)}, f32[2,64,47]{1,2,0:T(8,128)}, f32[2,25,256]{2,1,0:T(8,128)})) %all-reduce.14.cloned.1.call-update) | async-done | bytes 75980 | tf_op jit(solution)/shard_map/psum | solution.py:279
  771.2 40.2 %all-reduce.3 = (f32[]{:T(128)}, f32[]{:T(128)}) all-reduce(f32[]{:T(128)S(6)} %add.542, f32[]{:T(128)S(6)} %mul.1342), channel_id=1, replica_groups=mesh['dp'=8,'col'=4] {'dp','col'}, use_global_device_ids=true, to_apply=%region_45.46 | all-reduce | flops 2 | bytes 16 | tf_op jit(solution)/shard_map/psum | solution.py:236
  (319 shorter events, 245.1 us)
Async XLA Ops:
  7.2 273.8 %reduce-scatter.3.cloned.1.call-start = ((), (), s32[]{:S(2)}) async-start(), calls=%async_computation.4 | async-start | bytes 10485760 | tf_op jit(solution)/shard_map/reduce_scatter | solution.py:72
  13.0 187.3 %copy-start.11 = (f32[2,25,256]{2,0,1:T(2,128)S(1)}, f32[2,25,256]{2,0,1:T(2,128)}, u32[]{:S(2)}) copy-start(f32[2,25,256]{2,0,1:T(2,128)} %param.45) | copy-start | bytes 153604
  206.4 184.1 %reduce-scatter.5.cloned.1.call-start = ((), (), s32[]{:S(2)}) async-start(), calls=%async_computation.5 | async-start | bytes 2621440 | tf_op jit(solution)/shard_map/reduce_scatter | solution.py:72
  207.4 88.9 %copy-start.29 = (f32[64]{0:T(128)}, f32[64]{0:T(128)S(1)}, u32[]{:S(2)}) copy-start(f32[64]{0:T(128)S(1)} %get-tuple-element.505) | copy-start | bytes 772
  296.2 59.8 %copy-start.7 = (bf16[2048,1,64]{0,2,1:T(8,128)(2,1)}, bf16[2048,1,64]{0,2,1:T(8,128)(2,1)S(1)}, u32[]{:S(2)}) copy-start(bf16[2048,1,64]{0,2,1:T(8,128)(2,1)S(1)} %fusion.134) | copy-start | bytes 786436
  296.3 59.8 %copy-start.6 = (f32[2,64,256]{2,1,0:T(8,128)S(1)}, f32[2,64,256]{2,1,0:T(8,128)}, u32[]{:S(2)}) copy-start(f32[2,64,256]{2,1,0:T(8,128)} %param.46) | copy-start | bytes 393220
  400.0 19.0 %all-to-all-start = ((bf16[8,2,256]{2,1,0:T(2,128)(2,1)}), bf16[8,2,256]{2,1,0:T(2,128)(2,1)S(1)}, u32[]{:S(2)}, u32[]{:S(2)}) async-start(bf16[8,2,256]{2,1,0:T(2,128)(2,1)} %reshape.287), calls=%async_computation.2 | async-start | bytes 16384 | tf_op jit(solution)/shard_map/all_to_all | solution.py:225
  405.7 46.1 %all-reduce.10.cloned.1.call-start = ((), (), s32[]{:S(2)}) async-start(), calls=%async_computation.6 | async-start | bytes 196608 | tf_op jit(solution)/shard_map/psum | solution.py:206
  405.8 47.0 %copy-start.34 = (s32[512]{0:T(512)S(1)}, s32[512]{0:T(512)}, u32[]{:S(2)}) copy-start(s32[512]{0:T(512)} %param.40) | copy-start | bytes 6148
  405.8 50.4 %copy-start.3 = (f32[2048,64]{0,1:T(8,128)S(1)}, f32[2048,64]{0,1:T(8,128)}, u32[]{:S(2)}) copy-start(f32[2048,64]{0,1:T(8,128)} %reduce-scatter.5.cloned.1.call-done) | copy-start | bytes 1572868
  420.6 12.5 %all-to-all-start.1 = ((bf16[8,2,256]{2,1,0:T(2,128)(2,1)}), bf16[8,2,256]{2,1,0:T(2,128)(2,1)S(1)}, u32[]{:S(2)}, u32[]{:S(2)}) async-start(bf16[8,2,256]{2,1,0:T(2,128)(2,1)} %reshape.289), calls=%async_computation.3 | async-start | bytes 16384 | tf_op jit(solution)/shard_map/all_to_all | solution.py:240
  426.6 65.1 %all-gather.3.cloned.1.call-start = ((), (), s32[]{:S(2)}) async-start(), calls=%async_computation.7 | async-start | bytes 1310720 | tf_op jit(solution)/shard_map/all_gather | solution.py:115
  474.7 138.7 %all-gather.5.cloned.1.call-start = ((), (), s32[]{:S(2)}) async-start(), calls=%async_computation.8 | async-start | bytes 5242880 | tf_op jit(solution)/shard_map/all_gather | solution.py:115
  495.6 64.3 %copy-start = (f32[8192,64]{0,1:T(8,128)S(1)}, f32[8192,64]{0,1:T(8,128)}, u32[]{:S(2)}) copy-start(f32[8192,64]{0,1:T(8,128)} %reduce-scatter.3.cloned.1.call-done) | copy-start | bytes 6291460
  495.6 64.3 %copy-start.30 = (f32[64]{0:T(128)S(1)}, f32[64]{0:T(128)}, u32[]{:S(2)}) copy-start(f32[64]{0:T(128)} %copy-done.29) | copy-start | bytes 772
  577.6 109.7 %copy-start.20 = (f32[2,64,256]{2,1,0:T(8,128)S(1)}, f32[2,64,256]{2,1,0:T(8,128)}, u32[]{:S(2)}) copy-start(f32[2,64,256]{2,1,0:T(8,128)} %param.51) | copy-start | bytes 393220
  577.6 109.7 %copy-start.21 = (f32[2,64,256]{2,1,0:T(8,128)S(1)}, f32[2,64,256]{2,1,0:T(8,128)}, u32[]{:S(2)}) copy-start(f32[2,64,256]{2,1,0:T(8,128)} %param.56) | copy-start | bytes 393220
  577.6 109.7 %all-reduce.12.cloned.1.call-start = ((), (), s32[]{:S(2)}) async-start(), calls=%async_computation.9 | async-start | bytes 262144 | tf_op jit(solution)/shard_map/psum | solution.py:279
  581.0 180.1 %copy-start.12 = (f32[2,25,256]{2,0,1:T(2,128)S(1)}, f32[2,25,256]{2,0,1:T(2,128)}, u32[]{:S(2)}) copy-start(f32[2,25,256]{2,0,1:T(2,128)} %param.45) | copy-start | bytes 153604
  581.0 180.1 %copy-start.23 = (f32[2,25,256]{2,0,1:T(2,128)S(1)}, f32[2,25,256]{2,0,1:T(2,128)}, u32[]{:S(2)}) copy-start(f32[2,25,256]{2,0,1:T(2,128)} %param.50) | copy-start | bytes 153604
  581.0 180.1 %copy-start.24 = (f32[2,25,256]{2,0,1:T(2,128)S(1)}, f32[2,25,256]{2,0,1:T(2,128)}, u32[]{:S(2)}) copy-start(f32[2,25,256]{2,0,1:T(2,128)} %param.55) | copy-start | bytes 153604
  582.7 179.8 %copy-start.14 = (f32[2,64,47]{1,0,2:T(2,128)S(1)}, f32[2,64,47]{1,0,2:T(2,128)}, u32[]{:S(2)}) copy-start(f32[2,64,47]{1,0,2:T(2,128)} %param.47) | copy-start | bytes 72196
  582.8 179.8 %copy-start.25 = (f32[2,64,47]{1,0,2:T(2,128)S(1)}, f32[2,64,47]{1,0,2:T(2,128)}, u32[]{:S(2)}) copy-start(f32[2,64,47]{1,0,2:T(2,128)} %param.52) | copy-start | bytes 72196
  582.8 179.9 %copy-start.26 = (f32[2,64,47]{1,0,2:T(2,128)S(1)}, f32[2,64,47]{1,0,2:T(2,128)}, u32[]{:S(2)}) copy-start(f32[2,64,47]{1,0,2:T(2,128)} %param.57) | copy-start | bytes 72196
  582.8 181.3 %copy-start.33 = (f32[2,64]{1,0:T(2,128)S(1)}, f32[2,64]{1,0:T(2,128)}, u32[]{:S(2)}) copy-start(f32[2,64]{1,0:T(2,128)} %param.48) | copy-start | bytes 1540
  582.8 181.3 %copy-start.38 = (f32[2,64]{1,0:T(2,128)S(1)}, f32[2,64]{1,0:T(2,128)}, u32[]{:S(2)}) copy-start(f32[2,64]{1,0:T(2,128)} %param.53) | copy-start | bytes 1540
  582.8 181.3 %copy-start.39 = (f32[2,64]{1,0:T(2,128)S(1)}, f32[2,64]{1,0:T(2,128)}, u32[]{:S(2)}) copy-start(f32[2,64]{1,0:T(2,128)} %param.58) | copy-start | bytes 1540
  582.8 234.7 %copy-start.40 = (f32[47]{0:T(128)S(1)}, f32[47]{0:T(128)}, u32[]{:S(2)}) copy-start(f32[47]{0:T(128)} %param.54) | copy-start | bytes 568
  582.8 234.6 %copy-start.41 = (f32[47]{0:T(128)S(1)}, f32[47]{0:T(128)}, u32[]{:S(2)}) copy-start(f32[47]{0:T(128)} %param.59) | copy-start | bytes 568
  585.4 175.7 %all-reduce.14.cloned.1.call-start = ((), (), s32[]{:S(2)}) async-start(), calls=%async_computation.10 | async-start | bytes 232448 | tf_op jit(solution)/shard_map/psum | solution.py:279
  688.9 147.4 %copy-start.9 = (f32[2,64,256]{2,1,0:T(8,128)}, f32[2,64,256]{2,1,0:T(8,128)S(1)}, u32[]{:S(2)}) copy-start(f32[2,64,256]{2,1,0:T(8,128)S(1)} %get-tuple-element.415) | copy-start | bytes 393220
  689.0 147.4 %copy-start.10 = (f32[2,64,256]{2,1,0:T(8,128)}, f32[2,64,256]{2,1,0:T(8,128)S(1)}, u32[]{:S(2)}) copy-start(f32[2,64,256]{2,1,0:T(8,128)S(1)} %get-tuple-element.416) | copy-start | bytes 393220
  (20 other events, 247.9 us)
Sparse Core Ops, SparseCore 0:
  206.6 74.4 reduce-scatter.2
  358.0 32.5 reduce-scatter.4
  419.1 32.6 all-reduce.9
  474.8 16.8 all-gather.2
  577.8 35.5 all-gather.4
  617.5 69.7 all-reduce.11
  692.2 68.8 all-reduce.13
where the time goes:
time: 855 us; the launch traced here: 844 us
  waiting for transfers between devices  315 us (37%)
  matrix products  244 us (29%)
  blocking collectives  79.4 us (9%)
  other arithmetic  74.7 us (9%)
  local copies, waits for them, and re-layouts  60.8 us (7%)
  loops' own time  32.9 us (4%)
  between operations  24 us (3%)
  starting transfers between devices  12.1 us (1%)
    dot_general x21, matrix products, neighbor_one_block(): jnp.dot(counts, window, precision=EXACT, preferred_element_type=jnp.float32)  177 us
    psum x2, waiting for transfers between devices, shards(): lax.psum((grads_weight[0], grads_weight[1], grad_head_weight, grad_hidden...  142 us
    reduce_scatter x2, waiting for transfers between devices, summed_columns(): lax.psum_scatter(partial_value, 'col', scatter_dimension=1, tiled=True)  105 us
    dot_general x5, matrix products, spread_one_block(): lax.dot_general(counts, part, (((0,), (0,)), ((), ())), precision=EXACT,...  48.4 us
    all_gather x2, waiting for transfers between devices, column_grads(): grad_full = lax.all_gather(grad_result, 'col', axis=1, tiled=True)  43.7 us
    psum x1, blocking collectives, shards(): lax.psum((first_col * ce_total + dist_total, first_col * jnp.sum(weightin...  40.2 us
    another operation x2, loops' own time, neighbor_mean(): lax.map(neighbor_one_block, jnp.arange(count_blocks, dtype=jnp.int32))  27.5 us
    sub x24, other arithmetic, window_counts(): links[:, slot:slot + 1] - start == spots  25.2 us
  transfers between devices with their start and end apart: 9, of which 8 were waited for; matrix products, arithmetic and copies ran while one was open for 3% of the time, Pallas kernels for 0%

commit v1 on v0

v1 whole, which is shorter than its diff:
```python
import functools

import jax
import jax.numpy as jnp
from jax import lax
from jax.experimental import pallas as pl
from jax.experimental.pallas import tpu as pltpu
from jax.sharding import PartitionSpec as P

REACH = 64
STEP = 5
DIST_WEIGHT = 1.0
ROW_EPS = 1e-06
LEARN_RATE = 0.5
BETA_ONE = 0.9
BETA_TWO = 0.999
ADAM_EPS = 1e-06
DECAY_RATE = 0.01

BF = jnp.bfloat16
F32 = jnp.float32
LANES = 128
WINDOW = 768
SENTINEL = 4.0
PARAMS = pltpu.CompilerParams(vmem_limit_bytes=56 * 2**20)


class Sizes:
    def __init__(self, features, neighbors_one, neighbors_two, neighbors_three, weight_two, weight_three, serve_rows):
        self.feat = features.shape[0]
        self.hold = -(-self.feat // 16) * 16
        self.base = features.shape[1]
        self.low = neighbors_one.shape[1]
        self.mid = neighbors_two.shape[1]
        self.seeds = neighbors_three.shape[1]
        self.hid = weight_two.shape[2]
        self.group = weight_two.shape[1]
        self.classes = weight_three.shape[2]
        self.head = -(-self.classes // 16) * 16
        self.own = self.seeds // 4
        self.n_b = 4 * self.own + 2 * LANES
        self.n_a = 16 * self.own + 6 * LANES
        self.n_low = self.n_a + self.n_b + self.own
        self.n_mid = self.n_b + self.own
        self.slots = serve_rows.shape[0] * serve_rows.shape[1]
        self.slot = serve_rows.shape[1]
        self.dp = serve_rows.shape[0]
        self.w_lanes = self.hid + 2 * self.hid + 2 * LANES + LANES
        self.rows_one = 2 * 2 * self.hold
        self.rows_two = 4 * self.group
        self.misc = self.rows_one + self.rows_two + self.head
        self.pay = self.misc + 16

    def a_start(self, part):
        return jnp.clip(16 * self.own * part - 3 * LANES, 0, self.low - self.n_a)

    def b_start(self, part):
        return jnp.maximum(4 * self.own * part - LANES, 0)

    def b_columns(self, part, tile):
        return pl.ds(aligned(jnp.minimum(self.b_start(part) + LANES * tile, self.mid - LANES)), LANES)


def dot(a, b, over):
    return lax.dot_general(a, b, (((over[0],), (over[1],)), ((), ())), preferred_element_type=F32)


def two_parts(value):
    high = value.astype(BF)
    return high, (value - high.astype(F32)).astype(BF)


def three_parts(value):
    high = value.astype(BF).astype(F32)
    rest = value - high
    middle = rest.astype(BF).astype(F32)
    return high, middle, (rest - middle).astype(BF).astype(F32)


def aligned(value):
    return pl.multiple_of(value, LANES)


def sigmoid(value):
    return 1.0 / (1.0 + jnp.exp(-value))


def mean_kernel(sz, feat_ref, nbr_ref, pres_ref, out_ref):
    spare = jnp.zeros((sz.hold - sz.feat, LANES), F32)
    last = sz.base // LANES - 6

    def tile(step, carry):
        lane = aligned(step * LANES)
        valid = pres_ref[:, pl.ds(lane, LANES)].astype(F32)
        counts = jnp.maximum(jnp.sum(valid, 0, keepdims=True), 1.0)
        first = jnp.clip(4 * step - 1, 0, last)
        local = nbr_ref[:, pl.ds(lane, LANES)] - first * LANES
        piece = local >> 7
        spot = local & 127
        sources = [
            jnp.concatenate([feat_ref[:, pl.ds(aligned((first + j) * LANES), LANES)].astype(F32), spare], 0)
            for j in range(6)
        ]
        totals = [jnp.zeros((8, LANES), F32) for _ in range(sz.hold // 8)]
        for slot in range(nbr_ref.shape[0]):
            spots = jnp.broadcast_to(spot[slot : slot + 1], (8, LANES))
            pieces = jnp.broadcast_to(piece[slot : slot + 1], (8, LANES))
            marks = jnp.broadcast_to(valid[slot : slot + 1], (8, LANES))
            for h in range(sz.hold // 8):
                taken = None
                for j in range(6):
                    found = jnp.take_along_axis(
                        sources[j][8 * h : 8 * h + 8], spots, axis=1, mode="promise_in_bounds"
                    )
                    taken = found if j == 0 else jnp.where(pieces == j, found, taken)
                totals[h] = totals[h] + taken * marks
        average = jnp.concatenate(totals, 0) / counts
        own = jnp.concatenate([feat_ref[:, pl.ds(lane, LANES)].astype(F32), spare], 0)
        out_ref[:, pl.ds(lane, LANES)] = jnp.concatenate([own, average], 0).astype(BF)
        return carry

    lax.fori_loop(0, sz.low // LANES, tile, 0, unroll=4)


def layer_one_means(sz, features, neighbors, present):
    return pl.pallas_call(
        functools.partial(mean_kernel, sz),
        out_shape=jax.ShapeDtypeStruct((2 * sz.hold, sz.low), BF),
        compiler_params=PARAMS,
    )(features, neighbors, present)


def window_counts(local, rows):
    spots = lax.broadcasted_iota(jnp.int32, (rows, LANES), 0)
    counts = jnp.zeros((rows, LANES), F32)
    for slot in range(local.shape[0]):
        counts = counts + jnp.where(local[slot : slot + 1] == spots, 1.0, 0.0)
    return counts.astype(BF)


def slot_totals(present):
    return jnp.maximum(jnp.sum(present.astype(F32), 0, keepdims=True), 1.0)


def a_window(sz, part, tile):
    first = 4 * sz.b_start(part) + 4 * LANES * tile - LANES - sz.a_start(part)
    return aligned(jnp.clip(first, 0, sz.n_a - WINDOW))


def head_weight(sz, part, messages, low_ref):
    lane = sz.n_low + 3 * sz.hid
    for r in range(4):
        row = pl.multiple_of(2 * sz.group * (part ^ r), 2 * sz.group)
        low_ref[pl.ds(row, 2 * sz.group), :] = jnp.concatenate(
            [messages[r][:, lane + LANES * s : lane + LANES * s + LANES] for s in range(2)], 0
        )


def second_weight(sz, part, messages, low_ref):
    lane = sz.n_low + sz.hid
    for r in range(4):
        row = pl.multiple_of(2 * sz.group * (part ^ r), 2 * sz.group)
        low_ref[pl.ds(row, 2 * sz.group), :] = jnp.concatenate(
            [messages[r][:, lane + sz.hid * s : lane + sz.hid * s + sz.hid] for s in range(2)], 0
        )


def transposed(value):
    return value.astype(F32).T.astype(BF)


def forward_kernel(
    sz, m0, m1, m2, m3, nbr2, pres2, nbr3, pres3, info,
    result1, scale1, inputs2, result2, scale2, inputs3, counts2, counts3, sent,
    x_ref, high1, low1, w2_ref, bias_ref,
):
    part = lax.axis_index("col")
    messages = (m0, m1, m2, m3)
    n_a, n_b, own, hid, group = sz.n_a, sz.n_b, sz.own, sz.hid, sz.group
    for r in range(4):
        x_ref[2 * sz.hold * r : 2 * sz.hold * (r + 1), :] = messages[r][:, : sz.n_low]
        lane = sz.n_low + 3 * hid + 2 * LANES
        tail = messages[r][:, lane : lane + LANES].astype(F32)
        for layer in range(2):
            column = tail[:, 3 * layer : 3 * layer + 1] + tail[:, 3 * layer + 1 : 3 * layer + 2]
            column = column + tail[:, 3 * layer + 2 : 3 * layer + 3]
            row = pl.multiple_of(group * (part ^ r), group)
            bias_ref[pl.ds(row, group), LANES * layer : LANES * layer + LANES] = jnp.broadcast_to(column, (group, LANES))
    weight1 = transposed(
        jnp.concatenate([m[:, sz.n_low : sz.n_low + hid] for m in messages], 0)
    )
    second_weight(sz, part, messages, w2_ref)
    weight2 = transposed(w2_ref[...])

    def first_layer(lane):
        result = dot(weight1, x_ref[:, pl.ds(lane, LANES)], (1, 0)) + bias_ref[:, :LANES]
        active = result * sigmoid(result)
        scale = lax.rsqrt(jnp.sum(active * active, 0, keepdims=True) + ROW_EPS)
        result1[:, pl.ds(lane, LANES)] = result
        scale1[:, pl.ds(lane, LANES)] = scale
        high, low = two_parts(active * scale)
        high1[:, pl.ds(lane, LANES)] = high
        low1[:, pl.ds(lane, LANES)] = low

    def first_step(step, carry):
        first_layer(aligned(step * LANES))
        return carry

    lax.fori_loop(0, sz.n_low // LANES, first_step, 0)

    def second_inputs(lane, self_lane, window, local, totals, tile):
        counts = window_counts(local, WINDOW)
        counts2[WINDOW * tile : WINDOW * (tile + 1), :] = counts
        average = dot(high1[:, pl.ds(window, WINDOW)], counts, (1, 0))
        average = (average + dot(low1[:, pl.ds(window, WINDOW)], counts, (1, 0))) / totals
        average = average.astype(BF)
        for c in range(4):
            inputs2[2 * group * c : 2 * group * c + group, lane : lane + LANES] = high1[
                group * c : group * (c + 1), self_lane : self_lane + LANES
            ]
            inputs2[2 * group * c + group : 2 * group * (c + 1), lane : lane + LANES] = average[
                group * c : group * (c + 1)
            ]

    b_start = sz.b_start(part)
    for tile in range(n_b // LANES):
        columns = sz.b_columns(part, tile)
        window = a_window(sz, part, tile)
        marks = pres2[:, columns]
        local = jnp.where(marks > 0, nbr2[:, columns] - (sz.a_start(part) + window), -1)
        second_inputs(LANES * tile, n_a + LANES * tile, window, local, slot_totals(marks), tile)
    for tile in range(own // LANES):
        columns = pl.ds(aligned(own * part + LANES * tile), LANES)
        marks = pres2[:, columns]
        local = jnp.where(marks > 0, nbr2[:, columns] - b_start, -1)
        second_inputs(n_b + LANES * tile, n_a + n_b + LANES * tile, n_a, local, slot_totals(marks), n_b // LANES + tile)

    result = dot(weight2, inputs2[...], (1, 0)) + bias_ref[:, LANES : LANES + 1]
    active = result * sigmoid(result)
    scale = lax.rsqrt(jnp.sum(active * active, 0, keepdims=True) + ROW_EPS)
    result2[...] = result
    scale2[...] = scale
    high2, low2 = two_parts(active * scale)
    columns = pl.ds(aligned(own * part), own)
    marks = pres3[:, columns]
    local = jnp.where(marks > 0, nbr3[:, columns] - b_start, -1)
    counts = window_counts(local, n_b)
    counts3[...] = counts
    average = dot(high2[:, :n_b], counts, (1, 0)) + dot(low2[:, :n_b], counts, (1, 0))
    average = (average / slot_totals(marks)).astype(BF)
    embed_high, embed_low = high2[:, n_b:], low2[:, n_b:]
    for c in range(4):
        inputs3[2 * group * c : 2 * group * c + group, :] = embed_high[group * c : group * (c + 1)]
        inputs3[2 * group * c + group : 2 * group * (c + 1), :] = average[group * c : group * (c + 1)]
    spots = lax.broadcasted_iota(jnp.int32, (sz.slots, own), 1) + own * part
    serve = jnp.where(info[:, 0:1] == spots, 1.0, 0.0).astype(BF)
    take = jnp.where(info[:, 1:2] == spots, 1.0, 0.0)
    owned = jnp.sum(take, 1, keepdims=True)
    take = take.astype(BF)
    sent[:, :hid] = dot(serve, embed_high, (1, 1)).astype(BF)
    local_high = dot(take, embed_high, (1, 1))
    dead = (lax.broadcasted_iota(jnp.int32, (sz.slots, hid), 1) == 0) & ((owned > 0.5) & (info[:, 2:3] == 0))
    sent[:, hid : 2 * hid] = jnp.where(dead, SENTINEL, local_high).astype(BF)
    sent[:, 2 * hid :] = dot(take, embed_low, (1, 1)).astype(BF)


def forward(sz, messages, nbr2, pres2, nbr3, pres3, info):
    tiles = sz.n_mid // LANES
    shape = jax.ShapeDtypeStruct
    return pl.pallas_call(
        functools.partial(forward_kernel, sz),
        out_shape=(
            shape((sz.hid, sz.n_low), F32),
            shape((1, sz.n_low), F32),
            shape((2 * sz.hid, sz.n_mid), BF),
            shape((sz.hid, sz.n_mid), F32),
            shape((1, sz.n_mid), F32),
            shape((2 * sz.hid, sz.own), BF),
            shape((WINDOW * tiles, LANES), BF),
            shape((sz.n_b, sz.own), BF),
            shape((sz.slots, 3 * sz.hid), BF),
        ),
        scratch_shapes=[
            pltpu.VMEM((8 * sz.hold, sz.n_low), BF),
            pltpu.VMEM((sz.hid, sz.n_low), BF),
            pltpu.VMEM((sz.hid, sz.n_low), BF),
            pltpu.VMEM((2 * sz.hid, sz.hid), BF),
            pltpu.VMEM((sz.hid, 2 * LANES), F32),
        ],
        compiler_params=PARAMS,
    )(*messages, nbr2, pres2, nbr3, pres3, info)


def norm_backward(grad, result, scale):
    gate = sigmoid(result)
    active = result * gate
    inner = jnp.sum(grad * active, 0, keepdims=True)
    grad_active = scale * grad - active * (scale * scale * scale * inner)
    return (grad_active * gate * (1.0 + result * (1.0 - gate))).astype(BF)


def backward_kernel(
    sz, m0, m1, m2, m3, pres2, pres3, info, labels, weighting, head_bias,
    result1, scale1, inputs2, result2, scale2, inputs3, counts2, counts3, sent, received,
    keep, send,
    x_ref, w2_ref, w3_ref, grad_a, grad_bc, grad_mid, low_grad1, g2_ref, g3_ref, gb_ref,
):
    part = lax.axis_index("col")
    messages = (m0, m1, m2, m3)
    n_a, n_b, own, hid, group = sz.n_a, sz.n_b, sz.own, sz.hid, sz.group
    for r in range(4):
        x_ref[2 * sz.hold * r : 2 * sz.hold * (r + 1), :] = messages[r][:, : sz.n_low]
    second_weight(sz, part, messages, w2_ref)
    head_weight(sz, part, messages, w3_ref)

    columns = pl.ds(aligned(own * part), own)
    classes = lax.broadcasted_iota(jnp.int32, (sz.head, own), 0)
    logits = dot(transposed(w3_ref[...])[: sz.head], inputs3[...], (1, 0)) + head_bias[...]
    logits = jnp.where(classes < sz.classes, logits, -1e30)
    highest = jnp.max(logits, 0, keepdims=True)
    expo = jnp.exp(logits - highest)
    totals = jnp.sum(expo, 0, keepdims=True)
    onehot = jnp.where(classes == labels[:, columns], 1.0, 0.0)
    weights = weighting[:, columns].astype(F32)
    target = jnp.sum(jnp.where(classes == labels[:, columns], logits, 0.0), 0, keepdims=True)
    ce_total = jnp.sum(weights * (highest + jnp.log(totals) - target))
    seed_count = jnp.sum(weights)
    grad_logits = (weights * (expo / totals - onehot)).astype(BF)
    g3_ref[...] = dot(grad_logits, inputs3[...], (1, 1))
    grad_inputs3 = dot(w3_ref[:, : sz.head], grad_logits, (1, 0))
    pieces = [grad_inputs3[group * c : group * (c + 1)] for c in range(8)]
    scaled = jnp.concatenate(pieces[1::2], 0) / slot_totals(pres3[:, columns])
    high, low = two_parts(scaled)
    grad_mid[:, :n_b] = dot(high, counts3[...], (1, 1)) + dot(low, counts3[...], (1, 1))
    grad_embed = jnp.concatenate(pieces[0::2], 0)

    spots = lax.broadcasted_iota(jnp.int32, (sz.slots, own), 1) + own * part
    serve = jnp.where(info[:, 0:1] == spots, 1.0, 0.0)
    take = jnp.where(info[:, 1:2] == spots, 1.0, 0.0)
    served = jnp.sum(serve, 1, keepdims=True)
    taken = jnp.sum(take, 1, keepdims=True)
    alive = info[:, 2:3].astype(F32)
    arrived = received[...].astype(F32).reshape(sz.dp, 4, sz.slot, 3 * hid)
    arrived = jnp.sum(arrived, 1).reshape(sz.slots, 3 * hid)
    fetched = arrived[:, :hid]
    theirs = arrived[:, hid : 2 * hid]
    alive_there = jnp.where(theirs[:, 0:1] < 0.5 * SENTINEL, 1.0, 0.0)
    theirs = theirs + arrived[:, 2 * hid :]
    mine = sent[...].astype(F32)
    differ = (mine[:, hid : 2 * hid] + mine[:, 2 * hid :] - fetched)
    mask = (taken > 0.5) & (alive > 0.5)
    differ = jnp.where(mask, differ, 0.0)
    dist_total = DIST_WEIGHT * jnp.sum(differ * differ)
    local_high, local_low = two_parts(2.0 * DIST_WEIGHT * differ)
    back = jnp.where((served > 0.5) & (alive_there > 0.5), theirs - mine[:, :hid], 0.0)
    back = (-2.0 * DIST_WEIGHT * back).astype(BF)
    take = take.astype(BF)
    serve = serve.astype(BF)
    grad_embed = grad_embed + dot(local_high, take, (0, 0)) + dot(local_low, take, (0, 0))
    grad_embed = grad_embed + dot(back, serve, (0, 0))
    grad_mid[:, n_b:] = grad_embed

    low_grad2 = norm_backward(grad_mid[...], result2[...], scale2[...])
    g2_ref[...] = dot(inputs2[...], low_grad2, (1, 1))
    ones = jnp.ones((16, sz.n_mid), BF)
    gb_ref[:, hid : 2 * hid] = dot(ones, low_grad2, (1, 1))
    grad_a[...] = jnp.zeros_like(grad_a)
    tiles_b = n_b // LANES
    for tile in range(sz.n_mid // LANES):
        lane = LANES * tile
        in_b = tile < tiles_b
        columns = sz.b_columns(part, tile) if in_b else pl.ds(aligned(own * part + lane - n_b), LANES)
        marks = pres2[:, columns]
        grad_inputs = dot(w2_ref[...], low_grad2[:, lane : lane + LANES], (1, 0))
        pieces = [grad_inputs[group * c : group * (c + 1)] for c in range(8)]
        high, low = two_parts(jnp.concatenate(pieces[1::2], 0) / slot_totals(marks))
        counts = counts2[WINDOW * tile : WINDOW * (tile + 1), :]
        spread = dot(high, counts, (1, 1)) + dot(low, counts, (1, 1))
        grad_bc[:, lane : lane + LANES] = jnp.concatenate(pieces[0::2], 0)
        if in_b:
            window = pl.ds(a_window(sz, part, tile), WINDOW)
            grad_a[:, window] = grad_a[:, window] + spread
        else:
            grad_bc[:, :n_b] = grad_bc[:, :n_b] + spread

    def first_back(grad, lane):
        low_grad1[:, pl.ds(lane, LANES)] = norm_backward(
            grad, result1[:, pl.ds(lane, LANES)], scale1[:, pl.ds(lane, LANES)]
        )

    def step_a(step, carry):
        lane = aligned(step * LANES)
        first_back(grad_a[:, pl.ds(lane, LANES)], lane)
        return carry

    def step_bc(step, carry):
        lane = aligned(step * LANES)
        first_back(grad_bc[:, pl.ds(lane, LANES)], aligned(n_a + lane))
        return carry

    lax.fori_loop(0, n_a // LANES, step_a, 0)
    lax.fori_loop(0, sz.n_mid // LANES, step_bc, 0)
    g1 = dot(x_ref[...], low_grad1[...], (1, 1))
    ones = jnp.ones((16, sz.n_low), BF)
    gb_ref[:, :hid] = dot(ones, low_grad1[...], (1, 1))
    head_row = dot(jnp.ones((16, own), BF), grad_logits, (1, 1))
    head_row = jnp.concatenate([head_row, jnp.zeros((16, LANES - sz.head), F32)], 1)
    lane_at = lax.broadcasted_iota(jnp.int32, (16, LANES), 1)
    row_at = lax.broadcasted_iota(jnp.int32, (16, LANES), 0)
    sums = three_parts(
        jnp.where(lane_at == 0, ce_total + dist_total, jnp.where(lane_at == 1, seed_count, 0.0))
    )
    for r in range(4):
        target_ref = (keep, send)[r % 2]
        base = sz.pay * (r // 2)
        shard = part ^ r
        rows1 = g1[2 * sz.hold * r : 2 * sz.hold * (r + 1)]
        rows2 = g2_ref[pl.ds(pl.multiple_of(2 * group * shard, 2 * group), 2 * group), :]
        at = base
        for rows in (rows1, rows2):
            for half in range(hid // LANES):
                piece = rows[:, LANES * half : LANES * (half + 1)]
                target_ref[at : at + piece.shape[0], :] = piece.astype(BF)
                at += piece.shape[0]
        target_ref[at : at + sz.head, :] = g3_ref[:, pl.ds(aligned(2 * group * shard), LANES)].astype(BF)
        at += sz.head
        odd = (shard % 2) == 1
        block = aligned((shard // 2) * LANES)
        one = gb_ref[:, pl.ds(block, LANES)]
        two = gb_ref[:, pl.ds(aligned(hid + block), LANES)]
        one = jnp.where(odd, pltpu.roll(one, group, 1), one)
        two = jnp.where(odd, two, pltpu.roll(two, group, 1))
        bias_row = jnp.where(lane_at < group, one, two)
        misc = jnp.where(row_at == 0, bias_row, jnp.where(row_at == 1, head_row, 0.0))
        for i in range(3):
            misc = jnp.where(row_at == 2 + i, sums[i], misc)
        target_ref[at : at + 16, :] = misc.astype(BF)


def backward(sz, messages, pres2, pres3, info, labels, weighting, head_bias, saved, received):
    shape = jax.ShapeDtypeStruct
    return pl.pallas_call(
        functools.partial(backward_kernel, sz),
        out_shape=(shape((2 * sz.pay, LANES), BF), shape((2 * sz.pay, LANES), BF)),
        scratch_shapes=[
            pltpu.VMEM((8 * sz.hold, sz.n_low), BF),
            pltpu.VMEM((2 * sz.hid, sz.hid), BF),
            pltpu.VMEM((2 * sz.hid, LANES), BF),
            pltpu.VMEM((sz.hid, sz.n_a), F32),
            pltpu.VMEM((sz.hid, sz.n_mid), F32),
            pltpu.VMEM((sz.hid, sz.n_mid), F32),
            pltpu.VMEM((sz.hid, sz.n_low), BF),
            pltpu.VMEM((2 * sz.hid, sz.hid), F32),
            pltpu.VMEM((sz.head, 2 * sz.hid), F32),
            pltpu.VMEM((16, 2 * sz.hid), F32),
        ],
        compiler_params=PARAMS,
    )(*messages, pres2, pres3, info, labels, weighting, head_bias, *saved, received)


def add_kernel(sz, own, other, out):
    for i in range(own.shape[0] // sz.pay):
        at = sz.pay * i
        rows = slice(at, at + sz.misc)
        out[rows, :] = (own[rows, :].astype(F32) + other[rows, :].astype(F32)).astype(out.dtype)
        rows = slice(at + sz.misc, at + sz.pay)
        total = own[rows, :].astype(F32) + other[rows, :].astype(F32)
        parts = three_parts(total[2:3] + total[3:4] + total[4:5])
        row_at = lax.broadcasted_iota(jnp.int32, total.shape, 0)
        for j in range(3):
            total = jnp.where(row_at == 2 + j, parts[j], total)
        out[rows, :] = total.astype(out.dtype)


def add_pay(sz, own, other, kind):
    return pl.pallas_call(
        functools.partial(add_kernel, sz),
        out_shape=jax.ShapeDtypeStruct(own.shape, kind),
        compiler_params=PARAMS,
    )(own, other)


def unpacked(sz, grad):
    def wide(at, rows):
        return jnp.concatenate([grad[at : at + rows, :], grad[at + rows : at + 2 * rows, :]], 1)

    one = wide(0, 2 * sz.hold)
    two = wide(sz.rows_one, 2 * sz.group)
    at = sz.rows_one + sz.rows_two
    three = grad[at : at + sz.head, :].T
    misc = grad[sz.misc : sz.misc + 8, :]
    hidden = jnp.concatenate([misc[0:1, : sz.group], misc[0:1, sz.group : 2 * sz.group]], 0)
    return (
        [one[s * sz.hold : s * sz.hold + sz.feat] for s in range(2)],
        [two[s * sz.group : (s + 1) * sz.group] for s in range(2)],
        [three[s * sz.group : (s + 1) * sz.group, : sz.classes] for s in range(2)],
        [hidden],
        [misc[1:2, : sz.classes]],
        misc,
    )


def lamb_kernel(sz, grad, w1, w2, w3, wh, wb, f1, f2, f3, fh, fb, s1, s2, s3, sh, sb, *outs):
    params = (w1, w2, w3, wh, wb)
    firsts = (f1, f2, f3, fh, fb)
    seconds = (s1, s2, s3, sh, sb)
    moments, squares, updates = outs[:5], outs[5:10], outs[10:15]
    sums_ref, totals_ref = outs[15], outs[16]
    grads = unpacked(sz, grad)
    lane_at = lax.broadcasted_iota(jnp.int32, (8, LANES), 1)
    row_at = lax.broadcasted_iota(jnp.int32, (8, LANES), 0)
    sums = jnp.zeros((8, LANES), F32)
    for i in range(5):
        weight_sum = jnp.zeros((1, 1), F32)
        update_sum = jnp.zeros((1, 1), F32)
        for s in range(len(grads[i])):
            at = (s,) if i < 3 else (Ellipsis,)
            g = grads[i][s]
            w = params[i][at]
            m = BETA_ONE * firsts[i][at] + (1.0 - BETA_ONE) * g
            v = BETA_TWO * seconds[i][at] + (1.0 - BETA_TWO) * g * g
            u = (m / (1.0 - BETA_ONE**STEP)) / (jnp.sqrt(v / (1.0 - BETA_TWO**STEP)) + ADAM_EPS) + DECAY_RATE * w
            moments[i][at] = m
            squares[i][at] = v
            updates[i][at] = u
            weight_sum = weight_sum + jnp.sum(jnp.sum(w * w, 0, keepdims=True), 1, keepdims=True)
            update_sum = update_sum + jnp.sum(jnp.sum(u * u, 0, keepdims=True), 1, keepdims=True)
        if i == 4:
            weight_sum = 0.25 * weight_sum
            update_sum = 0.25 * update_sum
        sums = jnp.where((lane_at == i) & (row_at == 0), weight_sum, sums)
        sums = jnp.where((lane_at == i) & (row_at == 1), update_sum, sums)
    sums_ref[...] = sums
    misc = grads[5]
    totals_ref[...] = jnp.broadcast_to(misc[2:3] + misc[3:4] + misc[4:5], (8, LANES))


def lamb(sz, grad, params, firsts, seconds):
    shape = jax.ShapeDtypeStruct
    like = [shape(item.shape, F32) for item in params]
    return pl.pallas_call(
        functools.partial(lamb_kernel, sz),
        out_shape=tuple(like * 3 + [shape((8, LANES), F32)] * 2),
        compiler_params=PARAMS,
    )(grad, *params, *firsts, *seconds)


def step_kernel(own, other, w1, w2, w3, wh, wb, u1, u2, u3, uh, ub, n1, n2, n3, nh, nb, norms_ref):
    norms = jnp.sqrt(own[...] + other[...])
    norms_ref[...] = norms[0:2, 0:5]
    for i, (w, u, n) in enumerate(
        ((w1, u1, n1), (w2, u2, n2), (w3, u3, n3), (wh, uh, nh), (wb, ub, nb))
    ):
        ratio = LEARN_RATE * (norms[0:1, i : i + 1] / norms[1:2, i : i + 1])
        for s in range(w.shape[0] if i < 3 else 1):
            at = (s,) if i < 3 else (Ellipsis,)
            n[at] = w[at] - ratio * u[at]


def take_step(own, other, params, updates):
    shape = jax.ShapeDtypeStruct
    return pl.pallas_call(
        step_kernel,
        out_shape=tuple([shape(item.shape, F32) for item in params] + [shape((2, 5), F32)]),
        compiler_params=PARAMS,
    )(own, other, *params, *updates)


def swap(value, axis, count, bit):
    return lax.ppermute(value, axis, [(i, i ^ bit) for i in range(count)])


def weight_message(sz, w1, w2, w3, hidden_bias):
    one = jnp.pad(w1, ((0, 0), (0, sz.hold - sz.feat), (0, 0))).reshape(2 * sz.hold, sz.hid)
    two = jnp.concatenate([w2[0], w2[1]], 1)
    three = jnp.pad(w3, ((0, 0), (0, 0), (0, LANES - sz.classes)))
    three = jnp.concatenate([three[0], three[1]], 1)
    high = lax.reduce_precision(hidden_bias, 8, 7)
    middle = lax.reduce_precision(hidden_bias - high, 8, 7)
    bias = jnp.stack([high, middle, hidden_bias - high - middle], 1).reshape(6, sz.group).T
    bias = jnp.pad(bias, ((0, 0), (0, LANES - 6)))
    return jnp.concatenate([one, two, three, bias], 1).astype(BF)


def shards(
    features, neighbors_one, present_one, neighbors_two, present_two, neighbors_three, present_three,
    labels, seed_weight, serve_rows, take_seed, fetch_live,
    weight_one, weight_two, weight_three, hidden_bias, head_bias,
    first_one, first_two, first_three, first_hidden, first_head,
    second_one, second_two, second_three, second_hidden, second_head,
):
    sz = Sizes(features, neighbors_one, neighbors_two, neighbors_three, weight_two, weight_three, serve_rows)
    part = lax.axis_index("col")
    mixed = layer_one_means(sz, features, neighbors_one, present_one)
    weights = weight_message(sz, weight_one, weight_two, weight_three, hidden_bias)

    def message(target):
        return jnp.concatenate(
            [
                lax.dynamic_slice_in_dim(mixed, sz.a_start(target), sz.n_a, 1),
                lax.dynamic_slice_in_dim(mixed, sz.b_start(target), sz.n_b, 1),
                lax.dynamic_slice_in_dim(mixed, sz.own * target, sz.own, 1),
                weights,
            ],
            1,
        )

    messages = [message(part)]
    for r in range(1, 4):
        messages.append(swap(message(part ^ r), "col", 4, r))
    alive = jnp.arange(sz.slot, dtype=jnp.int32)[None, :] < fetch_live[:, None]
    info = jnp.stack([serve_rows.reshape(-1), take_seed.reshape(-1), alive.astype(jnp.int32).reshape(-1)], 1)
    saved = forward(sz, messages, neighbors_two, present_two, neighbors_three, present_three, info)
    sent = jnp.broadcast_to(saved[-1].reshape(sz.dp, 1, sz.slot, 3 * sz.hid), (sz.dp, 4, sz.slot, 3 * sz.hid))
    received = lax.all_to_all(
        sent.reshape(4 * sz.slots, 3 * sz.hid), ("dp", "col"), split_axis=0, concat_axis=0, tiled=True
    )
    bias_column = jnp.pad(head_bias, (0, sz.head - sz.classes))[:, None]
    keep, send = backward(
        sz, messages, present_two, present_three, info, labels[None, :], seed_weight[None, :], bias_column, saved, received
    )
    total = add_pay(sz, keep, swap(send, "col", 4, 1), BF)
    grad = add_pay(sz, total[: sz.pay], swap(total[sz.pay :], "col", 4, 2), BF)
    bit = 1
    while bit < sz.dp:
        grad = add_pay(sz, grad, swap(grad, "dp", sz.dp, bit), BF if 2 * bit < sz.dp else F32)
        bit *= 2
    params = (weight_one, weight_two, weight_three, hidden_bias, head_bias[None, :])
    firsts = (first_one, first_two, first_three, first_hidden, first_head[None, :])
    seconds = (second_one, second_two, second_three, second_hidden, second_head[None, :])
    outs = lamb(sz, grad, params, firsts, seconds)
    moments, squares, updates = outs[:5], outs[5:10], outs[10:15]
    sums, totals = outs[15], outs[16]
    pair = sums + swap(sums, "col", 4, 1)
    fresh = take_step(pair, swap(pair, "col", 4, 2), params, updates)
    return (
        *fresh[:4],
        fresh[4][0],
        *moments[:4],
        moments[4][0],
        *squares[:4],
        squares[4][0],
        fresh[5],
        totals[0, 0],
        totals[0, 1],
    )


def solution(mesh):
    wide = P(None, "col", None)
    tree = [wide, wide, wide, P(None, "col"), P()]
    return jax.shard_map(
        shards,
        mesh=mesh,
        in_specs=(
            P("col", "dp"),
            *[P(None, "dp")] * 6,
            P("dp"),
            P("dp"),
            P("dp", None),
            P("dp", None),
            P("dp"),
            *tree,
            *tree,
            *tree,
        ),
        out_specs=(*tree, *tree, *tree, P(), P(), P()),
        check_vma=False,
    )
```

time: 855 us -> 164 us (0.19); the launches traced: 844 us -> 163 us
  waiting for transfers between devices: 315 us -> 57.7 us
  matrix products: 244 us -> 0 us
  blocking collectives: 79.4 us -> 0 us
  other arithmetic: 74.7 us -> 3.23 us
  Pallas kernels: 0 us -> 52.1 us
  loops' own time: 32.9 us -> 0 us
  local copies, waits for them, and re-layouts: 60.8 us -> 35.3 us
  between operations: 24 us -> 0.88 us
    dot_general x38 -> x0, matrix products: 244 us -> none  [the longest x21 177 us: neighbor_one_block(): jnp.dot(counts, window, precision=EXACT, preferred_element_type=jnp.float32)]
    psum x3 -> x0, waiting for transfers between devices: 160 us -> none  [the longest x2 142 us: shards(): lax.psum((grads_weight[0], grads_weight[1], grad_head_weight, grad_hidden...]
    reduce_scatter x2 -> x0, waiting for transfers between devices: 105 us -> none  [summed_columns(): lax.psum_scatter(partial_value, 'col', scatter_dimension=1, tiled=True)]
    psum x6 -> x0, blocking collectives: 79.4 us -> none  [the longest x1 40.2 us: shards(): lax.psum((first_col * ce_total + dist_total, first_col * jnp.sum(weightin...]
    pallas_call x0 -> x10, Pallas kernels: none -> 52.1 us  [the longest x1 17.2 us: forward(): pl.pallas_call(functools.partial(forward_kernel, sz), out_shape=(shape((s...]
    ppermute x0 -> x10, waiting for transfers between devices: none -> 45.4 us  [swap(): return lax.ppermute(value, axis, [(i, i ^ bit) for i in range(count)])]
    all_gather x2 -> x0, waiting for transfers between devices: 43.7 us -> none  [column_grads(): grad_full = lax.all_gather(grad_result, 'col', axis=1, tiled=True)]
    another operation x3 -> x0, loops' own time: 32.9 us -> none  [the longest x2 27.5 us: neighbor_mean(): lax.map(neighbor_one_block, jnp.arange(count_blocks, dtype=jnp.int32))]
  transfers between devices with their start and end apart: 9 -> 11, of which waited for: 8 -> 9; matrix products, arithmetic and copies ran while one was open for 3% -> 8% of each run, Pallas kernels for 0% -> 0%
where the time goes in v1:
time: 164 us; the launch traced here: 163 us
  waiting for transfers between devices  57.7 us (35%)
  Pallas kernels  52.1 us (32%)
  local copies, waits for them, and re-layouts  35.3 us (22%)
  starting transfers between devices  13.6 us (8%)
  other arithmetic  3.23 us (2%)
    ppermute x10, waiting for transfers between devices, swap(): return lax.ppermute(value, axis, [(i, i ^ bit) for i in range(count)])  45.4 us
    unnamed x65, local copies, waits for them, and re-layouts  28.2 us
    pallas_call x1, Pallas kernels, forward(): pl.pallas_call(functools.partial(forward_kernel, sz), out_shape=(shape((s...  17.2 us
    pallas_call x1, Pallas kernels, backward(): pl.pallas_call(functools.partial(backward_kernel, sz), out_shape=(shape((...  13.1 us
    all_to_all x1, waiting for transfers between devices, shards(): lax.all_to_all(sent.reshape(4 * sz.slots, 3 * sz.hid), ('dp', 'col'), spl...  12.3 us
    pallas_call x1, Pallas kernels, layer_one_means(): pl.pallas_call(functools.partial(mean_kernel, sz), out_shape=jax.ShapeDty...  9.06 us
    pallas_call x5, Pallas kernels, add_pay(): pl.pallas_call(functools.partial(add_kernel, sz), out_shape=jax.ShapeDtyp...  8.43 us
    ppermute x10, starting transfers between devices, swap(): return lax.ppermute(value, axis, [(i, i ^ bit) for i in range(count)])  7.58 us
  transfers between devices with their start and end apart: 11, of which 9 were waited for; matrix products, arithmetic and copies ran while one was open for 8% of the time, Pallas kernels for 0%

profile of v1, /device:TPU:0, one launch (start us, length us, event | category | flops | bytes accessed | tf_op | source)
XLA Modules:
  0.0 162.8 jit_solution(5126702053156114038)
XLA Ops:
  4.2 9.1 %shard_map.394 = bf16[64,8192]{1,0:T(8,128)(2,1)} custom-call(bf16[25,32768]{1,0:T(8,128)(2,1)} %feat_ref.1, s32[5,8192]{1,0:T(8,128)} %nbr_ref.1, s32[5,8192]{1,0:T(8,128)} %pres_ref.1), custom_call_target="tpu_custom_call" | custom-call | tf_op jit(solution)/shard_map/pallas_call | solution.py:126
  13.3 2.8 %dynamic-slice_dynamic-update-slice_fusion = (bf16[64,4864]{1,0:T(8,128)(2,1)S(1)}, bf16[64,4864]{1,0:T(8,128)(2,1)}, bf16[64,4864]{1,0:T(8,128)(2,1)}, bf16[64,4864]{1,0:T(8,128)(2,1)S(1)}) fusion(bf16[64,8192]{1,0:T(8,128)(2,1)} %shard_map.394, s32[]{:T(128)S(6)} %min.16, s32[]{:T(128)S(6)} %min.15, s32[]{:T(128)S(6)} %min.14, s32[]{:T(128)S(6)} %min.13), kind=kLoop, calls=%fused_computation | loop fusion | bytes 2883600
  16.1 2.0 %dynamic-slice_dynamic-update-slice_fusion.4 = (bf16[64,4864]{1,0:T(8,128)(2,1)S(1)}, bf16[64,4864]{1,0:T(8,128)(2,1)}, bf16[64,4864]{1,0:T(8,128)(2,1)}, bf16[64,4864]{1,0:T(8,128)(2,1)S(1)}) fusion(bf16[64,4864]{1,0:T(8,128)(2,1)S(1)} %get-tuple-element.148, bf16[64,8192]{1,0:T(8,128)(2,1)} %shard_map.394, s32[]{:T(128)S(6)} %max.32, ...), kind=kLoop, calls=%fused_computation.4 | loop fusion | bytes 786448
  18.1 1.4 constant_dynamic-update-slice_fusion.27
  23.8 2.5 %collective-permute-start.1 = (bf16[64,4864]{1,0:T(8,128)(2,1)}, bf16[64,4864]{1,0:T(8,128)(2,1)S(1)}, u32[]{:S(2)}, u32[]{:S(2)}) collective-permute-start(bf16[64,4864]{1,0:T(8,128)(2,1)} %get-tuple-element.176), channel_id=1, source_target_pairs={{0,2},{1,3},{2,0},{3,1},{4,6},{5,7},{6,4},{7,5},{8,10},{9,11},{10,... | collective-permute-start | bytes 1867784 | tf_op jit(solution)/shard_map/ppermute | solution.py:570
  27.5 13.9 %collective-permute-done.1.m2 = bf16[64,4864]{1,0:T(8,128)(2,1)S(1)} collective-permute-done((bf16[64,4864]{1,0:T(8,128)(2,1)}, bf16[64,4864]{1,0:T(8,128)(2,1)S(1)}, u32[]{:S(2)}, u32[]{:S(2)}) %collective-permute-start.1) | collective-permute-done | bytes 622624 | tf_op jit(solution)/shard_map/ppermute | solution.py:570
  41.4 13.0 %collective-permute-done.2.m3 = bf16[64,4864]{1,0:T(8,128)(2,1)S(1)} collective-permute-done((bf16[64,4864]{1,0:T(8,128)(2,1)S(1)}, bf16[64,4864]{1,0:T(8,128)(2,1)S(1)}, u32[]{:S(2)}, u32[]{:S(2)}) %collective-permute-start.2) | collective-permute-done | bytes 622624 | tf_op jit(solution)/shard_map/ppermute | solution.py:570
  55.2 17.2 %shard_map.395 = (f32[256,3712]{1,0:T(8,128)}, f32[1,3712]{1,0:T(1,128)}, bf16[512,896]{1,0:T(8,128)(2,1)}, f32[256,896]{1,0:T(8,128)}, f32[1,896]{1,0:T(1,128)}...) custom-call(bf16[64,4864]{1,0:T(8,128)(2,1)} %copy-done, ...), custom_call_target="tpu_custom_call" | custom-call | tf_op jit(solution)/shard_map/pallas_call | solution.py:270
  72.3 1.7 %broadcast_in_dim.31 = bf16[8,4,8,768]{3,2,1,0:T(8,128)(2,1)} broadcast(bf16[8,8,768]{2,1,0:T(8,128)(2,1)} %bitcast.64), dimensions={0,2,3} | broadcast | bytes 491520 | tf_op jit(solution)/shard_map/broadcast_in_dim | solution.py:614
  74.0 6.1 %all-to-all-start = ((bf16[32,8,768]{2,1,0:T(8,128)(2,1)}), bf16[32,8,768]{2,1,0:T(8,128)(2,1)S(1)}, u32[]{:S(2)}, u32[]{:S(2)}) async-start(bf16[32,8,768]{2,1,0:T(8,128)(2,1)} %bitcast.13), calls=%async_computation | async-start | bytes 786432 | tf_op jit(solution)/shard_map/all_to_all | solution.py:615
  80.8 12.3 %all-to-all-done = bf16[32,8,768]{2,1,0:T(8,128)(2,1)S(1)} async-done(((bf16[32,8,768]{2,1,0:T(8,128)(2,1)}), bf16[32,8,768]{2,1,0:T(8,128)(2,1)S(1)}, u32[]{:S(2)}, u32[]{:S(2)}) %all-to-all-start) | async-done | bytes 393248 | tf_op jit(solution)/shard_map/all_to_all | solution.py:615
  93.8 13.1 %shard_map.396 = (bf16[896,128]{1,0:T(8,128)(2,1)}, bf16[896,128]{1,0:T(8,128)(2,1)}) custom-call(bf16[64,4864]{1,0:T(8,128)(2,1)} %copy-done, bf16[64,4864]{1,0:T(8,128)(2,1)} %copy-done.1, bf16[64,4864]{1,0:T(8,128)(2,1)} %copy-done.2, bf16[64,4864]{1,0:T(8,128)(2,1)} %copy-done.3, s32[10,2048]{1,0:T(8,128)} %pres2.3, s32[15,512]{1,0:T(8,128)} %pres3.3, ...), custom_call_target="tpu_custom_call" | custom-call | tf_op jit(solution)/shard_map/pallas_call | solution.py:442
  107.1 1.7 %collective-permute-done.3.other = bf16[896,128]{1,0:T(8,128)(2,1)S(1)} collective-permute-done((bf16[896,128]{1,0:T(8,128)(2,1)}, bf16[896,128]{1,0:T(8,128)(2,1)S(1)}, u32[]{:S(2)}, u32[]{:S(2)}) %collective-permute-start.3) | collective-permute-done | bytes 229408 | tf_op jit(solution)/shard_map/ppermute | solution.py:570
  109.5 1.8 %shard_map.397 = bf16[896,128]{1,0:T(8,128)(2,1)} custom-call(bf16[896,128]{1,0:T(8,128)(2,1)} %get-tuple-element.61.own, bf16[896,128]{1,0:T(8,128)(2,1)} %copy-done.6), custom_call_target="tpu_custom_call" | custom-call | tf_op jit(solution)/shard_map/pallas_call | solution.py:476
  111.3 1.6 fusion.5
  113.5 4.6 %collective-permute-done.4.other = bf16[448,128]{1,0:T(8,128)(2,1)S(1)} collective-permute-done((bf16[448,128]{1,0:T(8,128)(2,1)S(1)}, bf16[448,128]{1,0:T(8,128)(2,1)S(1)}, u32[]{:S(2)}, u32[]{:S(2)}) %collective-permute-start.4) | collective-permute-done | bytes 114720 | tf_op jit(solution)/shard_map/ppermute | solution.py:570
  118.8 1.6 %shard_map.398.own = bf16[448,128]{1,0:T(8,128)(2,1)} custom-call(bf16[448,128]{1,0:T(8,128)(2,1)} %get-tuple-element.153.own, bf16[448,128]{1,0:T(8,128)(2,1)} %copy-done.9), custom_call_target="tpu_custom_call" | custom-call | tf_op jit(solution)/shard_map/pallas_call | solution.py:476
  121.4 4.0 %collective-permute-done.5.other = bf16[448,128]{1,0:T(8,128)(2,1)S(1)} collective-permute-done((bf16[448,128]{1,0:T(8,128)(2,1)}, bf16[448,128]{1,0:T(8,128)(2,1)S(1)}, u32[]{:S(2)}, u32[]{:S(2)}) %collective-permute-start.5) | collective-permute-done | bytes 114720 | tf_op jit(solution)/shard_map/ppermute | solution.py:570
  126.0 1.6 %shard_map.399.own = bf16[448,128]{1,0:T(8,128)(2,1)} custom-call(bf16[448,128]{1,0:T(8,128)(2,1)} %shard_map.398.own, bf16[448,128]{1,0:T(8,128)(2,1)} %copy-done.10), custom_call_target="tpu_custom_call" | custom-call | tf_op jit(solution)/shard_map/pallas_call | solution.py:476
  128.7 4.0 %collective-permute-done.6.other = bf16[448,128]{1,0:T(8,128)(2,1)S(1)} collective-permute-done((bf16[448,128]{1,0:T(8,128)(2,1)}, bf16[448,128]{1,0:T(8,128)(2,1)S(1)}, u32[]{:S(2)}, u32[]{:S(2)}) %collective-permute-start.6) | collective-permute-done | bytes 114720 | tf_op jit(solution)/shard_map/ppermute | solution.py:570
  133.3 1.6 %shard_map.400.own = bf16[448,128]{1,0:T(8,128)(2,1)} custom-call(bf16[448,128]{1,0:T(8,128)(2,1)} %shard_map.399.own, bf16[448,128]{1,0:T(8,128)(2,1)} %copy-done.11), custom_call_target="tpu_custom_call" | custom-call | tf_op jit(solution)/shard_map/pallas_call | solution.py:476
  139.2 2.9 %collective-permute-done.7.other = bf16[448,128]{1,0:T(8,128)(2,1)S(1)} collective-permute-done((bf16[448,128]{1,0:T(8,128)(2,1)}, bf16[448,128]{1,0:T(8,128)(2,1)S(1)}, u32[]{:S(2)}, u32[]{:S(2)}) %collective-permute-start.7) | collective-permute-done | bytes 114720 | tf_op jit(solution)/shard_map/ppermute | solution.py:570
  142.8 1.7 %shard_map.401.grad = f32[448,128]{1,0:T(8,128)} custom-call(bf16[448,128]{1,0:T(8,128)(2,1)} %shard_map.400.own, bf16[448,128]{1,0:T(8,128)(2,1)} %copy-done.8), custom_call_target="tpu_custom_call" | custom-call | tf_op jit(solution)/shard_map/pallas_call | solution.py:476
  144.4 2.4 %shard_map.402 = (f32[2,25,256]{2,1,0:T(8,128)}, f32[2,64,256]{2,1,0:T(8,128)}, f32[2,64,47]{2,1,0:T(8,128)}, f32[2,64]{1,0:T(2,128)}, f32[1,47]{1,0:T(1,128)}, ...) custom-call(f32[448,128]{1,0:T(8,128)} %shard_map.401.grad, ...), custom_call_target="tpu_custom_call" | custom-call | tf_op jit(solution)/shard_map/pallas_call | solution.py:541
  146.9 1.4 collective-permute-done.8
  151.1 1.5 copy.105
  152.6 1.5 copy.107
  154.1 1.5 copy.106
  155.7 1.5 copy.108
  157.8 2.0 %shard_map.403 = (f32[2,25,256]{2,1,0:T(8,128)}, f32[2,64,256]{2,1,0:T(8,128)}, f32[2,64,47]{2,1,0:T(8,128)}, f32[2,64]{1,0:T(2,128)}, f32[1,47]{1,0:T(1,128)}, /*index=5*/f32[2,5]{1,0:T(2,128)}) custom-call(f32[8,128]{1,0:T(8,128)} %copy-done.16, f32[8,128]{1,0:T(8,128)} %copy-done.17, f32[2,25,256]{2,1,0:T(8,128)} %copy.95.w1, f32[2,64,256]{2,1,0:T(8,128)} %w2.3, ...), custom_call_target="tpu_custom_call" | custom-call | tf_op jit(solution)/shard_map/pallas_call | solution.py:562
  159.8 1.5 copy.103
  161.3 1.5 copy.104
  (87 shorter events, 25.0 us)
Async XLA Ops:
  3.3 12.8 %copy-start.5 = (f32[2,64,47]{2,1,0:T(8,128)}, f32[2,64,47]{2,1,0:T(8,128)S(1)}, u32[]{:S(2)}) copy-start(f32[2,64,47]{2,1,0:T(8,128)S(1)} %copy.89.w3) | copy-start | bytes 72196
  13.3 13.1 %copy-start.21 = (s32[8]{0:T(128)S(1)}, s32[8]{0:T(128)}, u32[]{:S(2)}) copy-start(s32[8]{0:T(128)} %param.38) | copy-start | bytes 100
  13.3 13.3 %copy-start.18 = (s32[8,8]{1,0:T(8,128)S(1)}, s32[8,8]{1,0:T(8,128)}, u32[]{:S(2)}) copy-start(s32[8,8]{1,0:T(8,128)} %param.36) | copy-start | bytes 772
  13.3 13.3 %copy-start.19 = (s32[8,8]{1,0:T(8,128)S(1)}, s32[8,8]{1,0:T(8,128)}, u32[]{:S(2)}) copy-start(s32[8,8]{1,0:T(8,128)} %param.37) | copy-start | bytes 772
  23.3 31.0 %copy-start = (bf16[64,4864]{1,0:T(8,128)(2,1)}, bf16[64,4864]{1,0:T(8,128)(2,1)S(1)}, u32[]{:S(2)}) copy-start(bf16[64,4864]{1,0:T(8,128)(2,1)S(1)} %get-tuple-element.177.m0) | copy-start | bytes 1867780
  23.3 4.2 %collective-permute-start = (bf16[64,4864]{1,0:T(8,128)(2,1)}, bf16[64,4864]{1,0:T(8,128)(2,1)S(1)}, u32[]{:S(2)}, u32[]{:S(2)}) collective-permute-start(bf16[64,4864]{1,0:T(8,128)(2,1)} %get-tuple-element.175), channel_id=1, source_target_pairs={{0,1},{1,0},{2,3},{3,2},{4,5},{5,4},{6,7},{7,6},{8,9},{9,8},{10,11... | collective-permute-start | bytes 1867784 | tf_op jit(solution)/shard_map/ppermute | solution.py:570
  23.8 17.6 %collective-permute-start.1 = (bf16[64,4864]{1,0:T(8,128)(2,1)}, bf16[64,4864]{1,0:T(8,128)(2,1)S(1)}, u32[]{:S(2)}, u32[]{:S(2)}) collective-permute-start(bf16[64,4864]{1,0:T(8,128)(2,1)} %get-tuple-element.176), channel_id=1, source_target_pairs={{0,2},{1,3},{2,0},{3,1},{4,6},{5,7},{6,4},{7,5},{8,10},{9,11},{10,... | collective-permute-start | bytes 1867784 | tf_op jit(solution)/shard_map/ppermute | solution.py:570
  26.3 53.8 %copy-start.20 = (f32[47]{0:T(128)S(1)}, f32[47]{0:T(128)}, u32[]{:S(2)}) copy-start(f32[47]{0:T(128)} %param.43) | copy-start | bytes 568
  26.3 28.1 %collective-permute-start.2 = (bf16[64,4864]{1,0:T(8,128)(2,1)S(1)}, bf16[64,4864]{1,0:T(8,128)(2,1)S(1)}, u32[]{:S(2)}, u32[]{:S(2)}) collective-permute-start(bf16[64,4864]{1,0:T(8,128)(2,1)S(1)} %get-tuple-element.174), channel_id=1, source_target_pairs={{0,3},{1,2},{2,1},{3,0},{4,7},{5,6},{6,5},{7,4},{8,11},{9,10},{10,... | collective-permute-start | bytes 1867784 | tf_op jit(solution)/shard_map/ppermute | solution.py:570
  27.5 26.9 %copy-start.1 = (bf16[64,4864]{1,0:T(8,128)(2,1)}, bf16[64,4864]{1,0:T(8,128)(2,1)S(1)}, u32[]{:S(2)}) copy-start(bf16[64,4864]{1,0:T(8,128)(2,1)S(1)} %collective-permute-done.m1) | copy-start | bytes 1867780
  41.4 13.0 %copy-start.2 = (bf16[64,4864]{1,0:T(8,128)(2,1)}, bf16[64,4864]{1,0:T(8,128)(2,1)S(1)}, u32[]{:S(2)}) copy-start(bf16[64,4864]{1,0:T(8,128)(2,1)S(1)} %collective-permute-done.1.m2) | copy-start | bytes 1867780
  54.3 0.8 copy-start.3
  74.0 19.1 %all-to-all-start = ((bf16[32,8,768]{2,1,0:T(8,128)(2,1)}), bf16[32,8,768]{2,1,0:T(8,128)(2,1)S(1)}, u32[]{:S(2)}, u32[]{:S(2)}) async-start(bf16[32,8,768]{2,1,0:T(8,128)(2,1)} %bitcast.13), calls=%async_computation | async-start | bytes 786432 | tf_op jit(solution)/shard_map/all_to_all | solution.py:615
  93.1 0.8 copy-start.4
  107.0 28.9 %copy-start.7 = (f32[2,25,256]{2,0,1:T(2,128)S(1)}, f32[2,25,256]{2,0,1:T(2,128)}, u32[]{:S(2)}) copy-start(f32[2,25,256]{2,0,1:T(2,128)} %param.39) | copy-start | bytes 153604
  107.0 29.6 %copy-start.14 = (f32[2,64,47]{1,0,2:T(2,128)S(1)}, f32[2,64,47]{1,0,2:T(2,128)}, u32[]{:S(2)}) copy-start(f32[2,64,47]{1,0,2:T(2,128)} %param.51) | copy-start | bytes 72196
  107.0 30.3 %copy-start.12 = (f32[2,25,256]{2,0,1:T(2,128)S(1)}, f32[2,25,256]{2,0,1:T(2,128)}, u32[]{:S(2)}) copy-start(f32[2,25,256]{2,0,1:T(2,128)} %param.44) | copy-start | bytes 153604
  107.0 30.9 %copy-start.15 = (f32[2,64,47]{1,0,2:T(2,128)S(1)}, f32[2,64,47]{1,0,2:T(2,128)}, u32[]{:S(2)}) copy-start(f32[2,64,47]{1,0,2:T(2,128)} %param.46) | copy-start | bytes 72196
  107.0 31.6 %copy-start.13 = (f32[2,25,256]{2,0,1:T(2,128)S(1)}, f32[2,25,256]{2,0,1:T(2,128)}, u32[]{:S(2)}) copy-start(f32[2,25,256]{2,0,1:T(2,128)} %param.49) | copy-start | bytes 153604
  107.0 1.8 %collective-permute-start.3 = (bf16[896,128]{1,0:T(8,128)(2,1)}, bf16[896,128]{1,0:T(8,128)(2,1)S(1)}, u32[]{:S(2)}, u32[]{:S(2)}) collective-permute-start(bf16[896,128]{1,0:T(8,128)(2,1)} %get-tuple-element.62), channel_id=1, source_target_pairs={{0,1},{1,0},{2,3},{3,2},{4,5},{5,4},{6,7},{7,6},{8,9},{9,8},{10,11... | collective-permute-start | bytes 688136 | tf_op jit(solution)/shard_map/ppermute | solution.py:570
  108.8 0.7 copy-start.6
  112.9 5.2 %collective-permute-start.4 = (bf16[448,128]{1,0:T(8,128)(2,1)S(1)}, bf16[448,128]{1,0:T(8,128)(2,1)S(1)}, u32[]{:S(2)}, u32[]{:S(2)}) collective-permute-start(bf16[448,128]{1,0:T(8,128)(2,1)S(1)} %get-tuple-element.152), channel_id=1, source_target_pairs={{0,2},{1,3},{2,0},{3,1},{4,6},{5,7},{6,4},{7,5},{8,10},{9,11},{10,... | collective-permute-start | bytes 344072 | tf_op jit(solution)/shard_map/ppermute | solution.py:570
  118.1 0.6 copy-start.9
  120.4 5.0 %collective-permute-start.5 = (bf16[448,128]{1,0:T(8,128)(2,1)}, bf16[448,128]{1,0:T(8,128)(2,1)S(1)}, u32[]{:S(2)}, u32[]{:S(2)}) collective-permute-start(bf16[448,128]{1,0:T(8,128)(2,1)} %shard_map.398.own), channel_id=1, source_target_pairs={{0,4},{4,0},{8,12},{12,8},{16,20},{20,16},{24,28},{28,24},{1,5},{5... | collective-permute-start | bytes 344072 | tf_op jit(solution)/shard_map/ppermute | solution.py:570
  125.4 0.6 copy-start.10
  127.7 5.0 %collective-permute-start.6 = (bf16[448,128]{1,0:T(8,128)(2,1)}, bf16[448,128]{1,0:T(8,128)(2,1)S(1)}, u32[]{:S(2)}, u32[]{:S(2)}) collective-permute-start(bf16[448,128]{1,0:T(8,128)(2,1)} %shard_map.399.own), channel_id=1, source_target_pairs={{0,8},{4,12},{8,0},{12,4},{16,24},{20,28},{24,16},{28,20},{1,9},{5... | collective-permute-start | bytes 344072 | tf_op jit(solution)/shard_map/ppermute | solution.py:570
  132.7 0.6 copy-start.11
  135.0 7.1 %collective-permute-start.7 = (bf16[448,128]{1,0:T(8,128)(2,1)}, bf16[448,128]{1,0:T(8,128)(2,1)S(1)}, u32[]{:S(2)}, u32[]{:S(2)}) collective-permute-start(bf16[448,128]{1,0:T(8,128)(2,1)} %shard_map.400.own), channel_id=1, source_target_pairs={{0,16},{4,20},{8,24},{12,28},{16,0},{20,4},{24,8},{28,12},{1,17},{... | collective-permute-start | bytes 344072 | tf_op jit(solution)/shard_map/ppermute | solution.py:570
  142.1 0.6 copy-start.8
  146.8 1.4 collective-permute-start.8
  149.0 8.3 %copy-start.16 = (f32[8,128]{1,0:T(8,128)}, f32[8,128]{1,0:T(8,128)S(1)}, u32[]{:S(2)}) copy-start(f32[8,128]{1,0:T(8,128)S(1)} %add.43.own) | copy-start | bytes 12292
  149.0 8.3 %collective-permute-start.9 = (f32[8,128]{1,0:T(8,128)S(1)}, f32[8,128]{1,0:T(8,128)S(1)}, u32[]{:S(2)}, u32[]{:S(2)}) collective-permute-start(f32[8,128]{1,0:T(8,128)S(1)} %add.43.own), channel_id=1, source_target_pairs={{0,2},{1,3},{2,0},{3,1},{4,6},{5,7},{6,4},{7,5},{8,10},{9,11},{10,... | collective-permute-start | bytes 12296 | tf_op jit(solution)/shard_map/ppermute | solution.py:570
  (1 other events, 0.6 us)

commit v2 on v1

v2 whole, which is shorter than its diff:
```python
import functools

import jax
import jax.numpy as jnp
from jax import lax
from jax.experimental import pallas as pl
from jax.experimental.pallas import tpu as pltpu
from jax.sharding import PartitionSpec as P

REACH = 64
STEP = 5
DIST_WEIGHT = 1.0
ROW_EPS = 1e-06
LEARN_RATE = 0.5
BETA_ONE = 0.9
BETA_TWO = 0.999
ADAM_EPS = 1e-06
DECAY_RATE = 0.01

BF = jnp.bfloat16
F32 = jnp.float32
LANES = 128
WINDOW = 768
SENTINEL = 4.0
MIB = 2**20
LOSS_BITS = 14
FIRST_MIB = 8
MEAN_MIB = 8
SEEDS_MIB = 16
REST_MIB = 28
BACK_MIB = 12


def cost(micros):
    return pl.CostEstimate(flops=int(micros * 10**9), bytes_accessed=1, transcendentals=0)


def call(kernel, outs, scratch, mib, *args, far_in=(), far_out=(), copies=0, micros=1):
    near = pl.BlockSpec(memory_space=pltpu.VMEM)
    far = pl.BlockSpec(memory_space=pltpu.HBM)
    scratch = [pltpu.VMEM(shape, kind) for shape, kind in scratch]
    args = [pltpu.with_memory_space_constraint(a, pltpu.HBM) if i in far_in else a for i, a in enumerate(args)]
    return pl.pallas_call(
        kernel,
        in_specs=[far if i in far_in else near for i in range(len(args))],
        out_specs=tuple(far if i in far_out else near for i in range(len(outs))),
        out_shape=tuple(
            pltpu.HBM(shape, kind) if i in far_out else jax.ShapeDtypeStruct(shape, kind)
            for i, (shape, kind) in enumerate(outs)
        ),
        scratch_shapes=scratch + ([pltpu.SemaphoreType.DMA((copies,))] if copies else []),
        compiler_params=pltpu.CompilerParams(vmem_limit_bytes=mib * MIB),
        cost_estimate=cost(micros),
    )(*args)


def start_copies(pairs, sems, first=0):
    copies = [pltpu.make_async_copy(src, dst, sems.at[first + i]) for i, (src, dst) in enumerate(pairs)]
    for copy in copies:
        copy.start()
    return copies


def wait_all(copies):
    for copy in copies:
        copy.wait()


class Sizes:
    def __init__(self, features, neighbors_one, neighbors_two, neighbors_three, weight_two, weight_three, serve_rows):
        self.feat = features.shape[0]
        self.main = self.feat - 1
        self.hold = 32
        self.base = features.shape[1]
        self.low = neighbors_one.shape[1]
        self.mid = neighbors_two.shape[1]
        self.seeds = neighbors_three.shape[1]
        self.hid = weight_two.shape[2]
        self.group = weight_two.shape[1]
        self.classes = weight_three.shape[2]
        self.head = -(-self.classes // 16) * 16
        self.own = self.seeds // 4
        self.n_b = 4 * self.own + 2 * LANES
        self.n_a = 16 * self.own + 6 * LANES
        self.n_mid = self.n_b + self.own
        self.n_low = self.n_a + self.n_mid
        self.tiles_b = self.n_b // LANES
        self.tiles_mid = self.n_mid // LANES
        self.tiles_low = self.n_low // LANES
        self.slots = serve_rows.shape[0] * serve_rows.shape[1]
        self.slot = serve_rows.shape[1]
        self.dp = serve_rows.shape[0]
        self.rows_one = 2 * 2 * self.hold
        self.rows_two = 4 * self.group
        self.at_three = self.rows_one + self.rows_two
        self.misc = self.at_three + self.head
        self.pay = self.misc + 16
        self.blocks = -(-self.pay // self.main)
        self.message_a = self.pair_lanes(self.n_a)
        self.message_b = self.pair_lanes(self.n_mid)
        self.full_b = self.message_b + LANES * self.blocks
        self.tiles_b_all = 16 * self.own // LANES + 1
        self.count_rows = WINDOW + 16
        hid, at = self.hid, self.n_mid
        places = {}
        for name, lanes in (
            ("turned1", hid), ("turned2", 2 * hid), ("weight2", 2 * hid), ("weight3", 2 * LANES), ("turned3", 2 * hid),
            ("states", self.n_b), ("embed", 2 * self.own), ("inputs2", 2 * self.own),
        ):
            places[name] = at
            at += lanes
        self.low_lanes = at
        at = 0
        for name, lanes in (("result1", self.n_mid), ("result2", self.own), ("bias", 2 * LANES)):
            places[name] = at
            at += lanes
        self.high_lanes = at
        at = 0
        for name, lanes in (("g1", hid), ("g2", 2 * hid), ("g3", 2 * hid), ("grad_b", self.n_b), ("grad_embed", self.own)):
            places[name] = at
            at += lanes
        self.part_lanes = at
        self.at = places

    def pair_lanes(self, lanes):
        return 2 * lanes + LANES * -(-2 * lanes // LANES // self.main)

    def a_start(self, part):
        return jnp.clip(16 * self.own * part - 3 * LANES, 0, self.low - self.n_a)

    def b_start(self, part):
        return jnp.maximum(4 * self.own * part - LANES, 0)

    def b_columns(self, part, tile):
        return pl.ds(aligned(jnp.minimum(self.b_start(part) + LANES * tile, self.mid - LANES)), LANES)

    def mid_columns(self, part, tile):
        if tile < self.tiles_b:
            return self.b_columns(part, tile)
        return pl.ds(aligned(self.own * part + LANES * (tile - self.tiles_b)), LANES)

    def ranges(self, part):
        return (
            (self.a_start(part), 0, self.n_a),
            (self.b_start(part), self.n_a, self.n_b),
            (self.own * part, self.n_a + self.n_b, self.own),
        )


def dot(a, b, over):
    return lax.dot_general(a, b, (((over[0],), (over[1],)), ((), ())), preferred_element_type=F32)


def two_parts(value):
    high = value.astype(BF)
    return high, (value - high.astype(F32)).astype(BF)


def three_parts(value):
    high = value.astype(BF).astype(F32)
    rest = value - high
    middle = rest.astype(BF).astype(F32)
    return high, middle, (rest - middle).astype(BF).astype(F32)


def aligned(value):
    return pl.multiple_of(value, LANES)


def sigmoid(value):
    return 1.0 / (1.0 + jnp.exp(-value))


def unpack_tile(sz, message, tail, tile):
    spare = jnp.zeros((sz.hold - sz.feat, LANES), F32)
    main = message[:, LANES * tile : LANES * (tile + 1)].astype(F32)
    return jnp.concatenate([main, tail[tile : tile + 1, :], spare], 0).astype(BF)


def mean_tiles(sz, tiles, feat_ref, nbr_ref, pres_ref, mean_ref, tail_ref, base_ref, code_ref, count_ref):
    last = feat_ref.shape[1] // LANES - 6
    slots = nbr_ref.shape[0]
    base_ref[...] = jnp.zeros_like(base_ref)
    if tiles % 8:
        code_ref[...] = jnp.full_like(code_ref, -1)
        count_ref[...] = jnp.ones_like(count_ref)
    for tile in range(feat_ref.shape[1] // LANES):
        row = feat_ref[:, LANES * tile : LANES * (tile + 1)].astype(F32)
        base_ref[8 + tile : 9 + tile, :] = row[sz.main : sz.feat]

    def one_tile(step, carry):
        lane = aligned(step * LANES)
        present = pres_ref[:, pl.ds(lane, LANES)]
        valid = present.astype(F32)
        counts = jnp.maximum(jnp.sum(valid, 0, keepdims=True), 1.0)
        first = jnp.clip(4 * step - 1, 0, last)
        links = nbr_ref[:, pl.ds(lane, LANES)]
        code = jnp.where(present > 0, links, -1)
        count_ref[pl.ds(step, 1), :] = counts
        for slot in range(slots):
            code_ref[slot, pl.ds(step, 1), :] = code[slot : slot + 1]
        local = links - first * LANES
        piece = local >> 7
        spot = local & 127
        sources = [
            feat_ref[:, pl.ds(aligned((first + j) * LANES), LANES)].astype(F32) for j in range(6)
        ]
        totals = [jnp.zeros((8, LANES), F32) for _ in range(sz.main // 8)]
        for slot in range(slots):
            spots = jnp.broadcast_to(spot[slot : slot + 1], (8, LANES))
            pieces = jnp.broadcast_to(piece[slot : slot + 1], (8, LANES))
            marks = jnp.broadcast_to(valid[slot : slot + 1], (8, LANES))
            for h in range(sz.main // 8):
                taken = None
                for j in range(6):
                    found = jnp.take_along_axis(
                        sources[j][8 * h : 8 * h + 8], spots, axis=1, mode="promise_in_bounds"
                    )
                    taken = found if j == 0 else jnp.where(pieces == j, found, taken)
                totals[h] = totals[h] + taken * marks
        mean_ref[:, pl.ds(lane, LANES)] = (jnp.concatenate(totals, 0) / counts).astype(BF)
        return carry

    lax.fori_loop(0, tiles // 4 * 4, one_tile, 0, unroll=4)
    for step in range(tiles // 4 * 4, tiles):
        one_tile(step, 0)
    sub = lax.broadcasted_iota(jnp.int32, (8, LANES), 0)

    for block in range(-(-tiles // 8)):
        total = jnp.zeros((8, LANES), F32)
        for slot in range(slots):
            code = code_ref[slot, 8 * block : 8 * (block + 1), :]
            piece = (code >> 7) - (4 * (8 * block + sub) - 1)
            taken = None
            for j in range(6):
                source = base_ref[pl.ds(8 + 32 * block - 1 + j, 8, stride=4), :]
                found = jnp.take_along_axis(source, code & 127, axis=1, mode="promise_in_bounds")
                taken = found if j == 0 else jnp.where(piece == j, found, taken)
            total = total + jnp.where(code >= 0, taken, 0.0)
        tail_ref[8 * block : 8 * (block + 1), :] = total / count_ref[8 * block : 8 * (block + 1), :]


def pack_pair(sz, ranges, feat_ref, base_ref, mean_ref, tail_ref, turn_ref, out_ref):
    turn_ref[...] = jnp.zeros_like(turn_ref)
    base = ranges[0][1]
    lanes = sum(count for _, _, count in ranges)
    tiles = lanes // LANES
    for first, at, count in ranges:
        at = at - base
        source = pl.ds(aligned(first), count)
        out_ref[:, at : at + count] = feat_ref[: sz.main, source]
        out_ref[:, lanes + at : lanes + at + count] = mean_ref[: sz.main, source]
        at, rows = at // LANES, count // LANES
        turn_ref[at : at + rows, :] = base_ref[pl.ds(8 + first // LANES, rows), :]
        turn_ref[tiles + at : tiles + at + rows, :] = tail_ref[pl.ds(first // LANES, rows), :]
    for block in range(-(-2 * tiles // sz.main)):
        at = 2 * lanes + LANES * block
        out_ref[:, at : at + LANES] = turn_ref[sz.main * block : sz.main * (block + 1), :].astype(BF)


def own_pair(sz, ranges, feat_ref, mean_ref, tail_ref, own_ref):
    spare = jnp.zeros((sz.hold - sz.feat, LANES), F32)
    base = ranges[0][1]
    for start, at, count in ranges:
        for tile in range(count // LANES):
            lanes = pl.ds(aligned(start + LANES * tile), LANES)
            out_lanes = slice(at - base + LANES * tile, at - base + LANES * (tile + 1))
            own = [feat_ref[:, lanes].astype(F32), spare]
            own_ref[: sz.hold, out_lanes] = jnp.concatenate(own, 0).astype(BF)
            tail = tail_ref[pl.ds(start // LANES + tile, 1), :]
            average = [mean_ref[:, lanes].astype(F32), tail, spare]
            own_ref[sz.hold :, out_lanes] = jnp.concatenate(average, 0).astype(BF)


def mean_scratch(sz, tiles, slots):
    return [
        ((sz.main, LANES * tiles), BF),
        ((-(-tiles // 8) * 8, LANES), F32),
        ((2 * sz.main, LANES), F32),
        ((4 * -(-tiles // 8) * 8 + 16, LANES), F32),
        ((slots, -(-tiles // 8) * 8, LANES), jnp.int32),
        ((-(-tiles // 8) * 8, LANES), F32),
    ]


def unpack_pair(sz, message, r, lanes, turn_ref, out_ref):
    tiles = lanes // LANES
    for block in range(-(-2 * tiles // sz.main)):
        at = 2 * lanes + LANES * block
        turn_ref[sz.main * block : sz.main * (block + 1), :] = message[:, at : at + LANES].astype(F32)
    tail = turn_ref[...]
    for tile in range(2 * tiles):
        row = sz.hold * (r if tile < tiles else 4 + r)
        at = LANES * (tile % tiles)
        out_ref[row : row + sz.hold, at : at + LANES] = unpack_tile(sz, message, tail, tile)


def first_kernel(
    sz, features, neighbors, present, w1_in, w2_in, w3_in, wh_in, own_b, packed, m1, m2, m3,
    feat_ref, nbr_ref, pres_ref, w1, w2, w3, wh, own_ref,
    mean_ref, tail_ref, turn_ref, base_ref, code_ref, count_ref, one_ref, three_ref, pack, sems,
):
    part = lax.axis_index("col")
    rows = pl.ds(0, nbr_ref.shape[1])
    copies = start_copies(
        (
            (features.at[:, pl.ds(0, feat_ref.shape[1])], feat_ref),
            (neighbors.at[:, rows], nbr_ref),
            (present.at[:, rows], pres_ref),
            (w1_in, w1),
            (w2_in, w2),
            (w3_in, w3),
            (wh_in, wh),
        ),
        sems,
    )
    wait_all(copies[:3])
    mean_tiles(sz, sz.tiles_b_all, feat_ref, nbr_ref, pres_ref, mean_ref, tail_ref, base_ref, code_ref, count_ref)
    wait_all(copies[3:])
    one_ref[...] = jnp.zeros_like(one_ref)
    three_ref[...] = jnp.zeros_like(three_ref)
    for s in range(2):
        for f in range(sz.feat):
            one_ref[s * sz.hold + f : s * sz.hold + f + 1, :] = w1[f, s : s + 1, :]
        for c in range(sz.classes):
            three_ref[c : c + 1, s * sz.group : (s + 1) * sz.group] = w3[c, s : s + 1, :]
    at = 0
    for half in range(sz.hid // LANES):
        pack[at : at + 2 * sz.hold, :] = one_ref[:, LANES * half : LANES * (half + 1)]
        at += 2 * sz.hold
    for half in range(sz.hid // LANES):
        for s in range(2):
            pack[at : at + sz.group, :] = w2[s, :, LANES * half : LANES * (half + 1)]
            at += sz.group
    pack[at : at + sz.head, :] = three_ref[...]
    row = jnp.concatenate([wh[0:1, :], wh[1:2, :]], 1)
    row_at = lax.broadcasted_iota(jnp.int32, (16, LANES), 0)
    misc = jnp.zeros((16, LANES), F32)
    for i, piece in enumerate(three_parts(row)):
        misc = jnp.where(row_at == i, piece, misc)
    pack[sz.misc : sz.pay, :] = misc
    pack[sz.pay :, :] = jnp.zeros((sz.main * sz.blocks - sz.pay, LANES), F32)
    store = start_copies(((pack, packed),), sems, 7)
    for block in range(sz.blocks):
        at = sz.message_b + LANES * block
        piece = pack[sz.main * block : sz.main * (block + 1), :].astype(BF)
        m1[:, at : at + LANES] = piece
        m2[:, at : at + LANES] = piece
    own_pair(sz, sz.ranges(part)[1:], feat_ref, mean_ref, tail_ref, own_ref)
    store += start_copies(((own_ref, own_b),), sems, 8)
    for r, out in ((1, m1), (2, m2), (3, m3)):
        pack_pair(sz, sz.ranges(part ^ r)[1:], feat_ref, base_ref, mean_ref, tail_ref, turn_ref, out)
    wait_all(store)


def first_messages(sz, features, neighbors, present, w1, w2, w3, hidden):
    rows = LANES * sz.tiles_b_all
    bases = min(4 * rows + LANES, sz.base)
    slots = neighbors.shape[0]
    return call(
        functools.partial(first_kernel, sz),
        [
            ((2 * sz.hold, sz.n_mid), BF),
            ((sz.main * sz.blocks, LANES), F32),
            ((sz.main, sz.full_b), BF),
            ((sz.main, sz.full_b), BF),
            ((sz.main, sz.message_b), BF),
        ],
        [
            ((sz.feat, bases), BF),
            ((slots, rows), jnp.int32),
            ((slots, rows), jnp.int32),
            (w1.shape, F32),
            (w2.shape, F32),
            (w3.shape, F32),
            (hidden.shape, F32),
            ((2 * sz.hold, sz.n_mid), BF),
            *mean_scratch(sz, sz.tiles_b_all, slots),
            ((2 * sz.hold, sz.hid), F32),
            ((sz.head, LANES), F32),
            ((sz.main * sz.blocks, LANES), F32),
        ],
        FIRST_MIB,
        features,
        neighbors,
        present,
        w1,
        w2,
        w3,
        hidden,
        far_in=range(7),
        far_out=(0, 1),
        copies=9,
        micros=4,
    )


def mean_kernel(
    sz, feat_ref, nbr_ref, pres_ref, own_a, a1, a2, a3,
    mean_ref, tail_ref, turn_ref, base_ref, code_ref, count_ref, own_ref, sems,
):
    part = lax.axis_index("col")
    tiles = sz.low // LANES
    mean_tiles(sz, tiles, feat_ref, nbr_ref, pres_ref, mean_ref, tail_ref, base_ref, code_ref, count_ref)
    own_pair(sz, sz.ranges(part)[:1], feat_ref, mean_ref, tail_ref, own_ref)
    store = start_copies(((own_ref, own_a),), sems)
    for r, out in ((1, a1), (2, a2), (3, a3)):
        pack_pair(sz, sz.ranges(part ^ r)[:1], feat_ref, base_ref, mean_ref, tail_ref, turn_ref, out)
    wait_all(store)


def mean_messages(sz, features, neighbors, present):
    return call(
        functools.partial(mean_kernel, sz),
        [((2 * sz.hold, sz.n_a), BF)] + [((sz.main, sz.message_a), BF)] * 3,
        mean_scratch(sz, sz.low // LANES, neighbors.shape[0]) + [((2 * sz.hold, sz.n_a), BF)],
        MEAN_MIB,
        features,
        neighbors,
        present,
        far_out=(0,),
        copies=1,
        micros=6,
    )


def window_counts(local, rows):
    spots = lax.broadcasted_iota(jnp.int32, (256, LANES), 0).astype(F32).astype(BF)
    blocks = []
    for first in range(0, rows, 256):
        place = local - first
        place = jnp.where((place >= 0) & (place < 256), place, -1).astype(F32)
        counts = jnp.zeros((256, LANES), BF)
        for slot in range(local.shape[0]):
            row = jnp.broadcast_to(place[slot : slot + 1], (16, LANES)).astype(BF)
            row = jnp.concatenate([row] * 16, 0)
            counts = counts + jnp.where(row == spots, jnp.bfloat16(1.0), jnp.bfloat16(0.0))
        blocks.append(counts)
    return jnp.concatenate(blocks, 0)


def slot_totals(present):
    return jnp.maximum(jnp.sum(present.astype(F32), 0, keepdims=True), 1.0)


def a_window(sz, part, tile):
    first = 4 * sz.b_start(part) + 4 * LANES * tile - LANES - sz.a_start(part)
    return aligned(jnp.clip(first, 0, sz.n_a - WINDOW))


def counts_kernel(sz, nbr2, pres2, nbr3, pres3, out, counts, sems):
    part = lax.axis_index("col")
    stores = []
    for tile in range(sz.tiles_mid + sz.own // LANES):
        start = sz.b_start(part)
        links, valid, slot = (nbr2, pres2, tile) if tile < sz.tiles_mid else (nbr3, pres3, tile - sz.tiles_mid)
        if tile < sz.tiles_mid:
            columns = sz.mid_columns(part, tile)
        else:
            columns = pl.ds(aligned(sz.own * part + LANES * slot), LANES)
        if tile < sz.tiles_b:
            start = sz.a_start(part) + a_window(sz, part, tile)
        at = sz.count_rows * tile
        marks = valid[:, columns]
        local = jnp.where(marks > 0, links[:, columns] - start, -1)
        counts[at : at + WINDOW, :] = window_counts(local, WINDOW)
        counts[at + WINDOW : at + sz.count_rows, :] = jnp.broadcast_to(slot_totals(marks), (16, LANES)).astype(BF)
        rows = pl.ds(at, sz.count_rows)
        stores += start_copies(((counts.at[rows, :], out.at[rows, :]),), sems, tile)
    wait_all(stores)


def make_counts(sz, nbr2, pres2, nbr3, pres3):
    tiles = sz.tiles_mid + sz.own // LANES
    shape = (sz.count_rows * tiles, LANES)
    return call(
        functools.partial(counts_kernel, sz),
        [(shape, BF)],
        [(shape, BF)],
        6,
        nbr2,
        pres2,
        nbr3,
        pres3,
        far_out=(0,),
        copies=tiles,
        micros=4,
    )[0]


def tile_counts(sz, counts, tile):
    at = sz.count_rows * tile
    totals = counts[at + WINDOW : at + WINDOW + 16, :].astype(F32)[0:1]
    return counts[at : at + WINDOW, :], totals


def first_layer(weight, inputs, bias):
    result = dot(weight, inputs, (1, 0)) + bias
    active = result * sigmoid(result)
    scale = lax.rsqrt(jnp.sum(active * active, 0, keepdims=True) + ROW_EPS)
    return result, scale, active * scale


def join_inputs(sz, own, average):
    pieces = []
    for c in range(4):
        pieces.append(own[sz.group * c : sz.group * (c + 1)])
        pieces.append(average[sz.group * c : sz.group * (c + 1)])
    return jnp.concatenate(pieces, 0)


def norm_backward(grad, result, scale):
    gate = sigmoid(result)
    active = result * gate
    inner = jnp.sum(grad * active, 0, keepdims=True)
    grad_active = scale * grad - active * (scale * scale * scale * inner)
    return (grad_active * gate * (1.0 + result * (1.0 - gate))).astype(BF)


def split_inputs(sz, grad):
    pieces = [grad[sz.group * c : sz.group * (c + 1)] for c in range(8)]
    return jnp.concatenate(pieces[0::2], 0), jnp.concatenate(pieces[1::2], 0)


def row_sums(grad):
    return dot(jnp.ones((16, grad.shape[1]), BF), grad, (1, 1))


def spread(sz, scaled, counts):
    high, low = two_parts(scaled)
    total = dot(jnp.concatenate([high, low], 0), counts, (1, 1))
    return total[: sz.hid] + total[sz.hid :]


def halves(ref, at, lanes):
    return jnp.concatenate([ref[:, at : at + lanes], ref[:, at + lanes : at + 2 * lanes]], 0)


def store_halves(ref, at, lanes, value):
    rows = value.shape[0] // 2
    ref[:rows, at : at + lanes] = value[:rows]
    ref[:rows, at + lanes : at + 2 * lanes] = value[rows:]


def seed_picks(sz, info, part):
    spots = lax.broadcasted_iota(jnp.int32, (sz.slots, sz.own), 1) + sz.own * part
    serve = jnp.where(info[:, 0:1] == spots, 1.0, 0.0)
    take = jnp.where(info[:, 1:2] == spots, 1.0, 0.0)
    return serve, take, jnp.sum(serve, 1, keepdims=True), jnp.sum(take, 1, keepdims=True)


def seeds_kernel(
    sz, own_b, packed, s1, s2, s3, passed, counts, info_in,
    low_out, high_out, sent,
    xb, pack, m1, m2, m3, p3, window_ref, info, low, high, turn_ref, w1_ref, w2_ref, states, sems,
):
    part = lax.axis_index("col")
    own, hid, n_b, group, hold, at = sz.own, sz.hid, sz.n_b, sz.group, sz.hold, sz.at
    n_mid = sz.n_mid
    copies = start_copies(
        (
            (packed, pack),
            (passed.at[:, pl.ds(sz.message_b, LANES * sz.blocks)], p3),
            (s1, m1),
            (s2, m2),
            (s3, m3),
            (own_b, xb),
            (counts.at[pl.ds(sz.count_rows * sz.tiles_b, sz.count_rows * (own // LANES)), :], window_ref),
            (info_in, info),
        ),
        sems,
    )
    wait_all(copies[:4])
    for r, (message, first_lane) in enumerate(((None, 0), (m1, sz.message_b), (m2, sz.message_b), (p3, 0))):
        for block in range(sz.blocks if r else 0):
            first = first_lane + LANES * block
            pack[sz.main * block : sz.main * (block + 1), :] = message[:, first : first + LANES].astype(F32)
        shard = part ^ r
        for half in range(hid // LANES):
            lanes = slice(LANES * half, LANES * (half + 1))
            for s in range(2):
                first = 2 * hold * half + hold * s
                w1_ref[4 * hold * s + hold * r : 4 * hold * s + hold * (r + 1), lanes] = pack[first : first + hold, :]
            first = sz.rows_one + 2 * group * half
            row = pl.multiple_of(2 * group * shard, 2 * group)
            w2_ref[pl.ds(row, 2 * group), lanes] = pack[first : first + 2 * group, :]
        low[: sz.head, pl.ds(aligned(at["turned3"] + 2 * group * shard), LANES)] = pack[sz.at_three : sz.misc, :].astype(BF)
        misc = pack[sz.misc : sz.misc + 8, :]
        column = jnp.broadcast_to(misc[0:1] + misc[1:2] + misc[2:3], (LANES, LANES)).T
        row = pl.multiple_of(group * shard, group)
        for layer in range(2):
            lanes = slice(at["bias"] + LANES * layer, at["bias"] + LANES * (layer + 1))
            high[pl.ds(row, group), lanes] = column[group * layer : group * (layer + 1)]
    turned1 = w1_ref[...].T.astype(BF)
    turned2 = w2_ref[...].T.astype(BF)
    low[:, at["turned1"] : at["turned1"] + hid] = turned1
    low[:, at["turned2"] : at["turned2"] + 2 * hid] = turned2
    store_halves(low, at["weight2"], hid, w2_ref[...].astype(BF))
    weight3 = low[: sz.head, at["turned3"] : at["turned3"] + 2 * hid].astype(F32).T
    weight3 = jnp.concatenate([weight3, jnp.zeros((2 * hid, LANES - sz.head), F32)], 1)
    store_halves(low, at["weight3"], LANES, weight3.astype(BF))

    def piece(lanes, count):
        return (low.at[:, pl.ds(lanes, count)], low_out.at[:, pl.ds(lanes, count)])

    stores = start_copies((piece(n_mid, at["states"] - n_mid),), sems, 8)
    wait_all(copies[4:])
    low[:hold, :n_mid] = xb[:hold, :]
    low[4 * hold : 5 * hold, :n_mid] = xb[hold:, :]
    for r, message in ((1, m1), (2, m2), (3, m3)):
        unpack_pair(sz, message, r, n_mid, turn_ref, low)
    stores += start_copies((piece(0, n_mid),), sems, 9)
    bias1 = high[:hid, at["bias"] : at["bias"] + LANES]
    bias2 = high[:hid, at["bias"] + LANES : at["bias"] + 2 * LANES]
    for tile in range(sz.tiles_mid):
        lanes = slice(LANES * tile, LANES * (tile + 1))
        result, scale, state = first_layer(turned1, low[:, lanes], bias1)
        high[:hid, lanes] = result
        high[hid:, lanes] = jnp.broadcast_to(scale, (8, LANES))
        upper, lower = two_parts(state)
        states[:hid, lanes] = upper
        states[hid:, lanes] = lower
    low[:, at["states"] : at["states"] + n_b] = states[:hid, :n_b]
    for tile in range(own // LANES):
        window, totals = tile_counts(sz, window_ref, tile)
        total = dot(states[:, :n_b], window, (1, 0))
        average = ((total[:hid] + total[hid:]) / totals).astype(BF)
        x = join_inputs(sz, states[:hid, n_b + LANES * tile : n_b + LANES * (tile + 1)], average)
        first = at["inputs2"] + LANES * tile
        low[:, first : first + LANES] = x[:hid]
        low[:, first + own : first + own + LANES] = x[hid:]
        result, scale, state = first_layer(turned2, x, bias2)
        first = at["result2"] + LANES * tile
        high[:hid, first : first + LANES] = result
        high[hid:, first : first + LANES] = jnp.broadcast_to(scale, (8, LANES))
        upper, lower = two_parts(state)
        first = at["embed"] + LANES * tile
        low[:, first : first + LANES] = upper
        low[:, first + own : first + own + LANES] = lower
    tail = (piece(at["states"], sz.low_lanes - at["states"]), (high, high_out))
    stores += start_copies(tail, sems, 10)
    serve, take, _, owned = seed_picks(sz, info, part)
    value = sent_rows(sz, low, at["embed"], serve, take)
    dead = (owned > 0.5) & (info[:, 2:3] == 0)
    lane_at = lax.broadcasted_iota(jnp.int32, (sz.slots, 3 * hid), 1)
    value = jnp.where((lane_at == hid) & dead, SENTINEL, value)
    value = value.reshape(sz.dp, 1, sz.slot, 3 * hid)
    value = jnp.broadcast_to(value, (sz.dp, 4, sz.slot, 3 * hid))
    sent[...] = value.reshape(4 * sz.slots, 3 * hid).astype(BF)
    wait_all(stores)


def sent_rows(sz, low, at, serve, take):
    embed_high = low[:, at : at + sz.own]
    embed_low = low[:, at + sz.own : at + 2 * sz.own]
    take = take.astype(BF)
    return jnp.concatenate(
        [dot(serve.astype(BF), embed_high, (1, 1)), dot(take, embed_high, (1, 1)), dot(take, embed_low, (1, 1))], 1
    )


def seeds_forward(sz, messages, counts, info):
    hid = sz.hid
    tail = (sz.main, LANES * sz.blocks)
    return call(
        functools.partial(seeds_kernel, sz),
        [
            ((hid, sz.low_lanes), BF),
            ((hid + 8, sz.high_lanes), F32),
            ((4 * sz.slots, 3 * hid), BF),
        ],
        [
            ((2 * sz.hold, sz.n_mid), BF),
            ((sz.main * sz.blocks, LANES), F32),
            ((sz.main, sz.full_b), BF),
            ((sz.main, sz.full_b), BF),
            ((sz.main, sz.message_b), BF),
            (tail, BF),
            ((sz.count_rows * (sz.own // LANES), LANES), BF),
            (info.shape, jnp.int32),
            ((hid, sz.low_lanes), BF),
            ((hid + 8, sz.high_lanes), F32),
            ((2 * sz.main, LANES), F32),
            ((8 * sz.hold, hid), F32),
            ((2 * hid, hid), F32),
            ((2 * hid, sz.n_mid), BF),
        ],
        SEEDS_MIB,
        *messages,
        counts,
        info,
        far_in=range(8),
        micros=4,
        far_out=(0, 1),
        copies=12,
    )


def rest_kernel(
    sz, low_in, high_in, counts_in, own_a, v1, v2, v3, labels_in, weighting_in, head_in, part_out,
    labels, weighting, head_bias, low, xa, bias, counts, xo, a1, a2, a3, turn_ref,
    states, states2, result1, scale1, inputs2, result2, scale2, grad_a, low_grad, part_ref, sems,
):
    part = lax.axis_index("col")
    own, hid, n_a, n_b, hold = sz.own, sz.hid, sz.n_a, sz.n_b, sz.hold
    at = dict(sz.at)
    for name in ("turned1", "turned2", "weight2", "weight3", "turned3", "states", "embed"):
        at[name] -= sz.n_mid
    lanes = at["embed"] + own
    copies = start_copies(
        (
            (own_a, xo),
            (v1, a1),
            (v2, a2),
            (v3, a3),
            (low_in.at[:, pl.ds(sz.n_mid, hid)], low.at[:, pl.ds(0, hid)]),
            (high_in.at[:, pl.ds(sz.at["bias"], 2 * LANES)], bias),
            (low_in.at[:, pl.ds(sz.n_mid + hid, lanes - hid)], low.at[:, pl.ds(hid, lanes - hid)]),
            (counts_in, counts),
            (labels_in, labels),
            (weighting_in, weighting),
            (head_in, head_bias),
        ),
        sems,
    )
    wait_all(copies[:4])
    xa[:hold, :] = xo[:hold, :]
    xa[4 * hold : 5 * hold, :] = xo[hold:, :]
    for r, message in ((1, a1), (2, a2), (3, a3)):
        unpack_pair(sz, message, r, n_a, turn_ref, xa)
    wait_all(copies[4:6])
    turned1 = low[:, at["turned1"] : at["turned1"] + hid]
    bias1 = bias[:hid, :LANES]
    bias2 = bias[:hid, LANES:]

    def forward_step(index, carry):
        lanes = pl.ds(aligned(index * LANES), LANES)
        result, scale, state = first_layer(turned1, xa[:, lanes], bias1)
        result1[:, lanes] = result
        scale1[:, lanes] = scale
        upper, lower = two_parts(state)
        states[:hid, lanes] = upper
        states[hid:, lanes] = lower
        return carry

    lax.fori_loop(0, n_a // LANES, forward_step, 0, unroll=2)
    wait_all(copies[6:])
    turned2 = low[:, at["turned2"] : at["turned2"] + 2 * hid]
    for tile in range(sz.tiles_b):
        lanes = slice(LANES * tile, LANES * (tile + 1))
        window, totals = tile_counts(sz, counts, tile)
        total = dot(states[:, pl.ds(a_window(sz, part, tile), WINDOW)], window, (1, 0))
        average = ((total[:hid] + total[hid:]) / totals).astype(BF)
        x = join_inputs(sz, low[:, at["states"] + LANES * tile : at["states"] + LANES * (tile + 1)], average)
        inputs2[:, lanes] = x
        result, scale, state = first_layer(turned2, x, bias2)
        result2[:, lanes] = result
        scale2[:, lanes] = scale
        upper, lower = two_parts(state)
        states2[:hid, lanes] = upper
        states2[hid:, lanes] = lower
    counts3, totals3 = tile_counts(sz, counts, sz.tiles_mid)
    total = dot(states2[...], counts3, (1, 0))
    average = ((total[:hid] + total[hid:]) / totals3).astype(BF)
    inputs3 = join_inputs(sz, low[:, at["embed"] : at["embed"] + own], average)

    columns = pl.ds(aligned(own * part), own)
    classes = lax.broadcasted_iota(jnp.int32, (sz.head, own), 0)
    head_row = jnp.concatenate([head_bias[...], jnp.zeros((1, LANES - sz.classes), F32)], 1)
    head_column = jnp.broadcast_to(head_row, (LANES, LANES)).T[: sz.head]
    logits = dot(low[: sz.head, at["turned3"] : at["turned3"] + 2 * hid], inputs3, (1, 0)) + head_column
    logits = jnp.where(classes < sz.classes, logits, -1e30)
    highest = jnp.max(logits, 0, keepdims=True)
    expo = jnp.exp(logits - highest)
    totals = jnp.sum(expo, 0, keepdims=True)
    hit = classes == labels[:, columns]
    weights = weighting[:, columns].astype(F32)
    target = jnp.sum(jnp.where(hit, logits, 0.0), 0, keepdims=True)
    ce_total = jnp.sum(weights * (highest + jnp.log(totals) - target), 1, keepdims=True)
    seed_count = jnp.sum(weights, 1, keepdims=True)
    grad_logits = (weights * (expo / totals - jnp.where(hit, 1.0, 0.0))).astype(BF)
    g3 = at["g3"]
    part_ref[: sz.head, g3 : g3 + 2 * hid] = dot(grad_logits, inputs3, (1, 1))
    head_sums = jnp.concatenate([row_sums(grad_logits), jnp.zeros((16, LANES - sz.head), F32)], 1)
    part_ref[sz.head + 16 : sz.head + 32, g3 : g3 + LANES] = head_sums
    lane_at = lax.broadcasted_iota(jnp.int32, (16, LANES), 1)
    sums = jnp.where(lane_at == 0, ce_total, jnp.where(lane_at == 1, seed_count, 0.0))
    part_ref[sz.head + 16 : sz.head + 32, g3 + LANES : g3 + 2 * LANES] = sums
    own_part, average_part = split_inputs(sz, dot(halves(low, at["weight3"], LANES)[:, : sz.head], grad_logits, (1, 0)))
    part_ref[:hid, at["grad_embed"] : at["grad_embed"] + own] = own_part
    grad_mid = spread(sz, average_part / totals3, counts3)
    low_grad2 = norm_backward(grad_mid, result2[...], scale2[...])
    g2 = dot(inputs2[...], low_grad2, (1, 1))
    part_ref[:hid, at["g2"] : at["g2"] + hid] = g2[:hid]
    part_ref[:hid, at["g2"] + hid : at["g2"] + 2 * hid] = g2[hid:]
    part_ref[sz.head : sz.head + 16, g3 + hid : g3 + 2 * hid] = row_sums(low_grad2)
    weight2 = halves(low, at["weight2"], hid)
    grad_a[...] = jnp.zeros_like(grad_a)
    for tile in range(sz.tiles_b):
        lanes = slice(LANES * tile, LANES * (tile + 1))
        own_part, average_part = split_inputs(sz, dot(weight2, low_grad2[:, lanes], (1, 0)))
        part_ref[:hid, at["grad_b"] + LANES * tile : at["grad_b"] + LANES * (tile + 1)] = own_part
        window, totals = tile_counts(sz, counts, tile)
        lanes = pl.ds(a_window(sz, part, tile), WINDOW)
        grad_a[:, lanes] = grad_a[:, lanes] + spread(sz, average_part / totals, window)

    rows = pl.ds(0, hid + 8)
    split = at["g2"]
    stores = start_copies(
        (
            (part_ref.at[rows, pl.ds(split, hid * 2)], part_out.at[rows, pl.ds(split, hid * 2)]),
            (
                part_ref.at[rows, pl.ds(at["grad_b"], n_b + own)],
                part_out.at[rows, pl.ds(at["grad_b"], n_b + own)],
            ),
        ),
        sems,
        11,
    )

    def backward_step(index, carry):
        lanes = pl.ds(aligned(index * LANES), LANES)
        low_grad[:, lanes] = norm_backward(grad_a[:, lanes], result1[:, lanes], scale1[:, lanes])
        return carry

    lax.fori_loop(0, n_a // LANES, backward_step, 0, unroll=2)
    part_ref[:hid, at["g1"] : at["g1"] + hid] = dot(xa[...], low_grad[...], (1, 1))
    part_ref[sz.head : sz.head + 16, g3 : g3 + hid] = row_sums(low_grad[...])
    stores += start_copies(
        (
            (part_ref.at[rows, pl.ds(0, hid)], part_out.at[rows, pl.ds(0, hid)]),
            (part_ref.at[rows, pl.ds(g3, 2 * hid)], part_out.at[rows, pl.ds(g3, 2 * hid)]),
        ),
        sems,
        13,
    )
    wait_all(stores)


def rest_step(sz, low, high, counts, means, labels, weighting, head_bias):
    hid = sz.hid
    return call(
        functools.partial(rest_kernel, sz),
        [((hid + 8, sz.part_lanes), F32)],
        [
            (labels.shape, jnp.int32),
            (weighting.shape, jnp.int32),
            (head_bias.shape, F32),
            ((hid, sz.at["embed"] + sz.own - sz.n_mid), BF),
            ((hid, sz.n_a), BF),
            ((hid + 8, 2 * LANES), F32),
            (counts.shape, BF),
            ((2 * sz.hold, sz.n_a), BF),
            ((sz.main, sz.message_a), BF),
            ((sz.main, sz.message_a), BF),
            ((sz.main, sz.message_a), BF),
            ((2 * sz.main, LANES), F32),
            ((2 * hid, sz.n_a), BF),
            ((2 * hid, sz.n_b), BF),
            ((hid, sz.n_a), F32),
            ((1, sz.n_a), F32),
            ((2 * hid, sz.n_b), BF),
            ((hid, sz.n_b), F32),
            ((1, sz.n_b), F32),
            ((hid, sz.n_a), F32),
            ((hid, sz.n_a), BF),
            ((hid + 8, sz.part_lanes), F32),
        ],
        REST_MIB,
        low,
        high,
        counts,
        *means,
        labels,
        weighting,
        head_bias,
        far_in=range(10),
        micros=14,
        far_out=(0,),
        copies=15,
    )[0]


def seeds_back_kernel(
    sz, info_in, received, low_in, high_in, counts_in, part_in, keep0, keep1, send,
    info, x_ref, weight_ref, low, high, window_ref, partial, g1_ref, g2_ref, gb_ref, sems,
):
    part = lax.axis_index("col")
    own, hid, group, n_b, n_mid = sz.own, sz.hid, sz.group, sz.n_b, sz.n_mid
    at = dict(sz.at)
    at["inputs2"] -= at["embed"]
    split = at["grad_b"]
    copies = start_copies(
        (
            (info_in, info),
            (low_in.at[:, pl.ds(at["embed"], 4 * own)], low),
            (part_in.at[:, pl.ds(split, n_b + own)], partial.at[:, pl.ds(split, n_b + own)]),
            (high_in, high),
            (low_in.at[:, pl.ds(at["weight2"], 2 * hid)], weight_ref),
            (counts_in.at[pl.ds(sz.count_rows * sz.tiles_b, sz.count_rows * (own // LANES)), :], window_ref),
            (part_in.at[:, pl.ds(0, split)], partial.at[:, pl.ds(0, split)]),
            (low_in.at[:, pl.ds(0, n_mid)], x_ref),
        ),
        sems,
    )
    arrived = received[...].astype(F32).reshape(sz.dp, 4, sz.slot, 3 * hid)
    arrived = jnp.sum(arrived, 1).reshape(sz.slots, 3 * hid)
    at["embed"] = 0
    wait_all(copies[:2])
    serve, take, served, taken = seed_picks(sz, info, part)
    mine = sent_rows(sz, low, 0, serve, take)
    theirs = arrived[:, hid : 2 * hid]
    alive_there = theirs[:, 0:1] < 0.5 * SENTINEL
    theirs = theirs + arrived[:, 2 * hid :]
    differ = mine[:, hid : 2 * hid] + mine[:, 2 * hid :] - arrived[:, :hid]
    differ = jnp.where((taken > 0.5) & (info[:, 2:3] > 0), differ, 0.0)
    dist_total = DIST_WEIGHT * jnp.sum(jnp.sum(differ * differ, 0, keepdims=True), 1, keepdims=True)
    local_high, local_low = two_parts(2.0 * DIST_WEIGHT * differ)
    back = jnp.where((served > 0.5) & alive_there, theirs - mine[:, :hid], 0.0)
    back = (-2.0 * DIST_WEIGHT * back).astype(BF)
    take = take.astype(BF)
    serve = serve.astype(BF)
    wait_all(copies[2:])
    grad = partial[:hid, at["grad_embed"] : at["grad_embed"] + own]
    grad = grad + dot(local_high, take, (0, 0)) + dot(local_low, take, (0, 0)) + dot(back, serve, (0, 0))
    lanes = slice(at["result2"], at["result2"] + own)
    low_grad2 = norm_backward(grad, high[:hid, lanes], high[hid:, lanes][0:1])
    added = dot(halves(low, at["inputs2"], own), low_grad2, (1, 1))
    for half in range(2):
        lanes = slice(at["g2"] + hid * half, at["g2"] + hid * (half + 1))
        g2_ref[hid * half : hid * (half + 1), :] = partial[:hid, lanes] + added[hid * half : hid * (half + 1)]
    g3 = at["g3"]
    sums = partial[sz.head : sz.head + 16, g3 : g3 + 2 * hid]
    gb_ref[:, hid:] = sums[:, hid:] + row_sums(low_grad2)
    weight2 = halves(weight_ref, 0, hid)
    own_part, average_part = split_inputs(sz, dot(weight2, low_grad2, (1, 0)))
    total_b = partial[:hid, at["grad_b"] : at["grad_b"] + n_b]
    for tile in range(own // LANES):
        window, totals = tile_counts(sz, window_ref, tile)
        total_b = total_b + spread(sz, average_part[:, LANES * tile : LANES * (tile + 1)] / totals, window)
    low_grad = jnp.concatenate(
        [
            norm_backward(total_b, high[:hid, :n_b], high[hid:, :n_b][0:1]),
            norm_backward(own_part, high[:hid, n_b:n_mid], high[hid:, n_b:n_mid][0:1]),
        ],
        1,
    )
    half = 4 * sz.hold
    g1_ref[...] = partial[:hid, at["g1"] : at["g1"] + hid] + dot(x_ref[...], low_grad, (1, 1))
    gb_ref[:, :hid] = sums[:, :hid] + row_sums(low_grad)
    head_row = partial[sz.head + 16 : sz.head + 32, g3 : g3 + LANES]
    totals = partial[sz.head + 16 : sz.head + 32, g3 + LANES : g3 + 2 * LANES]
    lane_at = lax.broadcasted_iota(jnp.int32, (16, LANES), 1)
    row_at = lax.broadcasted_iota(jnp.int32, (16, LANES), 0)
    fixed = ((totals[0:1, 0:1] + dist_total) * float(2**LOSS_BITS) + 0.5).astype(jnp.int32)
    count = totals[0:1, 1:2].astype(jnp.int32)
    whole = jnp.where(lane_at < 32, fixed, count)
    bits = (lax.shift_right_logical(whole, lane_at & 31) & 1).astype(F32)
    bits = jnp.where(lane_at < 64, bits, 0.0)
    for r, (target_ref, base) in enumerate(((keep0, 0), (send, 0), (keep1, 0), (send, sz.pay))):
        shard = part ^ r
        block2 = pl.ds(pl.multiple_of(2 * group * shard, 2 * group), 2 * group)
        row = base
        for h in range(hid // LANES):
            lanes = slice(LANES * h, LANES * (h + 1))
            for s in range(2):
                rows = slice(half * s + sz.hold * r, half * s + sz.hold * (r + 1))
                target_ref[row : row + sz.hold, :] = g1_ref[rows, lanes].astype(BF)
                row += sz.hold
        for h in range(hid // LANES):
            target_ref[row : row + 2 * group, :] = g2_ref[block2, LANES * h : LANES * (h + 1)].astype(BF)
            row += 2 * group
        third = partial[: sz.head, pl.ds(aligned(g3 + 2 * group * shard), LANES)]
        target_ref[row : row + sz.head, :] = third.astype(BF)
        row += sz.head
        odd = (shard % 2) == 1
        block = aligned((shard // 2) * LANES)
        one = gb_ref[:, pl.ds(block, LANES)]
        two = gb_ref[:, pl.ds(aligned(hid + block), LANES)]
        one = jnp.where(odd, pltpu.roll(one, group, 1), one)
        two = jnp.where(odd, two, pltpu.roll(two, group, 1))
        bias_row = jnp.where(lane_at < group, one, two)
        misc = jnp.where(row_at == 0, bias_row, jnp.where(row_at == 1, head_row, jnp.where(row_at == 2, bits, 0.0)))
        target_ref[row : row + 16, :] = misc.astype(BF)


def seeds_backward(sz, info, received, low, high, counts, partial):
    hid = sz.hid
    return call(
        functools.partial(seeds_back_kernel, sz),
        [((sz.pay, LANES), BF), ((sz.pay, LANES), BF), ((2 * sz.pay, LANES), BF)],
        [
            (info.shape, jnp.int32),
            ((hid, sz.n_mid), BF),
            ((hid, 2 * hid), BF),
            ((hid, 4 * sz.own), BF),
            ((hid + 8, sz.high_lanes), F32),
            ((sz.count_rows * (sz.own // LANES), LANES), BF),
            ((hid + 8, sz.part_lanes), F32),
            ((8 * sz.hold, hid), F32),
            ((2 * hid, hid), F32),
            ((16, 2 * hid), F32),
        ],
        BACK_MIB,
        info,
        received,
        low,
        high,
        counts,
        partial,
        far_in=(0, 2, 3, 4, 5),
        micros=3,
        copies=8,
    )


def lamb_kernel(sz, grad, w1, w2, w3, wh, wb, f1, f2, f3, fh, fb, s1, s2, s3, sh, sb, *rest):
    params = (w1, w2, w3, wh, wb)
    firsts = (f1, f2, f3, fh, fb)
    seconds = (s1, s2, s3, sh, sb)
    moments, squares, updates = rest[:5], rest[5:10], rest[10:15]
    sums_ref, totals_ref, one_ref, three_ref = rest[15:]
    group, hold = sz.group, sz.hold

    def wide(at, rows):
        return jnp.concatenate([grad[at : at + rows, :], grad[at + rows : at + 2 * rows, :]], 1)

    one = wide(0, 2 * hold)
    three = grad[sz.at_three : sz.misc, :]
    turned = pltpu.roll(three, group, 1)
    for f in range(sz.feat):
        one_ref[f, 0:1, :] = one[f : f + 1]
        one_ref[f, 1:2, :] = one[hold + f : hold + f + 1]
    for c in range(sz.classes):
        three_ref[c, 0:1, :] = three[c : c + 1, :group]
        three_ref[c, 1:2, :] = turned[c : c + 1, :group]
    misc = grad[sz.misc : sz.misc + 8, :]
    hidden = jnp.concatenate([misc[0:1, :group], misc[0:1, group : 2 * group]], 0)
    two = wide(sz.rows_one, 2 * group).reshape(2, group, sz.hid)
    grads = (one_ref[...], two, three_ref[...], hidden, misc[1:2, : sz.classes])
    lane_at = lax.broadcasted_iota(jnp.int32, (8, LANES), 1)
    row_at = lax.broadcasted_iota(jnp.int32, (8, LANES), 0)
    sums = jnp.zeros((8, LANES), F32)
    for i in range(5):
        g = grads[i]
        w = params[i][...]
        m = BETA_ONE * firsts[i][...] + (1.0 - BETA_ONE) * g
        v = BETA_TWO * seconds[i][...] + (1.0 - BETA_TWO) * g * g
        u = (m / (1.0 - BETA_ONE**STEP)) / (jnp.sqrt(v / (1.0 - BETA_TWO**STEP)) + ADAM_EPS) + DECAY_RATE * w
        moments[i][...] = m
        squares[i][...] = v
        updates[i][...] = u
        for row, item in ((0, w), (1, u)):
            item = item * item
            if i < 3:
                item = jnp.sum(item, 0)
            total = jnp.sum(jnp.sum(item, 0, keepdims=True), 1, keepdims=True)
            if i == 4:
                total = 0.25 * total
            sums = jnp.where((lane_at == i) & (row_at == row), total, sums)
    sums_ref[...] = sums
    power = (1 << (lane_at & 15)).astype(F32)
    power = jnp.where((lane_at & 31) < 16, power, power * float(2**16))
    bits = jnp.broadcast_to(misc[2:3], (8, LANES)) * power
    loss = jnp.sum(jnp.where(lane_at < 32, bits, 0.0), 1, keepdims=True) * float(2.0**-LOSS_BITS)
    count = jnp.sum(jnp.where((lane_at >= 32) & (lane_at < 64), bits, 0.0), 1, keepdims=True)
    totals_ref[...] = jnp.where(lane_at == 0, loss, count)


def lamb(sz, grad, params, firsts, seconds):
    like = [(item.shape, F32) for item in params]
    return call(
        functools.partial(lamb_kernel, sz),
        like * 3 + [((8, LANES), F32)] * 2,
        [(params[0].shape, F32), (params[2].shape, F32)],
        6,
        grad,
        *params,
        *firsts,
        *seconds,
    )


def step_kernel(own, other, w1, w2, w3, wh, wb, u1, u2, u3, uh, ub, n1, n2, n3, nh, nb, norms_ref):
    norms = jnp.sqrt(own[...] + other[...])
    norms_ref[...] = norms[0:2, 0:5]
    for i, (w, u, n) in enumerate(
        ((w1, u1, n1), (w2, u2, n2), (w3, u3, n3), (wh, uh, nh), (wb, ub, nb))
    ):
        ratio = LEARN_RATE * (norms[0:1, i : i + 1] / norms[1:2, i : i + 1])
        n[...] = w[...] - ratio * u[...]


def take_step(own, other, params, updates):
    return call(
        step_kernel,
        [(item.shape, F32) for item in params] + [((2, 5), F32)],
        [],
        3,
        own,
        other,
        *params,
        *updates,
    )


def swap(value, axis, count, bit):
    return lax.ppermute(value, axis, [(i, i ^ bit) for i in range(count)])


def merged(own, other):
    return lax.reduce_precision(own.astype(F32) + other.astype(F32), 8, 7)


def shards(
    features, neighbors_one, present_one, neighbors_two, present_two, neighbors_three, present_three,
    labels, seed_weight, serve_rows, take_seed, fetch_live,
    weight_one, weight_two, weight_three, hidden_bias, head_bias,
    first_one, first_two, first_three, first_hidden, first_head,
    second_one, second_two, second_three, second_hidden, second_head,
):
    sz = Sizes(features, neighbors_one, neighbors_two, neighbors_three, weight_two, weight_three, serve_rows)

    def tree(one, two, three, hidden, head):
        return (one.transpose(1, 0, 2), two, three.transpose(2, 0, 1), hidden, head[None, :])

    def back(one, two, three, hidden, head):
        return (one.transpose(1, 0, 2), two, three.transpose(1, 2, 0), hidden, head[0])

    params = tree(weight_one, weight_two, weight_three, hidden_bias, head_bias)
    firsts = tree(first_one, first_two, first_three, first_hidden, first_head)
    seconds = tree(second_one, second_two, second_three, second_hidden, second_head)

    own_b, packed, *sent = first_messages(sz, features, neighbors_one, present_one, *params[:4])
    s1, s2, s3 = [swap(sent[r - 1], "col", 4, r) for r in (1, 2, 3)]
    own_a, *means = mean_messages(sz, features, neighbors_one, present_one)
    s1, *means = lax.optimization_barrier((s1, *means))
    means = [swap(means[r - 1], "col", 4, r) for r in (1, 2, 3)]
    neighbors_two, s2 = lax.optimization_barrier((neighbors_two, s2))
    counts = make_counts(sz, neighbors_two, present_two, neighbors_three, present_three)
    later, _ = lax.optimization_barrier((s2, own_a))
    passed = swap(later, "col", 4, 1)
    alive = jnp.arange(sz.slot, dtype=jnp.int32)[None, :] < fetch_live[:, None]
    info = jnp.stack([serve_rows.reshape(-1), take_seed.reshape(-1), alive.astype(jnp.int32).reshape(-1)], 1)
    low, high, rows = seeds_forward(sz, (own_b, packed, s1, s2, s3, passed), counts, info)
    received = lax.all_to_all(rows, ("dp", "col"), split_axis=0, concat_axis=0, tiled=True)
    partial = rest_step(sz, low, high, counts, (own_a, *means), labels[None, :], seed_weight[None, :], head_bias[None, :])
    keep0, keep1, send = seeds_backward(sz, info, received, low, high, counts, partial)
    other = swap(send, "col", 4, 1)
    grad = merged(keep0, other[: sz.pay])
    grad = merged(grad, swap(merged(keep1, other[sz.pay :]).astype(BF), "col", 4, 2))
    bit = 1
    while bit < sz.dp:
        grad = merged(grad, swap(grad.astype(BF), "dp", sz.dp, bit))
        bit *= 2
    outs = lamb(sz, grad, params, firsts, seconds)
    moments, squares, updates = outs[:5], outs[5:10], outs[10:15]
    sums, totals = outs[15], outs[16]
    pair = sums + swap(sums, "col", 4, 1)
    fresh = take_step(pair, swap(pair, "col", 4, 2), params, updates)
    return (*back(*fresh[:5]), *back(*moments), *back(*squares), fresh[5], totals[0, 0], totals[0, 1])


def solution(mesh):
    wide = P(None, "col", None)
    tree = [wide, wide, wide, P(None, "col"), P()]
    return jax.shard_map(
        shards,
        mesh=mesh,
        in_specs=(
            P("col", "dp"),
            *[P(None, "dp")] * 6,
            P("dp"),
            P("dp"),
            P("dp", None),
            P("dp", None),
            P("dp"),
            *tree,
            *tree,
            *tree,
        ),
        out_specs=(*tree, *tree, *tree, P(), P(), P()),
        check_vma=False,
    )
```

time: 164 us -> 86.2 us (0.53)
  waiting for transfers between devices: 57.7 us -> 18.2 us
  local copies, waits for them, and re-layouts: 35.3 us -> 3.27 us
  Pallas kernels: 52.1 us -> 41.3 us
  starting transfers between devices: 13.6 us -> 21.5 us
  other arithmetic: 3.23 us -> 0.49 us
    ppermute x10 -> x14, waiting for transfers between devices: 45.4 us -> 18.2 us  [swap(): return lax.ppermute(value, axis, [(i, i ^ bit) for i in range(count)])]
    unnamed x65 -> x64, local copies, waits for them, and re-layouts: 28.2 us -> 1.74 us
    all_to_all x1, waiting for transfers between devices: 12.3 us -> 0.01 us  [shards(): lax.all_to_all(rows, ('dp', 'col'), split_axis=0, concat_axis=0, tiled=True)]
    pallas_call x10 -> x8, Pallas kernels: 52.1 us -> 41.3 us  [call(): pl.pallas_call(kernel, in_specs=[far if i in far_in else near for i in ra...]
    ppermute x10 -> x14, starting transfers between devices: 7.58 us -> 15.3 us  [swap(): return lax.ppermute(value, axis, [(i, i ^ bit) for i in range(count)])]
    another operation x4 -> x0, other arithmetic: 2.46 us -> none
    broadcast_in_dim x3 -> x0, local copies, waits for them, and re-layouts: 2.38 us -> none  [the longest x1 1.68 us: shards(): jnp.broadcast_to(saved[-1].reshape(sz.dp, 1, sz.slot, 3 * sz.hid), (sz.dp...]
  transfers between devices with their start and end apart: 11 -> 15, of which waited for: 9 -> 7; matrix products, arithmetic and copies ran while one was open for 8% -> 2% of each run, Pallas kernels for 0% -> 36%
where the time goes in v2:
time: 86.2 us; the launch traced here: 86 us
  Pallas kernels  41.3 us (48%)
  starting transfers between devices  21.5 us (25%)
  waiting for transfers between devices  18.2 us (21%)
  local copies, waits for them, and re-layouts  3.27 us (4%)
  between operations  1.21 us (1%)
    pallas_call x8, Pallas kernels, call(): pl.pallas_call(kernel, in_specs=[far if i in far_in else near for i in ra...  41.3 us
    ppermute x14, waiting for transfers between devices, swap(): return lax.ppermute(value, axis, [(i, i ^ bit) for i in range(count)])  18.2 us
    ppermute x14, starting transfers between devices, swap(): return lax.ppermute(value, axis, [(i, i ^ bit) for i in range(count)])  15.3 us
    all_to_all x1, starting transfers between devices, shards(): lax.all_to_all(rows, ('dp', 'col'), split_axis=0, concat_axis=0, tiled=True)  6.25 us
    unnamed x64, local copies, waits for them, and re-layouts  1.74 us
  transfers between devices with their start and end apart: 15, of which 7 were waited for; matrix products, arithmetic and copies ran while one was open for 2% of the time, Pallas kernels for 36%

profile of v2, /device:TPU:0, one launch (start us, length us, event | category | flops | bytes accessed | tf_op | source)
XLA Modules:
  0.0 86.0 jit_solution(13640452391966712664)
XLA Ops:
  0.7 3.8 %shard_map.394 = (bf16[64,896]{1,0:T(8,128)(2,1)}, f32[456,128]{1,0:T(8,128)}, bf16[24,4352]{1,0:T(8,128)(2,1)S(1)}, bf16[24,4352]{1,0:T(8,128)(2,1)S(1)}, bf16[24,1920]{1,0:T(8,128)(2,1)S(1)}) custom-call(bf16[25,32768]{1,0:T(8,128)(2,1)} %feat_ref.1, s32[5,8192]{1,0:T(8,128)} %nbr_ref.1, s32[5,8192]{1,0:T(8,128)} %pres_ref.1, f32[25,2,256]{2,1,0:T(2,128)} %bitcast.27, ...), custom_call_target="tpu_custom_call" | custom-call | flops 4000000000 | bytes 1 | tf_op jit(solution)/shard_map/pallas_call | solution.py:43
  4.5 2.5 %collective-permute-start.2 = (bf16[24,1920]{1,0:T(8,128)(2,1)S(1)}, bf16[24,1920]{1,0:T(8,128)(2,1)S(1)}, u32[]{:S(2)}, u32[]{:S(2)}) collective-permute-start(bf16[24,1920]{1,0:T(8,128)(2,1)S(1)} %get-tuple-element.72), channel_id=1, source_target_pairs={{0,3},{1,2},{2,1},{3,0},{4,7},{5,6},{6,5},{7,4},{8,11},{9,10},{10,... | collective-permute-start | bytes 276488 | tf_op jit(solution)/shard_map/ppermute | solution.py:1108
  7.0 0.7 collective-permute-start
  7.8 6.7 %shard_map.395 = (bf16[64,2816]{1,0:T(8,128)(2,1)}, bf16[24,5888]{1,0:T(8,128)(2,1)S(1)}, bf16[24,5888]{1,0:T(8,128)(2,1)S(1)}, bf16[24,5888]{1,0:T(8,128)(2,1)S(1)}) custom-call(bf16[25,32768]{1,0:T(8,128)(2,1)S(1)} %copy-done, s32[5,8192]{1,0:T(8,128)S(1)} %copy-done.1, s32[5,8192]{1,0:T(8,128)S(1)} %copy-done.2), custom_call_target="tpu_custom_call" | custom-call | flops 6000000000 | bytes 1 | tf_op jit(solution)/shard_map/pallas_call | solution.py:43
  14.9 0.7 copy.49.info_in
  15.6 0.2 collective-permute-start.3
  15.8 0.4 collective-permute-start.4
  16.2 2.0 %collective-permute-start.5 = (bf16[24,5888]{1,0:T(8,128)(2,1)S(1)}, bf16[24,5888]{1,0:T(8,128)(2,1)S(1)}, u32[]{:S(2)}, u32[]{:S(2)}) collective-permute-start(bf16[24,5888]{1,0:T(8,128)(2,1)S(1)} %get-tuple-element.80), channel_id=1, source_target_pairs={{0,2},{1,3},{2,0},{3,1},{4,6},{5,7},{6,4},{7,5},{8,10},{9,11},{10,... | collective-permute-start | bytes 847880 | tf_op jit(solution)/shard_map/ppermute | solution.py:1108
  18.2 2.6 %shard_map.396.counts.counts_in = bf16[6272,128]{1,0:T(8,128)(2,1)} custom-call(s32[10,2048]{1,0:T(8,128)S(1)} %copy-done.3, s32[10,2048]{1,0:T(8,128)S(1)} %copy-done.4, s32[15,512]{1,0:T(8,128)S(1)} %copy-done.14, s32[15,512]{1,0:T(8,128)S(1)} %copy-done.15), custom_call_target="tpu_custom_call" | custom-call | flops 4000000000 | bytes 1 | tf_op jit(solution)/shard_map/pallas_call | solution.py:43
  20.9 0.6 copy-done.31
  21.6 4.9 %shard_map.397 = (bf16[256,4224]{1,0:T(8,128)(2,1)}, f32[264,1280]{1,0:T(8,128)}, bf16[256,768]{1,0:T(8,128)(2,1)}) custom-call(bf16[64,896]{1,0:T(8,128)(2,1)} %get-tuple-element.63.own_b, f32[456,128]{1,0:T(8,128)} %get-tuple-element.64.packed, bf16[24,4352]{1,0:T(8,128)(2,1)} %copy-done.28, bf16[24,4352]{1,0:T(8,128)(2,1)} %copy-done.29, ...), custom_call_target="tpu_custom_call" | custom-call | flops 4000000000 | bytes 1 | tf_op jit(solution)/shard_map/pallas_call | solution.py:43
  26.5 6.2 %all-to-all-start = ((bf16[32,8,768]{2,1,0:T(8,128)(2,1)}), bf16[32,8,768]{2,1,0:T(8,128)(2,1)S(1)}, u32[]{:S(2)}, u32[]{:S(2)}) async-start(bf16[32,8,768]{2,1,0:T(8,128)(2,1)} %bitcast.2), calls=%async_computation | async-start | bytes 786432 | tf_op jit(solution)/shard_map/all_to_all | solution.py:1146
  32.8 0.7 copy-done.25
  33.5 0.1 copy-done.26
  33.7 16.9 %shard_map.398.part_in = f32[264,2176]{1,0:T(8,128)} custom-call(bf16[256,4224]{1,0:T(8,128)(2,1)} %get-tuple-element.77.low_in, f32[264,1280]{1,0:T(8,128)} %get-tuple-element.78.high_in, bf16[6272,128]{1,0:T(8,128)(2,1)} %shard_map.396.counts.counts_in, bf16[64,2816]{1,0:T(8,128)(2,1)} %get-tuple-element.73.own_a, bf16[24,5888]{1,0:T(8,128)(2,1)} %copy-done.25, ...), custom_call_target="tpu_custom_call" | custom-call | flops 14000000000 | bytes 1 | tf_op jit(solution)/shard_map/pallas_call | solution.py:43
  50.6 4.1 %shard_map.399 = (bf16[448,128]{1,0:T(8,128)(2,1)S(1)}, bf16[448,128]{1,0:T(8,128)(2,1)S(1)}, bf16[896,128]{1,0:T(8,128)(2,1)S(1)}) custom-call(s32[64,3]{1,0:T(8,128)} %copy.49.info_in, bf16[256,768]{1,0:T(8,128)(2,1)S(1)} %bitcast.24, bf16[256,4224]{1,0:T(8,128)(2,1)} %get-tuple-element.77.low_in, f32[264,1280]{1,0:T(8,128)} %get-tuple-element.78.high_in, ...), custom_call_target="tpu_custom_call" | custom-call | flops 3000000000 | bytes 1 | tf_op jit(solution)/shard_map/pallas_call | solution.py:43
  55.0 1.4 %collective-permute-done.7 = bf16[896,128]{1,0:T(8,128)(2,1)S(1)} collective-permute-done((bf16[896,128]{1,0:T(8,128)(2,1)S(1)}, bf16[896,128]{1,0:T(8,128)(2,1)S(1)}, u32[]{:S(2)}, u32[]{:S(2)}) %collective-permute-start.7) | collective-permute-done | bytes 229408 | tf_op jit(solution)/shard_map/ppermute | solution.py:1108
  56.4 1.6 %collective-permute-start.8 = (bf16[448,128]{1,0:T(8,128)(2,1)S(1)}, bf16[448,128]{1,0:T(8,128)(2,1)S(1)}, u32[]{:S(2)}, u32[]{:S(2)}) collective-permute-start(bf16[448,128]{1,0:T(8,128)(2,1)S(1)} %reduce-precision_convert_fusion), channel_id=1, source_target_pairs={{0,2},{1,3},{2,0},{3,1},{4,6},{5,7},{6,4},{7,5},{8,10},{9,11},{10,... | collective-permute-start | bytes 344072 | tf_op jit(solution)/shard_map/ppermute | solution.py:1108
  58.1 3.6 %collective-permute-done.8 = bf16[448,128]{1,0:T(8,128)(2,1)S(1)} collective-permute-done((bf16[448,128]{1,0:T(8,128)(2,1)S(1)}, bf16[448,128]{1,0:T(8,128)(2,1)S(1)}, u32[]{:S(2)}, u32[]{:S(2)}) %collective-permute-start.8) | collective-permute-done | bytes 114720 | tf_op jit(solution)/shard_map/ppermute | solution.py:1108
  61.8 1.7 %collective-permute-start.9 = (bf16[448,128]{1,0:T(8,128)(2,1)S(1)}, bf16[448,128]{1,0:T(8,128)(2,1)S(1)}, u32[]{:S(2)}, u32[]{:S(2)}) collective-permute-start(bf16[448,128]{1,0:T(8,128)(2,1)S(1)} %fusion.3), channel_id=1, source_target_pairs={{0,4},{4,0},{8,12},{12,8},{16,20},{20,16},{24,28},{28,24},{1,5},{5... | collective-permute-start | bytes 344072 | tf_op jit(solution)/shard_map/ppermute | solution.py:1108
  63.4 3.2 %collective-permute-done.9 = bf16[448,128]{1,0:T(8,128)(2,1)S(1)} collective-permute-done((bf16[448,128]{1,0:T(8,128)(2,1)S(1)}, bf16[448,128]{1,0:T(8,128)(2,1)S(1)}, u32[]{:S(2)}, u32[]{:S(2)}) %collective-permute-start.9) | collective-permute-done | bytes 114720 | tf_op jit(solution)/shard_map/ppermute | solution.py:1108
  66.7 1.7 %collective-permute-start.10 = (bf16[448,128]{1,0:T(8,128)(2,1)S(1)}, bf16[448,128]{1,0:T(8,128)(2,1)S(1)}, u32[]{:S(2)}, u32[]{:S(2)}) collective-permute-start(bf16[448,128]{1,0:T(8,128)(2,1)S(1)} %fusion), channel_id=1, source_target_pairs={{0,8},{4,12},{8,0},{12,4},{16,24},{20,28},{24,16},{28,20},{1,9},{5... | collective-permute-start | bytes 344072 | tf_op jit(solution)/shard_map/ppermute | solution.py:1108
  68.4 3.2 %collective-permute-done.10 = bf16[448,128]{1,0:T(8,128)(2,1)S(1)} collective-permute-done((bf16[448,128]{1,0:T(8,128)(2,1)S(1)}, bf16[448,128]{1,0:T(8,128)(2,1)S(1)}, u32[]{:S(2)}, u32[]{:S(2)}) %collective-permute-start.10) | collective-permute-done | bytes 114720 | tf_op jit(solution)/shard_map/ppermute | solution.py:1108
  71.7 2.8 %collective-permute-start.11 = (bf16[448,128]{1,0:T(8,128)(2,1)S(1)}, bf16[448,128]{1,0:T(8,128)(2,1)S(1)}, u32[]{:S(2)}, u32[]{:S(2)}) collective-permute-start(bf16[448,128]{1,0:T(8,128)(2,1)S(1)} %fusion.1), channel_id=1, source_target_pairs={{0,16},{4,20},{8,24},{12,28},{16,0},{20,4},{24,8},{28,12},{1,17},{... | collective-permute-start | bytes 344072 | tf_op jit(solution)/shard_map/ppermute | solution.py:1108
  74.4 4.2 %collective-permute-done.11 = bf16[448,128]{1,0:T(8,128)(2,1)S(1)} collective-permute-done((bf16[448,128]{1,0:T(8,128)(2,1)S(1)}, bf16[448,128]{1,0:T(8,128)(2,1)S(1)}, u32[]{:S(2)}, u32[]{:S(2)}) %collective-permute-start.11) | collective-permute-done | bytes 114720 | tf_op jit(solution)/shard_map/ppermute | solution.py:1108
  78.6 0.1 add_reduce-precision_fusion.grad
  78.9 1.5 %shard_map.400 = (f32[25,2,256]{2,1,0:T(2,128)}, f32[2,64,256]{2,1,0:T(8,128)}, f32[47,2,64]{2,1,0:T(2,128)}, f32[2,64]{1,0:T(2,128)}, f32[1,47]{1,0:T(1,128)}, ...) custom-call(f32[448,128]{1,0:T(8,128)S(1)} %add_reduce-precision_fus, ...), custom_call_target="tpu_custom_call" | custom-call | flops 1000000000 | bytes 1 | tf_op jit(solution)/shard_map/pallas_call | solution.py:43
  80.4 1.2 %collective-permute-done.12 = f32[8,128]{1,0:T(8,128)S(1)} collective-permute-done((f32[8,128]{1,0:T(8,128)S(1)}, f32[8,128]{1,0:T(8,128)S(1)}, u32[]{:S(2)}, u32[]{:S(2)}) %collective-permute-start.12) | collective-permute-done | bytes 4128 | tf_op jit(solution)/shard_map/ppermute | solution.py:1108
  81.6 1.6 %collective-permute-start.13 = (f32[8,128]{1,0:T(8,128)S(1)}, f32[8,128]{1,0:T(8,128)S(1)}, u32[]{:S(2)}, u32[]{:S(2)}) collective-permute-start(f32[8,128]{1,0:T(8,128)S(1)} %add.27.own), channel_id=1, source_target_pairs={{0,2},{1,3},{2,0},{3,1},{4,6},{5,7},{6,4},{7,5},{8,10},{9,11},{10,... | collective-permute-start | bytes 12296 | tf_op jit(solution)/shard_map/ppermute | solution.py:1108
  83.2 0.6 fusion.4
  83.7 1.4 %collective-permute-done.13.other = f32[8,128]{1,0:T(8,128)S(1)} collective-permute-done((f32[8,128]{1,0:T(8,128)S(1)}, f32[8,128]{1,0:T(8,128)S(1)}, u32[]{:S(2)}, u32[]{:S(2)}) %collective-permute-start.13) | collective-permute-done | bytes 4128 | tf_op jit(solution)/shard_map/ppermute | solution.py:1108
  85.2 0.8 shard_map.401
  (83 shorter events, 1.1 us)
Async XLA Ops:
  4.5 16.3 %collective-permute-start.2 = (bf16[24,1920]{1,0:T(8,128)(2,1)S(1)}, bf16[24,1920]{1,0:T(8,128)(2,1)S(1)}, u32[]{:S(2)}, u32[]{:S(2)}) collective-permute-start(bf16[24,1920]{1,0:T(8,128)(2,1)S(1)} %get-tuple-element.72), channel_id=1, source_target_pairs={{0,3},{1,2},{2,1},{3,0},{4,7},{5,6},{6,5},{7,4},{8,11},{9,10},{10,... | collective-permute-start | bytes 276488 | tf_op jit(solution)/shard_map/ppermute | solution.py:1108
  7.0 8.6 %collective-permute-start = (bf16[24,4352]{1,0:T(8,128)(2,1)S(1)}, bf16[24,4352]{1,0:T(8,128)(2,1)S(1)}, u32[]{:S(2)}, u32[]{:S(2)}) collective-permute-start(bf16[24,4352]{1,0:T(8,128)(2,1)S(1)} %get-tuple-element.65), channel_id=1, source_target_pairs={{0,1},{1,0},{2,3},{3,2},{4,5},{5,4},{6,7},{7,6},{8,9},{9,8},{10,11... | collective-permute-start | bytes 626696 | tf_op jit(solution)/shard_map/ppermute | solution.py:1108
  7.7 10.5 %copy-start.3 = (s32[10,2048]{1,0:T(8,128)S(1)}, s32[10,2048]{1,0:T(8,128)}, u32[]{:S(2)}) copy-start(s32[10,2048]{1,0:T(8,128)} %nbr2) | copy-start | bytes 245764
  7.7 10.5 %copy-start.4 = (s32[10,2048]{1,0:T(8,128)S(1)}, s32[10,2048]{1,0:T(8,128)}, u32[]{:S(2)}) copy-start(s32[10,2048]{1,0:T(8,128)} %pres2.1) | copy-start | bytes 245764
  7.7 7.8 %collective-permute-start.1 = (bf16[24,4352]{1,0:T(8,128)(2,1)S(1)}, bf16[24,4352]{1,0:T(8,128)(2,1)S(1)}, u32[]{:S(2)}, u32[]{:S(2)}) collective-permute-start(bf16[24,4352]{1,0:T(8,128)(2,1)S(1)} %get-tuple-element.70), channel_id=1, source_target_pairs={{0,2},{1,3},{2,0},{3,1},{4,6},{5,7},{6,4},{7,5},{8,10},{9,11},{10,... | collective-permute-start | bytes 626696 | tf_op jit(solution)/shard_map/ppermute | solution.py:1108
  15.6 5.3 %collective-permute-start.3 = (bf16[24,4352]{1,0:T(8,128)(2,1)S(1)}, bf16[24,4352]{1,0:T(8,128)(2,1)S(1)}, u32[]{:S(2)}, u32[]{:S(2)}) collective-permute-start(bf16[24,4352]{1,0:T(8,128)(2,1)S(1)} %collective-permute-done.1.s2), channel_id=1, source_target_pairs={{0,1},{1,0},{2,3},{3,2},{4,5},{5,4},{6,7},{7,6},{8,9},{9,8},{10,11... | collective-permute-start | bytes 626696 | tf_op jit(solution)/shard_map/ppermute | solution.py:1108
  15.8 16.9 %collective-permute-start.4 = (bf16[24,5888]{1,0:T(8,128)(2,1)S(1)}, bf16[24,5888]{1,0:T(8,128)(2,1)S(1)}, u32[]{:S(2)}, u32[]{:S(2)}) collective-permute-start(bf16[24,5888]{1,0:T(8,128)(2,1)S(1)} %get-tuple-element.79), channel_id=1, source_target_pairs={{0,1},{1,0},{2,3},{3,2},{4,5},{5,4},{6,7},{7,6},{8,9},{9,8},{10,11... | collective-permute-start | bytes 847880 | tf_op jit(solution)/shard_map/ppermute | solution.py:1108
  16.2 16.6 %collective-permute-start.5 = (bf16[24,5888]{1,0:T(8,128)(2,1)S(1)}, bf16[24,5888]{1,0:T(8,128)(2,1)S(1)}, u32[]{:S(2)}, u32[]{:S(2)}) collective-permute-start(bf16[24,5888]{1,0:T(8,128)(2,1)S(1)} %get-tuple-element.80), channel_id=1, source_target_pairs={{0,2},{1,3},{2,0},{3,1},{4,6},{5,7},{6,4},{7,5},{8,10},{9,11},{10,... | collective-permute-start | bytes 847880 | tf_op jit(solution)/shard_map/ppermute | solution.py:1108
  18.2 14.6 %collective-permute-start.6 = (bf16[24,5888]{1,0:T(8,128)(2,1)S(1)}, bf16[24,5888]{1,0:T(8,128)(2,1)S(1)}, u32[]{:S(2)}, u32[]{:S(2)}) collective-permute-start(bf16[24,5888]{1,0:T(8,128)(2,1)S(1)} %get-tuple-element.81), channel_id=1, source_target_pairs={{0,3},{1,2},{2,1},{3,0},{4,7},{5,6},{6,5},{7,4},{8,11},{9,10},{10,... | collective-permute-start | bytes 847880 | tf_op jit(solution)/shard_map/ppermute | solution.py:1108
  26.5 24.1 %all-to-all-start = ((bf16[32,8,768]{2,1,0:T(8,128)(2,1)}), bf16[32,8,768]{2,1,0:T(8,128)(2,1)S(1)}, u32[]{:S(2)}, u32[]{:S(2)}) async-start(bf16[32,8,768]{2,1,0:T(8,128)(2,1)} %bitcast.2), calls=%async_computation | async-start | bytes 786432 | tf_op jit(solution)/shard_map/all_to_all | solution.py:1146
  54.7 24.1 %copy-start.5 = (f32[2,64,256]{2,1,0:T(8,128)S(1)}, f32[2,64,256]{2,1,0:T(8,128)}, u32[]{:S(2)}) copy-start(f32[2,64,256]{2,1,0:T(8,128)} %f2.1) | copy-start | bytes 393220
  54.7 24.1 %copy-start.6 = (f32[2,64,256]{2,1,0:T(8,128)S(1)}, f32[2,64,256]{2,1,0:T(8,128)}, u32[]{:S(2)}) copy-start(f32[2,64,256]{2,1,0:T(8,128)} %s2_.1) | copy-start | bytes 393220
  54.7 24.1 %copy-start.7 = (f32[2,64,256]{2,1,0:T(8,128)S(1)}, f32[2,64,256]{2,1,0:T(8,128)}, u32[]{:S(2)}) copy-start(f32[2,64,256]{2,1,0:T(8,128)} %w2.3) | copy-start | bytes 393220
  54.7 24.1 %copy-start.8 = (f32[2,25,256]{2,0,1:T(2,128)S(1)}, f32[2,25,256]{2,0,1:T(2,128)}, u32[]{:S(2)}) copy-start(f32[2,25,256]{2,0,1:T(2,128)} %param.44) | copy-start | bytes 153604
  54.7 24.1 %copy-start.9 = (f32[2,25,256]{2,0,1:T(2,128)S(1)}, f32[2,25,256]{2,0,1:T(2,128)}, u32[]{:S(2)}) copy-start(f32[2,25,256]{2,0,1:T(2,128)} %param.49) | copy-start | bytes 153604
  54.7 24.1 %copy-start.10 = (f32[2,25,256]{2,0,1:T(2,128)S(1)}, f32[2,25,256]{2,0,1:T(2,128)}, u32[]{:S(2)}) copy-start(f32[2,25,256]{2,0,1:T(2,128)} %param.39) | copy-start | bytes 153604
  54.7 24.1 %copy-start.11 = (f32[2,64,47]{1,0,2:T(2,128)S(1)}, f32[2,64,47]{1,0,2:T(2,128)}, u32[]{:S(2)}) copy-start(f32[2,64,47]{1,0,2:T(2,128)} %param.46) | copy-start | bytes 72196
  54.7 24.1 %copy-start.12 = (f32[2,64,47]{1,0,2:T(2,128)S(1)}, f32[2,64,47]{1,0,2:T(2,128)}, u32[]{:S(2)}) copy-start(f32[2,64,47]{1,0,2:T(2,128)} %param.51) | copy-start | bytes 72196
  54.8 24.1 %copy-start.13 = (f32[2,64,47]{1,0,2:T(2,128)S(1)}, f32[2,64,47]{1,0,2:T(2,128)}, u32[]{:S(2)}) copy-start(f32[2,64,47]{1,0,2:T(2,128)} %param.41) | copy-start | bytes 72196
  54.8 24.1 %copy-start.16 = (f32[2,64]{1,0:T(2,128)S(1)}, f32[2,64]{1,0:T(2,128)}, u32[]{:S(2)}) copy-start(f32[2,64]{1,0:T(2,128)} %fh.1) | copy-start | bytes 1540
  54.8 24.1 %copy-start.17 = (f32[2,64]{1,0:T(2,128)S(1)}, f32[2,64]{1,0:T(2,128)}, u32[]{:S(2)}) copy-start(f32[2,64]{1,0:T(2,128)} %sh.1) | copy-start | bytes 1540
  54.8 24.1 %copy-start.18 = (f32[2,64]{1,0:T(2,128)S(1)}, f32[2,64]{1,0:T(2,128)}, u32[]{:S(2)}) copy-start(f32[2,64]{1,0:T(2,128)} %wh.3) | copy-start | bytes 1540
  54.8 24.1 %copy-start.19 = (f32[47]{0:T(128)S(1)}, f32[47]{0:T(128)}, u32[]{:S(2)}) copy-start(f32[47]{0:T(128)} %param.48) | copy-start | bytes 568
  54.8 24.1 %copy-start.20 = (f32[47]{0:T(128)S(1)}, f32[47]{0:T(128)}, u32[]{:S(2)}) copy-start(f32[47]{0:T(128)} %param.53) | copy-start | bytes 568
  54.8 24.1 %copy-start.21 = (f32[47]{0:T(128)S(1)}, f32[47]{0:T(128)}, u32[]{:S(2)}) copy-start(f32[47]{0:T(128)} %param.43) | copy-start | bytes 568
  54.8 1.6 %collective-permute-start.7 = (bf16[896,128]{1,0:T(8,128)(2,1)S(1)}, bf16[896,128]{1,0:T(8,128)(2,1)S(1)}, u32[]{:S(2)}, u32[]{:S(2)}) collective-permute-start(bf16[896,128]{1,0:T(8,128)(2,1)S(1)} %get-tuple-element.83), channel_id=1, source_target_pairs={{0,1},{1,0},{2,3},{3,2},{4,5},{5,4},{6,7},{7,6},{8,9},{9,8},{10,11... | collective-permute-start | bytes 688136 | tf_op jit(solution)/shard_map/ppermute | solution.py:1108
  56.4 5.3 %collective-permute-start.8 = (bf16[448,128]{1,0:T(8,128)(2,1)S(1)}, bf16[448,128]{1,0:T(8,128)(2,1)S(1)}, u32[]{:S(2)}, u32[]{:S(2)}) collective-permute-start(bf16[448,128]{1,0:T(8,128)(2,1)S(1)} %reduce-precision_convert_fusion), channel_id=1, source_target_pairs={{0,2},{1,3},{2,0},{3,1},{4,6},{5,7},{6,4},{7,5},{8,10},{9,11},{10,... | collective-permute-start | bytes 344072 | tf_op jit(solution)/shard_map/ppermute | solution.py:1108
  61.8 4.9 %collective-permute-start.9 = (bf16[448,128]{1,0:T(8,128)(2,1)S(1)}, bf16[448,128]{1,0:T(8,128)(2,1)S(1)}, u32[]{:S(2)}, u32[]{:S(2)}) collective-permute-start(bf16[448,128]{1,0:T(8,128)(2,1)S(1)} %fusion.3), channel_id=1, source_target_pairs={{0,4},{4,0},{8,12},{12,8},{16,20},{20,16},{24,28},{28,24},{1,5},{5... | collective-permute-start | bytes 344072 | tf_op jit(solution)/shard_map/ppermute | solution.py:1108
  66.7 4.9 %collective-permute-start.10 = (bf16[448,128]{1,0:T(8,128)(2,1)S(1)}, bf16[448,128]{1,0:T(8,128)(2,1)S(1)}, u32[]{:S(2)}, u32[]{:S(2)}) collective-permute-start(bf16[448,128]{1,0:T(8,128)(2,1)S(1)} %fusion), channel_id=1, source_target_pairs={{0,8},{4,12},{8,0},{12,4},{16,24},{20,28},{24,16},{28,20},{1,9},{5... | collective-permute-start | bytes 344072 | tf_op jit(solution)/shard_map/ppermute | solution.py:1108
  71.7 7.0 %collective-permute-start.11 = (bf16[448,128]{1,0:T(8,128)(2,1)S(1)}, bf16[448,128]{1,0:T(8,128)(2,1)S(1)}, u32[]{:S(2)}, u32[]{:S(2)}) collective-permute-start(bf16[448,128]{1,0:T(8,128)(2,1)S(1)} %fusion.1), channel_id=1, source_target_pairs={{0,16},{4,20},{8,24},{12,28},{16,0},{20,4},{24,8},{28,12},{1,17},{... | collective-permute-start | bytes 344072 | tf_op jit(solution)/shard_map/ppermute | solution.py:1108
  80.4 1.2 %collective-permute-start.12 = (f32[8,128]{1,0:T(8,128)S(1)}, f32[8,128]{1,0:T(8,128)S(1)}, u32[]{:S(2)}, u32[]{:S(2)}) collective-permute-start(f32[8,128]{1,0:T(8,128)S(1)} %get-tuple-element.85), channel_id=1, source_target_pairs={{0,1},{1,0},{2,3},{3,2},{4,5},{5,4},{6,7},{7,6},{8,9},{9,8},{10,11... | collective-permute-start | bytes 12296 | tf_op jit(solution)/shard_map/ppermute | solution.py:1108
  81.6 3.6 %collective-permute-start.13 = (f32[8,128]{1,0:T(8,128)S(1)}, f32[8,128]{1,0:T(8,128)S(1)}, u32[]{:S(2)}, u32[]{:S(2)}) collective-permute-start(f32[8,128]{1,0:T(8,128)S(1)} %add.27.own), channel_id=1, source_target_pairs={{0,2},{1,3},{2,0},{3,1},{4,6},{5,7},{6,4},{7,5},{8,10},{9,11},{10,... | collective-permute-start | bytes 12296 | tf_op jit(solution)/shard_map/ppermute | solution.py:1108
  (15 other events, 77.4 us)

commit v3 on v2

--- a/solution.py
+++ b/solution.py
@@ -24,6 +24,7 @@
 SENTINEL = 4.0
 MIB = 2**20
 LOSS_BITS = 14
+EARLY = 6
 FIRST_MIB = 8
 MEAN_MIB = 8
 SEEDS_MIB = 16
@@ -35,14 +36,15 @@
     return pl.CostEstimate(flops=int(micros * 10**9), bytes_accessed=1, transcendentals=0)
 
 
-def call(kernel, outs, scratch, mib, *args, far_in=(), far_out=(), copies=0, micros=1):
+def call(kernel, outs, scratch, mib, *args, far_in=(), far_out=(), copies=0, micros=1, loose=(), name=None):
     near = pl.BlockSpec(memory_space=pltpu.VMEM)
     far = pl.BlockSpec(memory_space=pltpu.HBM)
+    free = pl.BlockSpec(memory_space=pl.ANY)
     scratch = [pltpu.VMEM(shape, kind) for shape, kind in scratch]
     args = [pltpu.with_memory_space_constraint(a, pltpu.HBM) if i in far_in else a for i, a in enumerate(args)]
     return pl.pallas_call(
         kernel,
-        in_specs=[far if i in far_in else near for i in range(len(args))],
+        in_specs=[free if i in loose else far if i in far_in else near for i in range(len(args))],
         out_specs=tuple(far if i in far_out else near for i in range(len(outs))),
         out_shape=tuple(
             pltpu.HBM(shape, kind) if i in far_out else jax.ShapeDtypeStruct(shape, kind)
@@ -51,6 +53,7 @@
         scratch_shapes=scratch + ([pltpu.SemaphoreType.DMA((copies,))] if copies else []),
         compiler_params=pltpu.CompilerParams(vmem_limit_bytes=mib * MIB),
         cost_estimate=cost(micros),
+        name=name,
     )(*args)
 
 
@@ -96,8 +99,9 @@
         self.misc = self.at_three + self.head
         self.pay = self.misc + 16
         self.blocks = -(-self.pay // self.main)
-        self.message_a = self.pair_lanes(self.n_a)
-        self.message_b = self.pair_lanes(self.n_mid)
+        self.early = EARLY * LANES
+        self.message_a = self.pair_lanes(self.n_a, self.n_a - self.early)
+        self.message_b = self.pair_lanes(self.n_mid, self.n_mid + self.early)
         self.full_b = self.message_b + LANES * self.blocks
         self.tiles_b_all = 16 * self.own // LANES + 1
         self.count_rows = WINDOW + 16
@@ -122,8 +126,19 @@
         self.part_lanes = at
         self.at = places
 
-    def pair_lanes(self, lanes):
-        return 2 * lanes + LANES * -(-2 * lanes // LANES // self.main)
+    def pair_lanes(self, means, own):
+        lanes = means + own
+        return lanes + LANES * -(-lanes // LANES // self.main)
+
+    def first_ranges(self, part):
+        a, b, c = self.ranges(part)
+        b = (b[0], 0, b[2])
+        c = (c[0], b[2], c[2])
+        return [b, c, (a[0], self.n_mid, self.early)], [b, c]
+
+    def second_ranges(self, part):
+        first = self.a_start(part)
+        return [(first + self.early, 0, self.n_a - self.early)], [(first, 0, self.n_a)]
 
     def a_start(self, part):
         return jnp.clip(16 * self.own * part - 3 * LANES, 0, self.low - self.n_a)
@@ -168,7 +183,7 @@
 
 
 def sigmoid(value):
-    return 1.0 / (1.0 + jnp.exp(-value))
+    return 0.5 * jnp.tanh(0.5 * value) + 0.5
 
 
 def unpack_tile(sz, message, tail, tile):
@@ -177,11 +192,11 @@
     return jnp.concatenate([main, tail[tile : tile + 1, :], spare], 0).astype(BF)
 
 
-def mean_tiles(sz, tiles, feat_ref, nbr_ref, pres_ref, mean_ref, tail_ref, base_ref, code_ref, count_ref):
+def mean_tiles(sz, begin, tiles, feat_ref, nbr_ref, pres_ref, mean_ref, tail_ref, base_ref, code_ref, count_ref):
     last = feat_ref.shape[1] // LANES - 6
     slots = nbr_ref.shape[0]
     base_ref[...] = jnp.zeros_like(base_ref)
-    if tiles % 8:
+    if begin % 8 or tiles % 8:
         code_ref[...] = jnp.full_like(code_ref, -1)
         count_ref[...] = jnp.ones_like(count_ref)
     for tile in range(feat_ref.shape[1] // LANES):
@@ -221,12 +236,13 @@
         mean_ref[:, pl.ds(lane, LANES)] = (jnp.concatenate(totals, 0) / counts).astype(BF)
         return carry
 
-    lax.fori_loop(0, tiles // 4 * 4, one_tile, 0, unroll=4)
-    for step in range(tiles // 4 * 4, tiles):
+    even = begin + (tiles - begin) // 4 * 4
+    lax.fori_loop(begin, even, one_tile, 0, unroll=4)
+    for step in range(even, tiles):
         one_tile(step, 0)
     sub = lax.broadcasted_iota(jnp.int32, (8, LANES), 0)
 
-    for block in range(-(-tiles // 8)):
+    for block in range(begin // 8, -(-tiles // 8)):
         total = jnp.zeros((8, LANES), F32)
         for slot in range(slots):
             code = code_ref[slot, 8 * block : 8 * (block + 1), :]
@@ -242,19 +258,16 @@
 
 def pack_pair(sz, ranges, feat_ref, base_ref, mean_ref, tail_ref, turn_ref, out_ref):
     turn_ref[...] = jnp.zeros_like(turn_ref)
-    base = ranges[0][1]
-    lanes = sum(count for _, _, count in ranges)
-    tiles = lanes // LANES
-    for first, at, count in ranges:
-        at = at - base
-        source = pl.ds(aligned(first), count)
-        out_ref[:, at : at + count] = feat_ref[: sz.main, source]
-        out_ref[:, lanes + at : lanes + at + count] = mean_ref[: sz.main, source]
-        at, rows = at // LANES, count // LANES
-        turn_ref[at : at + rows, :] = base_ref[pl.ds(8 + first // LANES, rows), :]
-        turn_ref[tiles + at : tiles + at + rows, :] = tail_ref[pl.ds(first // LANES, rows), :]
-    for block in range(-(-2 * tiles // sz.main)):
-        at = 2 * lanes + LANES * block
+    lanes = 0
+    for source_ref, rows_ref, shift, group in zip((feat_ref, mean_ref), (base_ref, tail_ref), (8, 0), ranges):
+        for first, at, count in group:
+            at = at + lanes
+            out_ref[:, at : at + count] = source_ref[: sz.main, pl.ds(aligned(first), count)]
+            at, rows = at // LANES, count // LANES
+            turn_ref[at : at + rows, :] = rows_ref[pl.ds(shift + first // LANES, rows), :]
+        lanes += sum(count for _, _, count in group)
+    for block in range(-(-lanes // LANES // sz.main)):
+        at = lanes + LANES * block
         out_ref[:, at : at + LANES] = turn_ref[sz.main * block : sz.main * (block + 1), :].astype(BF)
 
 
@@ -283,40 +296,37 @@
     ]
 
 
-def unpack_pair(sz, message, r, lanes, turn_ref, out_ref):
-    tiles = lanes // LANES
-    for block in range(-(-2 * tiles // sz.main)):
-        at = 2 * lanes + LANES * block
+def unpack_tails(sz, message, lanes, turn_ref):
+    for block in range(-(-lanes // LANES // sz.main)):
+        at = lanes + LANES * block
         turn_ref[sz.main * block : sz.main * (block + 1), :] = message[:, at : at + LANES].astype(F32)
-    tail = turn_ref[...]
-    for tile in range(2 * tiles):
-        row = sz.hold * (r if tile < tiles else 4 + r)
-        at = LANES * (tile % tiles)
-        out_ref[row : row + sz.hold, at : at + LANES] = unpack_tile(sz, message, tail, tile)
+    return turn_ref[...]
+
+
+def unpack_tiles(sz, message, tail, first, tiles, row, at, out_ref):
+    for tile in range(tiles):
+        lane = at + LANES * tile
+        out_ref[row : row + sz.hold, lane : lane + LANES] = unpack_tile(sz, message, tail, first + tile)
 
 
 def first_kernel(
-    sz, features, neighbors, present, w1_in, w2_in, w3_in, wh_in, own_b, packed, m1, m2, m3,
+    sz, features, neighbors, present, w1_in, w2_in, w3_in, wh_in, own_b, packed, mean_out, tail_out, m1, m2, m3,
     feat_ref, nbr_ref, pres_ref, w1, w2, w3, wh, own_ref,
     mean_ref, tail_ref, turn_ref, base_ref, code_ref, count_ref, one_ref, three_ref, pack, sems,
 ):
     part = lax.axis_index("col")
     rows = pl.ds(0, nbr_ref.shape[1])
+    weights = start_copies(((w1_in, w1), (w2_in, w2), (w3_in, w3), (wh_in, wh)), sems)
     copies = start_copies(
         (
             (features.at[:, pl.ds(0, feat_ref.shape[1])], feat_ref),
             (neighbors.at[:, rows], nbr_ref),
             (present.at[:, rows], pres_ref),
-            (w1_in, w1),
-            (w2_in, w2),
-            (w3_in, w3),
-            (wh_in, wh),
         ),
         sems,
-    )
-    wait_all(copies[:3])
-    mean_tiles(sz, sz.tiles_b_all, feat_ref, nbr_ref, pres_ref, mean_ref, tail_ref, base_ref, code_ref, count_ref)
-    wait_all(copies[3:])
+        4,
+    )
+    wait_all(weights)
     one_ref[...] = jnp.zeros_like(one_ref)
     three_ref[...] = jnp.zeros_like(three_ref)
     for s in range(2):
@@ -346,10 +356,13 @@
         piece = pack[sz.main * block : sz.main * (block + 1), :].astype(BF)
         m1[:, at : at + LANES] = piece
         m2[:, at : at + LANES] = piece
+    wait_all(copies)
+    mean_tiles(sz, 0, sz.tiles_b_all, feat_ref, nbr_ref, pres_ref, mean_ref, tail_ref, base_ref, code_ref, count_ref)
+    store += start_copies(((mean_ref, mean_out), (tail_ref, tail_out)), sems, 9)
     own_pair(sz, sz.ranges(part)[1:], feat_ref, mean_ref, tail_ref, own_ref)
     store += start_copies(((own_ref, own_b),), sems, 8)
     for r, out in ((1, m1), (2, m2), (3, m3)):
-        pack_pair(sz, sz.ranges(part ^ r)[1:], feat_ref, base_ref, mean_ref, tail_ref, turn_ref, out)
+        pack_pair(sz, sz.first_ranges(part ^ r), feat_ref, base_ref, mean_ref, tail_ref, turn_ref, out)
     wait_all(store)
 
 
@@ -362,6 +375,8 @@
         [
             ((2 * sz.hold, sz.n_mid), BF),
             ((sz.main * sz.blocks, LANES), F32),
+            ((sz.main, rows), BF),
+            ((-(-sz.tiles_b_all // 8) * 8, LANES), F32),
             ((sz.main, sz.full_b), BF),
             ((sz.main, sz.full_b), BF),
             ((sz.main, sz.message_b), BF),
@@ -389,37 +404,48 @@
         w3,
         hidden,
         far_in=range(7),
-        far_out=(0, 1),
-        copies=9,
+        far_out=(0, 1, 2, 3),
+        copies=11,
         micros=4,
     )
 
 
 def mean_kernel(
-    sz, feat_ref, nbr_ref, pres_ref, own_a, a1, a2, a3,
-    mean_ref, tail_ref, turn_ref, base_ref, code_ref, count_ref, own_ref, sems,
+    sz, feat_ref, nbr_ref, pres_ref, mean_in, tail_in, nbr2, pres2, nbr3, pres3, own_a, counts_out, a1, a2, a3,
+    mean_ref, tail_ref, turn_ref, base_ref, code_ref, count_ref, own_ref, kept_ref, counts, sems,
 ):
     part = lax.axis_index("col")
     tiles = sz.low // LANES
-    mean_tiles(sz, tiles, feat_ref, nbr_ref, pres_ref, mean_ref, tail_ref, base_ref, code_ref, count_ref)
+    begin = sz.tiles_b_all
+    loads = start_copies(((mean_in, mean_ref.at[:, pl.ds(0, LANES * begin)]), (tail_in, kept_ref)), sems, 1)
+    fill_counts(sz, part, nbr2, pres2, nbr3, pres3, counts)
+    store = start_copies(((counts, counts_out),), sems, 3)
+    mean_tiles(sz, begin, tiles, feat_ref, nbr_ref, pres_ref, mean_ref, tail_ref, base_ref, code_ref, count_ref)
+    wait_all(loads)
+    tail_ref[:begin, :] = kept_ref[:begin, :]
     own_pair(sz, sz.ranges(part)[:1], feat_ref, mean_ref, tail_ref, own_ref)
-    store = start_copies(((own_ref, own_a),), sems)
+    store += start_copies(((own_ref, own_a),), sems)
     for r, out in ((1, a1), (2, a2), (3, a3)):
-        pack_pair(sz, sz.ranges(part ^ r)[:1], feat_ref, base_ref, mean_ref, tail_ref, turn_ref, out)
+        pack_pair(sz, sz.second_ranges(part ^ r), feat_ref, base_ref, mean_ref, tail_ref, turn_ref, out)
     wait_all(store)
 
 
-def mean_messages(sz, features, neighbors, present):
+def mean_messages(sz, features, neighbors, present, mean, tail, links):
+    counts = (sz.count_rows * (sz.tiles_b + sz.own // LANES), LANES)
     return call(
         functools.partial(mean_kernel, sz),
-        [((2 * sz.hold, sz.n_a), BF)] + [((sz.main, sz.message_a), BF)] * 3,
-        mean_scratch(sz, sz.low // LANES, neighbors.shape[0]) + [((2 * sz.hold, sz.n_a), BF)],
+        [((2 * sz.hold, sz.n_a), BF), (counts, BF)] + [((sz.main, sz.message_a), BF)] * 3,
+        mean_scratch(sz, sz.low // LANES, neighbors.shape[0]) + [((2 * sz.hold, sz.n_a), BF), (tail.shape, F32), (counts, BF)],
         MEAN_MIB,
         features,
         neighbors,
         present,
-        far_out=(0,),
-        copies=1,
+        mean,
+        tail,
+        *links,
+        far_in=(3, 4),
+        far_out=(0, 1),
+        copies=4,
         micros=6,
     )
 
@@ -448,50 +474,33 @@
     return aligned(jnp.clip(first, 0, sz.n_a - WINDOW))
 
 
-def counts_kernel(sz, nbr2, pres2, nbr3, pres3, out, counts, sems):
-    part = lax.axis_index("col")
-    stores = []
-    for tile in range(sz.tiles_mid + sz.own // LANES):
-        start = sz.b_start(part)
-        links, valid, slot = (nbr2, pres2, tile) if tile < sz.tiles_mid else (nbr3, pres3, tile - sz.tiles_mid)
-        if tile < sz.tiles_mid:
-            columns = sz.mid_columns(part, tile)
-        else:
-            columns = pl.ds(aligned(sz.own * part + LANES * slot), LANES)
-        if tile < sz.tiles_b:
-            start = sz.a_start(part) + a_window(sz, part, tile)
-        at = sz.count_rows * tile
-        marks = valid[:, columns]
-        local = jnp.where(marks > 0, links[:, columns] - start, -1)
-        counts[at : at + WINDOW, :] = window_counts(local, WINDOW)
-        counts[at + WINDOW : at + sz.count_rows, :] = jnp.broadcast_to(slot_totals(marks), (16, LANES)).astype(BF)
-        rows = pl.ds(at, sz.count_rows)
-        stores += start_copies(((counts.at[rows, :], out.at[rows, :]),), sems, tile)
-    wait_all(stores)
-
-
-def make_counts(sz, nbr2, pres2, nbr3, pres3):
-    tiles = sz.tiles_mid + sz.own // LANES
-    shape = (sz.count_rows * tiles, LANES)
-    return call(
-        functools.partial(counts_kernel, sz),
-        [(shape, BF)],
-        [(shape, BF)],
-        6,
-        nbr2,
-        pres2,
-        nbr3,
-        pres3,
-        far_out=(0,),
-        copies=tiles,
-        micros=4,
-    )[0]
+def counts_tile(sz, links, marks, start, at, counts):
+    local = jnp.where(marks > 0, links - start, -1)
+    counts[at : at + WINDOW, :] = window_counts(local, WINDOW)
+    counts[at + WINDOW : at + sz.count_rows, :] = jnp.broadcast_to(slot_totals(marks), (16, LANES)).astype(BF)
+
+
+def fill_counts(sz, part, nbr2, pres2, nbr3, pres3, counts):
+    for tile in range(sz.tiles_b):
+        columns = sz.b_columns(part, tile)
+        start = sz.a_start(part) + a_window(sz, part, tile)
+        counts_tile(sz, nbr2[:, columns], pres2[:, columns], start, sz.count_rows * tile, counts)
+    for tile in range(sz.own // LANES):
+        columns = pl.ds(aligned(sz.own * part + LANES * tile), LANES)
+        at = sz.count_rows * (sz.tiles_b + tile)
+        counts_tile(sz, nbr3[:, columns], pres3[:, columns], sz.b_start(part), at, counts)
 
 
 def tile_counts(sz, counts, tile):
     at = sz.count_rows * tile
     totals = counts[at + WINDOW : at + WINDOW + 16, :].astype(F32)[0:1]
     return counts[at : at + WINDOW, :], totals
+
+
+def activate(result):
+    active = result * sigmoid(result)
+    scale = lax.rsqrt(jnp.sum(active * active, 0, keepdims=True) + ROW_EPS)
+    return result, scale, active * scale
 
 
 def first_layer(weight, inputs, bias):
@@ -542,17 +551,32 @@
     ref[:rows, at + lanes : at + 2 * lanes] = value[rows:]
 
 
-def seed_picks(sz, info, part):
-    spots = lax.broadcasted_iota(jnp.int32, (sz.slots, sz.own), 1) + sz.own * part
-    serve = jnp.where(info[:, 0:1] == spots, 1.0, 0.0)
-    take = jnp.where(info[:, 1:2] == spots, 1.0, 0.0)
+def slot_column(table):
+    rows, slots = table.shape
+    wide = jnp.broadcast_to(table.astype(F32)[:, None, :], (rows, slots, slots))
+    hit = lax.broadcasted_iota(jnp.int32, wide.shape, 1) == lax.broadcasted_iota(jnp.int32, wide.shape, 2)
+    return jnp.sum(jnp.where(hit, wide, 0.0), 2, keepdims=True).reshape(rows * slots, 1)
+
+
+def alive_column(sz, live):
+    shape = (sz.dp, sz.dp)
+    hit = lax.broadcasted_iota(jnp.int32, shape, 0) == lax.broadcasted_iota(jnp.int32, shape, 1)
+    counts = jnp.sum(jnp.where(hit, jnp.broadcast_to(live.astype(F32), shape), 0.0), 1, keepdims=True)
+    slot = lax.broadcasted_iota(jnp.int32, (sz.dp, sz.slot), 1).astype(F32)
+    return slot_column(jnp.where(slot < counts, 1.0, 0.0))
+
+
+def seed_picks(sz, serve_rows, take_rows, part):
+    spots = (lax.broadcasted_iota(jnp.int32, (sz.slots, sz.own), 1) + sz.own * part).astype(F32)
+    serve = jnp.where(slot_column(serve_rows) == spots, 1.0, 0.0)
+    take = jnp.where(slot_column(take_rows) == spots, 1.0, 0.0)
     return serve, take, jnp.sum(serve, 1, keepdims=True), jnp.sum(take, 1, keepdims=True)
 
 
 def seeds_kernel(
-    sz, own_b, packed, s1, s2, s3, passed, counts, info_in,
-    low_out, high_out, sent,
-    xb, pack, m1, m2, m3, p3, window_ref, info, low, high, turn_ref, w1_ref, w2_ref, states, sems,
+    sz, own_b, packed, s1, s2, s3, passed, nbr2_in, pres2_in, serve_in, take_in, live_in,
+    low_out, high_out, window_out, sent,
+    xb, pack, m1, m2, m3, p3, nbr2, pres2, window_ref, serve_rows, take_rows, live_rows, low, high, turn_ref, w1_ref, w2_ref, states, sems,
 ):
     part = lax.axis_index("col")
     own, hid, n_b, group, hold, at = sz.own, sz.hid, sz.n_b, sz.group, sz.hold, sz.at
@@ -565,8 +589,11 @@
             (s2, m2),
             (s3, m3),
             (own_b, xb),
-            (counts.at[pl.ds(sz.count_rows * sz.tiles_b, sz.count_rows * (own // LANES)), :], window_ref),
-            (info_in, info),
+            (nbr2_in.at[:, pl.ds(aligned(own * part), own)], nbr2),
+            (pres2_in.at[:, pl.ds(aligned(own * part), own)], pres2),
+            (serve_in, serve_rows),
+            (take_in, take_rows),
+            (live_in, live_rows),
         ),
         sems,
     )
@@ -603,24 +630,43 @@
     def piece(lanes, count):
         return (low.at[:, pl.ds(lanes, count)], low_out.at[:, pl.ds(lanes, count)])
 
-    stores = start_copies((piece(n_mid, at["states"] - n_mid),), sems, 8)
+    stores = start_copies((piece(n_mid, at["states"] - n_mid),), sems, 11)
     wait_all(copies[4:])
+    for tile in range(own // LANES):
+        lanes = slice(LANES * tile, LANES * (tile + 1))
+        counts_tile(sz, nbr2[:, lanes], pres2[:, lanes], sz.b_start(part), sz.count_rows * tile, window_ref)
+    stores += start_copies(((window_ref, window_out),), sems, 18)
     low[:hold, :n_mid] = xb[:hold, :]
     low[4 * hold : 5 * hold, :n_mid] = xb[hold:, :]
     for r, message in ((1, m1), (2, m2), (3, m3)):
-        unpack_pair(sz, message, r, n_mid, turn_ref, low)
-    stores += start_copies((piece(0, n_mid),), sems, 9)
+        tail = unpack_tails(sz, message, 2 * n_mid + sz.early, turn_ref)
+        unpack_tiles(sz, message, tail, 0, sz.tiles_mid, hold * r, 0, low)
+        first = (n_mid + sz.early) // LANES
+        unpack_tiles(sz, message, tail, first, sz.tiles_mid, hold * (4 + r), 0, low)
+    stores += start_copies((piece(0, n_mid),), sems, 12)
     bias1 = high[:hid, at["bias"] : at["bias"] + LANES]
     bias2 = high[:hid, at["bias"] + LANES : at["bias"] + 2 * LANES]
+    high[:hid, :n_mid] = dot(turned1, low[:, :n_mid], (1, 0))
     for tile in range(sz.tiles_mid):
         lanes = slice(LANES * tile, LANES * (tile + 1))
-        result, scale, state = first_layer(turned1, low[:, lanes], bias1)
+        result, scale, state = activate(high[:hid, lanes] + bias1)
         high[:hid, lanes] = result
         high[hid:, lanes] = jnp.broadcast_to(scale, (8, LANES))
         upper, lower = two_parts(state)
         states[:hid, lanes] = upper
         states[hid:, lanes] = lower
     low[:, at["states"] : at["states"] + n_b] = states[:hid, :n_b]
+    rows = pl.ds(0, hid + 8)
+    others = pl.ds(at["bias"], 2 * LANES)
+    stores += start_copies(
+        (
+            piece(at["states"], n_b),
+            (high.at[rows, pl.ds(0, n_mid)], high_out.at[rows, pl.ds(0, n_mid)]),
+            (high.at[rows, others], high_out.at[rows, others]),
+        ),
+        sems,
+        13,
+    )
     for tile in range(own // LANES):
         window, totals = tile_counts(sz, window_ref, tile)
         total = dot(states[:, :n_b], window, (1, 0))
@@ -637,11 +683,12 @@
         first = at["embed"] + LANES * tile
         low[:, first : first + LANES] = upper
         low[:, first + own : first + own + LANES] = lower
-    tail = (piece(at["states"], sz.low_lanes - at["states"]), (high, high_out))
-    stores += start_copies(tail, sems, 10)
-    serve, take, _, owned = seed_picks(sz, info, part)
+    last = pl.ds(at["result2"], own)
+    tail = (piece(at["embed"], sz.low_lanes - at["embed"]), (high.at[rows, last], high_out.at[rows, last]))
+    stores += start_copies(tail, sems, 16)
+    serve, take, _, owned = seed_picks(sz, serve_rows[...], take_rows[...], part)
     value = sent_rows(sz, low, at["embed"], serve, take)
-    dead = (owned > 0.5) & (info[:, 2:3] == 0)
+    dead = (owned > 0.5) & (alive_column(sz, live_rows[...]) < 0.5)
     lane_at = lax.broadcasted_iota(jnp.int32, (sz.slots, 3 * hid), 1)
     value = jnp.where((lane_at == hid) & dead, SENTINEL, value)
     value = value.reshape(sz.dp, 1, sz.slot, 3 * hid)
@@ -659,7 +706,7 @@
     )
 
 
-def seeds_forward(sz, messages, counts, info):
+def seeds_forward(sz, messages, nbr2, pres2, tables):
     hid = sz.hid
     tail = (sz.main, LANES * sz.blocks)
     return call(
@@ -667,6 +714,7 @@
         [
             ((hid, sz.low_lanes), BF),
             ((hid + 8, sz.high_lanes), F32),
+            ((sz.count_rows * (sz.own // LANES), LANES), BF),
             ((4 * sz.slots, 3 * hid), BF),
         ],
         [
@@ -676,8 +724,10 @@
             ((sz.main, sz.full_b), BF),
             ((sz.main, sz.message_b), BF),
             (tail, BF),
+            ((nbr2.shape[0], sz.own), jnp.int32),
+            ((nbr2.shape[0], sz.own), jnp.int32),
             ((sz.count_rows * (sz.own // LANES), LANES), BF),
-            (info.shape, jnp.int32),
+            *[(item.shape, jnp.int32) for item in tables],
             ((hid, sz.low_lanes), BF),
             ((hid + 8, sz.high_lanes), F32),
             ((2 * sz.main, LANES), F32),
@@ -687,18 +737,20 @@
         ],
         SEEDS_MIB,
         *messages,
-        counts,
-        info,
-        far_in=range(8),
+        nbr2,
+        pres2,
+        *tables,
+        far_in=(0, 1, 6, 7, 8, 9, 10),
+        loose=(2, 3, 4, 5),
         micros=4,
-        far_out=(0, 1),
-        copies=12,
+        far_out=(0, 1, 2),
+        copies=19,
     )
 
 
 def rest_kernel(
-    sz, low_in, high_in, counts_in, own_a, v1, v2, v3, labels_in, weighting_in, head_in, part_out,
-    labels, weighting, head_bias, low, xa, bias, counts, xo, a1, a2, a3, turn_ref,
+    sz, low_in, high_in, counts_in, own_a, a1, a2, a3, e1, e2, e3, labels_in, weighting_in, head_in, part_out,
+    labels, weighting, head_bias, low, xa, bias, counts, xo, c1, c2, c3, turn_ref,
     states, states2, result1, scale1, inputs2, result2, scale2, grad_a, low_grad, part_ref, sems,
 ):
     part = lax.axis_index("col")
@@ -710,9 +762,11 @@
     copies = start_copies(
         (
             (own_a, xo),
-            (v1, a1),
-            (v2, a2),
-            (v3, a3),
+            *[(e.at[:, pl.ds(sz.n_mid, sz.early)], c.at[:, pl.ds(0, sz.early)]) for e, c in ((e1, c1), (e2, c2), (e3, c3))],
+            *[
+                (e.at[:, pl.ds(2 * sz.n_mid + sz.early, LANES)], c.at[:, pl.ds(sz.early, LANES)])
+                for e, c in ((e1, c1), (e2, c2), (e3, c3))
+            ],
             (low_in.at[:, pl.ds(sz.n_mid, hid)], low.at[:, pl.ds(0, hid)]),
             (high_in.at[:, pl.ds(sz.at["bias"], 2 * LANES)], bias),
             (low_in.at[:, pl.ds(sz.n_mid + hid, lanes - hid)], low.at[:, pl.ds(hid, lanes - hid)]),
@@ -723,19 +777,27 @@
         ),
         sems,
     )
-    wait_all(copies[:4])
+    late = (n_a - sz.early) // LANES
+    for r, message in ((1, a1), (2, a2), (3, a3)):
+        tail = unpack_tails(sz, message, 2 * n_a - sz.early, turn_ref)
+        unpack_tiles(sz, message, tail, 0, late, hold * r, sz.early, xa)
+        unpack_tiles(sz, message, tail, late, n_a // LANES, hold * (4 + r), 0, xa)
+    wait_all(copies[:7])
+    for r, before in ((1, c1), (2, c2), (3, c3)):
+        tail = before[:, sz.early :].astype(F32)[sz.tiles_mid : sz.tiles_mid + EARLY]
+        unpack_tiles(sz, before, tail, 0, EARLY, hold * r, 0, xa)
     xa[:hold, :] = xo[:hold, :]
     xa[4 * hold : 5 * hold, :] = xo[hold:, :]
-    for r, message in ((1, a1), (2, a2), (3, a3)):
-        unpack_pair(sz, message, r, n_a, turn_ref, xa)
-    wait_all(copies[4:6])
+    wait_all(copies[7:9])
     turned1 = low[:, at["turned1"] : at["turned1"] + hid]
     bias1 = bias[:hid, :LANES]
     bias2 = bias[:hid, LANES:]
 
+    result1[...] = dot(turned1, xa[...], (1, 0))
+
     def forward_step(index, carry):
         lanes = pl.ds(aligned(index * LANES), LANES)
-        result, scale, state = first_layer(turned1, xa[:, lanes], bias1)
+        result, scale, state = activate(result1[:, lanes] + bias1)
         result1[:, lanes] = result
         scale1[:, lanes] = scale
         upper, lower = two_parts(state)
@@ -744,22 +806,24 @@
         return carry
 
     lax.fori_loop(0, n_a // LANES, forward_step, 0, unroll=2)
-    wait_all(copies[6:])
+    wait_all(copies[9:])
     turned2 = low[:, at["turned2"] : at["turned2"] + 2 * hid]
     for tile in range(sz.tiles_b):
         lanes = slice(LANES * tile, LANES * (tile + 1))
         window, totals = tile_counts(sz, counts, tile)
         total = dot(states[:, pl.ds(a_window(sz, part, tile), WINDOW)], window, (1, 0))
         average = ((total[:hid] + total[hid:]) / totals).astype(BF)
-        x = join_inputs(sz, low[:, at["states"] + LANES * tile : at["states"] + LANES * (tile + 1)], average)
-        inputs2[:, lanes] = x
-        result, scale, state = first_layer(turned2, x, bias2)
+        inputs2[:, lanes] = join_inputs(sz, low[:, at["states"] + LANES * tile : at["states"] + LANES * (tile + 1)], average)
+    result2[...] = dot(turned2, inputs2[...], (1, 0))
+    for tile in range(sz.tiles_b):
+        lanes = slice(LANES * tile, LANES * (tile + 1))
+        result, scale, state = activate(result2[:, lanes] + bias2)
         result2[:, lanes] = result
         scale2[:, lanes] = scale
         upper, lower = two_parts(state)
         states2[:hid, lanes] = upper
         states2[hid:, lanes] = lower
-    counts3, totals3 = tile_counts(sz, counts, sz.tiles_mid)
+    counts3, totals3 = tile_counts(sz, counts, sz.tiles_b)
     total = dot(states2[...], counts3, (1, 0))
     average = ((total[:hid] + total[hid:]) / totals3).astype(BF)
     inputs3 = join_inputs(sz, low[:, at["embed"] : at["embed"] + own], average)
@@ -796,15 +860,13 @@
     part_ref[sz.head : sz.head + 16, g3 + hid : g3 + 2 * hid] = row_sums(low_grad2)
     weight2 = halves(low, at["weight2"], hid)
     grad_a[...] = jnp.zeros_like(grad_a)
+    own_part, average_part = split_inputs(sz, dot(weight2, low_grad2, (1, 0)))
+    part_ref[:hid, at["grad_b"] : at["grad_b"] + n_b] = own_part
     for tile in range(sz.tiles_b):
-        lanes = slice(LANES * tile, LANES * (tile + 1))
-        own_part, average_part = split_inputs(sz, dot(weight2, low_grad2[:, lanes], (1, 0)))
-        part_ref[:hid, at["grad_b"] + LANES * tile : at["grad_b"] + LANES * (tile + 1)] = own_part
         window, totals = tile_counts(sz, counts, tile)
         lanes = pl.ds(a_window(sz, part, tile), WINDOW)
-        grad_a[:, lanes] = grad_a[:, lanes] + spread(sz, average_part / totals, window)
-
-    rows = pl.ds(0, hid + 8)
+        grad_a[:, lanes] = grad_a[:, lanes] + spread(sz, average_part[:, LANES * tile : LANES * (tile + 1)] / totals, window)
+    rows, few = pl.ds(0, hid + 8), pl.ds(0, sz.head + 32)
     split = at["g2"]
     stores = start_copies(
         (
@@ -815,7 +877,7 @@
             ),
         ),
         sems,
-        11,
+        14,
     )
 
     def backward_step(index, carry):
@@ -829,10 +891,10 @@
     stores += start_copies(
         (
             (part_ref.at[rows, pl.ds(0, hid)], part_out.at[rows, pl.ds(0, hid)]),
-            (part_ref.at[rows, pl.ds(g3, 2 * hid)], part_out.at[rows, pl.ds(g3, 2 * hid)]),
+            (part_ref.at[few, pl.ds(g3, 2 * hid)], part_out.at[few, pl.ds(g3, 2 * hid)]),
         ),
         sems,
-        13,
+        16,
     )
     wait_all(stores)
 
@@ -851,9 +913,7 @@
             ((hid + 8, 2 * LANES), F32),
             (counts.shape, BF),
             ((2 * sz.hold, sz.n_a), BF),
-            ((sz.main, sz.message_a), BF),
-            ((sz.main, sz.message_a), BF),
-            ((sz.main, sz.message_a), BF),
+            *[((sz.main, sz.early + LANES), BF)] * 3,
             ((2 * sz.main, LANES), F32),
             ((2 * hid, sz.n_a), BF),
             ((2 * hid, sz.n_b), BF),
@@ -874,57 +934,81 @@
         labels,
         weighting,
         head_bias,
-        far_in=range(10),
+        far_in=(0, 1, 2, 3, 10, 11, 12),
+        loose=(7, 8, 9),
         micros=14,
         far_out=(0,),
-        copies=15,
+        copies=18,
     )[0]
 
 
 def seeds_back_kernel(
-    sz, info_in, received, low_in, high_in, counts_in, part_in, keep0, keep1, send,
-    info, x_ref, weight_ref, low, high, window_ref, partial, g1_ref, g2_ref, gb_ref, sems,
+    sz, serve_in, take_in, live_in, received, low_in, high_in, counts_in, part_in, keep0, keep1, send,
+    serve_rows, take_rows, live_rows, x_ref, weight_ref, low, high, window_ref, partial, g1_ref, g2_ref, gb_ref, sems,
 ):
     part = lax.axis_index("col")
     own, hid, group, n_b, n_mid = sz.own, sz.hid, sz.group, sz.n_b, sz.n_mid
     at = dict(sz.at)
     at["inputs2"] -= at["embed"]
     split = at["grad_b"]
+    few = pl.ds(0, sz.head + 32)
+    lanes = pl.ds(at["result2"], own)
     copies = start_copies(
         (
-            (info_in, info),
+            (serve_in, serve_rows),
+            (take_in, take_rows),
+            (live_in, live_rows),
             (low_in.at[:, pl.ds(at["embed"], 4 * own)], low),
-            (part_in.at[:, pl.ds(split, n_b + own)], partial.at[:, pl.ds(split, n_b + own)]),
-            (high_in, high),
+            (part_in.at[:, pl.ds(split + n_b, own)], partial.at[:, pl.ds(split + n_b, own)]),
+            (high_in.at[:, lanes], high.at[:, lanes]),
             (low_in.at[:, pl.ds(at["weight2"], 2 * hid)], weight_ref),
-            (counts_in.at[pl.ds(sz.count_rows * sz.tiles_b, sz.count_rows * (own // LANES)), :], window_ref),
-            (part_in.at[:, pl.ds(0, split)], partial.at[:, pl.ds(0, split)]),
+            (counts_in.at[pl.ds(0, sz.count_rows * (own // LANES)), :], window_ref),
+            (part_in.at[:, pl.ds(split, n_b)], partial.at[:, pl.ds(split, n_b)]),
+            (high_in.at[:, pl.ds(0, n_mid)], high.at[:, pl.ds(0, n_mid)]),
             (low_in.at[:, pl.ds(0, n_mid)], x_ref),
+            (part_in.at[:, pl.ds(0, at["g3"])], partial.at[:, pl.ds(0, at["g3"])]),
+            (part_in.at[few, pl.ds(at["g3"], 2 * hid)], partial.at[few, pl.ds(at["g3"], 2 * hid)]),
         ),
         sems,
     )
     arrived = received[...].astype(F32).reshape(sz.dp, 4, sz.slot, 3 * hid)
     arrived = jnp.sum(arrived, 1).reshape(sz.slots, 3 * hid)
     at["embed"] = 0
-    wait_all(copies[:2])
-    serve, take, served, taken = seed_picks(sz, info, part)
+    wait_all(copies[:4])
+    serve, take, served, taken = seed_picks(sz, serve_rows[...], take_rows[...], part)
     mine = sent_rows(sz, low, 0, serve, take)
     theirs = arrived[:, hid : 2 * hid]
     alive_there = theirs[:, 0:1] < 0.5 * SENTINEL
     theirs = theirs + arrived[:, 2 * hid :]
     differ = mine[:, hid : 2 * hid] + mine[:, 2 * hid :] - arrived[:, :hid]
-    differ = jnp.where((taken > 0.5) & (info[:, 2:3] > 0), differ, 0.0)
+    differ = jnp.where((taken > 0.5) & (alive_column(sz, live_rows[...]) > 0.5), differ, 0.0)
     dist_total = DIST_WEIGHT * jnp.sum(jnp.sum(differ * differ, 0, keepdims=True), 1, keepdims=True)
     local_high, local_low = two_parts(2.0 * DIST_WEIGHT * differ)
     back = jnp.where((served > 0.5) & alive_there, theirs - mine[:, :hid], 0.0)
     back = (-2.0 * DIST_WEIGHT * back).astype(BF)
     take = take.astype(BF)
     serve = serve.astype(BF)
-    wait_all(copies[2:])
+    wait_all(copies[4:6])
     grad = partial[:hid, at["grad_embed"] : at["grad_embed"] + own]
     grad = grad + dot(local_high, take, (0, 0)) + dot(local_low, take, (0, 0)) + dot(back, serve, (0, 0))
     lanes = slice(at["result2"], at["result2"] + own)
     low_grad2 = norm_backward(grad, high[:hid, lanes], high[hid:, lanes][0:1])
+    wait_all(copies[6:9])
+    weight2 = halves(weight_ref, 0, hid)
+    own_part, average_part = split_inputs(sz, dot(weight2, low_grad2, (1, 0)))
+    total_b = partial[:hid, at["grad_b"] : at["grad_b"] + n_b]
+    for tile in range(own // LANES):
+        window, totals = tile_counts(sz, window_ref, tile)
+        total_b = total_b + spread(sz, average_part[:, LANES * tile : LANES * (tile + 1)] / totals, window)
+    wait_all(copies[9:10])
+    low_grad = jnp.concatenate(
+        [
+            norm_backward(total_b, high[:hid, :n_b], high[hid:, :n_b][0:1]),
+            norm_backward(own_part, high[:hid, n_b:n_mid], high[hid:, n_b:n_mid][0:1]),
+        ],
+        1,
+    )
+    wait_all(copies[10:])
     added = dot(halves(low, at["inputs2"], own), low_grad2, (1, 1))
     for half in range(2):
         lanes = slice(at["g2"] + hid * half, at["g2"] + hid * (half + 1))
@@ -932,19 +1016,6 @@
     g3 = at["g3"]
     sums = partial[sz.head : sz.head + 16, g3 : g3 + 2 * hid]
     gb_ref[:, hid:] = sums[:, hid:] + row_sums(low_grad2)
-    weight2 = halves(weight_ref, 0, hid)
-    own_part, average_part = split_inputs(sz, dot(weight2, low_grad2, (1, 0)))
-    total_b = partial[:hid, at["grad_b"] : at["grad_b"] + n_b]
-    for tile in range(own // LANES):
-        window, totals = tile_counts(sz, window_ref, tile)
-        total_b = total_b + spread(sz, average_part[:, LANES * tile : LANES * (tile + 1)] / totals, window)
-    low_grad = jnp.concatenate(
-        [
-            norm_backward(total_b, high[:hid, :n_b], high[hid:, :n_b][0:1]),
-            norm_backward(own_part, high[:hid, n_b:n_mid], high[hid:, n_b:n_mid][0:1]),
-        ],
-        1,
-    )
     half = 4 * sz.hold
     g1_ref[...] = partial[:hid, at["g1"] : at["g1"] + hid] + dot(x_ref[...], low_grad, (1, 1))
     gb_ref[:, :hid] = sums[:, :hid] + row_sums(low_grad)
@@ -984,13 +1055,13 @@
         target_ref[row : row + 16, :] = misc.astype(BF)
 
 
-def seeds_backward(sz, info, received, low, high, counts, partial):
+def seeds_backward(sz, tables, received, low, high, counts, partial):
     hid = sz.hid
     return call(
         functools.partial(seeds_back_kernel, sz),
         [((sz.pay, LANES), BF), ((sz.pay, LANES), BF), ((2 * sz.pay, LANES), BF)],
         [
-            (info.shape, jnp.int32),
+            *[(item.shape, jnp.int32) for item in tables],
             ((hid, sz.n_mid), BF),
             ((hid, 2 * hid), BF),
             ((hid, 4 * sz.own), BF),
@@ -1002,15 +1073,15 @@
             ((16, 2 * hid), F32),
         ],
         BACK_MIB,
-        info,
+        *tables,
         received,
         low,
         high,
         counts,
         partial,
-        far_in=(0, 2, 3, 4, 5),
+        far_in=(0, 1, 2, 4, 5, 6, 7),
         micros=3,
-        copies=8,
+        copies=13,
     )
 
 
@@ -1081,8 +1152,8 @@
     )
 
 
-def step_kernel(own, other, w1, w2, w3, wh, wb, u1, u2, u3, uh, ub, n1, n2, n3, nh, nb, norms_ref):
-    norms = jnp.sqrt(own[...] + other[...])
+def step_kernel(own, core, far, across, w1, w2, w3, wh, wb, u1, u2, u3, uh, ub, n1, n2, n3, nh, nb, norms_ref):
+    norms = jnp.sqrt((own[...] + core[...]) + (far[...] + across[...]))
     norms_ref[...] = norms[0:2, 0:5]
     for i, (w, u, n) in enumerate(
         ((w1, u1, n1), (w2, u2, n2), (w3, u3, n3), (wh, uh, nh), (wb, ub, nb))
@@ -1091,14 +1162,13 @@
         n[...] = w[...] - ratio * u[...]
 
 
-def take_step(own, other, params, updates):
+def take_step(sums, params, updates):
     return call(
         step_kernel,
         [(item.shape, F32) for item in params] + [((2, 5), F32)],
         [],
         3,
-        own,
-        other,
+        *sums,
         *params,
         *updates,
     )
@@ -1131,33 +1201,37 @@
     firsts = tree(first_one, first_two, first_three, first_hidden, first_head)
     seconds = tree(second_one, second_two, second_three, second_hidden, second_head)
 
-    own_b, packed, *sent = first_messages(sz, features, neighbors_one, present_one, *params[:4])
+    own_b, packed, mean, tail, *sent = first_messages(sz, features, neighbors_one, present_one, *params[:4])
     s1, s2, s3 = [swap(sent[r - 1], "col", 4, r) for r in (1, 2, 3)]
-    own_a, *means = mean_messages(sz, features, neighbors_one, present_one)
+    links = (neighbors_two, present_two, neighbors_three, present_three)
+    own_a, counts, *means = mean_messages(sz, features, neighbors_one, present_one, mean, tail, links)
     s1, *means = lax.optimization_barrier((s1, *means))
     means = [swap(means[r - 1], "col", 4, r) for r in (1, 2, 3)]
-    neighbors_two, s2 = lax.optimization_barrier((neighbors_two, s2))
-    counts = make_counts(sz, neighbors_two, present_two, neighbors_three, present_three)
-    later, _ = lax.optimization_barrier((s2, own_a))
+    later, s3, counts = lax.optimization_barrier((s2, s3, counts))
     passed = swap(later, "col", 4, 1)
-    alive = jnp.arange(sz.slot, dtype=jnp.int32)[None, :] < fetch_live[:, None]
-    info = jnp.stack([serve_rows.reshape(-1), take_seed.reshape(-1), alive.astype(jnp.int32).reshape(-1)], 1)
-    low, high, rows = seeds_forward(sz, (own_b, packed, s1, s2, s3, passed), counts, info)
+    tables = (serve_rows, take_seed, fetch_live[None, :])
+    low, high, window, rows = seeds_forward(
+        sz, (own_b, packed, s1, s2, s3, passed), neighbors_two, present_two, tables
+    )
     received = lax.all_to_all(rows, ("dp", "col"), split_axis=0, concat_axis=0, tiled=True)
-    partial = rest_step(sz, low, high, counts, (own_a, *means), labels[None, :], seed_weight[None, :], head_bias[None, :])
-    keep0, keep1, send = seeds_backward(sz, info, received, low, high, counts, partial)
+    partial = rest_step(sz, low, high, counts, (own_a, *means, s1, s2, s3), labels[None, :], seed_weight[None, :], head_bias[None, :])
+    keep0, keep1, send = seeds_backward(sz, tables, received, low, high, window, partial)
     other = swap(send, "col", 4, 1)
-    grad = merged(keep0, other[: sz.pay])
-    grad = merged(grad, swap(merged(keep1, other[sz.pay :]).astype(BF), "col", 4, 2))
-    bit = 1
+    own = merged(keep0, other[: sz.pay]).astype(BF)
+    far = merged(keep1, other[sz.pay :]).astype(BF)
+    pair = [[(d, c), (d ^ 1, c ^ 2)] for d in range(sz.dp) for c in range(4)]
+    pair = [(a * 4 + b, c * 4 + d) for (a, b), (c, d) in pair]
+    near = (swap(far, "col", 4, 2), swap(own, "dp", sz.dp, 1), lax.ppermute(far, ("dp", "col"), pair))
+    near = [item.astype(F32) for item in (own, *near)]
+    grad = lax.reduce_precision((near[0] + near[1]) + (near[2] + near[3]), 8, 7)
+    bit = 2
     while bit < sz.dp:
         grad = merged(grad, swap(grad.astype(BF), "dp", sz.dp, bit))
         bit *= 2
     outs = lamb(sz, grad, params, firsts, seconds)
     moments, squares, updates = outs[:5], outs[5:10], outs[10:15]
     sums, totals = outs[15], outs[16]
-    pair = sums + swap(sums, "col", 4, 1)
-    fresh = take_step(pair, swap(pair, "col", 4, 2), params, updates)
+    fresh = take_step([sums] + [swap(sums, "col", 4, r) for r in (1, 2, 3)], params, updates)
     return (*back(*fresh[:5]), *back(*moments), *back(*squares), fresh[5], totals[0, 0], totals[0, 1])
 
 

time: 86.2 us -> 77.8 us (0.903)
  Pallas kernels: 41.3 us -> 34.6 us
  local copies, waits for them, and re-layouts: 3.27 us -> 0.71 us
  waiting for transfers between devices: 18.2 us -> 19.1 us
    pallas_call x8 -> x7, Pallas kernels: 41.3 us -> 34.6 us  [call(): pl.pallas_call(kernel, in_specs=[free if i in loose else far if i in far_...]
    ppermute x0 -> x1, waiting for transfers between devices: none -> 3.4 us  [shards(): lax.ppermute(far, ('dp', 'col'), pair)]
    ppermute x14 -> x15, waiting for transfers between devices: 18.2 us -> 15.6 us  [swap(): return lax.ppermute(value, axis, [(i, i ^ bit) for i in range(count)])]
    ppermute x0 -> x1, starting transfers between devices: none -> 2.42 us  [shards(): lax.ppermute(far, ('dp', 'col'), pair)]
    ppermute x14 -> x15, starting transfers between devices: 15.3 us -> 13 us  [swap(): return lax.ppermute(value, axis, [(i, i ^ bit) for i in range(count)])]
    unnamed x64 -> x44, local copies, waits for them, and re-layouts: 1.74 us -> 0.13 us
    another operation x3 -> x0, local copies, waits for them, and re-layouts: 0.88 us -> none  [shards(): jnp.stack([serve_rows.reshape(-1), take_seed.reshape(-1), alive.astype(jn...]
  transfers between devices with their start and end apart: 15 -> 17, of which waited for: 7 -> 9; matrix products, arithmetic and copies ran while one was open for 2% -> 1% of each run, Pallas kernels for 36% -> 32%
where the time goes in v3:
time: 77.8 us; the launch traced here: 77.5 us
  Pallas kernels  34.6 us (44%)
  starting transfers between devices  21.6 us (28%)
  waiting for transfers between devices  19.1 us (25%)
  between operations  1.08 us (1%)
    pallas_call x7, Pallas kernels, call(): pl.pallas_call(kernel, in_specs=[free if i in loose else far if i in far_...  34.6 us
    ppermute x15, waiting for transfers between devices, swap(): return lax.ppermute(value, axis, [(i, i ^ bit) for i in range(count)])  15.6 us
    ppermute x15, starting transfers between devices, swap(): return lax.ppermute(value, axis, [(i, i ^ bit) for i in range(count)])  13 us
    all_to_all x1, starting transfers between devices, shards(): lax.all_to_all(rows, ('dp', 'col'), split_axis=0, concat_axis=0, tiled=True)  6.26 us
    ppermute x1, waiting for transfers between devices, shards(): lax.ppermute(far, ('dp', 'col'), pair)  3.4 us
    ppermute x1, starting transfers between devices, shards(): lax.ppermute(far, ('dp', 'col'), pair)  2.42 us
  transfers between devices with their start and end apart: 17, of which 9 were waited for; matrix products, arithmetic and copies ran while one was open for 1% of the time, Pallas kernels for 32%

profile of v3, /device:TPU:0, one launch (start us, length us, event | category | flops | bytes accessed | tf_op | source)
XLA Modules:
  0.0 77.5 jit_solution(15357699072679405356)
XLA Ops:
  0.7 3.7 %shard_map.394 = (bf16[64,896]{1,0:T(8,128)(2,1)}, f32[456,128]{1,0:T(8,128)}, bf16[24,2176]{1,0:T(8,128)(2,1)}, f32[24,128]{1,0:T(8,128)}, bf16[24,5120]{1,0:T(...) custom-call(bf16[25,32768]{1,0:T(8,128)(2,1)} %feat_ref.1, s32[5,8192]{1,0:T(8,128)} %nbr_ref.1, ...), custom_call_target="tpu_custom_call" | custom-call | flops 4000000000 | bytes 1 | tf_op jit(solution)/shard_map/pallas_call | solution.py:45
  4.5 0.5 collective-permute-start
  5.0 2.6 %collective-permute-start.1 = (bf16[24,5120]{1,0:T(8,128)(2,1)S(1)}, bf16[24,5120]{1,0:T(8,128)(2,1)S(1)}, u32[]{:S(2)}, u32[]{:S(2)}) collective-permute-start(bf16[24,5120]{1,0:T(8,128)(2,1)S(1)} %get-tuple-element.76), channel_id=1, source_target_pairs={{0,2},{1,3},{2,0},{3,1},{4,6},{5,7},{6,4},{7,5},{8,10},{9,11},{10,... | collective-permute-start | bytes 737288 | tf_op jit(solution)/shard_map/ppermute | solution.py:1178
  7.7 6.8 %shard_map.395 = (bf16[64,2816]{1,0:T(8,128)(2,1)}, bf16[5488,128]{1,0:T(8,128)(2,1)}, bf16[24,5120]{1,0:T(8,128)(2,1)S(1)}, bf16[24,5120]{1,0:T(8,128)(2,1)S(1)}, bf16[24,5120]{1,0:T(8,128)(2,1)S(1)}) custom-call(bf16[25,32768]{1,0:T(8,128)(2,1)S(1)} %copy-done, s32[5,8192]{1,0:T(8,128)S(1)} %copy-done.1, s32[5,8192]{1,0:T(8,128)S(1)} %copy-done.2, ...), custom_call_target="tpu_custom_call" | custom-call | flops 6000000000 | bytes 1 | tf_op jit(solution)/shard_map/pallas_call | solution.py:45
  14.5 2.1 %collective-permute-done.2.s3.e3 = bf16[24,2688]{1,0:T(8,128)(2,1)S(1)} collective-permute-done((bf16[24,2688]{1,0:T(8,128)(2,1)S(1)}, bf16[24,2688]{1,0:T(8,128)(2,1)S(1)}, u32[]{:S(2)}, u32[]{:S(2)}) %collective-permute-start.2) | collective-permute-done | bytes 129056 | tf_op jit(solution)/shard_map/ppermute | solution.py:1178
  16.6 0.1 collective-permute-start.3
  16.7 0.4 collective-permute-start.4
  17.1 1.6 %collective-permute-start.5 = (bf16[24,5120]{1,0:T(8,128)(2,1)S(1)}, bf16[24,5120]{1,0:T(8,128)(2,1)S(1)}, u32[]{:S(2)}, u32[]{:S(2)}) collective-permute-start(bf16[24,5120]{1,0:T(8,128)(2,1)S(1)} %get-tuple-element.88), channel_id=1, source_target_pairs={{0,2},{1,3},{2,0},{3,1},{4,6},{5,7},{6,4},{7,5},{8,10},{9,11},{10,... | collective-permute-start | bytes 737288 | tf_op jit(solution)/shard_map/ppermute | solution.py:1178
  18.7 5.1 %shard_map.396 = (bf16[256,4224]{1,0:T(8,128)(2,1)}, f32[264,1280]{1,0:T(8,128)}, bf16[784,128]{1,0:T(8,128)(2,1)}, bf16[256,768]{1,0:T(8,128)(2,1)}) custom-call(bf16[64,896]{1,0:T(8,128)(2,1)} %get-tuple-element.67.own_b, f32[456,128]{1,0:T(8,128)} %get-tuple-element.68.packed, bf16[24,5120]{1,0:T(8,128)(2,1)S(1)} %collective-permute-done.s1.e1, ...), custom_call_target="tpu_custom_call" | custom-call | flops 4000000000 | bytes 1 | tf_op jit(solution)/shard_map/pallas_call | solution.py:45
  23.8 6.3 %all-to-all-start = ((bf16[32,8,768]{2,1,0:T(8,128)(2,1)}), bf16[32,8,768]{2,1,0:T(8,128)(2,1)S(1)}, u32[]{:S(2)}, u32[]{:S(2)}) async-start(bf16[32,8,768]{2,1,0:T(8,128)(2,1)} %bitcast.3), calls=%async_computation | async-start | bytes 786432 | tf_op jit(solution)/shard_map/all_to_all | solution.py:1216
  30.1 12.8 %shard_map.397.part_in = f32[264,2176]{1,0:T(8,128)} custom-call(bf16[256,4224]{1,0:T(8,128)(2,1)} %get-tuple-element.82.low_in, f32[264,1280]{1,0:T(8,128)} %get-tuple-element.83.high_in, bf16[5488,128]{1,0:T(8,128)(2,1)} %get-tuple-element.85.counts_in, bf16[64,2816]{1,0:T(8,128)(2,1)} %get-tuple-element.86.own_a, ...), custom_call_target="tpu_custom_call" | custom-call | flops 14000000000 | bytes 1 | tf_op jit(solution)/shard_map/pallas_call | solution.py:45
  42.9 0.2 all-to-all-done
  43.1 3.8 %shard_map.398 = (bf16[448,128]{1,0:T(8,128)(2,1)S(1)}, bf16[448,128]{1,0:T(8,128)(2,1)S(1)}, bf16[896,128]{1,0:T(8,128)(2,1)S(1)}) custom-call(s32[8,8]{1,0:T(8,128)} %serve_in.3, s32[8,8]{1,0:T(8,128)} %take_in.3, s32[1,8]{1,0:T(1,128)} %bitcast.44, bf16[256,768]{1,0:T(8,128)(2,1)S(1)} %bitcast.25, bf16[256,4224]{1,0:T(8,128)(2,1)} %get-tuple-element.82.low_in, ...), custom_call_target="tpu_custom_call" | custom-call | flops 3000000000 | bytes 1 | tf_op jit(solution)/shard_map/pallas_call | solution.py:45
  47.2 1.5 %collective-permute-done.7 = bf16[896,128]{1,0:T(8,128)(2,1)S(1)} collective-permute-done((bf16[896,128]{1,0:T(8,128)(2,1)S(1)}, bf16[896,128]{1,0:T(8,128)(2,1)S(1)}, u32[]{:S(2)}, u32[]{:S(2)}) %collective-permute-start.7) | collective-permute-done | bytes 229408 | tf_op jit(solution)/shard_map/ppermute | solution.py:1178
  48.7 2.4 %collective-permute-start.10 = (bf16[448,128]{1,0:T(8,128)(2,1)S(1)}, bf16[448,128]{1,0:T(8,128)(2,1)S(1)}, u32[]{:S(2)}, u32[]{:S(2)}) collective-permute-start(bf16[448,128]{1,0:T(8,128)(2,1)S(1)} %get-tuple-element.117), channel_id=1, source_target_pairs={{0,6},{1,7},{2,4},{3,5},{4,2},{5,3},{6,0},{7,1},{8,14},{9,15},{10,... | collective-permute-start | bytes 344072 | tf_op jit(solution)/shard_map/ppermute | solution.py:1224
  51.1 0.6 collective-permute-start.9
  51.7 0.6 collective-permute-start.8
  52.3 3.4 %collective-permute-done.10 = bf16[448,128]{1,0:T(8,128)(2,1)S(1)} collective-permute-done((bf16[448,128]{1,0:T(8,128)(2,1)S(1)}, bf16[448,128]{1,0:T(8,128)(2,1)S(1)}, u32[]{:S(2)}, u32[]{:S(2)}) %collective-permute-start.10) | collective-permute-done | bytes 114720 | tf_op jit(solution)/shard_map/ppermute | solution.py:1224
  55.7 1.7 %collective-permute-done.9 = bf16[448,128]{1,0:T(8,128)(2,1)S(1)} collective-permute-done((bf16[448,128]{1,0:T(8,128)(2,1)S(1)}, bf16[448,128]{1,0:T(8,128)(2,1)S(1)}, u32[]{:S(2)}, u32[]{:S(2)}) %collective-permute-start.9) | collective-permute-done | bytes 114720 | tf_op jit(solution)/shard_map/ppermute | solution.py:1178
  57.5 1.6 %collective-permute-start.11 = (bf16[448,128]{1,0:T(8,128)(2,1)S(1)}, bf16[448,128]{1,0:T(8,128)(2,1)S(1)}, u32[]{:S(2)}, u32[]{:S(2)}) collective-permute-start(bf16[448,128]{1,0:T(8,128)(2,1)S(1)} %fusion.1), channel_id=1, source_target_pairs={{0,8},{4,12},{8,0},{12,4},{16,24},{20,28},{24,16},{28,20},{1,9},{5... | collective-permute-start | bytes 344072 | tf_op jit(solution)/shard_map/ppermute | solution.py:1178
  59.1 3.2 %collective-permute-done.11 = bf16[448,128]{1,0:T(8,128)(2,1)S(1)} collective-permute-done((bf16[448,128]{1,0:T(8,128)(2,1)S(1)}, bf16[448,128]{1,0:T(8,128)(2,1)S(1)}, u32[]{:S(2)}, u32[]{:S(2)}) %collective-permute-start.11) | collective-permute-done | bytes 114720 | tf_op jit(solution)/shard_map/ppermute | solution.py:1178
  62.4 0.1 fusion
  62.5 2.7 %collective-permute-start.12 = (bf16[448,128]{1,0:T(8,128)(2,1)S(1)}, bf16[448,128]{1,0:T(8,128)(2,1)S(1)}, u32[]{:S(2)}, u32[]{:S(2)}) collective-permute-start(bf16[448,128]{1,0:T(8,128)(2,1)S(1)} %fusion), channel_id=1, source_target_pairs={{0,16},{4,20},{8,24},{12,28},{16,0},{20,4},{24,8},{28,12},{1,17},{... | collective-permute-start | bytes 344072 | tf_op jit(solution)/shard_map/ppermute | solution.py:1178
  65.1 4.7 %collective-permute-done.12 = bf16[448,128]{1,0:T(8,128)(2,1)S(1)} collective-permute-done((bf16[448,128]{1,0:T(8,128)(2,1)S(1)}, bf16[448,128]{1,0:T(8,128)(2,1)S(1)}, u32[]{:S(2)}, u32[]{:S(2)}) %collective-permute-start.12) | collective-permute-done | bytes 114720 | tf_op jit(solution)/shard_map/ppermute | solution.py:1178
  69.8 0.1 add_reduce-precision_fusion.grad
  70.1 1.5 %shard_map.399 = (f32[25,2,256]{2,1,0:T(2,128)}, f32[2,64,256]{2,1,0:T(8,128)}, f32[47,2,64]{2,1,0:T(2,128)}, f32[2,64]{1,0:T(2,128)}, f32[1,47]{1,0:T(1,128)}, ...) custom-call(f32[448,128]{1,0:T(8,128)S(1)} %add_reduce-precision_fus, ...), custom_call_target="tpu_custom_call" | custom-call | flops 1000000000 | bytes 1 | tf_op jit(solution)/shard_map/pallas_call | solution.py:45
  71.5 2.1 %collective-permute-start.14 = (f32[8,128]{1,0:T(8,128)S(1)}, f32[8,128]{1,0:T(8,128)S(1)}, u32[]{:S(2)}, u32[]{:S(2)}) collective-permute-start(f32[8,128]{1,0:T(8,128)S(1)} %get-tuple-element.93.own), channel_id=1, source_target_pairs={{0,2},{1,3},{2,0},{3,1},{4,6},{5,7},{6,4},{7,5},{8,10},{9,11},{10,... | collective-permute-start | bytes 12296 | tf_op jit(solution)/shard_map/ppermute | solution.py:1178
  73.6 0.1 collective-permute-start.15
  73.7 0.6 fusion.2
  74.3 0.9 %collective-permute-done.14.far = f32[8,128]{1,0:T(8,128)S(1)} collective-permute-done((f32[8,128]{1,0:T(8,128)S(1)}, f32[8,128]{1,0:T(8,128)S(1)}, u32[]{:S(2)}, u32[]{:S(2)}) %collective-permute-start.14) | collective-permute-done | bytes 4128 | tf_op jit(solution)/shard_map/ppermute | solution.py:1178
  75.2 1.4 %collective-permute-done.15.across = f32[8,128]{1,0:T(8,128)S(1)} collective-permute-done((f32[8,128]{1,0:T(8,128)S(1)}, f32[8,128]{1,0:T(8,128)S(1)}, u32[]{:S(2)}, u32[]{:S(2)}) %collective-permute-start.15) | collective-permute-done | bytes 4128 | tf_op jit(solution)/shard_map/ppermute | solution.py:1178
  76.7 0.8 %shard_map.400 = (f32[25,2,256]{2,1,0:T(2,128)}, f32[2,64,256]{2,1,0:T(8,128)}, f32[47,2,64]{2,1,0:T(2,128)}, f32[2,64]{1,0:T(2,128)}, f32[1,47]{1,0:T(1,128)}, /*index=5*/f32[2,5]{1,0:T(2,128)}) custom-call(f32[8,128]{1,0:T(8,128)S(1)} %get-tuple-element.93.own, f32[8,128]{1,0:T(8,128)S(1)} %collective-permute-done.13.core, ...), custom_call_target="tpu_custom_call" | custom-call | flops 1000000000 | bytes 1 | tf_op jit(solution)/shard_map/pallas_call | solution.py:45
  (58 shorter events, 0.4 us)
Async XLA Ops:
  4.5 12.3 %collective-permute-start = (bf16[24,5120]{1,0:T(8,128)(2,1)S(1)}, bf16[24,5120]{1,0:T(8,128)(2,1)S(1)}, u32[]{:S(2)}, u32[]{:S(2)}) collective-permute-start(bf16[24,5120]{1,0:T(8,128)(2,1)S(1)} %get-tuple-element.69), channel_id=1, source_target_pairs={{0,1},{1,0},{2,3},{3,2},{4,5},{5,4},{6,7},{7,6},{8,9},{9,8},{10,11... | collective-permute-start | bytes 737288 | tf_op jit(solution)/shard_map/ppermute | solution.py:1178
  5.0 11.6 %collective-permute-start.1 = (bf16[24,5120]{1,0:T(8,128)(2,1)S(1)}, bf16[24,5120]{1,0:T(8,128)(2,1)S(1)}, u32[]{:S(2)}, u32[]{:S(2)}) collective-permute-start(bf16[24,5120]{1,0:T(8,128)(2,1)S(1)} %get-tuple-element.76), channel_id=1, source_target_pairs={{0,2},{1,3},{2,0},{3,1},{4,6},{5,7},{6,4},{7,5},{8,10},{9,11},{10,... | collective-permute-start | bytes 737288 | tf_op jit(solution)/shard_map/ppermute | solution.py:1178
  7.6 9.0 %collective-permute-start.2 = (bf16[24,2688]{1,0:T(8,128)(2,1)S(1)}, bf16[24,2688]{1,0:T(8,128)(2,1)S(1)}, u32[]{:S(2)}, u32[]{:S(2)}) collective-permute-start(bf16[24,2688]{1,0:T(8,128)(2,1)S(1)} %get-tuple-element.77), channel_id=1, source_target_pairs={{0,3},{1,2},{2,1},{3,0},{4,7},{5,6},{6,5},{7,4},{8,11},{9,10},{10,... | collective-permute-start | bytes 387080 | tf_op jit(solution)/shard_map/ppermute | solution.py:1178
  16.6 2.1 %collective-permute-start.3 = (bf16[24,5120]{1,0:T(8,128)(2,1)S(1)}, bf16[24,5120]{1,0:T(8,128)(2,1)S(1)}, u32[]{:S(2)}, u32[]{:S(2)}) collective-permute-start(bf16[24,5120]{1,0:T(8,128)(2,1)S(1)} %collective-permute-done.1.s2.e2), channel_id=1, source_target_pairs={{0,1},{1,0},{2,3},{3,2},{4,5},{5,4},{6,7},{7,6},{8,9},{9,8},{10,11... | collective-permute-start | bytes 737288 | tf_op jit(solution)/shard_map/ppermute | solution.py:1178
  16.7 13.3 %collective-permute-start.4 = (bf16[24,5120]{1,0:T(8,128)(2,1)S(1)}, bf16[24,5120]{1,0:T(8,128)(2,1)S(1)}, u32[]{:S(2)}, u32[]{:S(2)}) collective-permute-start(bf16[24,5120]{1,0:T(8,128)(2,1)S(1)} %get-tuple-element.87), channel_id=1, source_target_pairs={{0,1},{1,0},{2,3},{3,2},{4,5},{5,4},{6,7},{7,6},{8,9},{9,8},{10,11... | collective-permute-start | bytes 737288 | tf_op jit(solution)/shard_map/ppermute | solution.py:1178
  17.1 13.0 %collective-permute-start.5 = (bf16[24,5120]{1,0:T(8,128)(2,1)S(1)}, bf16[24,5120]{1,0:T(8,128)(2,1)S(1)}, u32[]{:S(2)}, u32[]{:S(2)}) collective-permute-start(bf16[24,5120]{1,0:T(8,128)(2,1)S(1)} %get-tuple-element.88), channel_id=1, source_target_pairs={{0,2},{1,3},{2,0},{3,1},{4,6},{5,7},{6,4},{7,5},{8,10},{9,11},{10,... | collective-permute-start | bytes 737288 | tf_op jit(solution)/shard_map/ppermute | solution.py:1178
  18.7 11.4 %collective-permute-start.6 = (bf16[24,5120]{1,0:T(8,128)(2,1)S(1)}, bf16[24,5120]{1,0:T(8,128)(2,1)S(1)}, u32[]{:S(2)}, u32[]{:S(2)}) collective-permute-start(bf16[24,5120]{1,0:T(8,128)(2,1)S(1)} %get-tuple-element.89), channel_id=1, source_target_pairs={{0,3},{1,2},{2,1},{3,0},{4,7},{5,6},{6,5},{7,4},{8,11},{9,10},{10,... | collective-permute-start | bytes 737288 | tf_op jit(solution)/shard_map/ppermute | solution.py:1178
  23.8 19.3 %all-to-all-start = ((bf16[32,8,768]{2,1,0:T(8,128)(2,1)}), bf16[32,8,768]{2,1,0:T(8,128)(2,1)S(1)}, u32[]{:S(2)}, u32[]{:S(2)}) async-start(bf16[32,8,768]{2,1,0:T(8,128)(2,1)} %bitcast.3), calls=%async_computation | async-start | bytes 786432 | tf_op jit(solution)/shard_map/all_to_all | solution.py:1216
  46.9 23.0 %copy-start.5 = (f32[2,64,256]{2,1,0:T(8,128)S(1)}, f32[2,64,256]{2,1,0:T(8,128)}, u32[]{:S(2)}) copy-start(f32[2,64,256]{2,1,0:T(8,128)} %f2.1) | copy-start | bytes 393220
  46.9 23.0 %copy-start.6 = (f32[2,64,256]{2,1,0:T(8,128)S(1)}, f32[2,64,256]{2,1,0:T(8,128)}, u32[]{:S(2)}) copy-start(f32[2,64,256]{2,1,0:T(8,128)} %s2_.1) | copy-start | bytes 393220
  47.0 23.0 %copy-start.7 = (f32[2,64,256]{2,1,0:T(8,128)S(1)}, f32[2,64,256]{2,1,0:T(8,128)}, u32[]{:S(2)}) copy-start(f32[2,64,256]{2,1,0:T(8,128)} %w2.3) | copy-start | bytes 393220
  47.0 23.0 %copy-start.8 = (f32[2,25,256]{2,0,1:T(2,128)S(1)}, f32[2,25,256]{2,0,1:T(2,128)}, u32[]{:S(2)}) copy-start(f32[2,25,256]{2,0,1:T(2,128)} %param.44) | copy-start | bytes 153604
  47.0 23.0 %copy-start.9 = (f32[2,25,256]{2,0,1:T(2,128)S(1)}, f32[2,25,256]{2,0,1:T(2,128)}, u32[]{:S(2)}) copy-start(f32[2,25,256]{2,0,1:T(2,128)} %param.49) | copy-start | bytes 153604
  47.0 23.0 %copy-start.10 = (f32[2,25,256]{2,0,1:T(2,128)S(1)}, f32[2,25,256]{2,0,1:T(2,128)}, u32[]{:S(2)}) copy-start(f32[2,25,256]{2,0,1:T(2,128)} %param.39) | copy-start | bytes 153604
  47.0 23.0 %copy-start.11 = (f32[2,64,47]{1,0,2:T(2,128)S(1)}, f32[2,64,47]{1,0,2:T(2,128)}, u32[]{:S(2)}) copy-start(f32[2,64,47]{1,0,2:T(2,128)} %param.46) | copy-start | bytes 72196
  47.0 23.0 %copy-start.12 = (f32[2,64,47]{1,0,2:T(2,128)S(1)}, f32[2,64,47]{1,0,2:T(2,128)}, u32[]{:S(2)}) copy-start(f32[2,64,47]{1,0,2:T(2,128)} %param.51) | copy-start | bytes 72196
  47.0 23.0 %copy-start.13 = (f32[2,64,47]{1,0,2:T(2,128)S(1)}, f32[2,64,47]{1,0,2:T(2,128)}, u32[]{:S(2)}) copy-start(f32[2,64,47]{1,0,2:T(2,128)} %param.41) | copy-start | bytes 72196
  47.0 23.0 %copy-start.16 = (f32[2,64]{1,0:T(2,128)S(1)}, f32[2,64]{1,0:T(2,128)}, u32[]{:S(2)}) copy-start(f32[2,64]{1,0:T(2,128)} %fh.1) | copy-start | bytes 1540
  47.0 23.0 %copy-start.17 = (f32[2,64]{1,0:T(2,128)S(1)}, f32[2,64]{1,0:T(2,128)}, u32[]{:S(2)}) copy-start(f32[2,64]{1,0:T(2,128)} %sh.1) | copy-start | bytes 1540
  47.1 23.0 %copy-start.18 = (f32[2,64]{1,0:T(2,128)S(1)}, f32[2,64]{1,0:T(2,128)}, u32[]{:S(2)}) copy-start(f32[2,64]{1,0:T(2,128)} %wh.3) | copy-start | bytes 1540
  47.1 23.0 %copy-start.19 = (f32[47]{0:T(128)S(1)}, f32[47]{0:T(128)}, u32[]{:S(2)}) copy-start(f32[47]{0:T(128)} %param.48) | copy-start | bytes 568
  47.1 23.0 %copy-start.20 = (f32[47]{0:T(128)S(1)}, f32[47]{0:T(128)}, u32[]{:S(2)}) copy-start(f32[47]{0:T(128)} %param.53) | copy-start | bytes 568
  47.1 23.0 %copy-start.21 = (f32[47]{0:T(128)S(1)}, f32[47]{0:T(128)}, u32[]{:S(2)}) copy-start(f32[47]{0:T(128)} %param.43) | copy-start | bytes 568
  47.1 1.6 %collective-permute-start.7 = (bf16[896,128]{1,0:T(8,128)(2,1)S(1)}, bf16[896,128]{1,0:T(8,128)(2,1)S(1)}, u32[]{:S(2)}, u32[]{:S(2)}) collective-permute-start(bf16[896,128]{1,0:T(8,128)(2,1)S(1)} %get-tuple-element.91), channel_id=1, source_target_pairs={{0,1},{1,0},{2,3},{3,2},{4,5},{5,4},{6,7},{7,6},{8,9},{9,8},{10,11... | collective-permute-start | bytes 688136 | tf_op jit(solution)/shard_map/ppermute | solution.py:1178
  48.7 7.0 %collective-permute-start.10 = (bf16[448,128]{1,0:T(8,128)(2,1)S(1)}, bf16[448,128]{1,0:T(8,128)(2,1)S(1)}, u32[]{:S(2)}, u32[]{:S(2)}) collective-permute-start(bf16[448,128]{1,0:T(8,128)(2,1)S(1)} %get-tuple-element.117), channel_id=1, source_target_pairs={{0,6},{1,7},{2,4},{3,5},{4,2},{5,3},{6,0},{7,1},{8,14},{9,15},{10,... | collective-permute-start | bytes 344072 | tf_op jit(solution)/shard_map/ppermute | solution.py:1224
  51.1 6.3 %collective-permute-start.9 = (bf16[448,128]{1,0:T(8,128)(2,1)S(1)}, bf16[448,128]{1,0:T(8,128)(2,1)S(1)}, u32[]{:S(2)}, u32[]{:S(2)}) collective-permute-start(bf16[448,128]{1,0:T(8,128)(2,1)S(1)} %get-tuple-element.116), channel_id=1, source_target_pairs={{0,4},{4,0},{8,12},{12,8},{16,20},{20,16},{24,28},{28,24},{1,5},{5... | collective-permute-start | bytes 344072 | tf_op jit(solution)/shard_map/ppermute | solution.py:1178
  51.7 5.7 %collective-permute-start.8 = (bf16[448,128]{1,0:T(8,128)(2,1)S(1)}, bf16[448,128]{1,0:T(8,128)(2,1)S(1)}, u32[]{:S(2)}, u32[]{:S(2)}) collective-permute-start(bf16[448,128]{1,0:T(8,128)(2,1)S(1)} %get-tuple-element.117), channel_id=1, source_target_pairs={{0,2},{1,3},{2,0},{3,1},{4,6},{5,7},{6,4},{7,5},{8,10},{9,11},{10,... | collective-permute-start | bytes 344072 | tf_op jit(solution)/shard_map/ppermute | solution.py:1178
  57.5 4.9 %collective-permute-start.11 = (bf16[448,128]{1,0:T(8,128)(2,1)S(1)}, bf16[448,128]{1,0:T(8,128)(2,1)S(1)}, u32[]{:S(2)}, u32[]{:S(2)}) collective-permute-start(bf16[448,128]{1,0:T(8,128)(2,1)S(1)} %fusion.1), channel_id=1, source_target_pairs={{0,8},{4,12},{8,0},{12,4},{16,24},{20,28},{24,16},{28,20},{1,9},{5... | collective-permute-start | bytes 344072 | tf_op jit(solution)/shard_map/ppermute | solution.py:1178
  62.5 7.3 %collective-permute-start.12 = (bf16[448,128]{1,0:T(8,128)(2,1)S(1)}, bf16[448,128]{1,0:T(8,128)(2,1)S(1)}, u32[]{:S(2)}, u32[]{:S(2)}) collective-permute-start(bf16[448,128]{1,0:T(8,128)(2,1)S(1)} %fusion), channel_id=1, source_target_pairs={{0,16},{4,20},{8,24},{12,28},{16,0},{20,4},{24,8},{28,12},{1,17},{... | collective-permute-start | bytes 344072 | tf_op jit(solution)/shard_map/ppermute | solution.py:1178
  71.5 2.8 %collective-permute-start.13 = (f32[8,128]{1,0:T(8,128)S(1)}, f32[8,128]{1,0:T(8,128)S(1)}, u32[]{:S(2)}, u32[]{:S(2)}) collective-permute-start(f32[8,128]{1,0:T(8,128)S(1)} %get-tuple-element.93.own), channel_id=1, source_target_pairs={{0,1},{1,0},{2,3},{3,2},{4,5},{5,4},{6,7},{7,6},{8,9},{9,8},{10,11... | collective-permute-start | bytes 12296 | tf_op jit(solution)/shard_map/ppermute | solution.py:1178
  71.5 3.7 %collective-permute-start.14 = (f32[8,128]{1,0:T(8,128)S(1)}, f32[8,128]{1,0:T(8,128)S(1)}, u32[]{:S(2)}, u32[]{:S(2)}) collective-permute-start(f32[8,128]{1,0:T(8,128)S(1)} %get-tuple-element.93.own), channel_id=1, source_target_pairs={{0,2},{1,3},{2,0},{3,1},{4,6},{5,7},{6,4},{7,5},{8,10},{9,11},{10,... | collective-permute-start | bytes 12296 | tf_op jit(solution)/shard_map/ppermute | solution.py:1178
  73.6 3.0 %collective-permute-start.15 = (f32[8,128]{1,0:T(8,128)S(1)}, f32[8,128]{1,0:T(8,128)S(1)}, u32[]{:S(2)}, u32[]{:S(2)}) collective-permute-start(f32[8,128]{1,0:T(8,128)S(1)} %get-tuple-element.93.own), channel_id=1, source_target_pairs={{0,3},{1,2},{2,1},{3,0},{4,7},{5,6},{6,5},{7,4},{8,11},{9,10},{10,... | collective-permute-start | bytes 12296 | tf_op jit(solution)/shard_map/ppermute | solution.py:1178
  (7 other events, 48.8 us)

commit v4 on v3

--- a/solution.py
+++ b/solution.py
@@ -536,9 +536,7 @@
 
 
 def spread(sz, scaled, counts):
-    high, low = two_parts(scaled)
-    total = dot(jnp.concatenate([high, low], 0), counts, (1, 1))
-    return total[: sz.hid] + total[sz.hid :]
+    return dot(scaled.astype(BF), counts, (1, 1))
 
 
 def halves(ref, at, lanes):
@@ -687,13 +685,15 @@
     tail = (piece(at["embed"], sz.low_lanes - at["embed"]), (high.at[rows, last], high_out.at[rows, last]))
     stores += start_copies(tail, sems, 16)
     serve, take, _, owned = seed_picks(sz, serve_rows[...], take_rows[...], part)
-    value = sent_rows(sz, low, at["embed"], serve, take)
+    embed_high = low[:, at["embed"] : at["embed"] + own]
+    served = dot(serve.astype(BF), embed_high, (1, 1))
+    taken = dot(take.astype(BF), embed_high, (1, 1))
     dead = (owned > 0.5) & (alive_column(sz, live_rows[...]) < 0.5)
-    lane_at = lax.broadcasted_iota(jnp.int32, (sz.slots, 3 * hid), 1)
-    value = jnp.where((lane_at == hid) & dead, SENTINEL, value)
-    value = value.reshape(sz.dp, 1, sz.slot, 3 * hid)
-    value = jnp.broadcast_to(value, (sz.dp, 4, sz.slot, 3 * hid))
-    sent[...] = value.reshape(4 * sz.slots, 3 * hid).astype(BF)
+    first = lax.broadcasted_iota(jnp.int32, (sz.slots, hid), 1) == 0
+    value = jnp.concatenate([served, jnp.where(first & dead, SENTINEL, taken)], 1)
+    value = value.reshape(sz.dp, 1, sz.slot, 2 * hid)
+    value = jnp.broadcast_to(value, (sz.dp, 4, sz.slot, 2 * hid))
+    sent[...] = value.reshape(4 * sz.slots, 2 * hid).astype(BF)
     wait_all(stores)
 
 
@@ -715,7 +715,7 @@
             ((hid, sz.low_lanes), BF),
             ((hid + 8, sz.high_lanes), F32),
             ((sz.count_rows * (sz.own // LANES), LANES), BF),
-            ((4 * sz.slots, 3 * hid), BF),
+            ((4 * sz.slots, 2 * hid), BF),
         ],
         [
             ((2 * sz.hold, sz.n_mid), BF),
@@ -971,15 +971,14 @@
         ),
         sems,
     )
-    arrived = received[...].astype(F32).reshape(sz.dp, 4, sz.slot, 3 * hid)
-    arrived = jnp.sum(arrived, 1).reshape(sz.slots, 3 * hid)
+    arrived = received[...].astype(F32).reshape(sz.dp, 4, sz.slot, 2 * hid)
+    arrived = jnp.sum(arrived, 1).reshape(sz.slots, 2 * hid)
     at["embed"] = 0
     wait_all(copies[:4])
     serve, take, served, taken = seed_picks(sz, serve_rows[...], take_rows[...], part)
     mine = sent_rows(sz, low, 0, serve, take)
-    theirs = arrived[:, hid : 2 * hid]
+    theirs = arrived[:, hid:]
     alive_there = theirs[:, 0:1] < 0.5 * SENTINEL
-    theirs = theirs + arrived[:, 2 * hid :]
     differ = mine[:, hid : 2 * hid] + mine[:, 2 * hid :] - arrived[:, :hid]
     differ = jnp.where((taken > 0.5) & (alive_column(sz, live_rows[...]) > 0.5), differ, 0.0)
     dist_total = DIST_WEIGHT * jnp.sum(jnp.sum(differ * differ, 0, keepdims=True), 1, keepdims=True)
@@ -1152,8 +1151,8 @@
     )
 
 
-def step_kernel(own, core, far, across, w1, w2, w3, wh, wb, u1, u2, u3, uh, ub, n1, n2, n3, nh, nb, norms_ref):
-    norms = jnp.sqrt((own[...] + core[...]) + (far[...] + across[...]))
+def step_kernel(own, far, w1, w2, w3, wh, wb, u1, u2, u3, uh, ub, n1, n2, n3, nh, nb, norms_ref):
+    norms = jnp.sqrt(own[...] + far[...])
     norms_ref[...] = norms[0:2, 0:5]
     for i, (w, u, n) in enumerate(
         ((w1, u1, n1), (w2, u2, n2), (w3, u3, n3), (wh, uh, nh), (wb, ub, nb))
@@ -1231,7 +1230,8 @@
     outs = lamb(sz, grad, params, firsts, seconds)
     moments, squares, updates = outs[:5], outs[5:10], outs[10:15]
     sums, totals = outs[15], outs[16]
-    fresh = take_step([sums] + [swap(sums, "col", 4, r) for r in (1, 2, 3)], params, updates)
+    pair = sums + swap(sums, "col", 4, 1)
+    fresh = take_step([pair, swap(pair, "col", 4, 2)], params, updates)
     return (*back(*fresh[:5]), *back(*moments), *back(*squares), fresh[5], totals[0, 0], totals[0, 1])
 
 

time: 77.8 us -> 76.7 us (0.986)
  Pallas kernels: 34.6 us -> 33.6 us
    pallas_call x7, Pallas kernels: 34.6 us -> 33.6 us  [call(): pl.pallas_call(kernel, in_specs=[free if i in loose else far if i in far_...]
    ppermute x15 -> x14, starting transfers between devices: 13 us -> 12.8 us  [swap(): return lax.ppermute(value, axis, [(i, i ^ bit) for i in range(count)])]
    ppermute x15 -> x14, waiting for transfers between devices: 15.6 us -> 15.5 us  [swap(): return lax.ppermute(value, axis, [(i, i ^ bit) for i in range(count)])]
  transfers between devices with their start and end apart: 17 -> 16, of which waited for: 9 -> 8; matrix products, arithmetic and copies ran while one was open for 1% -> 1% of each run, Pallas kernels for 32% -> 31%
where the time goes in v4:
time: 76.7 us; the launch traced here: 76.4 us
  Pallas kernels  33.6 us (44%)
  starting transfers between devices  21.7 us (28%)
  waiting for transfers between devices  18.9 us (25%)
  between operations  1.08 us (1%)
    pallas_call x7, Pallas kernels, call(): pl.pallas_call(kernel, in_specs=[free if i in loose else far if i in far_...  33.6 us
    ppermute x14, waiting for transfers between devices, swap(): return lax.ppermute(value, axis, [(i, i ^ bit) for i in range(count)])  15.5 us
    ppermute x14, starting transfers between devices, swap(): return lax.ppermute(value, axis, [(i, i ^ bit) for i in range(count)])  12.8 us
    all_to_all x1, starting transfers between devices, shards(): lax.all_to_all(rows, ('dp', 'col'), split_axis=0, concat_axis=0, tiled=True)  6.26 us
    ppermute x1, waiting for transfers between devices, shards(): lax.ppermute(far, ('dp', 'col'), pair)  3.39 us
    ppermute x1, starting transfers between devices, shards(): lax.ppermute(far, ('dp', 'col'), pair)  2.62 us
  transfers between devices with their start and end apart: 16, of which 8 were waited for; matrix products, arithmetic and copies ran while one was open for 1% of the time, Pallas kernels for 31%

profile of v4, /device:TPU:0, one launch (start us, length us, event | category | flops | bytes accessed | tf_op | source)
XLA Modules:
  0.0 76.4 jit_solution(10220790612302606508)
XLA Ops:
  0.7 3.7 %shard_map.394 = (bf16[64,896]{1,0:T(8,128)(2,1)}, f32[456,128]{1,0:T(8,128)}, bf16[24,2176]{1,0:T(8,128)(2,1)}, f32[24,128]{1,0:T(8,128)}, bf16[24,5120]{1,0:T(...) custom-call(bf16[25,32768]{1,0:T(8,128)(2,1)} %feat_ref.1, s32[5,8192]{1,0:T(8,128)} %nbr_ref.1, ...), custom_call_target="tpu_custom_call" | custom-call | flops 4000000000 | bytes 1 | tf_op jit(solution)/shard_map/pallas_call | solution.py:45
  4.5 0.5 collective-permute-start
  5.0 2.6 %collective-permute-start.1 = (bf16[24,5120]{1,0:T(8,128)(2,1)S(1)}, bf16[24,5120]{1,0:T(8,128)(2,1)S(1)}, u32[]{:S(2)}, u32[]{:S(2)}) collective-permute-start(bf16[24,5120]{1,0:T(8,128)(2,1)S(1)} %get-tuple-element.76), channel_id=1, source_target_pairs={{0,2},{1,3},{2,0},{3,1},{4,6},{5,7},{6,4},{7,5},{8,10},{9,11},{10,... | collective-permute-start | bytes 737288 | tf_op jit(solution)/shard_map/ppermute | solution.py:1177
  7.6 0.1 collective-permute-start.2
  7.7 6.8 %shard_map.395 = (bf16[64,2816]{1,0:T(8,128)(2,1)}, bf16[5488,128]{1,0:T(8,128)(2,1)}, bf16[24,5120]{1,0:T(8,128)(2,1)S(1)}, bf16[24,5120]{1,0:T(8,128)(2,1)S(1)}, bf16[24,5120]{1,0:T(8,128)(2,1)S(1)}) custom-call(bf16[25,32768]{1,0:T(8,128)(2,1)S(1)} %copy-done, s32[5,8192]{1,0:T(8,128)S(1)} %copy-done.1, s32[5,8192]{1,0:T(8,128)S(1)} %copy-done.2, ...), custom_call_target="tpu_custom_call" | custom-call | flops 6000000000 | bytes 1 | tf_op jit(solution)/shard_map/pallas_call | solution.py:45
  14.5 2.1 %collective-permute-done.2.s3.e3 = bf16[24,2688]{1,0:T(8,128)(2,1)S(1)} collective-permute-done((bf16[24,2688]{1,0:T(8,128)(2,1)S(1)}, bf16[24,2688]{1,0:T(8,128)(2,1)S(1)}, u32[]{:S(2)}, u32[]{:S(2)}) %collective-permute-start.2) | collective-permute-done | bytes 129056 | tf_op jit(solution)/shard_map/ppermute | solution.py:1177
  16.6 0.1 collective-permute-start.3
  16.7 0.4 collective-permute-start.4
  17.1 1.6 %collective-permute-start.5 = (bf16[24,5120]{1,0:T(8,128)(2,1)S(1)}, bf16[24,5120]{1,0:T(8,128)(2,1)S(1)}, u32[]{:S(2)}, u32[]{:S(2)}) collective-permute-start(bf16[24,5120]{1,0:T(8,128)(2,1)S(1)} %get-tuple-element.88), channel_id=1, source_target_pairs={{0,2},{1,3},{2,0},{3,1},{4,6},{5,7},{6,4},{7,5},{8,10},{9,11},{10,... | collective-permute-start | bytes 737288 | tf_op jit(solution)/shard_map/ppermute | solution.py:1177
  18.7 4.9 %shard_map.396 = (bf16[256,4224]{1,0:T(8,128)(2,1)}, f32[264,1280]{1,0:T(8,128)}, bf16[784,128]{1,0:T(8,128)(2,1)}, bf16[256,512]{1,0:T(8,128)(2,1)}) custom-call(bf16[64,896]{1,0:T(8,128)(2,1)} %get-tuple-element.67.own_b, f32[456,128]{1,0:T(8,128)} %get-tuple-element.68.packed, bf16[24,5120]{1,0:T(8,128)(2,1)S(1)} %collective-permute-done.s1.e1, ...), custom_call_target="tpu_custom_call" | custom-call | flops 4000000000 | bytes 1 | tf_op jit(solution)/shard_map/pallas_call | solution.py:45
  23.7 6.3 %all-to-all-start = ((bf16[32,8,512]{2,1,0:T(8,128)(2,1)}), bf16[32,8,512]{2,1,0:T(8,128)(2,1)S(1)}, u32[]{:S(2)}, u32[]{:S(2)}) async-start(bf16[32,8,512]{2,1,0:T(8,128)(2,1)} %bitcast.3), calls=%async_computation | async-start | bytes 524288 | tf_op jit(solution)/shard_map/all_to_all | solution.py:1215
  30.0 12.2 %shard_map.397.part_in = f32[264,2176]{1,0:T(8,128)} custom-call(bf16[256,4224]{1,0:T(8,128)(2,1)} %get-tuple-element.82.low_in, f32[264,1280]{1,0:T(8,128)} %get-tuple-element.83.high_in, bf16[5488,128]{1,0:T(8,128)(2,1)} %get-tuple-element.85.counts_in, bf16[64,2816]{1,0:T(8,128)(2,1)} %get-tuple-element.86.own_a, ...), custom_call_target="tpu_custom_call" | custom-call | flops 14000000000 | bytes 1 | tf_op jit(solution)/shard_map/pallas_call | solution.py:45
  42.1 3.8 %shard_map.398 = (bf16[448,128]{1,0:T(8,128)(2,1)S(1)}, bf16[448,128]{1,0:T(8,128)(2,1)S(1)}, bf16[896,128]{1,0:T(8,128)(2,1)S(1)}) custom-call(s32[8,8]{1,0:T(8,128)} %serve_in.3, s32[8,8]{1,0:T(8,128)} %take_in.3, s32[1,8]{1,0:T(1,128)} %bitcast.44, bf16[256,512]{1,0:T(8,128)(2,1)S(1)} %bitcast.25, bf16[256,4224]{1,0:T(8,128)(2,1)} %get-tuple-element.82.low_in, ...), custom_call_target="tpu_custom_call" | custom-call | flops 3000000000 | bytes 1 | tf_op jit(solution)/shard_map/pallas_call | solution.py:45
  46.1 0.3 collective-permute-start.7
  46.4 1.3 %collective-permute-done.7 = bf16[896,128]{1,0:T(8,128)(2,1)S(1)} collective-permute-done((bf16[896,128]{1,0:T(8,128)(2,1)S(1)}, bf16[896,128]{1,0:T(8,128)(2,1)S(1)}, u32[]{:S(2)}, u32[]{:S(2)}) %collective-permute-start.7) | collective-permute-done | bytes 229408 | tf_op jit(solution)/shard_map/ppermute | solution.py:1177
  47.7 2.6 %collective-permute-start.10 = (bf16[448,128]{1,0:T(8,128)(2,1)S(1)}, bf16[448,128]{1,0:T(8,128)(2,1)S(1)}, u32[]{:S(2)}, u32[]{:S(2)}) collective-permute-start(bf16[448,128]{1,0:T(8,128)(2,1)S(1)} %get-tuple-element.117), channel_id=1, source_target_pairs={{0,6},{1,7},{2,4},{3,5},{4,2},{5,3},{6,0},{7,1},{8,14},{9,15},{10,... | collective-permute-start | bytes 344072 | tf_op jit(solution)/shard_map/ppermute | solution.py:1223
  50.3 0.5 collective-permute-start.9
  50.9 0.4 collective-permute-start.8
  51.3 3.4 %collective-permute-done.10 = bf16[448,128]{1,0:T(8,128)(2,1)S(1)} collective-permute-done((bf16[448,128]{1,0:T(8,128)(2,1)S(1)}, bf16[448,128]{1,0:T(8,128)(2,1)S(1)}, u32[]{:S(2)}, u32[]{:S(2)}) %collective-permute-start.10) | collective-permute-done | bytes 114720 | tf_op jit(solution)/shard_map/ppermute | solution.py:1223
  54.6 2.1 %collective-permute-done.9 = bf16[448,128]{1,0:T(8,128)(2,1)S(1)} collective-permute-done((bf16[448,128]{1,0:T(8,128)(2,1)S(1)}, bf16[448,128]{1,0:T(8,128)(2,1)S(1)}, u32[]{:S(2)}, u32[]{:S(2)}) %collective-permute-start.9) | collective-permute-done | bytes 114720 | tf_op jit(solution)/shard_map/ppermute | solution.py:1177
  56.8 1.6 %collective-permute-start.11 = (bf16[448,128]{1,0:T(8,128)(2,1)S(1)}, bf16[448,128]{1,0:T(8,128)(2,1)S(1)}, u32[]{:S(2)}, u32[]{:S(2)}) collective-permute-start(bf16[448,128]{1,0:T(8,128)(2,1)S(1)} %fusion.1), channel_id=1, source_target_pairs={{0,8},{4,12},{8,0},{12,4},{16,24},{20,28},{24,16},{28,20},{1,9},{5... | collective-permute-start | bytes 344072 | tf_op jit(solution)/shard_map/ppermute | solution.py:1177
  58.4 3.2 %collective-permute-done.11 = bf16[448,128]{1,0:T(8,128)(2,1)S(1)} collective-permute-done((bf16[448,128]{1,0:T(8,128)(2,1)S(1)}, bf16[448,128]{1,0:T(8,128)(2,1)S(1)}, u32[]{:S(2)}, u32[]{:S(2)}) %collective-permute-start.11) | collective-permute-done | bytes 114720 | tf_op jit(solution)/shard_map/ppermute | solution.py:1177
  61.6 0.1 fusion
  61.7 2.7 %collective-permute-start.12 = (bf16[448,128]{1,0:T(8,128)(2,1)S(1)}, bf16[448,128]{1,0:T(8,128)(2,1)S(1)}, u32[]{:S(2)}, u32[]{:S(2)}) collective-permute-start(bf16[448,128]{1,0:T(8,128)(2,1)S(1)} %fusion), channel_id=1, source_target_pairs={{0,16},{4,20},{8,24},{12,28},{16,0},{20,4},{24,8},{28,12},{1,17},{... | collective-permute-start | bytes 344072 | tf_op jit(solution)/shard_map/ppermute | solution.py:1177
  64.4 4.7 %collective-permute-done.12 = bf16[448,128]{1,0:T(8,128)(2,1)S(1)} collective-permute-done((bf16[448,128]{1,0:T(8,128)(2,1)S(1)}, bf16[448,128]{1,0:T(8,128)(2,1)S(1)}, u32[]{:S(2)}, u32[]{:S(2)}) %collective-permute-start.12) | collective-permute-done | bytes 114720 | tf_op jit(solution)/shard_map/ppermute | solution.py:1177
  69.1 0.1 add_reduce-precision_fusion.grad
  69.4 1.5 %shard_map.399 = (f32[25,2,256]{2,1,0:T(2,128)}, f32[2,64,256]{2,1,0:T(8,128)}, f32[47,2,64]{2,1,0:T(2,128)}, f32[2,64]{1,0:T(2,128)}, f32[1,47]{1,0:T(1,128)}, ...) custom-call(f32[448,128]{1,0:T(8,128)S(1)} %add_reduce-precision_fus, ...), custom_call_target="tpu_custom_call" | custom-call | flops 1000000000 | bytes 1 | tf_op jit(solution)/shard_map/pallas_call | solution.py:45
  70.8 1.2 %collective-permute-done.13 = f32[8,128]{1,0:T(8,128)S(1)} collective-permute-done((f32[8,128]{1,0:T(8,128)S(1)}, f32[8,128]{1,0:T(8,128)S(1)}, u32[]{:S(2)}, u32[]{:S(2)}) %collective-permute-start.13) | collective-permute-done | bytes 4128 | tf_op jit(solution)/shard_map/ppermute | solution.py:1177
  72.0 2.0 %collective-permute-start.14 = (f32[8,128]{1,0:T(8,128)S(1)}, f32[8,128]{1,0:T(8,128)S(1)}, u32[]{:S(2)}, u32[]{:S(2)}) collective-permute-start(f32[8,128]{1,0:T(8,128)S(1)} %add.31.own), channel_id=1, source_target_pairs={{0,2},{1,3},{2,0},{3,1},{4,6},{5,7},{6,4},{7,5},{8,10},{9,11},{10,... | collective-permute-start | bytes 12296 | tf_op jit(solution)/shard_map/ppermute | solution.py:1177
  74.0 0.6 fusion.2
  74.6 1.0 %collective-permute-done.14.far = f32[8,128]{1,0:T(8,128)S(1)} collective-permute-done((f32[8,128]{1,0:T(8,128)S(1)}, f32[8,128]{1,0:T(8,128)S(1)}, u32[]{:S(2)}, u32[]{:S(2)}) %collective-permute-start.14) | collective-permute-done | bytes 4128 | tf_op jit(solution)/shard_map/ppermute | solution.py:1177
  75.6 0.8 %shard_map.400 = (f32[25,2,256]{2,1,0:T(2,128)}, f32[2,64,256]{2,1,0:T(8,128)}, f32[47,2,64]{2,1,0:T(2,128)}, f32[2,64]{1,0:T(2,128)}, f32[1,47]{1,0:T(1,128)}, /*index=5*/f32[2,5]{1,0:T(2,128)}) custom-call(f32[8,128]{1,0:T(8,128)S(1)} %add.31.own, f32[8,128]{1,0:T(8,128)S(1)} %collective-permute-done.14.far, f32[25,2,256]{2,1,0:T(2,128)S(1)} %bitcast.30, ...), custom_call_target="tpu_custom_call" | custom-call | flops 1000000000 | bytes 1 | tf_op jit(solution)/shard_map/pallas_call | solution.py:45
  (57 shorter events, 0.3 us)
Async XLA Ops:
  0.7 7.0 %copy-start = (bf16[25,32768]{1,0:T(8,128)(2,1)S(1)}, bf16[25,32768]{1,0:T(8,128)(2,1)}, u32[]{:S(2)}) copy-start(bf16[25,32768]{1,0:T(8,128)(2,1)} %feat_ref.1) | copy-start | bytes 4915204
  4.5 12.3 %collective-permute-start = (bf16[24,5120]{1,0:T(8,128)(2,1)S(1)}, bf16[24,5120]{1,0:T(8,128)(2,1)S(1)}, u32[]{:S(2)}, u32[]{:S(2)}) collective-permute-start(bf16[24,5120]{1,0:T(8,128)(2,1)S(1)} %get-tuple-element.69), channel_id=1, source_target_pairs={{0,1},{1,0},{2,3},{3,2},{4,5},{5,4},{6,7},{7,6},{8,9},{9,8},{10,11... | collective-permute-start | bytes 737288 | tf_op jit(solution)/shard_map/ppermute | solution.py:1177
  5.0 11.6 %collective-permute-start.1 = (bf16[24,5120]{1,0:T(8,128)(2,1)S(1)}, bf16[24,5120]{1,0:T(8,128)(2,1)S(1)}, u32[]{:S(2)}, u32[]{:S(2)}) collective-permute-start(bf16[24,5120]{1,0:T(8,128)(2,1)S(1)} %get-tuple-element.76), channel_id=1, source_target_pairs={{0,2},{1,3},{2,0},{3,1},{4,6},{5,7},{6,4},{7,5},{8,10},{9,11},{10,... | collective-permute-start | bytes 737288 | tf_op jit(solution)/shard_map/ppermute | solution.py:1177
  7.6 9.0 %collective-permute-start.2 = (bf16[24,2688]{1,0:T(8,128)(2,1)S(1)}, bf16[24,2688]{1,0:T(8,128)(2,1)S(1)}, u32[]{:S(2)}, u32[]{:S(2)}) collective-permute-start(bf16[24,2688]{1,0:T(8,128)(2,1)S(1)} %get-tuple-element.77), channel_id=1, source_target_pairs={{0,3},{1,2},{2,1},{3,0},{4,7},{5,6},{6,5},{7,4},{8,11},{9,10},{10,... | collective-permute-start | bytes 387080 | tf_op jit(solution)/shard_map/ppermute | solution.py:1177
  16.6 2.1 %collective-permute-start.3 = (bf16[24,5120]{1,0:T(8,128)(2,1)S(1)}, bf16[24,5120]{1,0:T(8,128)(2,1)S(1)}, u32[]{:S(2)}, u32[]{:S(2)}) collective-permute-start(bf16[24,5120]{1,0:T(8,128)(2,1)S(1)} %collective-permute-done.1.s2.e2), channel_id=1, source_target_pairs={{0,1},{1,0},{2,3},{3,2},{4,5},{5,4},{6,7},{7,6},{8,9},{9,8},{10,11... | collective-permute-start | bytes 737288 | tf_op jit(solution)/shard_map/ppermute | solution.py:1177
  16.7 13.2 %collective-permute-start.4 = (bf16[24,5120]{1,0:T(8,128)(2,1)S(1)}, bf16[24,5120]{1,0:T(8,128)(2,1)S(1)}, u32[]{:S(2)}, u32[]{:S(2)}) collective-permute-start(bf16[24,5120]{1,0:T(8,128)(2,1)S(1)} %get-tuple-element.87), channel_id=1, source_target_pairs={{0,1},{1,0},{2,3},{3,2},{4,5},{5,4},{6,7},{7,6},{8,9},{9,8},{10,11... | collective-permute-start | bytes 737288 | tf_op jit(solution)/shard_map/ppermute | solution.py:1177
  17.1 12.8 %collective-permute-start.5 = (bf16[24,5120]{1,0:T(8,128)(2,1)S(1)}, bf16[24,5120]{1,0:T(8,128)(2,1)S(1)}, u32[]{:S(2)}, u32[]{:S(2)}) collective-permute-start(bf16[24,5120]{1,0:T(8,128)(2,1)S(1)} %get-tuple-element.88), channel_id=1, source_target_pairs={{0,2},{1,3},{2,0},{3,1},{4,6},{5,7},{6,4},{7,5},{8,10},{9,11},{10,... | collective-permute-start | bytes 737288 | tf_op jit(solution)/shard_map/ppermute | solution.py:1177
  18.7 11.2 %collective-permute-start.6 = (bf16[24,5120]{1,0:T(8,128)(2,1)S(1)}, bf16[24,5120]{1,0:T(8,128)(2,1)S(1)}, u32[]{:S(2)}, u32[]{:S(2)}) collective-permute-start(bf16[24,5120]{1,0:T(8,128)(2,1)S(1)} %get-tuple-element.89), channel_id=1, source_target_pairs={{0,3},{1,2},{2,1},{3,0},{4,7},{5,6},{6,5},{7,4},{8,11},{9,10},{10,... | collective-permute-start | bytes 737288 | tf_op jit(solution)/shard_map/ppermute | solution.py:1177
  23.7 18.5 %all-to-all-start = ((bf16[32,8,512]{2,1,0:T(8,128)(2,1)}), bf16[32,8,512]{2,1,0:T(8,128)(2,1)S(1)}, u32[]{:S(2)}, u32[]{:S(2)}) async-start(bf16[32,8,512]{2,1,0:T(8,128)(2,1)} %bitcast.3), calls=%async_computation | async-start | bytes 524288 | tf_op jit(solution)/shard_map/all_to_all | solution.py:1215
  45.9 23.3 %copy-start.5 = (f32[2,64,256]{2,1,0:T(8,128)S(1)}, f32[2,64,256]{2,1,0:T(8,128)}, u32[]{:S(2)}) copy-start(f32[2,64,256]{2,1,0:T(8,128)} %f2.1) | copy-start | bytes 393220
  45.9 23.3 %copy-start.6 = (f32[2,64,256]{2,1,0:T(8,128)S(1)}, f32[2,64,256]{2,1,0:T(8,128)}, u32[]{:S(2)}) copy-start(f32[2,64,256]{2,1,0:T(8,128)} %s2_.1) | copy-start | bytes 393220
  45.9 23.3 %copy-start.7 = (f32[2,64,256]{2,1,0:T(8,128)S(1)}, f32[2,64,256]{2,1,0:T(8,128)}, u32[]{:S(2)}) copy-start(f32[2,64,256]{2,1,0:T(8,128)} %w2.3) | copy-start | bytes 393220
  45.9 23.3 %copy-start.8 = (f32[2,25,256]{2,0,1:T(2,128)S(1)}, f32[2,25,256]{2,0,1:T(2,128)}, u32[]{:S(2)}) copy-start(f32[2,25,256]{2,0,1:T(2,128)} %param.44) | copy-start | bytes 153604
  46.0 23.3 %copy-start.9 = (f32[2,25,256]{2,0,1:T(2,128)S(1)}, f32[2,25,256]{2,0,1:T(2,128)}, u32[]{:S(2)}) copy-start(f32[2,25,256]{2,0,1:T(2,128)} %param.49) | copy-start | bytes 153604
  46.0 23.3 %copy-start.10 = (f32[2,25,256]{2,0,1:T(2,128)S(1)}, f32[2,25,256]{2,0,1:T(2,128)}, u32[]{:S(2)}) copy-start(f32[2,25,256]{2,0,1:T(2,128)} %param.39) | copy-start | bytes 153604
  46.0 23.3 %copy-start.11 = (f32[2,64,47]{1,0,2:T(2,128)S(1)}, f32[2,64,47]{1,0,2:T(2,128)}, u32[]{:S(2)}) copy-start(f32[2,64,47]{1,0,2:T(2,128)} %param.46) | copy-start | bytes 72196
  46.0 23.3 %copy-start.12 = (f32[2,64,47]{1,0,2:T(2,128)S(1)}, f32[2,64,47]{1,0,2:T(2,128)}, u32[]{:S(2)}) copy-start(f32[2,64,47]{1,0,2:T(2,128)} %param.51) | copy-start | bytes 72196
  46.0 23.3 %copy-start.13 = (f32[2,64,47]{1,0,2:T(2,128)S(1)}, f32[2,64,47]{1,0,2:T(2,128)}, u32[]{:S(2)}) copy-start(f32[2,64,47]{1,0,2:T(2,128)} %param.41) | copy-start | bytes 72196
  46.0 23.3 %copy-start.16 = (f32[2,64]{1,0:T(2,128)S(1)}, f32[2,64]{1,0:T(2,128)}, u32[]{:S(2)}) copy-start(f32[2,64]{1,0:T(2,128)} %fh.1) | copy-start | bytes 1540
  46.0 23.3 %copy-start.17 = (f32[2,64]{1,0:T(2,128)S(1)}, f32[2,64]{1,0:T(2,128)}, u32[]{:S(2)}) copy-start(f32[2,64]{1,0:T(2,128)} %sh.1) | copy-start | bytes 1540
  46.0 23.3 %copy-start.18 = (f32[2,64]{1,0:T(2,128)S(1)}, f32[2,64]{1,0:T(2,128)}, u32[]{:S(2)}) copy-start(f32[2,64]{1,0:T(2,128)} %wh.3) | copy-start | bytes 1540
  46.0 23.3 %copy-start.19 = (f32[47]{0:T(128)S(1)}, f32[47]{0:T(128)}, u32[]{:S(2)}) copy-start(f32[47]{0:T(128)} %param.48) | copy-start | bytes 568
  46.1 23.3 %copy-start.20 = (f32[47]{0:T(128)S(1)}, f32[47]{0:T(128)}, u32[]{:S(2)}) copy-start(f32[47]{0:T(128)} %param.53) | copy-start | bytes 568
  46.1 23.3 %copy-start.21 = (f32[47]{0:T(128)S(1)}, f32[47]{0:T(128)}, u32[]{:S(2)}) copy-start(f32[47]{0:T(128)} %param.43) | copy-start | bytes 568
  46.1 1.6 %collective-permute-start.7 = (bf16[896,128]{1,0:T(8,128)(2,1)S(1)}, bf16[896,128]{1,0:T(8,128)(2,1)S(1)}, u32[]{:S(2)}, u32[]{:S(2)}) collective-permute-start(bf16[896,128]{1,0:T(8,128)(2,1)S(1)} %get-tuple-element.91), channel_id=1, source_target_pairs={{0,1},{1,0},{2,3},{3,2},{4,5},{5,4},{6,7},{7,6},{8,9},{9,8},{10,11... | collective-permute-start | bytes 688136 | tf_op jit(solution)/shard_map/ppermute | solution.py:1177
  47.7 6.9 %collective-permute-start.10 = (bf16[448,128]{1,0:T(8,128)(2,1)S(1)}, bf16[448,128]{1,0:T(8,128)(2,1)S(1)}, u32[]{:S(2)}, u32[]{:S(2)}) collective-permute-start(bf16[448,128]{1,0:T(8,128)(2,1)S(1)} %get-tuple-element.117), channel_id=1, source_target_pairs={{0,6},{1,7},{2,4},{3,5},{4,2},{5,3},{6,0},{7,1},{8,14},{9,15},{10,... | collective-permute-start | bytes 344072 | tf_op jit(solution)/shard_map/ppermute | solution.py:1223
  50.3 6.4 %collective-permute-start.9 = (bf16[448,128]{1,0:T(8,128)(2,1)S(1)}, bf16[448,128]{1,0:T(8,128)(2,1)S(1)}, u32[]{:S(2)}, u32[]{:S(2)}) collective-permute-start(bf16[448,128]{1,0:T(8,128)(2,1)S(1)} %get-tuple-element.116), channel_id=1, source_target_pairs={{0,4},{4,0},{8,12},{12,8},{16,20},{20,16},{24,28},{28,24},{1,5},{5... | collective-permute-start | bytes 344072 | tf_op jit(solution)/shard_map/ppermute | solution.py:1177
  50.9 5.8 %collective-permute-start.8 = (bf16[448,128]{1,0:T(8,128)(2,1)S(1)}, bf16[448,128]{1,0:T(8,128)(2,1)S(1)}, u32[]{:S(2)}, u32[]{:S(2)}) collective-permute-start(bf16[448,128]{1,0:T(8,128)(2,1)S(1)} %get-tuple-element.117), channel_id=1, source_target_pairs={{0,2},{1,3},{2,0},{3,1},{4,6},{5,7},{6,4},{7,5},{8,10},{9,11},{10,... | collective-permute-start | bytes 344072 | tf_op jit(solution)/shard_map/ppermute | solution.py:1177
  56.8 4.9 %collective-permute-start.11 = (bf16[448,128]{1,0:T(8,128)(2,1)S(1)}, bf16[448,128]{1,0:T(8,128)(2,1)S(1)}, u32[]{:S(2)}, u32[]{:S(2)}) collective-permute-start(bf16[448,128]{1,0:T(8,128)(2,1)S(1)} %fusion.1), channel_id=1, source_target_pairs={{0,8},{4,12},{8,0},{12,4},{16,24},{20,28},{24,16},{28,20},{1,9},{5... | collective-permute-start | bytes 344072 | tf_op jit(solution)/shard_map/ppermute | solution.py:1177
  61.7 7.3 %collective-permute-start.12 = (bf16[448,128]{1,0:T(8,128)(2,1)S(1)}, bf16[448,128]{1,0:T(8,128)(2,1)S(1)}, u32[]{:S(2)}, u32[]{:S(2)}) collective-permute-start(bf16[448,128]{1,0:T(8,128)(2,1)S(1)} %fusion), channel_id=1, source_target_pairs={{0,16},{4,20},{8,24},{12,28},{16,0},{20,4},{24,8},{28,12},{1,17},{... | collective-permute-start | bytes 344072 | tf_op jit(solution)/shard_map/ppermute | solution.py:1177
  70.8 1.2 %collective-permute-start.13 = (f32[8,128]{1,0:T(8,128)S(1)}, f32[8,128]{1,0:T(8,128)S(1)}, u32[]{:S(2)}, u32[]{:S(2)}) collective-permute-start(f32[8,128]{1,0:T(8,128)S(1)} %get-tuple-element.93), channel_id=1, source_target_pairs={{0,1},{1,0},{2,3},{3,2},{4,5},{5,4},{6,7},{7,6},{8,9},{9,8},{10,11... | collective-permute-start | bytes 12296 | tf_op jit(solution)/shard_map/ppermute | solution.py:1177
  72.0 3.6 %collective-permute-start.14 = (f32[8,128]{1,0:T(8,128)S(1)}, f32[8,128]{1,0:T(8,128)S(1)}, u32[]{:S(2)}, u32[]{:S(2)}) collective-permute-start(f32[8,128]{1,0:T(8,128)S(1)} %add.31.own), channel_id=1, source_target_pairs={{0,2},{1,3},{2,0},{3,1},{4,6},{5,7},{6,4},{7,5},{8,10},{9,11},{10,... | collective-permute-start | bytes 12296 | tf_op jit(solution)/shard_map/ppermute | solution.py:1177
  (6 other events, 41.8 us)

commit v5 on v4

--- a/solution.py
+++ b/solution.py
@@ -20,11 +20,13 @@
 BF = jnp.bfloat16
 F32 = jnp.float32
 LANES = 128
-WINDOW = 768
+WINDOW = 640
+HALF = 64
+FRONT = 320
 SENTINEL = 4.0
 MIB = 2**20
 LOSS_BITS = 14
-EARLY = 6
+EARLY = 4
 FIRST_MIB = 8
 MEAN_MIB = 8
 SEEDS_MIB = 16
@@ -83,8 +85,8 @@
         self.classes = weight_three.shape[2]
         self.head = -(-self.classes // 16) * 16
         self.own = self.seeds // 4
-        self.n_b = 4 * self.own + 2 * LANES
-        self.n_a = 16 * self.own + 6 * LANES
+        self.n_b = 4 * self.own + LANES
+        self.n_a = 16 * self.own + 5 * LANES
         self.n_mid = self.n_b + self.own
         self.n_low = self.n_a + self.n_mid
         self.tiles_b = self.n_b // LANES
@@ -104,6 +106,7 @@
         self.message_b = self.pair_lanes(self.n_mid, self.n_mid + self.early)
         self.full_b = self.message_b + LANES * self.blocks
         self.tiles_b_all = 16 * self.own // LANES + 1
+        self.tiles_all = self.low // LANES + 8
         self.count_rows = WINDOW + 16
         hid, at = self.hid, self.n_mid
         places = {}
@@ -137,28 +140,24 @@
         return [b, c, (a[0], self.n_mid, self.early)], [b, c]
 
     def second_ranges(self, part):
-        first = self.a_start(part)
+        first = 16 * self.own * part
         return [(first + self.early, 0, self.n_a - self.early)], [(first, 0, self.n_a)]
 
-    def a_start(self, part):
-        return jnp.clip(16 * self.own * part - 3 * LANES, 0, self.low - self.n_a)
-
-    def b_start(self, part):
-        return jnp.maximum(4 * self.own * part - LANES, 0)
-
-    def b_columns(self, part, tile):
-        return pl.ds(aligned(jnp.minimum(self.b_start(part) + LANES * tile, self.mid - LANES)), LANES)
-
-    def mid_columns(self, part, tile):
-        if tile < self.tiles_b:
-            return self.b_columns(part, tile)
-        return pl.ds(aligned(self.own * part + LANES * (tile - self.tiles_b)), LANES)
+    def a_row(self, part):
+        return 16 * self.own * part - FRONT
+
+    def b_row(self, part):
+        return 4 * self.own * part - HALF
+
+    def seed_window(self):
+        rows = self.count_rows * (self.own // LANES)
+        return pl.ds(self.count_rows * self.tiles_b + rows, rows)
 
     def ranges(self, part):
         return (
-            (self.a_start(part), 0, self.n_a),
-            (self.b_start(part), self.n_a, self.n_b),
-            (self.own * part, self.n_a + self.n_b, self.own),
+            (16 * self.own * part, 0, self.n_a),
+            (self.b_row(part) + FRONT, self.n_a, self.n_b),
+            (self.own * part + FRONT, self.n_a + self.n_b, self.own),
         )
 
 
@@ -192,7 +191,59 @@
     return jnp.concatenate([main, tail[tile : tile + 1, :], spare], 0).astype(BF)
 
 
-def mean_tiles(sz, begin, tiles, feat_ref, nbr_ref, pres_ref, mean_ref, tail_ref, base_ref, code_ref, count_ref):
+def half_tiles(left, right):
+    lane = lax.broadcasted_iota(jnp.int32, left.shape, 1)
+    return jnp.where(lane < HALF, pltpu.roll(left, HALF, 1), pltpu.roll(right, HALF, 1))
+
+
+def half_columns(ref, tile, tiles, spare):
+    if isinstance(tile, int):
+        left, right = max(tile - 1, 0), min(tile, tiles - 1)
+        left, right = [ref[:, LANES * i : LANES * (i + 1)] for i in (left, right)]
+        left = left if tile > 0 else jnp.full_like(left, spare)
+        right = right if tile < tiles else jnp.full_like(right, spare)
+        return half_tiles(left, right)
+    left = ref[:, pl.ds(aligned(jnp.maximum(tile - 1, 0) * LANES), LANES)]
+    right = ref[:, pl.ds(aligned(jnp.minimum(tile, tiles - 1) * LANES), LANES)]
+    left = jnp.where(tile > 0, left, spare)
+    right = jnp.where(tile < tiles, right, spare)
+    return half_tiles(left, right)
+
+
+def take_tile(ref, rows, first, half):
+    if not half:
+        return ref[:rows, pl.ds(aligned(first), LANES)].astype(F32)
+    first = first - HALF
+    left = ref[:rows, pl.ds(aligned(first), LANES)].astype(F32)
+    return half_tiles(left, ref[:rows, pl.ds(aligned(first + LANES), LANES)].astype(F32))
+
+
+def take_tail(ref, first, half):
+    if not half:
+        return ref[pl.ds(first // LANES, 1), :]
+    row = (first - HALF) // LANES
+    return half_tiles(ref[pl.ds(row, 1), :], ref[pl.ds(row + 1, 1), :])
+
+
+def fill_own(sz, feat_ref, self_ref, self_tail, places):
+    spare = jnp.zeros((sz.hold - sz.feat, LANES), F32)
+    zeros = jnp.zeros((sz.feat, LANES), BF)
+    count = min(sz.low, feat_ref.shape[1]) // LANES
+    lane = lax.broadcasted_iota(jnp.int32, (sz.feat, LANES), 1)
+    shift = FRONT // LANES
+    before = zeros
+    for place in range(places):
+        tile = place - shift
+        after = zeros
+        if tile >= 0 and tile < count:
+            after = pltpu.roll(feat_ref[:, LANES * tile : LANES * (tile + 1)], HALF, 1)
+        value = jnp.where(lane < HALF, before.astype(F32), after.astype(F32))
+        self_tail[place : place + 1, :] = value[sz.main : sz.feat]
+        self_ref[:, LANES * place : LANES * (place + 1)] = jnp.concatenate([value, spare], 0).astype(BF)
+        before = after
+
+
+def mean_tiles(sz, begin, tiles, feat_ref, nbr_ref, pres_ref, links_ref, present_ref, mean_ref, tail_ref, base_ref, code_ref, count_ref):
     last = feat_ref.shape[1] // LANES - 6
     slots = nbr_ref.shape[0]
     base_ref[...] = jnp.zeros_like(base_ref)
@@ -203,13 +254,18 @@
         row = feat_ref[:, LANES * tile : LANES * (tile + 1)].astype(F32)
         base_ref[8 + tile : 9 + tile, :] = row[sz.main : sz.feat]
 
+    for table, shifted in ((nbr_ref, links_ref), (pres_ref, present_ref)):
+        count = table.shape[1] // LANES
+        for tile in range(begin, tiles):
+            shifted[:, LANES * tile : LANES * (tile + 1)] = half_columns(table, tile, count, 0)
+
     def one_tile(step, carry):
-        lane = aligned(step * LANES)
-        present = pres_ref[:, pl.ds(lane, LANES)]
+        lanes = pl.ds(aligned(step * LANES), LANES)
+        present = present_ref[:, lanes]
         valid = present.astype(F32)
         counts = jnp.maximum(jnp.sum(valid, 0, keepdims=True), 1.0)
-        first = jnp.clip(4 * step - 1, 0, last)
-        links = nbr_ref[:, pl.ds(lane, LANES)]
+        first = jnp.clip(4 * step - 3, 0, last)
+        links = links_ref[:, lanes]
         code = jnp.where(present > 0, links, -1)
         count_ref[pl.ds(step, 1), :] = counts
         for slot in range(slots):
@@ -233,7 +289,7 @@
                     )
                     taken = found if j == 0 else jnp.where(pieces == j, found, taken)
                 totals[h] = totals[h] + taken * marks
-        mean_ref[:, pl.ds(lane, LANES)] = (jnp.concatenate(totals, 0) / counts).astype(BF)
+        mean_ref[:, pl.ds(aligned((step + 2) * LANES), LANES)] = (jnp.concatenate(totals, 0) / counts).astype(BF)
         return carry
 
     even = begin + (tiles - begin) // 4 * 4
@@ -246,53 +302,62 @@
         total = jnp.zeros((8, LANES), F32)
         for slot in range(slots):
             code = code_ref[slot, 8 * block : 8 * (block + 1), :]
-            piece = (code >> 7) - (4 * (8 * block + sub) - 1)
+            piece = (code >> 7) - (4 * (8 * block + sub) - 3)
             taken = None
             for j in range(6):
-                source = base_ref[pl.ds(8 + 32 * block - 1 + j, 8, stride=4), :]
+                source = base_ref[pl.ds(8 + 32 * block - 3 + j, 8, stride=4), :]
                 found = jnp.take_along_axis(source, code & 127, axis=1, mode="promise_in_bounds")
                 taken = found if j == 0 else jnp.where(piece == j, found, taken)
             total = total + jnp.where(code >= 0, taken, 0.0)
-        tail_ref[8 * block : 8 * (block + 1), :] = total / count_ref[8 * block : 8 * (block + 1), :]
-
-
-def pack_pair(sz, ranges, feat_ref, base_ref, mean_ref, tail_ref, turn_ref, out_ref):
+        tail_ref[8 * block + 2 : 8 * block + 10, :] = total / count_ref[8 * block : 8 * (block + 1), :]
+
+
+def pack_pair(sz, ranges, self_ref, self_tail, mean_ref, tail_ref, turn_ref, out_ref):
     turn_ref[...] = jnp.zeros_like(turn_ref)
     lanes = 0
-    for source_ref, rows_ref, shift, group in zip((feat_ref, mean_ref), (base_ref, tail_ref), (8, 0), ranges):
-        for first, at, count in group:
+    for source_ref, rows_ref, group in zip((self_ref, mean_ref), (self_tail, tail_ref), ranges):
+        for i, (first, at, count) in enumerate(group):
             at = at + lanes
-            out_ref[:, at : at + count] = source_ref[: sz.main, pl.ds(aligned(first), count)]
-            at, rows = at // LANES, count // LANES
-            turn_ref[at : at + rows, :] = rows_ref[pl.ds(shift + first // LANES, rows), :]
+            if i != 1:
+                out_ref[:, at : at + count] = source_ref[: sz.main, pl.ds(aligned(first), count)]
+                turn_ref[at // LANES : (at + count) // LANES, :] = rows_ref[pl.ds(first // LANES, count // LANES), :]
+                continue
+            for tile in range(count // LANES):
+                place = first + LANES * tile
+                piece = take_tile(source_ref, sz.main, place, True)
+                out_ref[:, at + LANES * tile : at + LANES * (tile + 1)] = piece.astype(BF)
+                turn_ref[at // LANES + tile : at // LANES + tile + 1, :] = take_tail(rows_ref, place, True)
         lanes += sum(count for _, _, count in group)
     for block in range(-(-lanes // LANES // sz.main)):
         at = lanes + LANES * block
         out_ref[:, at : at + LANES] = turn_ref[sz.main * block : sz.main * (block + 1), :].astype(BF)
 
 
-def own_pair(sz, ranges, feat_ref, mean_ref, tail_ref, own_ref):
+def own_pair(sz, ranges, self_ref, mean_ref, tail_ref, own_ref):
     spare = jnp.zeros((sz.hold - sz.feat, LANES), F32)
     base = ranges[0][1]
-    for start, at, count in ranges:
+    for i, (start, at, count) in enumerate(ranges):
         for tile in range(count // LANES):
-            lanes = pl.ds(aligned(start + LANES * tile), LANES)
+            place = start + LANES * tile
             out_lanes = slice(at - base + LANES * tile, at - base + LANES * (tile + 1))
-            own = [feat_ref[:, lanes].astype(F32), spare]
-            own_ref[: sz.hold, out_lanes] = jnp.concatenate(own, 0).astype(BF)
-            tail = tail_ref[pl.ds(start // LANES + tile, 1), :]
-            average = [mean_ref[:, lanes].astype(F32), tail, spare]
+            own_ref[: sz.hold, out_lanes] = take_tile(self_ref, sz.hold, place, i == 1).astype(BF)
+            average = [take_tile(mean_ref, sz.main, place, i == 1), take_tail(tail_ref, place, i == 1), spare]
             own_ref[sz.hold :, out_lanes] = jnp.concatenate(average, 0).astype(BF)
 
 
 def mean_scratch(sz, tiles, slots):
+    rows = -(-tiles // 8) * 8
     return [
-        ((sz.main, LANES * tiles), BF),
-        ((-(-tiles // 8) * 8, LANES), F32),
+        ((slots, LANES * tiles), jnp.int32),
+        ((slots, LANES * tiles), jnp.int32),
+        ((sz.hold, LANES * sz.tiles_all), BF),
+        ((sz.tiles_all, LANES), F32),
+        ((sz.main, LANES * sz.tiles_all), BF),
+        ((max(rows + 8, sz.tiles_all), LANES), F32),
         ((2 * sz.main, LANES), F32),
-        ((4 * -(-tiles // 8) * 8 + 16, LANES), F32),
-        ((slots, -(-tiles // 8) * 8, LANES), jnp.int32),
-        ((-(-tiles // 8) * 8, LANES), F32),
+        ((4 * rows + 16, LANES), F32),
+        ((slots, rows, LANES), jnp.int32),
+        ((rows, LANES), F32),
     ]
 
 
@@ -312,7 +377,7 @@
 def first_kernel(
     sz, features, neighbors, present, w1_in, w2_in, w3_in, wh_in, own_b, packed, mean_out, tail_out, m1, m2, m3,
     feat_ref, nbr_ref, pres_ref, w1, w2, w3, wh, own_ref,
-    mean_ref, tail_ref, turn_ref, base_ref, code_ref, count_ref, one_ref, three_ref, pack, sems,
+    links_ref, present_ref, self_ref, self_tail, mean_ref, tail_ref, turn_ref, base_ref, code_ref, count_ref, one_ref, three_ref, pack, sems,
 ):
     part = lax.axis_index("col")
     rows = pl.ds(0, nbr_ref.shape[1])
@@ -357,12 +422,16 @@
         m1[:, at : at + LANES] = piece
         m2[:, at : at + LANES] = piece
     wait_all(copies)
-    mean_tiles(sz, 0, sz.tiles_b_all, feat_ref, nbr_ref, pres_ref, mean_ref, tail_ref, base_ref, code_ref, count_ref)
-    store += start_copies(((mean_ref, mean_out), (tail_ref, tail_out)), sems, 9)
-    own_pair(sz, sz.ranges(part)[1:], feat_ref, mean_ref, tail_ref, own_ref)
+    fill_own(sz, feat_ref, self_ref, self_tail, 48 * sz.own // LANES + EARLY)
+    mean_ref[:, :FRONT] = jnp.zeros((sz.main, FRONT), BF)
+    tail_ref[...] = jnp.zeros_like(tail_ref)
+    mean_tiles(sz, 0, sz.tiles_b_all, feat_ref, nbr_ref, pres_ref, links_ref, present_ref, mean_ref, tail_ref, base_ref, code_ref, count_ref)
+    done = pl.ds(0, LANES * (sz.tiles_b_all + 2))
+    store += start_copies(((mean_ref.at[:, done], mean_out), (tail_ref, tail_out)), sems, 9)
+    own_pair(sz, sz.ranges(part)[1:], self_ref, mean_ref, tail_ref, own_ref)
     store += start_copies(((own_ref, own_b),), sems, 8)
     for r, out in ((1, m1), (2, m2), (3, m3)):
-        pack_pair(sz, sz.first_ranges(part ^ r), feat_ref, base_ref, mean_ref, tail_ref, turn_ref, out)
+        pack_pair(sz, sz.first_ranges(part ^ r), self_ref, self_tail, mean_ref, tail_ref, turn_ref, out)
     wait_all(store)
 
 
@@ -375,8 +444,8 @@
         [
             ((2 * sz.hold, sz.n_mid), BF),
             ((sz.main * sz.blocks, LANES), F32),
-            ((sz.main, rows), BF),
-            ((-(-sz.tiles_b_all // 8) * 8, LANES), F32),
+            ((sz.main, rows + 2 * LANES), BF),
+            ((max(-(-sz.tiles_b_all // 8) * 8 + 8, sz.tiles_all), LANES), F32),
             ((sz.main, sz.full_b), BF),
             ((sz.main, sz.full_b), BF),
             ((sz.main, sz.message_b), BF),
@@ -412,30 +481,34 @@
 
 def mean_kernel(
     sz, feat_ref, nbr_ref, pres_ref, mean_in, tail_in, nbr2, pres2, nbr3, pres3, own_a, counts_out, a1, a2, a3,
-    mean_ref, tail_ref, turn_ref, base_ref, code_ref, count_ref, own_ref, kept_ref, counts, sems,
+    links_ref, present_ref, self_ref, self_tail, mean_ref, tail_ref, turn_ref, base_ref, code_ref, count_ref, own_ref, kept_ref, counts, sems,
 ):
     part = lax.axis_index("col")
-    tiles = sz.low // LANES
+    tiles = sz.low // LANES + 1
     begin = sz.tiles_b_all
-    loads = start_copies(((mean_in, mean_ref.at[:, pl.ds(0, LANES * begin)]), (tail_in, kept_ref)), sems, 1)
+    loads = start_copies(((mean_in, mean_ref.at[:, pl.ds(0, LANES * (begin + 2))]), (tail_in, kept_ref)), sems, 1)
     fill_counts(sz, part, nbr2, pres2, nbr3, pres3, counts)
     store = start_copies(((counts, counts_out),), sems, 3)
-    mean_tiles(sz, begin, tiles, feat_ref, nbr_ref, pres_ref, mean_ref, tail_ref, base_ref, code_ref, count_ref)
+    fill_own(sz, feat_ref, self_ref, self_tail, (48 * sz.own + sz.n_a) // LANES)
+    last = LANES * (tiles + 2)
+    mean_ref[:, last:] = jnp.zeros((sz.main, LANES * sz.tiles_all - last), BF)
+    tail_ref[...] = jnp.zeros_like(tail_ref)
+    mean_tiles(sz, begin, tiles, feat_ref, nbr_ref, pres_ref, links_ref, present_ref, mean_ref, tail_ref, base_ref, code_ref, count_ref)
     wait_all(loads)
-    tail_ref[:begin, :] = kept_ref[:begin, :]
-    own_pair(sz, sz.ranges(part)[:1], feat_ref, mean_ref, tail_ref, own_ref)
+    tail_ref[: begin + 2, :] = kept_ref[: begin + 2, :]
+    own_pair(sz, sz.ranges(part)[:1], self_ref, mean_ref, tail_ref, own_ref)
     store += start_copies(((own_ref, own_a),), sems)
     for r, out in ((1, a1), (2, a2), (3, a3)):
-        pack_pair(sz, sz.second_ranges(part ^ r), feat_ref, base_ref, mean_ref, tail_ref, turn_ref, out)
+        pack_pair(sz, sz.second_ranges(part ^ r), self_ref, self_tail, mean_ref, tail_ref, turn_ref, out)
     wait_all(store)
 
 
 def mean_messages(sz, features, neighbors, present, mean, tail, links):
-    counts = (sz.count_rows * (sz.tiles_b + sz.own // LANES), LANES)
+    counts = (sz.count_rows * (sz.tiles_b + 2 * (sz.own // LANES)), LANES)
     return call(
         functools.partial(mean_kernel, sz),
         [((2 * sz.hold, sz.n_a), BF), (counts, BF)] + [((sz.main, sz.message_a), BF)] * 3,
-        mean_scratch(sz, sz.low // LANES, neighbors.shape[0]) + [((2 * sz.hold, sz.n_a), BF), (tail.shape, F32), (counts, BF)],
+        mean_scratch(sz, sz.low // LANES + 1, neighbors.shape[0]) + [((2 * sz.hold, sz.n_a), BF), (tail.shape, F32), (counts, BF)],
         MEAN_MIB,
         features,
         neighbors,
@@ -454,24 +527,20 @@
     spots = lax.broadcasted_iota(jnp.int32, (256, LANES), 0).astype(F32).astype(BF)
     blocks = []
     for first in range(0, rows, 256):
+        size = min(256, rows - first)
         place = local - first
-        place = jnp.where((place >= 0) & (place < 256), place, -1).astype(F32)
-        counts = jnp.zeros((256, LANES), BF)
+        place = jnp.where((place >= 0) & (place < size), place, -1).astype(F32)
+        counts = jnp.zeros((size, LANES), BF)
         for slot in range(local.shape[0]):
             row = jnp.broadcast_to(place[slot : slot + 1], (16, LANES)).astype(BF)
-            row = jnp.concatenate([row] * 16, 0)
-            counts = counts + jnp.where(row == spots, jnp.bfloat16(1.0), jnp.bfloat16(0.0))
+            row = jnp.concatenate([row] * (size // 16), 0)
+            counts = counts + jnp.where(row == spots[:size], jnp.bfloat16(1.0), jnp.bfloat16(0.0))
         blocks.append(counts)
     return jnp.concatenate(blocks, 0)
 
 
 def slot_totals(present):
     return jnp.maximum(jnp.sum(present.astype(F32), 0, keepdims=True), 1.0)
-
-
-def a_window(sz, part, tile):
-    first = 4 * sz.b_start(part) + 4 * LANES * tile - LANES - sz.a_start(part)
-    return aligned(jnp.clip(first, 0, sz.n_a - WINDOW))
 
 
 def counts_tile(sz, links, marks, start, at, counts):
@@ -481,14 +550,18 @@
 
 
 def fill_counts(sz, part, nbr2, pres2, nbr3, pres3, counts):
+    tiles = nbr2.shape[1] // LANES
     for tile in range(sz.tiles_b):
-        columns = sz.b_columns(part, tile)
-        start = sz.a_start(part) + a_window(sz, part, tile)
-        counts_tile(sz, nbr2[:, columns], pres2[:, columns], start, sz.count_rows * tile, counts)
+        column = 4 * sz.own // LANES * part + tile
+        start = sz.a_row(part) + 4 * LANES * tile
+        links, marks = half_columns(nbr2, column, tiles, 0), half_columns(pres2, column, tiles, 0)
+        counts_tile(sz, links, marks, start, sz.count_rows * tile, counts)
     for tile in range(sz.own // LANES):
         columns = pl.ds(aligned(sz.own * part + LANES * tile), LANES)
         at = sz.count_rows * (sz.tiles_b + tile)
-        counts_tile(sz, nbr3[:, columns], pres3[:, columns], sz.b_start(part), at, counts)
+        counts_tile(sz, nbr3[:, columns], pres3[:, columns], sz.b_row(part), at, counts)
+        at += sz.count_rows * (sz.own // LANES)
+        counts_tile(sz, nbr2[:, columns], pres2[:, columns], sz.b_row(part), at, counts)
 
 
 def tile_counts(sz, counts, tile):
@@ -572,9 +645,9 @@
 
 
 def seeds_kernel(
-    sz, own_b, packed, s1, s2, s3, passed, nbr2_in, pres2_in, serve_in, take_in, live_in,
-    low_out, high_out, window_out, sent,
-    xb, pack, m1, m2, m3, p3, nbr2, pres2, window_ref, serve_rows, take_rows, live_rows, low, high, turn_ref, w1_ref, w2_ref, states, sems,
+    sz, own_b, packed, s1, s2, s3, passed, counts_in, serve_in, take_in, live_in,
+    low_out, high_out, sent,
+    xb, pack, m1, m2, m3, p3, window_ref, serve_rows, take_rows, live_rows, low, high, turn_ref, w1_ref, w2_ref, states, sems,
 ):
     part = lax.axis_index("col")
     own, hid, n_b, group, hold, at = sz.own, sz.hid, sz.n_b, sz.group, sz.hold, sz.at
@@ -587,8 +660,7 @@
             (s2, m2),
             (s3, m3),
             (own_b, xb),
-            (nbr2_in.at[:, pl.ds(aligned(own * part), own)], nbr2),
-            (pres2_in.at[:, pl.ds(aligned(own * part), own)], pres2),
+            (counts_in.at[sz.seed_window(), :], window_ref),
             (serve_in, serve_rows),
             (take_in, take_rows),
             (live_in, live_rows),
@@ -630,10 +702,6 @@
 
     stores = start_copies((piece(n_mid, at["states"] - n_mid),), sems, 11)
     wait_all(copies[4:])
-    for tile in range(own // LANES):
-        lanes = slice(LANES * tile, LANES * (tile + 1))
-        counts_tile(sz, nbr2[:, lanes], pres2[:, lanes], sz.b_start(part), sz.count_rows * tile, window_ref)
-    stores += start_copies(((window_ref, window_out),), sems, 18)
     low[:hold, :n_mid] = xb[:hold, :]
     low[4 * hold : 5 * hold, :n_mid] = xb[hold:, :]
     for r, message in ((1, m1), (2, m2), (3, m3)):
@@ -706,7 +774,7 @@
     )
 
 
-def seeds_forward(sz, messages, nbr2, pres2, tables):
+def seeds_forward(sz, messages, counts, tables):
     hid = sz.hid
     tail = (sz.main, LANES * sz.blocks)
     return call(
@@ -714,7 +782,6 @@
         [
             ((hid, sz.low_lanes), BF),
             ((hid + 8, sz.high_lanes), F32),
-            ((sz.count_rows * (sz.own // LANES), LANES), BF),
             ((4 * sz.slots, 2 * hid), BF),
         ],
         [
@@ -724,8 +791,6 @@
             ((sz.main, sz.full_b), BF),
             ((sz.main, sz.message_b), BF),
             (tail, BF),
-            ((nbr2.shape[0], sz.own), jnp.int32),
-            ((nbr2.shape[0], sz.own), jnp.int32),
             ((sz.count_rows * (sz.own // LANES), LANES), BF),
             *[(item.shape, jnp.int32) for item in tables],
             ((hid, sz.low_lanes), BF),
@@ -737,13 +802,12 @@
         ],
         SEEDS_MIB,
         *messages,
-        nbr2,
-        pres2,
+        counts,
         *tables,
-        far_in=(0, 1, 6, 7, 8, 9, 10),
+        far_in=(0, 1, 6, 7, 8, 9),
         loose=(2, 3, 4, 5),
         micros=4,
-        far_out=(0, 1, 2),
+        far_out=(0, 1),
         copies=19,
     )
 
@@ -805,13 +869,13 @@
         states[hid:, lanes] = lower
         return carry
 
-    lax.fori_loop(0, n_a // LANES, forward_step, 0, unroll=2)
+    lax.fori_loop(0, n_a // LANES, forward_step, 0, unroll=3)
     wait_all(copies[9:])
     turned2 = low[:, at["turned2"] : at["turned2"] + 2 * hid]
     for tile in range(sz.tiles_b):
         lanes = slice(LANES * tile, LANES * (tile + 1))
         window, totals = tile_counts(sz, counts, tile)
-        total = dot(states[:, pl.ds(a_window(sz, part, tile), WINDOW)], window, (1, 0))
+        total = dot(states[:, 4 * LANES * tile : 4 * LANES * tile + WINDOW], window, (1, 0))
         average = ((total[:hid] + total[hid:]) / totals).astype(BF)
         inputs2[:, lanes] = join_inputs(sz, low[:, at["states"] + LANES * tile : at["states"] + LANES * (tile + 1)], average)
     result2[...] = dot(turned2, inputs2[...], (1, 0))
@@ -864,7 +928,7 @@
     part_ref[:hid, at["grad_b"] : at["grad_b"] + n_b] = own_part
     for tile in range(sz.tiles_b):
         window, totals = tile_counts(sz, counts, tile)
-        lanes = pl.ds(a_window(sz, part, tile), WINDOW)
+        lanes = slice(4 * LANES * tile, 4 * LANES * tile + WINDOW)
         grad_a[:, lanes] = grad_a[:, lanes] + spread(sz, average_part[:, LANES * tile : LANES * (tile + 1)] / totals, window)
     rows, few = pl.ds(0, hid + 8), pl.ds(0, sz.head + 32)
     split = at["g2"]
@@ -885,7 +949,7 @@
         low_grad[:, lanes] = norm_backward(grad_a[:, lanes], result1[:, lanes], scale1[:, lanes])
         return carry
 
-    lax.fori_loop(0, n_a // LANES, backward_step, 0, unroll=2)
+    lax.fori_loop(0, n_a // LANES, backward_step, 0, unroll=3)
     part_ref[:hid, at["g1"] : at["g1"] + hid] = dot(xa[...], low_grad[...], (1, 1))
     part_ref[sz.head : sz.head + 16, g3 : g3 + hid] = row_sums(low_grad[...])
     stores += start_copies(
@@ -962,7 +1026,7 @@
             (part_in.at[:, pl.ds(split + n_b, own)], partial.at[:, pl.ds(split + n_b, own)]),
             (high_in.at[:, lanes], high.at[:, lanes]),
             (low_in.at[:, pl.ds(at["weight2"], 2 * hid)], weight_ref),
-            (counts_in.at[pl.ds(0, sz.count_rows * (own // LANES)), :], window_ref),
+            (counts_in.at[sz.seed_window(), :], window_ref),
             (part_in.at[:, pl.ds(split, n_b)], partial.at[:, pl.ds(split, n_b)]),
             (high_in.at[:, pl.ds(0, n_mid)], high.at[:, pl.ds(0, n_mid)]),
             (low_in.at[:, pl.ds(0, n_mid)], x_ref),
@@ -1209,12 +1273,10 @@
     later, s3, counts = lax.optimization_barrier((s2, s3, counts))
     passed = swap(later, "col", 4, 1)
     tables = (serve_rows, take_seed, fetch_live[None, :])
-    low, high, window, rows = seeds_forward(
-        sz, (own_b, packed, s1, s2, s3, passed), neighbors_two, present_two, tables
-    )
+    low, high, rows = seeds_forward(sz, (own_b, packed, s1, s2, s3, passed), counts, tables)
     received = lax.all_to_all(rows, ("dp", "col"), split_axis=0, concat_axis=0, tiled=True)
     partial = rest_step(sz, low, high, counts, (own_a, *means, s1, s2, s3), labels[None, :], seed_weight[None, :], head_bias[None, :])
-    keep0, keep1, send = seeds_backward(sz, tables, received, low, high, window, partial)
+    keep0, keep1, send = seeds_backward(sz, tables, received, low, high, counts, partial)
     other = swap(send, "col", 4, 1)
     own = merged(keep0, other[: sz.pay]).astype(BF)
     far = merged(keep1, other[sz.pay :]).astype(BF)

time: 76.7 us -> 74.9 us (0.977)
  Pallas kernels: 33.6 us -> 32.4 us
  waiting for transfers between devices: 18.9 us -> 17.8 us
    pallas_call x7, Pallas kernels: 33.6 us -> 32.4 us  [call(): pl.pallas_call(kernel, in_specs=[free if i in loose else far if i in far_...]
  transfers between devices with their start and end apart: 16 -> 16, of which waited for: 8 -> 10; matrix products, arithmetic and copies ran while one was open for 1% -> 1% of each run, Pallas kernels for 31% -> 30%
where the time goes in v5:
time: 74.9 us; the launch traced here: 74.6 us
  Pallas kernels  32.4 us (43%)
  starting transfers between devices  22.3 us (30%)
  waiting for transfers between devices  17.8 us (24%)
  between operations  1.08 us (1%)
    pallas_call x7, Pallas kernels, call(): pl.pallas_call(kernel, in_specs=[free if i in loose else far if i in far_...  32.4 us
    ppermute x14, waiting for transfers between devices, swap(): return lax.ppermute(value, axis, [(i, i ^ bit) for i in range(count)])  14.8 us
    ppermute x14, starting transfers between devices, swap(): return lax.ppermute(value, axis, [(i, i ^ bit) for i in range(count)])  13.3 us
    all_to_all x1, starting transfers between devices, shards(): lax.all_to_all(rows, ('dp', 'col'), split_axis=0, concat_axis=0, tiled=True)  6.25 us
    ppermute x1, waiting for transfers between devices, shards(): lax.ppermute(far, ('dp', 'col'), pair)  2.95 us
    ppermute x1, starting transfers between devices, shards(): lax.ppermute(far, ('dp', 'col'), pair)  2.73 us
  transfers between devices with their start and end apart: 16, of which 10 were waited for; matrix products, arithmetic and copies ran while one was open for 1% of the time, Pallas kernels for 30%

profile of v5, /device:TPU:0, one launch (start us, length us, event | category | flops | bytes accessed | tf_op | source)
XLA Modules:
  0.0 74.6 jit_solution(13837271820607043638)
XLA Ops:
  0.7 4.0 %shard_map.394 = (bf16[64,768]{1,0:T(8,128)(2,1)}, f32[456,128]{1,0:T(8,128)}, bf16[24,2432]{1,0:T(8,128)(2,1)}, f32[72,128]{1,0:T(8,128)}, bf16[24,4608]{1,0:T(...) custom-call(bf16[25,32768]{1,0:T(8,128)(2,1)} %feat_ref.1, s32[5,8192]{1,0:T(8,128)} %nbr_ref.1, ...), custom_call_target="tpu_custom_call" | custom-call | flops 4000000000 | bytes 1 | tf_op jit(solution)/shard_map/pallas_call | solution.py:47
  4.8 2.5 %collective-permute-start.2 = (bf16[24,2176]{1,0:T(8,128)(2,1)S(1)}, bf16[24,2176]{1,0:T(8,128)(2,1)S(1)}, u32[]{:S(2)}, u32[]{:S(2)}) collective-permute-start(bf16[24,2176]{1,0:T(8,128)(2,1)S(1)} %get-tuple-element.76), channel_id=1, source_target_pairs={{0,3},{1,2},{2,1},{3,0},{4,7},{5,6},{6,5},{7,4},{8,11},{9,10},{10,... | collective-permute-start | bytes 313352 | tf_op jit(solution)/shard_map/ppermute | solution.py:1241
  7.3 0.7 collective-permute-start
  8.0 7.1 %shard_map.395 = (bf16[64,2688]{1,0:T(8,128)(2,1)}, bf16[4592,128]{1,0:T(8,128)(2,1)}, bf16[24,5120]{1,0:T(8,128)(2,1)S(1)}, bf16[24,5120]{1,0:T(8,128)(2,1)S(1)}, bf16[24,5120]{1,0:T(8,128)(2,1)S(1)}) custom-call(bf16[25,32768]{1,0:T(8,128)(2,1)S(1)} %copy-done, s32[5,8192]{1,0:T(8,128)S(1)} %copy-done.1, s32[5,8192]{1,0:T(8,128)S(1)} %copy-done.2, ...), custom_call_target="tpu_custom_call" | custom-call | flops 6000000000 | bytes 1 | tf_op jit(solution)/shard_map/pallas_call | solution.py:47
  15.2 0.3 collective-permute-done.1.s2.e2
  15.5 0.5 collective-permute-start.4
  16.0 2.3 %collective-permute-start.5 = (bf16[24,5120]{1,0:T(8,128)(2,1)S(1)}, bf16[24,5120]{1,0:T(8,128)(2,1)S(1)}, u32[]{:S(2)}, u32[]{:S(2)}) collective-permute-start(bf16[24,5120]{1,0:T(8,128)(2,1)S(1)} %get-tuple-element.86), channel_id=1, source_target_pairs={{0,2},{1,3},{2,0},{3,1},{4,6},{5,7},{6,4},{7,5},{8,10},{9,11},{10,... | collective-permute-start | bytes 737288 | tf_op jit(solution)/shard_map/ppermute | solution.py:1241
  18.3 4.6 %shard_map.396 = (bf16[256,3968]{1,0:T(8,128)(2,1)}, f32[264,1152]{1,0:T(8,128)}, bf16[256,512]{1,0:T(8,128)(2,1)}) custom-call(bf16[64,768]{1,0:T(8,128)(2,1)} %get-tuple-element.66.own_b, f32[456,128]{1,0:T(8,128)} %get-tuple-element.67.packed, bf16[24,4608]{1,0:T(8,128)(2,1)S(1)} %collective-permute-done.s1.e1, ...), custom_call_target="tpu_custom_call" | custom-call | flops 4000000000 | bytes 1 | tf_op jit(solution)/shard_map/pallas_call | solution.py:47
  22.9 6.3 %all-to-all-start = ((bf16[32,8,512]{2,1,0:T(8,128)(2,1)}), bf16[32,8,512]{2,1,0:T(8,128)(2,1)S(1)}, u32[]{:S(2)}, u32[]{:S(2)}) async-start(bf16[32,8,512]{2,1,0:T(8,128)(2,1)} %bitcast.3), calls=%async_computation | async-start | bytes 524288 | tf_op jit(solution)/shard_map/all_to_all | solution.py:1277
  29.1 0.1 collective-permute-done.6.a3
  29.2 10.9 %shard_map.397.part_in = f32[264,2048]{1,0:T(8,128)} custom-call(bf16[256,3968]{1,0:T(8,128)(2,1)} %get-tuple-element.82.low_in, f32[264,1152]{1,0:T(8,128)} %get-tuple-element.83.high_in, bf16[4592,128]{1,0:T(8,128)(2,1)} %get-tuple-element.80.counts_in, bf16[64,2688]{1,0:T(8,128)(2,1)} %get-tuple-element.84.own_a, ...), custom_call_target="tpu_custom_call" | custom-call | flops 14000000000 | bytes 1 | tf_op jit(solution)/shard_map/pallas_call | solution.py:47
  40.2 3.5 %shard_map.398 = (bf16[448,128]{1,0:T(8,128)(2,1)S(1)}, bf16[448,128]{1,0:T(8,128)(2,1)S(1)}, bf16[896,128]{1,0:T(8,128)(2,1)S(1)}) custom-call(s32[8,8]{1,0:T(8,128)} %serve_in.3, s32[8,8]{1,0:T(8,128)} %take_in.3, s32[1,8]{1,0:T(1,128)} %bitcast.44, bf16[256,512]{1,0:T(8,128)(2,1)S(1)} %bitcast.25, bf16[256,3968]{1,0:T(8,128)(2,1)} %get-tuple-element.82.low_in, ...), custom_call_target="tpu_custom_call" | custom-call | flops 3000000000 | bytes 1 | tf_op jit(solution)/shard_map/pallas_call | solution.py:47
  43.8 0.4 collective-permute-start.7
  44.2 1.1 %collective-permute-done.7 = bf16[896,128]{1,0:T(8,128)(2,1)S(1)} collective-permute-done((bf16[896,128]{1,0:T(8,128)(2,1)S(1)}, bf16[896,128]{1,0:T(8,128)(2,1)S(1)}, u32[]{:S(2)}, u32[]{:S(2)}) %collective-permute-start.7) | collective-permute-done | bytes 229408 | tf_op jit(solution)/shard_map/ppermute | solution.py:1241
  45.4 2.7 %collective-permute-start.10 = (bf16[448,128]{1,0:T(8,128)(2,1)S(1)}, bf16[448,128]{1,0:T(8,128)(2,1)S(1)}, u32[]{:S(2)}, u32[]{:S(2)}) collective-permute-start(bf16[448,128]{1,0:T(8,128)(2,1)S(1)} %get-tuple-element.115), channel_id=1, source_target_pairs={{0,6},{1,7},{2,4},{3,5},{4,2},{5,3},{6,0},{7,1},{8,14},{9,15},{10,... | collective-permute-start | bytes 344072 | tf_op jit(solution)/shard_map/ppermute | solution.py:1285
  48.2 0.4 collective-permute-start.8
  48.6 0.4 collective-permute-start.9
  49.0 3.0 %collective-permute-done.10 = bf16[448,128]{1,0:T(8,128)(2,1)S(1)} collective-permute-done((bf16[448,128]{1,0:T(8,128)(2,1)S(1)}, bf16[448,128]{1,0:T(8,128)(2,1)S(1)}, u32[]{:S(2)}, u32[]{:S(2)}) %collective-permute-start.10) | collective-permute-done | bytes 114720 | tf_op jit(solution)/shard_map/ppermute | solution.py:1285
  52.0 2.4 %collective-permute-done.8 = bf16[448,128]{1,0:T(8,128)(2,1)S(1)} collective-permute-done((bf16[448,128]{1,0:T(8,128)(2,1)S(1)}, bf16[448,128]{1,0:T(8,128)(2,1)S(1)}, u32[]{:S(2)}, u32[]{:S(2)}) %collective-permute-start.8) | collective-permute-done | bytes 114720 | tf_op jit(solution)/shard_map/ppermute | solution.py:1241
  54.3 0.3 collective-permute-done.9
  54.7 1.6 %collective-permute-start.11 = (bf16[448,128]{1,0:T(8,128)(2,1)S(1)}, bf16[448,128]{1,0:T(8,128)(2,1)S(1)}, u32[]{:S(2)}, u32[]{:S(2)}) collective-permute-start(bf16[448,128]{1,0:T(8,128)(2,1)S(1)} %fusion.1), channel_id=1, source_target_pairs={{0,8},{4,12},{8,0},{12,4},{16,24},{20,28},{24,16},{28,20},{1,9},{5... | collective-permute-start | bytes 344072 | tf_op jit(solution)/shard_map/ppermute | solution.py:1241
  56.3 3.2 %collective-permute-done.11 = bf16[448,128]{1,0:T(8,128)(2,1)S(1)} collective-permute-done((bf16[448,128]{1,0:T(8,128)(2,1)S(1)}, bf16[448,128]{1,0:T(8,128)(2,1)S(1)}, u32[]{:S(2)}, u32[]{:S(2)}) %collective-permute-start.11) | collective-permute-done | bytes 114720 | tf_op jit(solution)/shard_map/ppermute | solution.py:1241
  59.5 0.1 fusion
  59.6 2.8 %collective-permute-start.12 = (bf16[448,128]{1,0:T(8,128)(2,1)S(1)}, bf16[448,128]{1,0:T(8,128)(2,1)S(1)}, u32[]{:S(2)}, u32[]{:S(2)}) collective-permute-start(bf16[448,128]{1,0:T(8,128)(2,1)S(1)} %fusion), channel_id=1, source_target_pairs={{0,16},{4,20},{8,24},{12,28},{16,0},{20,4},{24,8},{28,12},{1,17},{... | collective-permute-start | bytes 344072 | tf_op jit(solution)/shard_map/ppermute | solution.py:1241
  62.4 4.9 %collective-permute-done.12 = bf16[448,128]{1,0:T(8,128)(2,1)S(1)} collective-permute-done((bf16[448,128]{1,0:T(8,128)(2,1)S(1)}, bf16[448,128]{1,0:T(8,128)(2,1)S(1)}, u32[]{:S(2)}, u32[]{:S(2)}) %collective-permute-start.12) | collective-permute-done | bytes 114720 | tf_op jit(solution)/shard_map/ppermute | solution.py:1241
  67.3 0.1 add_reduce-precision_fusion.grad
  67.6 1.5 %shard_map.399 = (f32[25,2,256]{2,1,0:T(2,128)}, f32[2,64,256]{2,1,0:T(8,128)}, f32[47,2,64]{2,1,0:T(2,128)}, f32[2,64]{1,0:T(2,128)}, f32[1,47]{1,0:T(1,128)}, ...) custom-call(f32[448,128]{1,0:T(8,128)S(1)} %add_reduce-precision_fus, ...), custom_call_target="tpu_custom_call" | custom-call | flops 1000000000 | bytes 1 | tf_op jit(solution)/shard_map/pallas_call | solution.py:47
  69.0 1.2 %collective-permute-done.13 = f32[8,128]{1,0:T(8,128)S(1)} collective-permute-done((f32[8,128]{1,0:T(8,128)S(1)}, f32[8,128]{1,0:T(8,128)S(1)}, u32[]{:S(2)}, u32[]{:S(2)}) %collective-permute-start.13) | collective-permute-done | bytes 4128 | tf_op jit(solution)/shard_map/ppermute | solution.py:1241
  70.2 1.7 %collective-permute-start.14 = (f32[8,128]{1,0:T(8,128)S(1)}, f32[8,128]{1,0:T(8,128)S(1)}, u32[]{:S(2)}, u32[]{:S(2)}) collective-permute-start(f32[8,128]{1,0:T(8,128)S(1)} %add.31.own), channel_id=1, source_target_pairs={{0,2},{1,3},{2,0},{3,1},{4,6},{5,7},{6,4},{7,5},{8,10},{9,11},{10,... | collective-permute-start | bytes 12296 | tf_op jit(solution)/shard_map/ppermute | solution.py:1241
  71.9 0.6 fusion.2
  72.5 1.3 %collective-permute-done.14.far = f32[8,128]{1,0:T(8,128)S(1)} collective-permute-done((f32[8,128]{1,0:T(8,128)S(1)}, f32[8,128]{1,0:T(8,128)S(1)}, u32[]{:S(2)}, u32[]{:S(2)}) %collective-permute-start.14) | collective-permute-done | bytes 4128 | tf_op jit(solution)/shard_map/ppermute | solution.py:1241
  73.8 0.8 %shard_map.400 = (f32[25,2,256]{2,1,0:T(2,128)}, f32[2,64,256]{2,1,0:T(8,128)}, f32[47,2,64]{2,1,0:T(2,128)}, f32[2,64]{1,0:T(2,128)}, f32[1,47]{1,0:T(1,128)}, /*index=5*/f32[2,5]{1,0:T(2,128)}) custom-call(f32[8,128]{1,0:T(8,128)S(1)} %add.31.own, f32[8,128]{1,0:T(8,128)S(1)} %collective-permute-done.14.far, f32[25,2,256]{2,1,0:T(2,128)S(1)} %bitcast.30, ...), custom_call_target="tpu_custom_call" | custom-call | flops 1000000000 | bytes 1 | tf_op jit(solution)/shard_map/pallas_call | solution.py:47
  (57 shorter events, 0.3 us)
Async XLA Ops:
  0.7 7.3 %copy-start = (bf16[25,32768]{1,0:T(8,128)(2,1)S(1)}, bf16[25,32768]{1,0:T(8,128)(2,1)}, u32[]{:S(2)}) copy-start(bf16[25,32768]{1,0:T(8,128)(2,1)} %feat_ref.1) | copy-start | bytes 4915204
  4.8 10.4 %collective-permute-start.2 = (bf16[24,2176]{1,0:T(8,128)(2,1)S(1)}, bf16[24,2176]{1,0:T(8,128)(2,1)S(1)}, u32[]{:S(2)}, u32[]{:S(2)}) collective-permute-start(bf16[24,2176]{1,0:T(8,128)(2,1)S(1)} %get-tuple-element.76), channel_id=1, source_target_pairs={{0,3},{1,2},{2,1},{3,0},{4,7},{5,6},{6,5},{7,4},{8,11},{9,10},{10,... | collective-permute-start | bytes 313352 | tf_op jit(solution)/shard_map/ppermute | solution.py:1241
  7.3 8.2 %collective-permute-start = (bf16[24,4608]{1,0:T(8,128)(2,1)S(1)}, bf16[24,4608]{1,0:T(8,128)(2,1)S(1)}, u32[]{:S(2)}, u32[]{:S(2)}) collective-permute-start(bf16[24,4608]{1,0:T(8,128)(2,1)S(1)} %get-tuple-element.68), channel_id=1, source_target_pairs={{0,1},{1,0},{2,3},{3,2},{4,5},{5,4},{6,7},{7,6},{8,9},{9,8},{10,11... | collective-permute-start | bytes 663560 | tf_op jit(solution)/shard_map/ppermute | solution.py:1241
  7.9 7.6 %collective-permute-start.1 = (bf16[24,4608]{1,0:T(8,128)(2,1)S(1)}, bf16[24,4608]{1,0:T(8,128)(2,1)S(1)}, u32[]{:S(2)}, u32[]{:S(2)}) collective-permute-start(bf16[24,4608]{1,0:T(8,128)(2,1)S(1)} %get-tuple-element.75), channel_id=1, source_target_pairs={{0,2},{1,3},{2,0},{3,1},{4,6},{5,7},{6,4},{7,5},{8,10},{9,11},{10,... | collective-permute-start | bytes 663560 | tf_op jit(solution)/shard_map/ppermute | solution.py:1241
  15.5 2.8 %collective-permute-start.3 = (bf16[24,4608]{1,0:T(8,128)(2,1)S(1)}, bf16[24,4608]{1,0:T(8,128)(2,1)S(1)}, u32[]{:S(2)}, u32[]{:S(2)}) collective-permute-start(bf16[24,4608]{1,0:T(8,128)(2,1)S(1)} %collective-permute-done.1.s2.e2), channel_id=1, source_target_pairs={{0,1},{1,0},{2,3},{3,2},{4,5},{5,4},{6,7},{7,6},{8,9},{9,8},{10,11... | collective-permute-start | bytes 663560 | tf_op jit(solution)/shard_map/ppermute | solution.py:1241
  15.5 13.6 %collective-permute-start.4 = (bf16[24,5120]{1,0:T(8,128)(2,1)S(1)}, bf16[24,5120]{1,0:T(8,128)(2,1)S(1)}, u32[]{:S(2)}, u32[]{:S(2)}) collective-permute-start(bf16[24,5120]{1,0:T(8,128)(2,1)S(1)} %get-tuple-element.85), channel_id=1, source_target_pairs={{0,1},{1,0},{2,3},{3,2},{4,5},{5,4},{6,7},{7,6},{8,9},{9,8},{10,11... | collective-permute-start | bytes 737288 | tf_op jit(solution)/shard_map/ppermute | solution.py:1241
  16.0 13.1 %collective-permute-start.5 = (bf16[24,5120]{1,0:T(8,128)(2,1)S(1)}, bf16[24,5120]{1,0:T(8,128)(2,1)S(1)}, u32[]{:S(2)}, u32[]{:S(2)}) collective-permute-start(bf16[24,5120]{1,0:T(8,128)(2,1)S(1)} %get-tuple-element.86), channel_id=1, source_target_pairs={{0,2},{1,3},{2,0},{3,1},{4,6},{5,7},{6,4},{7,5},{8,10},{9,11},{10,... | collective-permute-start | bytes 737288 | tf_op jit(solution)/shard_map/ppermute | solution.py:1241
  18.3 10.9 %collective-permute-start.6 = (bf16[24,5120]{1,0:T(8,128)(2,1)S(1)}, bf16[24,5120]{1,0:T(8,128)(2,1)S(1)}, u32[]{:S(2)}, u32[]{:S(2)}) collective-permute-start(bf16[24,5120]{1,0:T(8,128)(2,1)S(1)} %get-tuple-element.87), channel_id=1, source_target_pairs={{0,3},{1,2},{2,1},{3,0},{4,7},{5,6},{6,5},{7,4},{8,11},{9,10},{10,... | collective-permute-start | bytes 737288 | tf_op jit(solution)/shard_map/ppermute | solution.py:1241
  22.9 17.3 %all-to-all-start = ((bf16[32,8,512]{2,1,0:T(8,128)(2,1)}), bf16[32,8,512]{2,1,0:T(8,128)(2,1)S(1)}, u32[]{:S(2)}, u32[]{:S(2)}) async-start(bf16[32,8,512]{2,1,0:T(8,128)(2,1)} %bitcast.3), calls=%async_computation | async-start | bytes 524288 | tf_op jit(solution)/shard_map/all_to_all | solution.py:1277
  43.6 23.8 %copy-start.5 = (f32[2,64,256]{2,1,0:T(8,128)S(1)}, f32[2,64,256]{2,1,0:T(8,128)}, u32[]{:S(2)}) copy-start(f32[2,64,256]{2,1,0:T(8,128)} %f2.1) | copy-start | bytes 393220
  43.7 23.8 %copy-start.6 = (f32[2,64,256]{2,1,0:T(8,128)S(1)}, f32[2,64,256]{2,1,0:T(8,128)}, u32[]{:S(2)}) copy-start(f32[2,64,256]{2,1,0:T(8,128)} %s2_.1) | copy-start | bytes 393220
  43.7 23.8 %copy-start.7 = (f32[2,64,256]{2,1,0:T(8,128)S(1)}, f32[2,64,256]{2,1,0:T(8,128)}, u32[]{:S(2)}) copy-start(f32[2,64,256]{2,1,0:T(8,128)} %w2.3) | copy-start | bytes 393220
  43.7 23.8 %copy-start.8 = (f32[2,25,256]{2,0,1:T(2,128)S(1)}, f32[2,25,256]{2,0,1:T(2,128)}, u32[]{:S(2)}) copy-start(f32[2,25,256]{2,0,1:T(2,128)} %param.44) | copy-start | bytes 153604
  43.7 23.8 %copy-start.9 = (f32[2,25,256]{2,0,1:T(2,128)S(1)}, f32[2,25,256]{2,0,1:T(2,128)}, u32[]{:S(2)}) copy-start(f32[2,25,256]{2,0,1:T(2,128)} %param.49) | copy-start | bytes 153604
  43.7 23.8 %copy-start.10 = (f32[2,25,256]{2,0,1:T(2,128)S(1)}, f32[2,25,256]{2,0,1:T(2,128)}, u32[]{:S(2)}) copy-start(f32[2,25,256]{2,0,1:T(2,128)} %param.39) | copy-start | bytes 153604
  43.7 23.8 %copy-start.11 = (f32[2,64,47]{1,0,2:T(2,128)S(1)}, f32[2,64,47]{1,0,2:T(2,128)}, u32[]{:S(2)}) copy-start(f32[2,64,47]{1,0,2:T(2,128)} %param.46) | copy-start | bytes 72196
  43.7 23.8 %copy-start.12 = (f32[2,64,47]{1,0,2:T(2,128)S(1)}, f32[2,64,47]{1,0,2:T(2,128)}, u32[]{:S(2)}) copy-start(f32[2,64,47]{1,0,2:T(2,128)} %param.51) | copy-start | bytes 72196
  43.7 23.8 %copy-start.13 = (f32[2,64,47]{1,0,2:T(2,128)S(1)}, f32[2,64,47]{1,0,2:T(2,128)}, u32[]{:S(2)}) copy-start(f32[2,64,47]{1,0,2:T(2,128)} %param.41) | copy-start | bytes 72196
  43.8 23.8 %copy-start.16 = (f32[2,64]{1,0:T(2,128)S(1)}, f32[2,64]{1,0:T(2,128)}, u32[]{:S(2)}) copy-start(f32[2,64]{1,0:T(2,128)} %fh.1) | copy-start | bytes 1540
  43.8 23.8 %copy-start.17 = (f32[2,64]{1,0:T(2,128)S(1)}, f32[2,64]{1,0:T(2,128)}, u32[]{:S(2)}) copy-start(f32[2,64]{1,0:T(2,128)} %sh.1) | copy-start | bytes 1540
  43.8 23.8 %copy-start.18 = (f32[2,64]{1,0:T(2,128)S(1)}, f32[2,64]{1,0:T(2,128)}, u32[]{:S(2)}) copy-start(f32[2,64]{1,0:T(2,128)} %wh.3) | copy-start | bytes 1540
  43.8 23.8 %copy-start.19 = (f32[47]{0:T(128)S(1)}, f32[47]{0:T(128)}, u32[]{:S(2)}) copy-start(f32[47]{0:T(128)} %param.48) | copy-start | bytes 568
  43.8 23.8 %copy-start.20 = (f32[47]{0:T(128)S(1)}, f32[47]{0:T(128)}, u32[]{:S(2)}) copy-start(f32[47]{0:T(128)} %param.53) | copy-start | bytes 568
  43.8 23.8 %copy-start.21 = (f32[47]{0:T(128)S(1)}, f32[47]{0:T(128)}, u32[]{:S(2)}) copy-start(f32[47]{0:T(128)} %param.43) | copy-start | bytes 568
  43.8 1.6 %collective-permute-start.7 = (bf16[896,128]{1,0:T(8,128)(2,1)S(1)}, bf16[896,128]{1,0:T(8,128)(2,1)S(1)}, u32[]{:S(2)}, u32[]{:S(2)}) collective-permute-start(bf16[896,128]{1,0:T(8,128)(2,1)S(1)} %get-tuple-element.89), channel_id=1, source_target_pairs={{0,1},{1,0},{2,3},{3,2},{4,5},{5,4},{6,7},{7,6},{8,9},{9,8},{10,11... | collective-permute-start | bytes 688136 | tf_op jit(solution)/shard_map/ppermute | solution.py:1241
  45.4 6.5 %collective-permute-start.10 = (bf16[448,128]{1,0:T(8,128)(2,1)S(1)}, bf16[448,128]{1,0:T(8,128)(2,1)S(1)}, u32[]{:S(2)}, u32[]{:S(2)}) collective-permute-start(bf16[448,128]{1,0:T(8,128)(2,1)S(1)} %get-tuple-element.115), channel_id=1, source_target_pairs={{0,6},{1,7},{2,4},{3,5},{4,2},{5,3},{6,0},{7,1},{8,14},{9,15},{10,... | collective-permute-start | bytes 344072 | tf_op jit(solution)/shard_map/ppermute | solution.py:1285
  48.2 6.1 %collective-permute-start.8 = (bf16[448,128]{1,0:T(8,128)(2,1)S(1)}, bf16[448,128]{1,0:T(8,128)(2,1)S(1)}, u32[]{:S(2)}, u32[]{:S(2)}) collective-permute-start(bf16[448,128]{1,0:T(8,128)(2,1)S(1)} %get-tuple-element.115), channel_id=1, source_target_pairs={{0,2},{1,3},{2,0},{3,1},{4,6},{5,7},{6,4},{7,5},{8,10},{9,11},{10,... | collective-permute-start | bytes 344072 | tf_op jit(solution)/shard_map/ppermute | solution.py:1241
  48.6 6.0 %collective-permute-start.9 = (bf16[448,128]{1,0:T(8,128)(2,1)S(1)}, bf16[448,128]{1,0:T(8,128)(2,1)S(1)}, u32[]{:S(2)}, u32[]{:S(2)}) collective-permute-start(bf16[448,128]{1,0:T(8,128)(2,1)S(1)} %get-tuple-element.114), channel_id=1, source_target_pairs={{0,4},{4,0},{8,12},{12,8},{16,20},{20,16},{24,28},{28,24},{1,5},{5... | collective-permute-start | bytes 344072 | tf_op jit(solution)/shard_map/ppermute | solution.py:1241
  54.7 4.9 %collective-permute-start.11 = (bf16[448,128]{1,0:T(8,128)(2,1)S(1)}, bf16[448,128]{1,0:T(8,128)(2,1)S(1)}, u32[]{:S(2)}, u32[]{:S(2)}) collective-permute-start(bf16[448,128]{1,0:T(8,128)(2,1)S(1)} %fusion.1), channel_id=1, source_target_pairs={{0,8},{4,12},{8,0},{12,4},{16,24},{20,28},{24,16},{28,20},{1,9},{5... | collective-permute-start | bytes 344072 | tf_op jit(solution)/shard_map/ppermute | solution.py:1241
  59.6 7.7 %collective-permute-start.12 = (bf16[448,128]{1,0:T(8,128)(2,1)S(1)}, bf16[448,128]{1,0:T(8,128)(2,1)S(1)}, u32[]{:S(2)}, u32[]{:S(2)}) collective-permute-start(bf16[448,128]{1,0:T(8,128)(2,1)S(1)} %fusion), channel_id=1, source_target_pairs={{0,16},{4,20},{8,24},{12,28},{16,0},{20,4},{24,8},{28,12},{1,17},{... | collective-permute-start | bytes 344072 | tf_op jit(solution)/shard_map/ppermute | solution.py:1241
  69.0 1.2 %collective-permute-start.13 = (f32[8,128]{1,0:T(8,128)S(1)}, f32[8,128]{1,0:T(8,128)S(1)}, u32[]{:S(2)}, u32[]{:S(2)}) collective-permute-start(f32[8,128]{1,0:T(8,128)S(1)} %get-tuple-element.91), channel_id=1, source_target_pairs={{0,1},{1,0},{2,3},{3,2},{4,5},{5,4},{6,7},{7,6},{8,9},{9,8},{10,11... | collective-permute-start | bytes 12296 | tf_op jit(solution)/shard_map/ppermute | solution.py:1241
  70.2 3.6 %collective-permute-start.14 = (f32[8,128]{1,0:T(8,128)S(1)}, f32[8,128]{1,0:T(8,128)S(1)}, u32[]{:S(2)}, u32[]{:S(2)}) collective-permute-start(f32[8,128]{1,0:T(8,128)S(1)} %add.31.own), channel_id=1, source_target_pairs={{0,2},{1,3},{2,0},{3,1},{4,6},{5,7},{6,4},{7,5},{8,10},{9,11},{10,... | collective-permute-start | bytes 12296 | tf_op jit(solution)/shard_map/ppermute | solution.py:1241
  (6 other events, 43.7 us)

commit v6 on v5

--- a/solution.py
+++ b/solution.py
@@ -95,12 +95,12 @@
         self.slots = serve_rows.shape[0] * serve_rows.shape[1]
         self.slot = serve_rows.shape[1]
         self.dp = serve_rows.shape[0]
-        self.rows_one = 2 * 2 * self.hold
+        self.rows_one = 2 * 2 * self.feat
         self.rows_two = 4 * self.group
         self.at_three = self.rows_one + self.rows_two
-        self.misc = self.at_three + self.head
-        self.pay = self.misc + 16
-        self.blocks = -(-self.pay // self.main)
+        self.misc = self.at_three + self.classes
+        self.pay = -(-(self.misc + 5) // 16) * 16
+        self.blocks = -(-(self.misc + 3) // self.main)
         self.early = EARLY * LANES
         self.message_a = self.pair_lanes(self.n_a, self.n_a - self.early)
         self.message_b = self.pair_lanes(self.n_mid, self.n_mid + self.early)
@@ -377,7 +377,7 @@
 def first_kernel(
     sz, features, neighbors, present, w1_in, w2_in, w3_in, wh_in, own_b, packed, mean_out, tail_out, m1, m2, m3,
     feat_ref, nbr_ref, pres_ref, w1, w2, w3, wh, own_ref,
-    links_ref, present_ref, self_ref, self_tail, mean_ref, tail_ref, turn_ref, base_ref, code_ref, count_ref, one_ref, three_ref, pack, sems,
+    links_ref, present_ref, self_ref, self_tail, mean_ref, tail_ref, turn_ref, base_ref, code_ref, count_ref, pack, sems,
 ):
     part = lax.axis_index("col")
     rows = pl.ds(0, nbr_ref.shape[1])
@@ -392,29 +392,22 @@
         4,
     )
     wait_all(weights)
-    one_ref[...] = jnp.zeros_like(one_ref)
-    three_ref[...] = jnp.zeros_like(three_ref)
-    for s in range(2):
-        for f in range(sz.feat):
-            one_ref[s * sz.hold + f : s * sz.hold + f + 1, :] = w1[f, s : s + 1, :]
-        for c in range(sz.classes):
-            three_ref[c : c + 1, s * sz.group : (s + 1) * sz.group] = w3[c, s : s + 1, :]
-    at = 0
+    pack[sz.at_three :, :] = jnp.zeros((pack.shape[0] - sz.at_three, LANES), F32)
     for half in range(sz.hid // LANES):
-        pack[at : at + 2 * sz.hold, :] = one_ref[:, LANES * half : LANES * (half + 1)]
-        at += 2 * sz.hold
-    for half in range(sz.hid // LANES):
+        lanes = slice(LANES * half, LANES * (half + 1))
         for s in range(2):
-            pack[at : at + sz.group, :] = w2[s, :, LANES * half : LANES * (half + 1)]
-            at += sz.group
-    pack[at : at + sz.head, :] = three_ref[...]
+            for f in range(sz.feat):
+                at = sz.feat * (2 * half + s) + f
+                pack[at : at + 1, :] = w1[f, s : s + 1, lanes]
+            at = sz.rows_one + sz.group * (2 * half + s)
+            pack[at : at + sz.group, :] = w2[s, :, lanes]
+    for c in range(sz.classes):
+        for s in range(2):
+            at = sz.at_three + c
+            pack[at : at + 1, sz.group * s : sz.group * (s + 1)] = w3[c, s : s + 1, :]
     row = jnp.concatenate([wh[0:1, :], wh[1:2, :]], 1)
-    row_at = lax.broadcasted_iota(jnp.int32, (16, LANES), 0)
-    misc = jnp.zeros((16, LANES), F32)
     for i, piece in enumerate(three_parts(row)):
-        misc = jnp.where(row_at == i, piece, misc)
-    pack[sz.misc : sz.pay, :] = misc
-    pack[sz.pay :, :] = jnp.zeros((sz.main * sz.blocks - sz.pay, LANES), F32)
+        pack[sz.misc + i : sz.misc + i + 1, :] = piece
     store = start_copies(((pack, packed),), sems, 7)
     for block in range(sz.blocks):
         at = sz.message_b + LANES * block
@@ -460,8 +453,6 @@
             (hidden.shape, F32),
             ((2 * sz.hold, sz.n_mid), BF),
             *mean_scratch(sz, sz.tiles_b_all, slots),
-            ((2 * sz.hold, sz.hid), F32),
-            ((sz.head, LANES), F32),
             ((sz.main * sz.blocks, LANES), F32),
         ],
         FIRST_MIB,
@@ -667,6 +658,7 @@
         ),
         sems,
     )
+    w1_ref[...] = jnp.zeros_like(w1_ref)
     wait_all(copies[:4])
     for r, (message, first_lane) in enumerate(((None, 0), (m1, sz.message_b), (m2, sz.message_b), (p3, 0))):
         for block in range(sz.blocks if r else 0):
@@ -676,13 +668,15 @@
         for half in range(hid // LANES):
             lanes = slice(LANES * half, LANES * (half + 1))
             for s in range(2):
-                first = 2 * hold * half + hold * s
-                w1_ref[4 * hold * s + hold * r : 4 * hold * s + hold * (r + 1), lanes] = pack[first : first + hold, :]
+                first = sz.feat * (2 * half + s)
+                row = 4 * hold * s + hold * r
+                w1_ref[row : row + sz.feat, lanes] = pack[first : first + sz.feat, :]
             first = sz.rows_one + 2 * group * half
             row = pl.multiple_of(2 * group * shard, 2 * group)
             w2_ref[pl.ds(row, 2 * group), lanes] = pack[first : first + 2 * group, :]
-        low[: sz.head, pl.ds(aligned(at["turned3"] + 2 * group * shard), LANES)] = pack[sz.at_three : sz.misc, :].astype(BF)
-        misc = pack[sz.misc : sz.misc + 8, :]
+        third = jnp.concatenate([pack[sz.at_three : sz.misc, :], jnp.zeros((sz.head - sz.classes, LANES), F32)], 0)
+        low[: sz.head, pl.ds(aligned(at["turned3"] + 2 * group * shard), LANES)] = third.astype(BF)
+        misc = pack[sz.misc : sz.misc + 3, :]
         column = jnp.broadcast_to(misc[0:1] + misc[1:2] + misc[2:3], (LANES, LANES)).T
         row = pl.multiple_of(group * shard, group)
         for layer in range(2):
@@ -815,7 +809,7 @@
 def rest_kernel(
     sz, low_in, high_in, counts_in, own_a, a1, a2, a3, e1, e2, e3, labels_in, weighting_in, head_in, part_out,
     labels, weighting, head_bias, low, xa, bias, counts, xo, c1, c2, c3, turn_ref,
-    states, states2, result1, scale1, inputs2, result2, scale2, grad_a, low_grad, part_ref, sems,
+    states, states2, result1, slope1, scale1, inputs2, result2, scale2, grad_a, low_grad, part_ref, sems,
 ):
     part = lax.axis_index("col")
     own, hid, n_a, n_b, hold = sz.own, sz.hid, sz.n_a, sz.n_b, sz.hold
@@ -861,15 +855,19 @@
 
     def forward_step(index, carry):
         lanes = pl.ds(aligned(index * LANES), LANES)
-        result, scale, state = activate(result1[:, lanes] + bias1)
-        result1[:, lanes] = result
+        result = result1[:, lanes] + bias1
+        gate = sigmoid(result)
+        active = result * gate
+        scale = lax.rsqrt(jnp.sum(active * active, 0, keepdims=True) + ROW_EPS)
+        result1[:, lanes] = active
+        slope1[:, lanes] = gate + active * (1.0 - gate)
         scale1[:, lanes] = scale
-        upper, lower = two_parts(state)
+        upper, lower = two_parts(active * scale)
         states[:hid, lanes] = upper
         states[hid:, lanes] = lower
         return carry
 
-    lax.fori_loop(0, n_a // LANES, forward_step, 0, unroll=3)
+    lax.fori_loop(0, n_a // LANES, forward_step, 0, unroll=7)
     wait_all(copies[9:])
     turned2 = low[:, at["turned2"] : at["turned2"] + 2 * hid]
     for tile in range(sz.tiles_b):
@@ -923,13 +921,15 @@
     part_ref[:hid, at["g2"] + hid : at["g2"] + 2 * hid] = g2[hid:]
     part_ref[sz.head : sz.head + 16, g3 + hid : g3 + 2 * hid] = row_sums(low_grad2)
     weight2 = halves(low, at["weight2"], hid)
-    grad_a[...] = jnp.zeros_like(grad_a)
     own_part, average_part = split_inputs(sz, dot(weight2, low_grad2, (1, 0)))
     part_ref[:hid, at["grad_b"] : at["grad_b"] + n_b] = own_part
     for tile in range(sz.tiles_b):
         window, totals = tile_counts(sz, counts, tile)
-        lanes = slice(4 * LANES * tile, 4 * LANES * tile + WINDOW)
-        grad_a[:, lanes] = grad_a[:, lanes] + spread(sz, average_part[:, LANES * tile : LANES * (tile + 1)] / totals, window)
+        added = spread(sz, average_part[:, LANES * tile : LANES * (tile + 1)] / totals, window)
+        first = 4 * LANES * tile
+        shared = slice(first, first + LANES)
+        grad_a[:, shared] = added[:, :LANES] + grad_a[:, shared] if tile else added[:, :LANES]
+        grad_a[:, first + LANES : first + WINDOW] = added[:, LANES:]
     rows, few = pl.ds(0, hid + 8), pl.ds(0, sz.head + 32)
     split = at["g2"]
     stores = start_copies(
@@ -946,10 +946,19 @@
 
     def backward_step(index, carry):
         lanes = pl.ds(aligned(index * LANES), LANES)
-        low_grad[:, lanes] = norm_backward(grad_a[:, lanes], result1[:, lanes], scale1[:, lanes])
+        scale = scale1[:, lanes]
+        inner = jnp.zeros((8, LANES), F32)
+        for row in range(0, hid, 8):
+            rows = slice(row, row + 8)
+            inner = inner + grad_a[rows, lanes] * result1[rows, lanes]
+        inner = scale * scale * scale * jnp.sum(inner, 0, keepdims=True)
+        for row in range(0, hid, 16):
+            rows = slice(row, row + 16)
+            grad = scale * grad_a[rows, lanes] - inner * result1[rows, lanes]
+            low_grad[rows, lanes] = (grad * slope1[rows, lanes]).astype(BF)
         return carry
 
-    lax.fori_loop(0, n_a // LANES, backward_step, 0, unroll=3)
+    lax.fori_loop(0, n_a // LANES, backward_step, 0, unroll=7)
     part_ref[:hid, at["g1"] : at["g1"] + hid] = dot(xa[...], low_grad[...], (1, 1))
     part_ref[sz.head : sz.head + 16, g3 : g3 + hid] = row_sums(low_grad[...])
     stores += start_copies(
@@ -981,6 +990,7 @@
             ((2 * sz.main, LANES), F32),
             ((2 * hid, sz.n_a), BF),
             ((2 * hid, sz.n_b), BF),
+            ((hid, sz.n_a), F32),
             ((hid, sz.n_a), F32),
             ((1, sz.n_a), F32),
             ((2 * hid, sz.n_b), BF),
@@ -1008,7 +1018,7 @@
 
 def seeds_back_kernel(
     sz, serve_in, take_in, live_in, received, low_in, high_in, counts_in, part_in, keep0, keep1, send,
-    serve_rows, take_rows, live_rows, x_ref, weight_ref, low, high, window_ref, partial, g1_ref, g2_ref, gb_ref, sems,
+    serve_rows, take_rows, live_rows, x_ref, weight_ref, low, high, window_ref, partial, g1_ref, g2_ref, gb_ref, stage, sems,
 ):
     part = lax.axis_index("col")
     own, hid, group, n_b, n_mid = sz.own, sz.hid, sz.group, sz.n_b, sz.n_mid
@@ -1085,37 +1095,36 @@
     head_row = partial[sz.head + 16 : sz.head + 32, g3 : g3 + LANES]
     totals = partial[sz.head + 16 : sz.head + 32, g3 + LANES : g3 + 2 * LANES]
     lane_at = lax.broadcasted_iota(jnp.int32, (16, LANES), 1)
-    row_at = lax.broadcasted_iota(jnp.int32, (16, LANES), 0)
     fixed = ((totals[0:1, 0:1] + dist_total) * float(2**LOSS_BITS) + 0.5).astype(jnp.int32)
     count = totals[0:1, 1:2].astype(jnp.int32)
     whole = jnp.where(lane_at < 32, fixed, count)
     bits = (lax.shift_right_logical(whole, lane_at & 31) & 1).astype(F32)
     bits = jnp.where(lane_at < 64, bits, 0.0)
+    stage[sz.misc :, :] = jnp.zeros((sz.pay - sz.misc, LANES), F32)
     for r, (target_ref, base) in enumerate(((keep0, 0), (send, 0), (keep1, 0), (send, sz.pay))):
         shard = part ^ r
         block2 = pl.ds(pl.multiple_of(2 * group * shard, 2 * group), 2 * group)
-        row = base
         for h in range(hid // LANES):
             lanes = slice(LANES * h, LANES * (h + 1))
             for s in range(2):
-                rows = slice(half * s + sz.hold * r, half * s + sz.hold * (r + 1))
-                target_ref[row : row + sz.hold, :] = g1_ref[rows, lanes].astype(BF)
-                row += sz.hold
-        for h in range(hid // LANES):
-            target_ref[row : row + 2 * group, :] = g2_ref[block2, LANES * h : LANES * (h + 1)].astype(BF)
-            row += 2 * group
+                first, row = half * s + sz.hold * r, sz.feat * (2 * h + s)
+                stage[row : row + sz.feat, :] = g1_ref[first : first + sz.feat, lanes]
+            row = sz.rows_one + 2 * group * h
+            stage[row : row + 2 * group, :] = g2_ref[block2, lanes]
         third = partial[: sz.head, pl.ds(aligned(g3 + 2 * group * shard), LANES)]
-        target_ref[row : row + sz.head, :] = third.astype(BF)
-        row += sz.head
+        stage[sz.at_three : sz.misc, :] = third[: sz.classes]
         odd = (shard % 2) == 1
         block = aligned((shard // 2) * LANES)
         one = gb_ref[:, pl.ds(block, LANES)]
         two = gb_ref[:, pl.ds(aligned(hid + block), LANES)]
         one = jnp.where(odd, pltpu.roll(one, group, 1), one)
         two = jnp.where(odd, two, pltpu.roll(two, group, 1))
-        bias_row = jnp.where(lane_at < group, one, two)
-        misc = jnp.where(row_at == 0, bias_row, jnp.where(row_at == 1, head_row, jnp.where(row_at == 2, bits, 0.0)))
-        target_ref[row : row + 16, :] = misc.astype(BF)
+        bias_row = jnp.where(lane_at < group, one, two)[0:1]
+        rows = [bias_row, head_row[0:1], bits[0:1]]
+        rows += [item - item.astype(BF).astype(F32) for item in rows[:2]]
+        for i, item in enumerate(rows):
+            stage[sz.misc + i : sz.misc + i + 1, :] = item
+        target_ref[base : base + sz.pay, :] = stage[...].astype(BF)
 
 
 def seeds_backward(sz, tables, received, low, high, counts, partial):
@@ -1134,6 +1143,7 @@
             ((8 * sz.hold, hid), F32),
             ((2 * hid, hid), F32),
             ((16, 2 * hid), F32),
+            ((sz.pay, LANES), F32),
         ],
         BACK_MIB,
         *tables,
@@ -1154,24 +1164,25 @@
     seconds = (s1, s2, s3, sh, sb)
     moments, squares, updates = rest[:5], rest[5:10], rest[10:15]
     sums_ref, totals_ref, one_ref, three_ref = rest[15:]
-    group, hold = sz.group, sz.hold
+    group = sz.group
 
     def wide(at, rows):
         return jnp.concatenate([grad[at : at + rows, :], grad[at + rows : at + 2 * rows, :]], 1)
 
-    one = wide(0, 2 * hold)
+    one = wide(0, 2 * sz.feat)
     three = grad[sz.at_three : sz.misc, :]
     turned = pltpu.roll(three, group, 1)
     for f in range(sz.feat):
         one_ref[f, 0:1, :] = one[f : f + 1]
-        one_ref[f, 1:2, :] = one[hold + f : hold + f + 1]
+        one_ref[f, 1:2, :] = one[sz.feat + f : sz.feat + f + 1]
     for c in range(sz.classes):
         three_ref[c, 0:1, :] = three[c : c + 1, :group]
         three_ref[c, 1:2, :] = turned[c : c + 1, :group]
-    misc = grad[sz.misc : sz.misc + 8, :]
-    hidden = jnp.concatenate([misc[0:1, :group], misc[0:1, group : 2 * group]], 0)
+    misc = grad[sz.misc : sz.misc + 5, :]
+    fine = misc[0:2] + misc[3:5]
+    hidden = jnp.concatenate([fine[0:1, :group], fine[0:1, group : 2 * group]], 0)
     two = wide(sz.rows_one, 2 * group).reshape(2, group, sz.hid)
-    grads = (one_ref[...], two, three_ref[...], hidden, misc[1:2, : sz.classes])
+    grads = (one_ref[...], two, three_ref[...], hidden, fine[1:2, : sz.classes])
     lane_at = lax.broadcasted_iota(jnp.int32, (8, LANES), 1)
     row_at = lax.broadcasted_iota(jnp.int32, (8, LANES), 0)
     sums = jnp.zeros((8, LANES), F32)

time: 74.9 us -> 73.4 us (0.980)
  waiting for transfers between devices: 17.8 us -> 16.9 us
where the time goes in v6:
time: 73.4 us; the launch traced here: 73.2 us
  Pallas kernels  32 us (44%)
  starting transfers between devices  22.2 us (30%)
  waiting for transfers between devices  16.9 us (23%)
  between operations  1.08 us (1%)
    pallas_call x7, Pallas kernels, call(): pl.pallas_call(kernel, in_specs=[free if i in loose else far if i in far_...  32 us
    ppermute x14, waiting for transfers between devices, swap(): return lax.ppermute(value, axis, [(i, i ^ bit) for i in range(count)])  14.1 us
    ppermute x14, starting transfers between devices, swap(): return lax.ppermute(value, axis, [(i, i ^ bit) for i in range(count)])  13.2 us
    all_to_all x1, starting transfers between devices, shards(): lax.all_to_all(rows, ('dp', 'col'), split_axis=0, concat_axis=0, tiled=True)  6.25 us
    ppermute x1, waiting for transfers between devices, shards(): lax.ppermute(far, ('dp', 'col'), pair)  2.75 us
    ppermute x1, starting transfers between devices, shards(): lax.ppermute(far, ('dp', 'col'), pair)  2.73 us
  transfers between devices with their start and end apart: 16, of which 10 were waited for; matrix products, arithmetic and copies ran while one was open for 1% of the time, Pallas kernels for 30%

profile of v6, /device:TPU:0, one launch (start us, length us, event | category | flops | bytes accessed | tf_op | source)
XLA Modules:
  0.0 73.2 jit_solution(3223237471776240725)
XLA Ops:
  0.7 4.0 %shard_map.394 = (bf16[64,768]{1,0:T(8,128)(2,1)}, f32[408,128]{1,0:T(8,128)}, bf16[24,2432]{1,0:T(8,128)(2,1)}, f32[72,128]{1,0:T(8,128)}, bf16[24,4352]{1,0:T(...) custom-call(bf16[25,32768]{1,0:T(8,128)(2,1)} %feat_ref.1, s32[5,8192]{1,0:T(8,128)} %nbr_ref.1, ...), custom_call_target="tpu_custom_call" | custom-call | flops 4000000000 | bytes 1 | tf_op jit(solution)/shard_map/pallas_call | solution.py:47
  4.8 2.5 %collective-permute-start.2 = (bf16[24,2176]{1,0:T(8,128)(2,1)S(1)}, bf16[24,2176]{1,0:T(8,128)(2,1)S(1)}, u32[]{:S(2)}, u32[]{:S(2)}) collective-permute-start(bf16[24,2176]{1,0:T(8,128)(2,1)S(1)} %get-tuple-element.76), channel_id=1, source_target_pairs={{0,3},{1,2},{2,1},{3,0},{4,7},{5,6},{6,5},{7,4},{8,11},{9,10},{10,... | collective-permute-start | bytes 313352 | tf_op jit(solution)/shard_map/ppermute | solution.py:1252
  7.2 0.7 collective-permute-start
  8.0 7.1 %shard_map.395 = (bf16[64,2688]{1,0:T(8,128)(2,1)}, bf16[4592,128]{1,0:T(8,128)(2,1)}, bf16[24,5120]{1,0:T(8,128)(2,1)S(1)}, bf16[24,5120]{1,0:T(8,128)(2,1)S(1)}, bf16[24,5120]{1,0:T(8,128)(2,1)S(1)}) custom-call(bf16[25,32768]{1,0:T(8,128)(2,1)S(1)} %copy-done, s32[5,8192]{1,0:T(8,128)S(1)} %copy-done.1, s32[5,8192]{1,0:T(8,128)S(1)} %copy-done.2, ...), custom_call_target="tpu_custom_call" | custom-call | flops 6000000000 | bytes 1 | tf_op jit(solution)/shard_map/pallas_call | solution.py:47
  15.2 0.2 collective-permute-start.3
  15.4 0.3 collective-permute-start.4
  15.7 2.3 %collective-permute-start.5 = (bf16[24,5120]{1,0:T(8,128)(2,1)S(1)}, bf16[24,5120]{1,0:T(8,128)(2,1)S(1)}, u32[]{:S(2)}, u32[]{:S(2)}) collective-permute-start(bf16[24,5120]{1,0:T(8,128)(2,1)S(1)} %get-tuple-element.86), channel_id=1, source_target_pairs={{0,2},{1,3},{2,0},{3,1},{4,6},{5,7},{6,4},{7,5},{8,10},{9,11},{10,... | collective-permute-start | bytes 737288 | tf_op jit(solution)/shard_map/ppermute | solution.py:1252
  18.0 4.5 %shard_map.396 = (bf16[256,3968]{1,0:T(8,128)(2,1)}, f32[264,1152]{1,0:T(8,128)}, bf16[256,512]{1,0:T(8,128)(2,1)}) custom-call(bf16[64,768]{1,0:T(8,128)(2,1)} %get-tuple-element.66.own_b, f32[408,128]{1,0:T(8,128)} %get-tuple-element.67.packed, bf16[24,4352]{1,0:T(8,128)(2,1)S(1)} %collective-permute-done.s1.e1, ...), custom_call_target="tpu_custom_call" | custom-call | flops 4000000000 | bytes 1 | tf_op jit(solution)/shard_map/pallas_call | solution.py:47
  22.6 6.3 %all-to-all-start = ((bf16[32,8,512]{2,1,0:T(8,128)(2,1)}), bf16[32,8,512]{2,1,0:T(8,128)(2,1)S(1)}, u32[]{:S(2)}, u32[]{:S(2)}) async-start(bf16[32,8,512]{2,1,0:T(8,128)(2,1)} %bitcast.3), calls=%async_computation | async-start | bytes 524288 | tf_op jit(solution)/shard_map/all_to_all | solution.py:1288
  28.8 0.1 collective-permute-done.6.a3
  29.0 10.5 %shard_map.397.part_in = f32[264,2048]{1,0:T(8,128)} custom-call(bf16[256,3968]{1,0:T(8,128)(2,1)} %get-tuple-element.82.low_in, f32[264,1152]{1,0:T(8,128)} %get-tuple-element.83.high_in, bf16[4592,128]{1,0:T(8,128)(2,1)} %get-tuple-element.80.counts_in, bf16[64,2688]{1,0:T(8,128)(2,1)} %get-tuple-element.84.own_a, ...), custom_call_target="tpu_custom_call" | custom-call | flops 14000000000 | bytes 1 | tf_op jit(solution)/shard_map/pallas_call | solution.py:47
  39.5 3.6 %shard_map.398 = (bf16[416,128]{1,0:T(8,128)(2,1)S(1)}, bf16[416,128]{1,0:T(8,128)(2,1)S(1)}, bf16[832,128]{1,0:T(8,128)(2,1)S(1)}) custom-call(s32[8,8]{1,0:T(8,128)} %serve_in.3, s32[8,8]{1,0:T(8,128)} %take_in.3, s32[1,8]{1,0:T(1,128)} %bitcast.44, bf16[256,512]{1,0:T(8,128)(2,1)S(1)} %bitcast.25, bf16[256,3968]{1,0:T(8,128)(2,1)} %get-tuple-element.82.low_in, ...), custom_call_target="tpu_custom_call" | custom-call | flops 3000000000 | bytes 1 | tf_op jit(solution)/shard_map/pallas_call | solution.py:47
  43.2 0.4 collective-permute-start.7
  43.7 1.1 %collective-permute-done.7 = bf16[832,128]{1,0:T(8,128)(2,1)S(1)} collective-permute-done((bf16[832,128]{1,0:T(8,128)(2,1)S(1)}, bf16[832,128]{1,0:T(8,128)(2,1)S(1)}, u32[]{:S(2)}, u32[]{:S(2)}) %collective-permute-start.7) | collective-permute-done | bytes 213024 | tf_op jit(solution)/shard_map/ppermute | solution.py:1252
  44.8 2.7 %collective-permute-start.10 = (bf16[416,128]{1,0:T(8,128)(2,1)S(1)}, bf16[416,128]{1,0:T(8,128)(2,1)S(1)}, u32[]{:S(2)}, u32[]{:S(2)}) collective-permute-start(bf16[416,128]{1,0:T(8,128)(2,1)S(1)} %get-tuple-element.115), channel_id=1, source_target_pairs={{0,6},{1,7},{2,4},{3,5},{4,2},{5,3},{6,0},{7,1},{8,14},{9,15},{10,... | collective-permute-start | bytes 319496 | tf_op jit(solution)/shard_map/ppermute | solution.py:1296
  47.6 0.4 collective-permute-start.8
  48.0 0.4 collective-permute-start.9
  48.4 2.8 %collective-permute-done.10 = bf16[416,128]{1,0:T(8,128)(2,1)S(1)} collective-permute-done((bf16[416,128]{1,0:T(8,128)(2,1)S(1)}, bf16[416,128]{1,0:T(8,128)(2,1)S(1)}, u32[]{:S(2)}, u32[]{:S(2)}) %collective-permute-start.10) | collective-permute-done | bytes 106528 | tf_op jit(solution)/shard_map/ppermute | solution.py:1296
  51.1 2.2 %collective-permute-done.8 = bf16[416,128]{1,0:T(8,128)(2,1)S(1)} collective-permute-done((bf16[416,128]{1,0:T(8,128)(2,1)S(1)}, bf16[416,128]{1,0:T(8,128)(2,1)S(1)}, u32[]{:S(2)}, u32[]{:S(2)}) %collective-permute-start.8) | collective-permute-done | bytes 106528 | tf_op jit(solution)/shard_map/ppermute | solution.py:1252
  53.3 0.3 collective-permute-done.9
  53.7 1.6 %collective-permute-start.11 = (bf16[416,128]{1,0:T(8,128)(2,1)S(1)}, bf16[416,128]{1,0:T(8,128)(2,1)S(1)}, u32[]{:S(2)}, u32[]{:S(2)}) collective-permute-start(bf16[416,128]{1,0:T(8,128)(2,1)S(1)} %fusion.1), channel_id=1, source_target_pairs={{0,8},{4,12},{8,0},{12,4},{16,24},{20,28},{24,16},{28,20},{1,9},{5... | collective-permute-start | bytes 319496 | tf_op jit(solution)/shard_map/ppermute | solution.py:1252
  55.3 3.1 %collective-permute-done.11 = bf16[416,128]{1,0:T(8,128)(2,1)S(1)} collective-permute-done((bf16[416,128]{1,0:T(8,128)(2,1)S(1)}, bf16[416,128]{1,0:T(8,128)(2,1)S(1)}, u32[]{:S(2)}, u32[]{:S(2)}) %collective-permute-start.11) | collective-permute-done | bytes 106528 | tf_op jit(solution)/shard_map/ppermute | solution.py:1252
  58.4 0.1 fusion
  58.5 2.7 %collective-permute-start.12 = (bf16[416,128]{1,0:T(8,128)(2,1)S(1)}, bf16[416,128]{1,0:T(8,128)(2,1)S(1)}, u32[]{:S(2)}, u32[]{:S(2)}) collective-permute-start(bf16[416,128]{1,0:T(8,128)(2,1)S(1)} %fusion), channel_id=1, source_target_pairs={{0,16},{4,20},{8,24},{12,28},{16,0},{20,4},{24,8},{28,12},{1,17},{... | collective-permute-start | bytes 319496 | tf_op jit(solution)/shard_map/ppermute | solution.py:1252
  61.3 4.6 %collective-permute-done.12 = bf16[416,128]{1,0:T(8,128)(2,1)S(1)} collective-permute-done((bf16[416,128]{1,0:T(8,128)(2,1)S(1)}, bf16[416,128]{1,0:T(8,128)(2,1)S(1)}, u32[]{:S(2)}, u32[]{:S(2)}) %collective-permute-start.12) | collective-permute-done | bytes 106528 | tf_op jit(solution)/shard_map/ppermute | solution.py:1252
  65.9 0.1 add_reduce-precision_fusion.grad
  66.1 1.5 %shard_map.399 = (f32[25,2,256]{2,1,0:T(2,128)}, f32[2,64,256]{2,1,0:T(8,128)}, f32[47,2,64]{2,1,0:T(2,128)}, f32[2,64]{1,0:T(2,128)}, f32[1,47]{1,0:T(1,128)}, ...) custom-call(f32[416,128]{1,0:T(8,128)S(1)} %add_reduce-precision_fus, ...), custom_call_target="tpu_custom_call" | custom-call | flops 1000000000 | bytes 1 | tf_op jit(solution)/shard_map/pallas_call | solution.py:47
  67.6 1.2 %collective-permute-done.13 = f32[8,128]{1,0:T(8,128)S(1)} collective-permute-done((f32[8,128]{1,0:T(8,128)S(1)}, f32[8,128]{1,0:T(8,128)S(1)}, u32[]{:S(2)}, u32[]{:S(2)}) %collective-permute-start.13) | collective-permute-done | bytes 4128 | tf_op jit(solution)/shard_map/ppermute | solution.py:1252
  68.8 1.6 %collective-permute-start.14 = (f32[8,128]{1,0:T(8,128)S(1)}, f32[8,128]{1,0:T(8,128)S(1)}, u32[]{:S(2)}, u32[]{:S(2)}) collective-permute-start(f32[8,128]{1,0:T(8,128)S(1)} %add.31.own), channel_id=1, source_target_pairs={{0,2},{1,3},{2,0},{3,1},{4,6},{5,7},{6,4},{7,5},{8,10},{9,11},{10,... | collective-permute-start | bytes 12296 | tf_op jit(solution)/shard_map/ppermute | solution.py:1252
  70.4 0.6 fusion.2
  70.9 1.4 %collective-permute-done.14.far = f32[8,128]{1,0:T(8,128)S(1)} collective-permute-done((f32[8,128]{1,0:T(8,128)S(1)}, f32[8,128]{1,0:T(8,128)S(1)}, u32[]{:S(2)}, u32[]{:S(2)}) %collective-permute-start.14) | collective-permute-done | bytes 4128 | tf_op jit(solution)/shard_map/ppermute | solution.py:1252
  72.4 0.8 %shard_map.400 = (f32[25,2,256]{2,1,0:T(2,128)}, f32[2,64,256]{2,1,0:T(8,128)}, f32[47,2,64]{2,1,0:T(2,128)}, f32[2,64]{1,0:T(2,128)}, f32[1,47]{1,0:T(1,128)}, /*index=5*/f32[2,5]{1,0:T(2,128)}) custom-call(f32[8,128]{1,0:T(8,128)S(1)} %add.31.own, f32[8,128]{1,0:T(8,128)S(1)} %collective-permute-done.14.far, f32[25,2,256]{2,1,0:T(2,128)S(1)} %bitcast.30, ...), custom_call_target="tpu_custom_call" | custom-call | flops 1000000000 | bytes 1 | tf_op jit(solution)/shard_map/pallas_call | solution.py:47
  (57 shorter events, 0.4 us)
Async XLA Ops:
  0.7 7.3 %copy-start = (bf16[25,32768]{1,0:T(8,128)(2,1)S(1)}, bf16[25,32768]{1,0:T(8,128)(2,1)}, u32[]{:S(2)}) copy-start(bf16[25,32768]{1,0:T(8,128)(2,1)} %feat_ref.1) | copy-start | bytes 4915204
  4.8 10.4 %collective-permute-start.2 = (bf16[24,2176]{1,0:T(8,128)(2,1)S(1)}, bf16[24,2176]{1,0:T(8,128)(2,1)S(1)}, u32[]{:S(2)}, u32[]{:S(2)}) collective-permute-start(bf16[24,2176]{1,0:T(8,128)(2,1)S(1)} %get-tuple-element.76), channel_id=1, source_target_pairs={{0,3},{1,2},{2,1},{3,0},{4,7},{5,6},{6,5},{7,4},{8,11},{9,10},{10,... | collective-permute-start | bytes 313352 | tf_op jit(solution)/shard_map/ppermute | solution.py:1252
  7.2 8.2 %collective-permute-start = (bf16[24,4352]{1,0:T(8,128)(2,1)S(1)}, bf16[24,4352]{1,0:T(8,128)(2,1)S(1)}, u32[]{:S(2)}, u32[]{:S(2)}) collective-permute-start(bf16[24,4352]{1,0:T(8,128)(2,1)S(1)} %get-tuple-element.68), channel_id=1, source_target_pairs={{0,1},{1,0},{2,3},{3,2},{4,5},{5,4},{6,7},{7,6},{8,9},{9,8},{10,11... | collective-permute-start | bytes 626696 | tf_op jit(solution)/shard_map/ppermute | solution.py:1252
  7.9 7.3 %collective-permute-start.1 = (bf16[24,4352]{1,0:T(8,128)(2,1)S(1)}, bf16[24,4352]{1,0:T(8,128)(2,1)S(1)}, u32[]{:S(2)}, u32[]{:S(2)}) collective-permute-start(bf16[24,4352]{1,0:T(8,128)(2,1)S(1)} %get-tuple-element.75), channel_id=1, source_target_pairs={{0,2},{1,3},{2,0},{3,1},{4,6},{5,7},{6,4},{7,5},{8,10},{9,11},{10,... | collective-permute-start | bytes 626696 | tf_op jit(solution)/shard_map/ppermute | solution.py:1252
  15.2 2.8 %collective-permute-start.3 = (bf16[24,4352]{1,0:T(8,128)(2,1)S(1)}, bf16[24,4352]{1,0:T(8,128)(2,1)S(1)}, u32[]{:S(2)}, u32[]{:S(2)}) collective-permute-start(bf16[24,4352]{1,0:T(8,128)(2,1)S(1)} %collective-permute-done.1.s2.e2), channel_id=1, source_target_pairs={{0,1},{1,0},{2,3},{3,2},{4,5},{5,4},{6,7},{7,6},{8,9},{9,8},{10,11... | collective-permute-start | bytes 626696 | tf_op jit(solution)/shard_map/ppermute | solution.py:1252
  15.4 13.4 %collective-permute-start.4 = (bf16[24,5120]{1,0:T(8,128)(2,1)S(1)}, bf16[24,5120]{1,0:T(8,128)(2,1)S(1)}, u32[]{:S(2)}, u32[]{:S(2)}) collective-permute-start(bf16[24,5120]{1,0:T(8,128)(2,1)S(1)} %get-tuple-element.85), channel_id=1, source_target_pairs={{0,1},{1,0},{2,3},{3,2},{4,5},{5,4},{6,7},{7,6},{8,9},{9,8},{10,11... | collective-permute-start | bytes 737288 | tf_op jit(solution)/shard_map/ppermute | solution.py:1252
  15.7 13.1 %collective-permute-start.5 = (bf16[24,5120]{1,0:T(8,128)(2,1)S(1)}, bf16[24,5120]{1,0:T(8,128)(2,1)S(1)}, u32[]{:S(2)}, u32[]{:S(2)}) collective-permute-start(bf16[24,5120]{1,0:T(8,128)(2,1)S(1)} %get-tuple-element.86), channel_id=1, source_target_pairs={{0,2},{1,3},{2,0},{3,1},{4,6},{5,7},{6,4},{7,5},{8,10},{9,11},{10,... | collective-permute-start | bytes 737288 | tf_op jit(solution)/shard_map/ppermute | solution.py:1252
  18.0 10.9 %collective-permute-start.6 = (bf16[24,5120]{1,0:T(8,128)(2,1)S(1)}, bf16[24,5120]{1,0:T(8,128)(2,1)S(1)}, u32[]{:S(2)}, u32[]{:S(2)}) collective-permute-start(bf16[24,5120]{1,0:T(8,128)(2,1)S(1)} %get-tuple-element.87), channel_id=1, source_target_pairs={{0,3},{1,2},{2,1},{3,0},{4,7},{5,6},{6,5},{7,4},{8,11},{9,10},{10,... | collective-permute-start | bytes 737288 | tf_op jit(solution)/shard_map/ppermute | solution.py:1252
  22.6 16.9 %all-to-all-start = ((bf16[32,8,512]{2,1,0:T(8,128)(2,1)}), bf16[32,8,512]{2,1,0:T(8,128)(2,1)S(1)}, u32[]{:S(2)}, u32[]{:S(2)}) async-start(bf16[32,8,512]{2,1,0:T(8,128)(2,1)} %bitcast.3), calls=%async_computation | async-start | bytes 524288 | tf_op jit(solution)/shard_map/all_to_all | solution.py:1288
  43.1 22.9 %copy-start.5 = (f32[2,64,256]{2,1,0:T(8,128)S(1)}, f32[2,64,256]{2,1,0:T(8,128)}, u32[]{:S(2)}) copy-start(f32[2,64,256]{2,1,0:T(8,128)} %f2.1) | copy-start | bytes 393220
  43.1 22.9 %copy-start.6 = (f32[2,64,256]{2,1,0:T(8,128)S(1)}, f32[2,64,256]{2,1,0:T(8,128)}, u32[]{:S(2)}) copy-start(f32[2,64,256]{2,1,0:T(8,128)} %s2_.1) | copy-start | bytes 393220
  43.1 22.9 %copy-start.7 = (f32[2,64,256]{2,1,0:T(8,128)S(1)}, f32[2,64,256]{2,1,0:T(8,128)}, u32[]{:S(2)}) copy-start(f32[2,64,256]{2,1,0:T(8,128)} %w2.3) | copy-start | bytes 393220
  43.1 22.9 %copy-start.8 = (f32[2,25,256]{2,0,1:T(2,128)S(1)}, f32[2,25,256]{2,0,1:T(2,128)}, u32[]{:S(2)}) copy-start(f32[2,25,256]{2,0,1:T(2,128)} %param.44) | copy-start | bytes 153604
  43.1 22.9 %copy-start.9 = (f32[2,25,256]{2,0,1:T(2,128)S(1)}, f32[2,25,256]{2,0,1:T(2,128)}, u32[]{:S(2)}) copy-start(f32[2,25,256]{2,0,1:T(2,128)} %param.49) | copy-start | bytes 153604
  43.1 22.9 %copy-start.10 = (f32[2,25,256]{2,0,1:T(2,128)S(1)}, f32[2,25,256]{2,0,1:T(2,128)}, u32[]{:S(2)}) copy-start(f32[2,25,256]{2,0,1:T(2,128)} %param.39) | copy-start | bytes 153604
  43.1 22.9 %copy-start.11 = (f32[2,64,47]{1,0,2:T(2,128)S(1)}, f32[2,64,47]{1,0,2:T(2,128)}, u32[]{:S(2)}) copy-start(f32[2,64,47]{1,0,2:T(2,128)} %param.46) | copy-start | bytes 72196
  43.1 22.9 %copy-start.12 = (f32[2,64,47]{1,0,2:T(2,128)S(1)}, f32[2,64,47]{1,0,2:T(2,128)}, u32[]{:S(2)}) copy-start(f32[2,64,47]{1,0,2:T(2,128)} %param.51) | copy-start | bytes 72196
  43.2 22.9 %copy-start.13 = (f32[2,64,47]{1,0,2:T(2,128)S(1)}, f32[2,64,47]{1,0,2:T(2,128)}, u32[]{:S(2)}) copy-start(f32[2,64,47]{1,0,2:T(2,128)} %param.41) | copy-start | bytes 72196
  43.2 22.9 %copy-start.16 = (f32[2,64]{1,0:T(2,128)S(1)}, f32[2,64]{1,0:T(2,128)}, u32[]{:S(2)}) copy-start(f32[2,64]{1,0:T(2,128)} %fh.1) | copy-start | bytes 1540
  43.2 22.9 %copy-start.17 = (f32[2,64]{1,0:T(2,128)S(1)}, f32[2,64]{1,0:T(2,128)}, u32[]{:S(2)}) copy-start(f32[2,64]{1,0:T(2,128)} %sh.1) | copy-start | bytes 1540
  43.2 22.9 %copy-start.18 = (f32[2,64]{1,0:T(2,128)S(1)}, f32[2,64]{1,0:T(2,128)}, u32[]{:S(2)}) copy-start(f32[2,64]{1,0:T(2,128)} %wh.3) | copy-start | bytes 1540
  43.2 22.9 %copy-start.19 = (f32[47]{0:T(128)S(1)}, f32[47]{0:T(128)}, u32[]{:S(2)}) copy-start(f32[47]{0:T(128)} %param.48) | copy-start | bytes 568
  43.2 22.9 %copy-start.20 = (f32[47]{0:T(128)S(1)}, f32[47]{0:T(128)}, u32[]{:S(2)}) copy-start(f32[47]{0:T(128)} %param.53) | copy-start | bytes 568
  43.2 22.9 %copy-start.21 = (f32[47]{0:T(128)S(1)}, f32[47]{0:T(128)}, u32[]{:S(2)}) copy-start(f32[47]{0:T(128)} %param.43) | copy-start | bytes 568
  43.2 1.5 %collective-permute-start.7 = (bf16[832,128]{1,0:T(8,128)(2,1)S(1)}, bf16[832,128]{1,0:T(8,128)(2,1)S(1)}, u32[]{:S(2)}, u32[]{:S(2)}) collective-permute-start(bf16[832,128]{1,0:T(8,128)(2,1)S(1)} %get-tuple-element.89), channel_id=1, source_target_pairs={{0,1},{1,0},{2,3},{3,2},{4,5},{5,4},{6,7},{7,6},{8,9},{9,8},{10,11... | collective-permute-start | bytes 638984 | tf_op jit(solution)/shard_map/ppermute | solution.py:1252
  44.8 6.3 %collective-permute-start.10 = (bf16[416,128]{1,0:T(8,128)(2,1)S(1)}, bf16[416,128]{1,0:T(8,128)(2,1)S(1)}, u32[]{:S(2)}, u32[]{:S(2)}) collective-permute-start(bf16[416,128]{1,0:T(8,128)(2,1)S(1)} %get-tuple-element.115), channel_id=1, source_target_pairs={{0,6},{1,7},{2,4},{3,5},{4,2},{5,3},{6,0},{7,1},{8,14},{9,15},{10,... | collective-permute-start | bytes 319496 | tf_op jit(solution)/shard_map/ppermute | solution.py:1296
  47.6 5.8 %collective-permute-start.8 = (bf16[416,128]{1,0:T(8,128)(2,1)S(1)}, bf16[416,128]{1,0:T(8,128)(2,1)S(1)}, u32[]{:S(2)}, u32[]{:S(2)}) collective-permute-start(bf16[416,128]{1,0:T(8,128)(2,1)S(1)} %get-tuple-element.115), channel_id=1, source_target_pairs={{0,2},{1,3},{2,0},{3,1},{4,6},{5,7},{6,4},{7,5},{8,10},{9,11},{10,... | collective-permute-start | bytes 319496 | tf_op jit(solution)/shard_map/ppermute | solution.py:1252
  48.0 5.6 %collective-permute-start.9 = (bf16[416,128]{1,0:T(8,128)(2,1)S(1)}, bf16[416,128]{1,0:T(8,128)(2,1)S(1)}, u32[]{:S(2)}, u32[]{:S(2)}) collective-permute-start(bf16[416,128]{1,0:T(8,128)(2,1)S(1)} %get-tuple-element.114), channel_id=1, source_target_pairs={{0,4},{4,0},{8,12},{12,8},{16,20},{20,16},{24,28},{28,24},{1,5},{5... | collective-permute-start | bytes 319496 | tf_op jit(solution)/shard_map/ppermute | solution.py:1252
  53.7 4.8 %collective-permute-start.11 = (bf16[416,128]{1,0:T(8,128)(2,1)S(1)}, bf16[416,128]{1,0:T(8,128)(2,1)S(1)}, u32[]{:S(2)}, u32[]{:S(2)}) collective-permute-start(bf16[416,128]{1,0:T(8,128)(2,1)S(1)} %fusion.1), channel_id=1, source_target_pairs={{0,8},{4,12},{8,0},{12,4},{16,24},{20,28},{24,16},{28,20},{1,9},{5... | collective-permute-start | bytes 319496 | tf_op jit(solution)/shard_map/ppermute | solution.py:1252
  58.5 7.4 %collective-permute-start.12 = (bf16[416,128]{1,0:T(8,128)(2,1)S(1)}, bf16[416,128]{1,0:T(8,128)(2,1)S(1)}, u32[]{:S(2)}, u32[]{:S(2)}) collective-permute-start(bf16[416,128]{1,0:T(8,128)(2,1)S(1)} %fusion), channel_id=1, source_target_pairs={{0,16},{4,20},{8,24},{12,28},{16,0},{20,4},{24,8},{28,12},{1,17},{... | collective-permute-start | bytes 319496 | tf_op jit(solution)/shard_map/ppermute | solution.py:1252
  67.6 1.2 %collective-permute-start.13 = (f32[8,128]{1,0:T(8,128)S(1)}, f32[8,128]{1,0:T(8,128)S(1)}, u32[]{:S(2)}, u32[]{:S(2)}) collective-permute-start(f32[8,128]{1,0:T(8,128)S(1)} %get-tuple-element.91), channel_id=1, source_target_pairs={{0,1},{1,0},{2,3},{3,2},{4,5},{5,4},{6,7},{7,6},{8,9},{9,8},{10,11... | collective-permute-start | bytes 12296 | tf_op jit(solution)/shard_map/ppermute | solution.py:1252
  68.8 3.6 %collective-permute-start.14 = (f32[8,128]{1,0:T(8,128)S(1)}, f32[8,128]{1,0:T(8,128)S(1)}, u32[]{:S(2)}, u32[]{:S(2)}) collective-permute-start(f32[8,128]{1,0:T(8,128)S(1)} %add.31.own), channel_id=1, source_target_pairs={{0,2},{1,3},{2,0},{3,1},{4,6},{5,7},{6,4},{7,5},{8,10},{9,11},{10,... | collective-permute-start | bytes 12296 | tf_op jit(solution)/shard_map/ppermute | solution.py:1252
  (6 other events, 43.7 us)

commit v7 on v6

--- a/solution.py
+++ b/solution.py
@@ -1158,12 +1158,7 @@
     )
 
 
-def lamb_kernel(sz, grad, w1, w2, w3, wh, wb, f1, f2, f3, fh, fb, s1, s2, s3, sh, sb, *rest):
-    params = (w1, w2, w3, wh, wb)
-    firsts = (f1, f2, f3, fh, fb)
-    seconds = (s1, s2, s3, sh, sb)
-    moments, squares, updates = rest[:5], rest[5:10], rest[10:15]
-    sums_ref, totals_ref, one_ref, three_ref = rest[15:]
+def unpacked(sz, grad, one_ref, three_ref):
     group = sz.group
 
     def wide(at, rows):
@@ -1182,18 +1177,24 @@
     fine = misc[0:2] + misc[3:5]
     hidden = jnp.concatenate([fine[0:1, :group], fine[0:1, group : 2 * group]], 0)
     two = wide(sz.rows_one, 2 * group).reshape(2, group, sz.hid)
-    grads = (one_ref[...], two, three_ref[...], hidden, fine[1:2, : sz.classes])
+    return (one_ref[...], two, three_ref[...], hidden, fine[1:2, : sz.classes]), misc[2:3]
+
+
+def new_moments(first, second, g):
+    return BETA_ONE * first + (1.0 - BETA_ONE) * g, BETA_TWO * second + (1.0 - BETA_TWO) * g * g
+
+
+def lamb_kernel(sz, grad, *rest):
+    params, firsts, seconds, updates = rest[:5], rest[5:10], rest[10:15], rest[15:20]
+    sums_ref, totals_ref, one_ref, three_ref = rest[20:]
+    grads, bits_row = unpacked(sz, grad, one_ref, three_ref)
     lane_at = lax.broadcasted_iota(jnp.int32, (8, LANES), 1)
     row_at = lax.broadcasted_iota(jnp.int32, (8, LANES), 0)
     sums = jnp.zeros((8, LANES), F32)
     for i in range(5):
-        g = grads[i]
         w = params[i][...]
-        m = BETA_ONE * firsts[i][...] + (1.0 - BETA_ONE) * g
-        v = BETA_TWO * seconds[i][...] + (1.0 - BETA_TWO) * g * g
+        m, v = new_moments(firsts[i][...], seconds[i][...], grads[i])
         u = (m / (1.0 - BETA_ONE**STEP)) / (jnp.sqrt(v / (1.0 - BETA_TWO**STEP)) + ADAM_EPS) + DECAY_RATE * w
-        moments[i][...] = m
-        squares[i][...] = v
         updates[i][...] = u
         for row, item in ((0, w), (1, u)):
             item = item * item
@@ -1206,24 +1207,35 @@
     sums_ref[...] = sums
     power = (1 << (lane_at & 15)).astype(F32)
     power = jnp.where((lane_at & 31) < 16, power, power * float(2**16))
-    bits = jnp.broadcast_to(misc[2:3], (8, LANES)) * power
+    bits = jnp.broadcast_to(bits_row, (8, LANES)) * power
     loss = jnp.sum(jnp.where(lane_at < 32, bits, 0.0), 1, keepdims=True) * float(2.0**-LOSS_BITS)
     count = jnp.sum(jnp.where((lane_at >= 32) & (lane_at < 64), bits, 0.0), 1, keepdims=True)
     totals_ref[...] = jnp.where(lane_at == 0, loss, count)
 
 
+def moments_kernel(sz, grad, *rest):
+    firsts, seconds, moments, squares = rest[:5], rest[5:10], rest[10:15], rest[15:20]
+    grads, _ = unpacked(sz, grad, *rest[20:])
+    for i in range(5):
+        moments[i][...], squares[i][...] = new_moments(firsts[i][...], seconds[i][...], grads[i])
+
+
 def lamb(sz, grad, params, firsts, seconds):
     like = [(item.shape, F32) for item in params]
-    return call(
+    scratch = [(params[0].shape, F32), (params[2].shape, F32)]
+    outs = call(
         functools.partial(lamb_kernel, sz),
-        like * 3 + [((8, LANES), F32)] * 2,
-        [(params[0].shape, F32), (params[2].shape, F32)],
+        like + [((8, LANES), F32)] * 2,
+        scratch,
         6,
         grad,
         *params,
         *firsts,
         *seconds,
-    )
+        micros=1,
+    )
+    moments = call(functools.partial(moments_kernel, sz), like * 2, scratch, 6, grad, *firsts, *seconds, micros=2)
+    return outs, moments
 
 
 def step_kernel(own, far, w1, w2, w3, wh, wb, u1, u2, u3, uh, ub, n1, n2, n3, nh, nb, norms_ref):
@@ -1300,9 +1312,9 @@
     while bit < sz.dp:
         grad = merged(grad, swap(grad.astype(BF), "dp", sz.dp, bit))
         bit *= 2
-    outs = lamb(sz, grad, params, firsts, seconds)
-    moments, squares, updates = outs[:5], outs[5:10], outs[10:15]
-    sums, totals = outs[15], outs[16]
+    outs, moments = lamb(sz, grad, params, firsts, seconds)
+    moments, squares, updates = moments[:5], moments[5:], outs[:5]
+    sums, totals = outs[5], outs[6]
     pair = sums + swap(sums, "col", 4, 1)
     fresh = take_step([pair, swap(pair, "col", 4, 2)], params, updates)
     return (*back(*fresh[:5]), *back(*moments), *back(*squares), fresh[5], totals[0, 0], totals[0, 1])

time: 73.4 us -> 72.8 us (level)
  waiting for transfers between devices: 16.9 us -> 15.9 us
    ppermute x14, waiting for transfers between devices: 14.1 us -> 13.2 us  [swap(): return lax.ppermute(value, axis, [(i, i ^ bit) for i in range(count)])]
    pallas_call x7 -> x8, Pallas kernels: 32 us -> 32.2 us  [call(): pl.pallas_call(kernel, in_specs=[free if i in loose else far if i in far_...]
  transfers between devices with their start and end apart: 16 -> 16, of which waited for: 10 -> 10; matrix products, arithmetic and copies ran while one was open for 1% -> 1% of each run, Pallas kernels for 30% -> 32%
where the time goes in v7:
time: 72.8 us; the launch traced here: 72.5 us
  Pallas kernels  32.2 us (44%)
  starting transfers between devices  22.2 us (30%)
  waiting for transfers between devices  15.9 us (22%)
  between operations  1.09 us (1%)
    pallas_call x8, Pallas kernels, call(): pl.pallas_call(kernel, in_specs=[free if i in loose else far if i in far_...  32.2 us
    ppermute x14, starting transfers between devices, swap(): return lax.ppermute(value, axis, [(i, i ^ bit) for i in range(count)])  13.2 us
    ppermute x14, waiting for transfers between devices, swap(): return lax.ppermute(value, axis, [(i, i ^ bit) for i in range(count)])  13.2 us
    all_to_all x1, starting transfers between devices, shards(): lax.all_to_all(rows, ('dp', 'col'), split_axis=0, concat_axis=0, tiled=True)  6.25 us
    ppermute x1, waiting for transfers between devices, shards(): lax.ppermute(far, ('dp', 'col'), pair)  2.75 us
    ppermute x1, starting transfers between devices, shards(): lax.ppermute(far, ('dp', 'col'), pair)  2.73 us
  transfers between devices with their start and end apart: 16, of which 10 were waited for; matrix products, arithmetic and copies ran while one was open for 1% of the time, Pallas kernels for 32%

profile of v7, /device:TPU:0, one launch (start us, length us, event | category | flops | bytes accessed | tf_op | source)
XLA Modules:
  0.0 72.5 jit_solution(857123017515373661)
XLA Ops:
  0.7 4.0 %shard_map.394 = (bf16[64,768]{1,0:T(8,128)(2,1)}, f32[408,128]{1,0:T(8,128)}, bf16[24,2432]{1,0:T(8,128)(2,1)}, f32[72,128]{1,0:T(8,128)}, bf16[24,4352]{1,0:T(...) custom-call(bf16[25,32768]{1,0:T(8,128)(2,1)} %feat_ref.1, s32[5,8192]{1,0:T(8,128)} %nbr_ref.1, ...), custom_call_target="tpu_custom_call" | custom-call | flops 4000000000 | bytes 1 | tf_op jit(solution)/shard_map/pallas_call | solution.py:47
  4.8 2.5 %collective-permute-start.2 = (bf16[24,2176]{1,0:T(8,128)(2,1)S(1)}, bf16[24,2176]{1,0:T(8,128)(2,1)S(1)}, u32[]{:S(2)}, u32[]{:S(2)}) collective-permute-start(bf16[24,2176]{1,0:T(8,128)(2,1)S(1)} %get-tuple-element.76), channel_id=1, source_target_pairs={{0,3},{1,2},{2,1},{3,0},{4,7},{5,6},{6,5},{7,4},{8,11},{9,10},{10,... | collective-permute-start | bytes 313352 | tf_op jit(solution)/shard_map/ppermute | solution.py:1264
  7.2 0.7 collective-permute-start
  8.0 7.1 %shard_map.395 = (bf16[64,2688]{1,0:T(8,128)(2,1)}, bf16[4592,128]{1,0:T(8,128)(2,1)}, bf16[24,5120]{1,0:T(8,128)(2,1)S(1)}, bf16[24,5120]{1,0:T(8,128)(2,1)S(1)}, bf16[24,5120]{1,0:T(8,128)(2,1)S(1)}) custom-call(bf16[25,32768]{1,0:T(8,128)(2,1)S(1)} %copy-done, s32[5,8192]{1,0:T(8,128)S(1)} %copy-done.1, s32[5,8192]{1,0:T(8,128)S(1)} %copy-done.2, ...), custom_call_target="tpu_custom_call" | custom-call | flops 6000000000 | bytes 1 | tf_op jit(solution)/shard_map/pallas_call | solution.py:47
  15.2 0.2 collective-permute-start.3
  15.4 0.3 collective-permute-start.4
  15.7 2.3 %collective-permute-start.5 = (bf16[24,5120]{1,0:T(8,128)(2,1)S(1)}, bf16[24,5120]{1,0:T(8,128)(2,1)S(1)}, u32[]{:S(2)}, u32[]{:S(2)}) collective-permute-start(bf16[24,5120]{1,0:T(8,128)(2,1)S(1)} %get-tuple-element.86), channel_id=1, source_target_pairs={{0,2},{1,3},{2,0},{3,1},{4,6},{5,7},{6,4},{7,5},{8,10},{9,11},{10,... | collective-permute-start | bytes 737288 | tf_op jit(solution)/shard_map/ppermute | solution.py:1264
  18.0 4.5 %shard_map.396 = (bf16[256,3968]{1,0:T(8,128)(2,1)}, f32[264,1152]{1,0:T(8,128)}, bf16[256,512]{1,0:T(8,128)(2,1)}) custom-call(bf16[64,768]{1,0:T(8,128)(2,1)} %get-tuple-element.66.own_b, f32[408,128]{1,0:T(8,128)} %get-tuple-element.67.packed, bf16[24,4352]{1,0:T(8,128)(2,1)S(1)} %collective-permute-done.s1.e1, ...), custom_call_target="tpu_custom_call" | custom-call | flops 4000000000 | bytes 1 | tf_op jit(solution)/shard_map/pallas_call | solution.py:47
  22.6 6.3 %all-to-all-start = ((bf16[32,8,512]{2,1,0:T(8,128)(2,1)}), bf16[32,8,512]{2,1,0:T(8,128)(2,1)S(1)}, u32[]{:S(2)}, u32[]{:S(2)}) async-start(bf16[32,8,512]{2,1,0:T(8,128)(2,1)} %bitcast.3), calls=%async_computation | async-start | bytes 524288 | tf_op jit(solution)/shard_map/all_to_all | solution.py:1300
  28.9 0.1 collective-permute-done.6.a3
  29.0 10.5 %shard_map.397.part_in = f32[264,2048]{1,0:T(8,128)} custom-call(bf16[256,3968]{1,0:T(8,128)(2,1)} %get-tuple-element.82.low_in, f32[264,1152]{1,0:T(8,128)} %get-tuple-element.83.high_in, bf16[4592,128]{1,0:T(8,128)(2,1)} %get-tuple-element.80.counts_in, bf16[64,2688]{1,0:T(8,128)(2,1)} %get-tuple-element.84.own_a, ...), custom_call_target="tpu_custom_call" | custom-call | flops 14000000000 | bytes 1 | tf_op jit(solution)/shard_map/pallas_call | solution.py:47
  39.4 3.6 %shard_map.398 = (bf16[416,128]{1,0:T(8,128)(2,1)S(1)}, bf16[416,128]{1,0:T(8,128)(2,1)S(1)}, bf16[832,128]{1,0:T(8,128)(2,1)S(1)}) custom-call(s32[8,8]{1,0:T(8,128)} %serve_in.3, s32[8,8]{1,0:T(8,128)} %take_in.3, s32[1,8]{1,0:T(1,128)} %bitcast.50, bf16[256,512]{1,0:T(8,128)(2,1)S(1)} %bitcast.25, bf16[256,3968]{1,0:T(8,128)(2,1)} %get-tuple-element.82.low_in, ...), custom_call_target="tpu_custom_call" | custom-call | flops 3000000000 | bytes 1 | tf_op jit(solution)/shard_map/pallas_call | solution.py:47
  43.2 0.4 collective-permute-start.7
  43.6 1.1 %collective-permute-done.7 = bf16[832,128]{1,0:T(8,128)(2,1)S(1)} collective-permute-done((bf16[832,128]{1,0:T(8,128)(2,1)S(1)}, bf16[832,128]{1,0:T(8,128)(2,1)S(1)}, u32[]{:S(2)}, u32[]{:S(2)}) %collective-permute-start.7) | collective-permute-done | bytes 213024 | tf_op jit(solution)/shard_map/ppermute | solution.py:1264
  44.8 2.7 %collective-permute-start.10 = (bf16[416,128]{1,0:T(8,128)(2,1)S(1)}, bf16[416,128]{1,0:T(8,128)(2,1)S(1)}, u32[]{:S(2)}, u32[]{:S(2)}) collective-permute-start(bf16[416,128]{1,0:T(8,128)(2,1)S(1)} %get-tuple-element.115), channel_id=1, source_target_pairs={{0,6},{1,7},{2,4},{3,5},{4,2},{5,3},{6,0},{7,1},{8,14},{9,15},{10,... | collective-permute-start | bytes 319496 | tf_op jit(solution)/shard_map/ppermute | solution.py:1308
  47.5 0.4 collective-permute-start.8
  48.0 0.4 collective-permute-start.9
  48.4 2.8 %collective-permute-done.10 = bf16[416,128]{1,0:T(8,128)(2,1)S(1)} collective-permute-done((bf16[416,128]{1,0:T(8,128)(2,1)S(1)}, bf16[416,128]{1,0:T(8,128)(2,1)S(1)}, u32[]{:S(2)}, u32[]{:S(2)}) %collective-permute-start.10) | collective-permute-done | bytes 106528 | tf_op jit(solution)/shard_map/ppermute | solution.py:1308
  51.1 2.2 %collective-permute-done.8 = bf16[416,128]{1,0:T(8,128)(2,1)S(1)} collective-permute-done((bf16[416,128]{1,0:T(8,128)(2,1)S(1)}, bf16[416,128]{1,0:T(8,128)(2,1)S(1)}, u32[]{:S(2)}, u32[]{:S(2)}) %collective-permute-start.8) | collective-permute-done | bytes 106528 | tf_op jit(solution)/shard_map/ppermute | solution.py:1264
  53.3 0.3 collective-permute-done.9
  53.6 1.6 %collective-permute-start.11 = (bf16[416,128]{1,0:T(8,128)(2,1)S(1)}, bf16[416,128]{1,0:T(8,128)(2,1)S(1)}, u32[]{:S(2)}, u32[]{:S(2)}) collective-permute-start(bf16[416,128]{1,0:T(8,128)(2,1)S(1)} %fusion.1), channel_id=1, source_target_pairs={{0,8},{4,12},{8,0},{12,4},{16,24},{20,28},{24,16},{28,20},{1,9},{5... | collective-permute-start | bytes 319496 | tf_op jit(solution)/shard_map/ppermute | solution.py:1264
  55.3 3.1 %collective-permute-done.11 = bf16[416,128]{1,0:T(8,128)(2,1)S(1)} collective-permute-done((bf16[416,128]{1,0:T(8,128)(2,1)S(1)}, bf16[416,128]{1,0:T(8,128)(2,1)S(1)}, u32[]{:S(2)}, u32[]{:S(2)}) %collective-permute-start.11) | collective-permute-done | bytes 106528 | tf_op jit(solution)/shard_map/ppermute | solution.py:1264
  58.5 2.7 %collective-permute-start.12 = (bf16[416,128]{1,0:T(8,128)(2,1)S(1)}, bf16[416,128]{1,0:T(8,128)(2,1)S(1)}, u32[]{:S(2)}, u32[]{:S(2)}) collective-permute-start(bf16[416,128]{1,0:T(8,128)(2,1)S(1)} %fusion), channel_id=1, source_target_pairs={{0,16},{4,20},{8,24},{12,28},{16,0},{20,4},{24,8},{28,12},{1,17},{... | collective-permute-start | bytes 319496 | tf_op jit(solution)/shard_map/ppermute | solution.py:1264
  61.2 4.6 %collective-permute-done.12 = bf16[416,128]{1,0:T(8,128)(2,1)S(1)} collective-permute-done((bf16[416,128]{1,0:T(8,128)(2,1)S(1)}, bf16[416,128]{1,0:T(8,128)(2,1)S(1)}, u32[]{:S(2)}, u32[]{:S(2)}) %collective-permute-start.12) | collective-permute-done | bytes 106528 | tf_op jit(solution)/shard_map/ppermute | solution.py:1264
  65.9 0.1 add_reduce-precision_fusion.grad
  66.1 0.8 %shard_map.399 = (f32[25,2,256]{2,1,0:T(2,128)S(1)}, f32[2,64,256]{2,1,0:T(8,128)S(1)}, f32[47,2,64]{2,1,0:T(2,128)S(1)}, f32[2,64]{1,0:T(2,128)S(1)}, f32[1,47]...) custom-call(f32[416,128]{1,0:T(8,128)S(1)} %add_reduce-precision_fusion.grad, f32[25,2,256]{2,1,0:T(2,128)S(1)} %bitcast.31, ...), custom_call_target="tpu_custom_call" | custom-call | flops 1000000000 | bytes 1 | tf_op jit(solution)/shard_map/pallas_call | solution.py:47
  66.9 0.9 %shard_map.401 = (f32[25,2,256]{2,1,0:T(2,128)}, f32[2,64,256]{2,1,0:T(8,128)}, f32[47,2,64]{2,1,0:T(2,128)}, f32[2,64]{1,0:T(2,128)}, f32[1,47]{1,0:T(1,128)}, ...) custom-call(f32[416,128]{1,0:T(8,128)S(1)} %add_reduce-precision_fus, ...), custom_call_target="tpu_custom_call" | custom-call | flops 2000000000 | bytes 1 | tf_op jit(solution)/shard_map/pallas_call | solution.py:47
  67.8 0.2 collective-permute-done.13
  68.1 1.6 %collective-permute-start.14 = (f32[8,128]{1,0:T(8,128)S(1)}, f32[8,128]{1,0:T(8,128)S(1)}, u32[]{:S(2)}, u32[]{:S(2)}) collective-permute-start(f32[8,128]{1,0:T(8,128)S(1)} %add.31.own), channel_id=1, source_target_pairs={{0,2},{1,3},{2,0},{3,1},{4,6},{5,7},{6,4},{7,5},{8,10},{9,11},{10,... | collective-permute-start | bytes 12296 | tf_op jit(solution)/shard_map/ppermute | solution.py:1264
  69.7 0.6 fusion.2
  70.3 1.4 %collective-permute-done.14.far = f32[8,128]{1,0:T(8,128)S(1)} collective-permute-done((f32[8,128]{1,0:T(8,128)S(1)}, f32[8,128]{1,0:T(8,128)S(1)}, u32[]{:S(2)}, u32[]{:S(2)}) %collective-permute-start.14) | collective-permute-done | bytes 4128 | tf_op jit(solution)/shard_map/ppermute | solution.py:1264
  71.7 0.8 %shard_map.400 = (f32[25,2,256]{2,1,0:T(2,128)}, f32[2,64,256]{2,1,0:T(8,128)}, f32[47,2,64]{2,1,0:T(2,128)}, f32[2,64]{1,0:T(2,128)}, f32[1,47]{1,0:T(1,128)}, /*index=5*/f32[2,5]{1,0:T(2,128)}) custom-call(f32[8,128]{1,0:T(8,128)S(1)} %add.31.own, f32[8,128]{1,0:T(8,128)S(1)} %collective-permute-done.14.far, f32[25,2,256]{2,1,0:T(2,128)S(1)} %bitcast.32, ...), custom_call_target="tpu_custom_call" | custom-call | flops 1000000000 | bytes 1 | tf_op jit(solution)/shard_map/pallas_call | solution.py:47
  (58 shorter events, 0.5 us)
Async XLA Ops:
  0.7 7.3 %copy-start = (bf16[25,32768]{1,0:T(8,128)(2,1)S(1)}, bf16[25,32768]{1,0:T(8,128)(2,1)}, u32[]{:S(2)}) copy-start(bf16[25,32768]{1,0:T(8,128)(2,1)} %feat_ref.1) | copy-start | bytes 4915204
  4.8 10.4 %collective-permute-start.2 = (bf16[24,2176]{1,0:T(8,128)(2,1)S(1)}, bf16[24,2176]{1,0:T(8,128)(2,1)S(1)}, u32[]{:S(2)}, u32[]{:S(2)}) collective-permute-start(bf16[24,2176]{1,0:T(8,128)(2,1)S(1)} %get-tuple-element.76), channel_id=1, source_target_pairs={{0,3},{1,2},{2,1},{3,0},{4,7},{5,6},{6,5},{7,4},{8,11},{9,10},{10,... | collective-permute-start | bytes 313352 | tf_op jit(solution)/shard_map/ppermute | solution.py:1264
  7.2 8.2 %collective-permute-start = (bf16[24,4352]{1,0:T(8,128)(2,1)S(1)}, bf16[24,4352]{1,0:T(8,128)(2,1)S(1)}, u32[]{:S(2)}, u32[]{:S(2)}) collective-permute-start(bf16[24,4352]{1,0:T(8,128)(2,1)S(1)} %get-tuple-element.68), channel_id=1, source_target_pairs={{0,1},{1,0},{2,3},{3,2},{4,5},{5,4},{6,7},{7,6},{8,9},{9,8},{10,11... | collective-permute-start | bytes 626696 | tf_op jit(solution)/shard_map/ppermute | solution.py:1264
  7.9 7.3 %collective-permute-start.1 = (bf16[24,4352]{1,0:T(8,128)(2,1)S(1)}, bf16[24,4352]{1,0:T(8,128)(2,1)S(1)}, u32[]{:S(2)}, u32[]{:S(2)}) collective-permute-start(bf16[24,4352]{1,0:T(8,128)(2,1)S(1)} %get-tuple-element.75), channel_id=1, source_target_pairs={{0,2},{1,3},{2,0},{3,1},{4,6},{5,7},{6,4},{7,5},{8,10},{9,11},{10,... | collective-permute-start | bytes 626696 | tf_op jit(solution)/shard_map/ppermute | solution.py:1264
  15.2 2.8 %collective-permute-start.3 = (bf16[24,4352]{1,0:T(8,128)(2,1)S(1)}, bf16[24,4352]{1,0:T(8,128)(2,1)S(1)}, u32[]{:S(2)}, u32[]{:S(2)}) collective-permute-start(bf16[24,4352]{1,0:T(8,128)(2,1)S(1)} %collective-permute-done.1.s2.e2), channel_id=1, source_target_pairs={{0,1},{1,0},{2,3},{3,2},{4,5},{5,4},{6,7},{7,6},{8,9},{9,8},{10,11... | collective-permute-start | bytes 626696 | tf_op jit(solution)/shard_map/ppermute | solution.py:1264
  15.4 13.4 %collective-permute-start.4 = (bf16[24,5120]{1,0:T(8,128)(2,1)S(1)}, bf16[24,5120]{1,0:T(8,128)(2,1)S(1)}, u32[]{:S(2)}, u32[]{:S(2)}) collective-permute-start(bf16[24,5120]{1,0:T(8,128)(2,1)S(1)} %get-tuple-element.85), channel_id=1, source_target_pairs={{0,1},{1,0},{2,3},{3,2},{4,5},{5,4},{6,7},{7,6},{8,9},{9,8},{10,11... | collective-permute-start | bytes 737288 | tf_op jit(solution)/shard_map/ppermute | solution.py:1264
  15.7 13.1 %collective-permute-start.5 = (bf16[24,5120]{1,0:T(8,128)(2,1)S(1)}, bf16[24,5120]{1,0:T(8,128)(2,1)S(1)}, u32[]{:S(2)}, u32[]{:S(2)}) collective-permute-start(bf16[24,5120]{1,0:T(8,128)(2,1)S(1)} %get-tuple-element.86), channel_id=1, source_target_pairs={{0,2},{1,3},{2,0},{3,1},{4,6},{5,7},{6,4},{7,5},{8,10},{9,11},{10,... | collective-permute-start | bytes 737288 | tf_op jit(solution)/shard_map/ppermute | solution.py:1264
  18.0 10.9 %collective-permute-start.6 = (bf16[24,5120]{1,0:T(8,128)(2,1)S(1)}, bf16[24,5120]{1,0:T(8,128)(2,1)S(1)}, u32[]{:S(2)}, u32[]{:S(2)}) collective-permute-start(bf16[24,5120]{1,0:T(8,128)(2,1)S(1)} %get-tuple-element.87), channel_id=1, source_target_pairs={{0,3},{1,2},{2,1},{3,0},{4,7},{5,6},{6,5},{7,4},{8,11},{9,10},{10,... | collective-permute-start | bytes 737288 | tf_op jit(solution)/shard_map/ppermute | solution.py:1264
  22.6 16.9 %all-to-all-start = ((bf16[32,8,512]{2,1,0:T(8,128)(2,1)}), bf16[32,8,512]{2,1,0:T(8,128)(2,1)S(1)}, u32[]{:S(2)}, u32[]{:S(2)}) async-start(bf16[32,8,512]{2,1,0:T(8,128)(2,1)} %bitcast.3), calls=%async_computation | async-start | bytes 524288 | tf_op jit(solution)/shard_map/all_to_all | solution.py:1300
  43.0 22.9 %copy-start.5 = (f32[2,64,256]{2,1,0:T(8,128)S(1)}, f32[2,64,256]{2,1,0:T(8,128)}, u32[]{:S(2)}) copy-start(f32[2,64,256]{2,1,0:T(8,128)} %rest_1_.3) | copy-start | bytes 393220
  43.1 22.9 %copy-start.6 = (f32[2,64,256]{2,1,0:T(8,128)S(1)}, f32[2,64,256]{2,1,0:T(8,128)}, u32[]{:S(2)}) copy-start(f32[2,64,256]{2,1,0:T(8,128)} %rest_6_.3) | copy-start | bytes 393220
  43.1 22.9 %copy-start.7 = (f32[2,64,256]{2,1,0:T(8,128)S(1)}, f32[2,64,256]{2,1,0:T(8,128)}, u32[]{:S(2)}) copy-start(f32[2,64,256]{2,1,0:T(8,128)} %w2.1) | copy-start | bytes 393220
  43.1 22.9 %copy-start.8 = (f32[2,25,256]{2,0,1:T(2,128)S(1)}, f32[2,25,256]{2,0,1:T(2,128)}, u32[]{:S(2)}) copy-start(f32[2,25,256]{2,0,1:T(2,128)} %param.44) | copy-start | bytes 153604
  43.1 22.9 %copy-start.9 = (f32[2,25,256]{2,0,1:T(2,128)S(1)}, f32[2,25,256]{2,0,1:T(2,128)}, u32[]{:S(2)}) copy-start(f32[2,25,256]{2,0,1:T(2,128)} %param.49) | copy-start | bytes 153604
  43.1 22.9 %copy-start.10 = (f32[2,25,256]{2,0,1:T(2,128)S(1)}, f32[2,25,256]{2,0,1:T(2,128)}, u32[]{:S(2)}) copy-start(f32[2,25,256]{2,0,1:T(2,128)} %param.39) | copy-start | bytes 153604
  43.1 22.9 %copy-start.11 = (f32[2,64,47]{1,0,2:T(2,128)S(1)}, f32[2,64,47]{1,0,2:T(2,128)}, u32[]{:S(2)}) copy-start(f32[2,64,47]{1,0,2:T(2,128)} %param.46) | copy-start | bytes 72196
  43.1 22.9 %copy-start.12 = (f32[2,64,47]{1,0,2:T(2,128)S(1)}, f32[2,64,47]{1,0,2:T(2,128)}, u32[]{:S(2)}) copy-start(f32[2,64,47]{1,0,2:T(2,128)} %param.51) | copy-start | bytes 72196
  43.1 22.9 %copy-start.13 = (f32[2,64,47]{1,0,2:T(2,128)S(1)}, f32[2,64,47]{1,0,2:T(2,128)}, u32[]{:S(2)}) copy-start(f32[2,64,47]{1,0,2:T(2,128)} %param.41) | copy-start | bytes 72196
  43.2 22.9 %copy-start.16 = (f32[2,64]{1,0:T(2,128)S(1)}, f32[2,64]{1,0:T(2,128)}, u32[]{:S(2)}) copy-start(f32[2,64]{1,0:T(2,128)} %rest_3_.3) | copy-start | bytes 1540
  43.2 22.9 %copy-start.17 = (f32[2,64]{1,0:T(2,128)S(1)}, f32[2,64]{1,0:T(2,128)}, u32[]{:S(2)}) copy-start(f32[2,64]{1,0:T(2,128)} %rest_8_.3) | copy-start | bytes 1540
  43.2 22.9 %copy-start.18 = (f32[2,64]{1,0:T(2,128)S(1)}, f32[2,64]{1,0:T(2,128)}, u32[]{:S(2)}) copy-start(f32[2,64]{1,0:T(2,128)} %wh.1) | copy-start | bytes 1540
  43.2 22.9 %copy-start.19 = (f32[47]{0:T(128)S(1)}, f32[47]{0:T(128)}, u32[]{:S(2)}) copy-start(f32[47]{0:T(128)} %param.48) | copy-start | bytes 568
  43.2 22.9 %copy-start.20 = (f32[47]{0:T(128)S(1)}, f32[47]{0:T(128)}, u32[]{:S(2)}) copy-start(f32[47]{0:T(128)} %param.53) | copy-start | bytes 568
  43.2 22.9 %copy-start.21 = (f32[47]{0:T(128)S(1)}, f32[47]{0:T(128)}, u32[]{:S(2)}) copy-start(f32[47]{0:T(128)} %param.43) | copy-start | bytes 568
  43.2 1.5 %collective-permute-start.7 = (bf16[832,128]{1,0:T(8,128)(2,1)S(1)}, bf16[832,128]{1,0:T(8,128)(2,1)S(1)}, u32[]{:S(2)}, u32[]{:S(2)}) collective-permute-start(bf16[832,128]{1,0:T(8,128)(2,1)S(1)} %get-tuple-element.89), channel_id=1, source_target_pairs={{0,1},{1,0},{2,3},{3,2},{4,5},{5,4},{6,7},{7,6},{8,9},{9,8},{10,11... | collective-permute-start | bytes 638984 | tf_op jit(solution)/shard_map/ppermute | solution.py:1264
  44.8 6.3 %collective-permute-start.10 = (bf16[416,128]{1,0:T(8,128)(2,1)S(1)}, bf16[416,128]{1,0:T(8,128)(2,1)S(1)}, u32[]{:S(2)}, u32[]{:S(2)}) collective-permute-start(bf16[416,128]{1,0:T(8,128)(2,1)S(1)} %get-tuple-element.115), channel_id=1, source_target_pairs={{0,6},{1,7},{2,4},{3,5},{4,2},{5,3},{6,0},{7,1},{8,14},{9,15},{10,... | collective-permute-start | bytes 319496 | tf_op jit(solution)/shard_map/ppermute | solution.py:1308
  47.5 5.8 %collective-permute-start.8 = (bf16[416,128]{1,0:T(8,128)(2,1)S(1)}, bf16[416,128]{1,0:T(8,128)(2,1)S(1)}, u32[]{:S(2)}, u32[]{:S(2)}) collective-permute-start(bf16[416,128]{1,0:T(8,128)(2,1)S(1)} %get-tuple-element.115), channel_id=1, source_target_pairs={{0,2},{1,3},{2,0},{3,1},{4,6},{5,7},{6,4},{7,5},{8,10},{9,11},{10,... | collective-permute-start | bytes 319496 | tf_op jit(solution)/shard_map/ppermute | solution.py:1264
  48.0 5.6 %collective-permute-start.9 = (bf16[416,128]{1,0:T(8,128)(2,1)S(1)}, bf16[416,128]{1,0:T(8,128)(2,1)S(1)}, u32[]{:S(2)}, u32[]{:S(2)}) collective-permute-start(bf16[416,128]{1,0:T(8,128)(2,1)S(1)} %get-tuple-element.114), channel_id=1, source_target_pairs={{0,4},{4,0},{8,12},{12,8},{16,20},{20,16},{24,28},{28,24},{1,5},{5... | collective-permute-start | bytes 319496 | tf_op jit(solution)/shard_map/ppermute | solution.py:1264
  53.6 4.8 %collective-permute-start.11 = (bf16[416,128]{1,0:T(8,128)(2,1)S(1)}, bf16[416,128]{1,0:T(8,128)(2,1)S(1)}, u32[]{:S(2)}, u32[]{:S(2)}) collective-permute-start(bf16[416,128]{1,0:T(8,128)(2,1)S(1)} %fusion.1), channel_id=1, source_target_pairs={{0,8},{4,12},{8,0},{12,4},{16,24},{20,28},{24,16},{28,20},{1,9},{5... | collective-permute-start | bytes 319496 | tf_op jit(solution)/shard_map/ppermute | solution.py:1264
  58.5 7.4 %collective-permute-start.12 = (bf16[416,128]{1,0:T(8,128)(2,1)S(1)}, bf16[416,128]{1,0:T(8,128)(2,1)S(1)}, u32[]{:S(2)}, u32[]{:S(2)}) collective-permute-start(bf16[416,128]{1,0:T(8,128)(2,1)S(1)} %fusion), channel_id=1, source_target_pairs={{0,16},{4,20},{8,24},{12,28},{16,0},{20,4},{24,8},{28,12},{1,17},{... | collective-permute-start | bytes 319496 | tf_op jit(solution)/shard_map/ppermute | solution.py:1264
  66.9 1.2 %collective-permute-start.13 = (f32[8,128]{1,0:T(8,128)S(1)}, f32[8,128]{1,0:T(8,128)S(1)}, u32[]{:S(2)}, u32[]{:S(2)}) collective-permute-start(f32[8,128]{1,0:T(8,128)S(1)} %get-tuple-element.91), channel_id=1, source_target_pairs={{0,1},{1,0},{2,3},{3,2},{4,5},{5,4},{6,7},{7,6},{8,9},{9,8},{10,11... | collective-permute-start | bytes 12296 | tf_op jit(solution)/shard_map/ppermute | solution.py:1264
  68.1 3.6 %collective-permute-start.14 = (f32[8,128]{1,0:T(8,128)S(1)}, f32[8,128]{1,0:T(8,128)S(1)}, u32[]{:S(2)}, u32[]{:S(2)}) collective-permute-start(f32[8,128]{1,0:T(8,128)S(1)} %add.31.own), channel_id=1, source_target_pairs={{0,2},{1,3},{2,0},{3,1},{4,6},{5,7},{6,4},{7,5},{8,10},{9,11},{10,... | collective-permute-start | bytes 12296 | tf_op jit(solution)/shard_map/ppermute | solution.py:1264
  (6 other events, 43.7 us)

commit v8 on v7

--- a/solution.py
+++ b/solution.py
@@ -292,8 +292,8 @@
         mean_ref[:, pl.ds(aligned((step + 2) * LANES), LANES)] = (jnp.concatenate(totals, 0) / counts).astype(BF)
         return carry
 
-    even = begin + (tiles - begin) // 4 * 4
-    lax.fori_loop(begin, even, one_tile, 0, unroll=4)
+    even = begin + (tiles - begin) // 8 * 8
+    lax.fori_loop(begin, even, one_tile, 0, unroll=8)
     for step in range(even, tiles):
         one_tile(step, 0)
     sub = lax.broadcasted_iota(jnp.int32, (8, LANES), 0)

time: 72.8 us -> 72.6 us (level)
  transfers between devices with their start and end apart: 16 -> 16, of which waited for: 10 -> 10; matrix products, arithmetic and copies ran while one was open for 1% -> 1% of each run, Pallas kernels for 32% -> 31%
where the time goes in v8:
time: 72.6 us; the launch traced here: 72.3 us
  Pallas kernels  31.6 us (44%)
  starting transfers between devices  22.2 us (31%)
  waiting for transfers between devices  16.4 us (23%)
  between operations  1.09 us (2%)
    pallas_call x8, Pallas kernels, call(): pl.pallas_call(kernel, in_specs=[free if i in loose else far if i in far_...  31.6 us
    ppermute x14, waiting for transfers between devices, swap(): return lax.ppermute(value, axis, [(i, i ^ bit) for i in range(count)])  13.6 us
    ppermute x14, starting transfers between devices, swap(): return lax.ppermute(value, axis, [(i, i ^ bit) for i in range(count)])  13.2 us
    all_to_all x1, starting transfers between devices, shards(): lax.all_to_all(rows, ('dp', 'col'), split_axis=0, concat_axis=0, tiled=True)  6.25 us
    ppermute x1, waiting for transfers between devices, shards(): lax.ppermute(far, ('dp', 'col'), pair)  2.75 us
    ppermute x1, starting transfers between devices, shards(): lax.ppermute(far, ('dp', 'col'), pair)  2.74 us
  transfers between devices with their start and end apart: 16, of which 10 were waited for; matrix products, arithmetic and copies ran while one was open for 1% of the time, Pallas kernels for 31%

profile of v8, /device:TPU:0, one launch (start us, length us, event | category | flops | bytes accessed | tf_op | source)
XLA Modules:
  0.0 72.3 jit_solution(14708224691560673002)
XLA Ops:
  0.7 3.9 %shard_map.394 = (bf16[64,768]{1,0:T(8,128)(2,1)}, f32[408,128]{1,0:T(8,128)}, bf16[24,2432]{1,0:T(8,128)(2,1)}, f32[72,128]{1,0:T(8,128)}, bf16[24,4352]{1,0:T(...) custom-call(bf16[25,32768]{1,0:T(8,128)(2,1)} %feat_ref.1, s32[5,8192]{1,0:T(8,128)} %nbr_ref.1, ...), custom_call_target="tpu_custom_call" | custom-call | flops 4000000000 | bytes 1 | tf_op jit(solution)/shard_map/pallas_call | solution.py:47
  4.6 2.5 %collective-permute-start.2 = (bf16[24,2176]{1,0:T(8,128)(2,1)S(1)}, bf16[24,2176]{1,0:T(8,128)(2,1)S(1)}, u32[]{:S(2)}, u32[]{:S(2)}) collective-permute-start(bf16[24,2176]{1,0:T(8,128)(2,1)S(1)} %get-tuple-element.76), channel_id=1, source_target_pairs={{0,3},{1,2},{2,1},{3,0},{4,7},{5,6},{6,5},{7,4},{8,11},{9,10},{10,... | collective-permute-start | bytes 313352 | tf_op jit(solution)/shard_map/ppermute | solution.py:1264
  7.1 0.7 collective-permute-start
  7.9 6.7 %shard_map.395 = (bf16[64,2688]{1,0:T(8,128)(2,1)}, bf16[4592,128]{1,0:T(8,128)(2,1)}, bf16[24,5120]{1,0:T(8,128)(2,1)S(1)}, bf16[24,5120]{1,0:T(8,128)(2,1)S(1)}, bf16[24,5120]{1,0:T(8,128)(2,1)S(1)}) custom-call(bf16[25,32768]{1,0:T(8,128)(2,1)S(1)} %copy-done, s32[5,8192]{1,0:T(8,128)S(1)} %copy-done.1, s32[5,8192]{1,0:T(8,128)S(1)} %copy-done.2, ...), custom_call_target="tpu_custom_call" | custom-call | flops 6000000000 | bytes 1 | tf_op jit(solution)/shard_map/pallas_call | solution.py:47
  14.5 0.5 collective-permute-done.1.s2.e2
  15.1 0.5 collective-permute-start.4
  15.6 2.3 %collective-permute-start.5 = (bf16[24,5120]{1,0:T(8,128)(2,1)S(1)}, bf16[24,5120]{1,0:T(8,128)(2,1)S(1)}, u32[]{:S(2)}, u32[]{:S(2)}) collective-permute-start(bf16[24,5120]{1,0:T(8,128)(2,1)S(1)} %get-tuple-element.86), channel_id=1, source_target_pairs={{0,2},{1,3},{2,0},{3,1},{4,6},{5,7},{6,4},{7,5},{8,10},{9,11},{10,... | collective-permute-start | bytes 737288 | tf_op jit(solution)/shard_map/ppermute | solution.py:1264
  17.9 4.5 %shard_map.396 = (bf16[256,3968]{1,0:T(8,128)(2,1)}, f32[264,1152]{1,0:T(8,128)}, bf16[256,512]{1,0:T(8,128)(2,1)}) custom-call(bf16[64,768]{1,0:T(8,128)(2,1)} %get-tuple-element.66.own_b, f32[408,128]{1,0:T(8,128)} %get-tuple-element.67.packed, bf16[24,4352]{1,0:T(8,128)(2,1)S(1)} %collective-permute-done.s1.e1, ...), custom_call_target="tpu_custom_call" | custom-call | flops 4000000000 | bytes 1 | tf_op jit(solution)/shard_map/pallas_call | solution.py:47
  22.4 6.3 %all-to-all-start = ((bf16[32,8,512]{2,1,0:T(8,128)(2,1)}), bf16[32,8,512]{2,1,0:T(8,128)(2,1)S(1)}, u32[]{:S(2)}, u32[]{:S(2)}) async-start(bf16[32,8,512]{2,1,0:T(8,128)(2,1)} %bitcast.3), calls=%async_computation | async-start | bytes 524288 | tf_op jit(solution)/shard_map/all_to_all | solution.py:1300
  28.7 0.1 collective-permute-done.6.a3
  28.8 10.5 %shard_map.397.part_in = f32[264,2048]{1,0:T(8,128)} custom-call(bf16[256,3968]{1,0:T(8,128)(2,1)} %get-tuple-element.82.low_in, f32[264,1152]{1,0:T(8,128)} %get-tuple-element.83.high_in, bf16[4592,128]{1,0:T(8,128)(2,1)} %get-tuple-element.80.counts_in, bf16[64,2688]{1,0:T(8,128)(2,1)} %get-tuple-element.84.own_a, ...), custom_call_target="tpu_custom_call" | custom-call | flops 14000000000 | bytes 1 | tf_op jit(solution)/shard_map/pallas_call | solution.py:47
  39.3 3.6 %shard_map.398 = (bf16[416,128]{1,0:T(8,128)(2,1)S(1)}, bf16[416,128]{1,0:T(8,128)(2,1)S(1)}, bf16[832,128]{1,0:T(8,128)(2,1)S(1)}) custom-call(s32[8,8]{1,0:T(8,128)} %serve_in.3, s32[8,8]{1,0:T(8,128)} %take_in.3, s32[1,8]{1,0:T(1,128)} %bitcast.50, bf16[256,512]{1,0:T(8,128)(2,1)S(1)} %bitcast.25, bf16[256,3968]{1,0:T(8,128)(2,1)} %get-tuple-element.82.low_in, ...), custom_call_target="tpu_custom_call" | custom-call | flops 3000000000 | bytes 1 | tf_op jit(solution)/shard_map/pallas_call | solution.py:47
  43.1 0.4 collective-permute-start.7
  43.5 1.1 %collective-permute-done.7 = bf16[832,128]{1,0:T(8,128)(2,1)S(1)} collective-permute-done((bf16[832,128]{1,0:T(8,128)(2,1)S(1)}, bf16[832,128]{1,0:T(8,128)(2,1)S(1)}, u32[]{:S(2)}, u32[]{:S(2)}) %collective-permute-start.7) | collective-permute-done | bytes 213024 | tf_op jit(solution)/shard_map/ppermute | solution.py:1264
  44.7 2.7 %collective-permute-start.10 = (bf16[416,128]{1,0:T(8,128)(2,1)S(1)}, bf16[416,128]{1,0:T(8,128)(2,1)S(1)}, u32[]{:S(2)}, u32[]{:S(2)}) collective-permute-start(bf16[416,128]{1,0:T(8,128)(2,1)S(1)} %get-tuple-element.115), channel_id=1, source_target_pairs={{0,6},{1,7},{2,4},{3,5},{4,2},{5,3},{6,0},{7,1},{8,14},{9,15},{10,... | collective-permute-start | bytes 319496 | tf_op jit(solution)/shard_map/ppermute | solution.py:1308
  47.4 0.5 collective-permute-start.8
  47.8 0.4 collective-permute-start.9
  48.2 2.7 %collective-permute-done.10 = bf16[416,128]{1,0:T(8,128)(2,1)S(1)} collective-permute-done((bf16[416,128]{1,0:T(8,128)(2,1)S(1)}, bf16[416,128]{1,0:T(8,128)(2,1)S(1)}, u32[]{:S(2)}, u32[]{:S(2)}) %collective-permute-start.10) | collective-permute-done | bytes 106528 | tf_op jit(solution)/shard_map/ppermute | solution.py:1308
  51.0 2.2 %collective-permute-done.8 = bf16[416,128]{1,0:T(8,128)(2,1)S(1)} collective-permute-done((bf16[416,128]{1,0:T(8,128)(2,1)S(1)}, bf16[416,128]{1,0:T(8,128)(2,1)S(1)}, u32[]{:S(2)}, u32[]{:S(2)}) %collective-permute-start.8) | collective-permute-done | bytes 106528 | tf_op jit(solution)/shard_map/ppermute | solution.py:1264
  53.2 0.3 collective-permute-done.9
  53.5 1.6 %collective-permute-start.11 = (bf16[416,128]{1,0:T(8,128)(2,1)S(1)}, bf16[416,128]{1,0:T(8,128)(2,1)S(1)}, u32[]{:S(2)}, u32[]{:S(2)}) collective-permute-start(bf16[416,128]{1,0:T(8,128)(2,1)S(1)} %fusion.1), channel_id=1, source_target_pairs={{0,8},{4,12},{8,0},{12,4},{16,24},{20,28},{24,16},{28,20},{1,9},{5... | collective-permute-start | bytes 319496 | tf_op jit(solution)/shard_map/ppermute | solution.py:1264
  55.1 3.1 %collective-permute-done.11 = bf16[416,128]{1,0:T(8,128)(2,1)S(1)} collective-permute-done((bf16[416,128]{1,0:T(8,128)(2,1)S(1)}, bf16[416,128]{1,0:T(8,128)(2,1)S(1)}, u32[]{:S(2)}, u32[]{:S(2)}) %collective-permute-start.11) | collective-permute-done | bytes 106528 | tf_op jit(solution)/shard_map/ppermute | solution.py:1264
  58.3 2.7 %collective-permute-start.12 = (bf16[416,128]{1,0:T(8,128)(2,1)S(1)}, bf16[416,128]{1,0:T(8,128)(2,1)S(1)}, u32[]{:S(2)}, u32[]{:S(2)}) collective-permute-start(bf16[416,128]{1,0:T(8,128)(2,1)S(1)} %fusion), channel_id=1, source_target_pairs={{0,16},{4,20},{8,24},{12,28},{16,0},{20,4},{24,8},{28,12},{1,17},{... | collective-permute-start | bytes 319496 | tf_op jit(solution)/shard_map/ppermute | solution.py:1264
  61.1 4.6 %collective-permute-done.12 = bf16[416,128]{1,0:T(8,128)(2,1)S(1)} collective-permute-done((bf16[416,128]{1,0:T(8,128)(2,1)S(1)}, bf16[416,128]{1,0:T(8,128)(2,1)S(1)}, u32[]{:S(2)}, u32[]{:S(2)}) %collective-permute-start.12) | collective-permute-done | bytes 106528 | tf_op jit(solution)/shard_map/ppermute | solution.py:1264
  65.7 0.1 add_reduce-precision_fusion.grad
  66.0 0.8 %shard_map.399 = (f32[25,2,256]{2,1,0:T(2,128)S(1)}, f32[2,64,256]{2,1,0:T(8,128)S(1)}, f32[47,2,64]{2,1,0:T(2,128)S(1)}, f32[2,64]{1,0:T(2,128)S(1)}, f32[1,47]...) custom-call(f32[416,128]{1,0:T(8,128)S(1)} %add_reduce-precision_fusion.grad, f32[25,2,256]{2,1,0:T(2,128)S(1)} %bitcast.31, ...), custom_call_target="tpu_custom_call" | custom-call | flops 1000000000 | bytes 1 | tf_op jit(solution)/shard_map/pallas_call | solution.py:47
  66.8 0.9 %shard_map.401 = (f32[25,2,256]{2,1,0:T(2,128)}, f32[2,64,256]{2,1,0:T(8,128)}, f32[47,2,64]{2,1,0:T(2,128)}, f32[2,64]{1,0:T(2,128)}, f32[1,47]{1,0:T(1,128)}, ...) custom-call(f32[416,128]{1,0:T(8,128)S(1)} %add_reduce-precision_fus, ...), custom_call_target="tpu_custom_call" | custom-call | flops 2000000000 | bytes 1 | tf_op jit(solution)/shard_map/pallas_call | solution.py:47
  67.7 0.2 collective-permute-done.13
  67.9 1.6 %collective-permute-start.14 = (f32[8,128]{1,0:T(8,128)S(1)}, f32[8,128]{1,0:T(8,128)S(1)}, u32[]{:S(2)}, u32[]{:S(2)}) collective-permute-start(f32[8,128]{1,0:T(8,128)S(1)} %add.31.own), channel_id=1, source_target_pairs={{0,2},{1,3},{2,0},{3,1},{4,6},{5,7},{6,4},{7,5},{8,10},{9,11},{10,... | collective-permute-start | bytes 12296 | tf_op jit(solution)/shard_map/ppermute | solution.py:1264
  69.5 0.6 fusion.2
  70.1 1.4 %collective-permute-done.14.far = f32[8,128]{1,0:T(8,128)S(1)} collective-permute-done((f32[8,128]{1,0:T(8,128)S(1)}, f32[8,128]{1,0:T(8,128)S(1)}, u32[]{:S(2)}, u32[]{:S(2)}) %collective-permute-start.14) | collective-permute-done | bytes 4128 | tf_op jit(solution)/shard_map/ppermute | solution.py:1264
  71.5 0.8 %shard_map.400 = (f32[25,2,256]{2,1,0:T(2,128)}, f32[2,64,256]{2,1,0:T(8,128)}, f32[47,2,64]{2,1,0:T(2,128)}, f32[2,64]{1,0:T(2,128)}, f32[1,47]{1,0:T(1,128)}, /*index=5*/f32[2,5]{1,0:T(2,128)}) custom-call(f32[8,128]{1,0:T(8,128)S(1)} %add.31.own, f32[8,128]{1,0:T(8,128)S(1)} %collective-permute-done.14.far, f32[25,2,256]{2,1,0:T(2,128)S(1)} %bitcast.32, ...), custom_call_target="tpu_custom_call" | custom-call | flops 1000000000 | bytes 1 | tf_op jit(solution)/shard_map/pallas_call | solution.py:47
  (58 shorter events, 0.4 us)
Async XLA Ops:
  0.7 7.2 %copy-start = (bf16[25,32768]{1,0:T(8,128)(2,1)S(1)}, bf16[25,32768]{1,0:T(8,128)(2,1)}, u32[]{:S(2)}) copy-start(bf16[25,32768]{1,0:T(8,128)(2,1)} %feat_ref.1) | copy-start | bytes 4915204
  4.6 9.9 %collective-permute-start.2 = (bf16[24,2176]{1,0:T(8,128)(2,1)S(1)}, bf16[24,2176]{1,0:T(8,128)(2,1)S(1)}, u32[]{:S(2)}, u32[]{:S(2)}) collective-permute-start(bf16[24,2176]{1,0:T(8,128)(2,1)S(1)} %get-tuple-element.76), channel_id=1, source_target_pairs={{0,3},{1,2},{2,1},{3,0},{4,7},{5,6},{6,5},{7,4},{8,11},{9,10},{10,... | collective-permute-start | bytes 313352 | tf_op jit(solution)/shard_map/ppermute | solution.py:1264
  7.1 8.0 %collective-permute-start = (bf16[24,4352]{1,0:T(8,128)(2,1)S(1)}, bf16[24,4352]{1,0:T(8,128)(2,1)S(1)}, u32[]{:S(2)}, u32[]{:S(2)}) collective-permute-start(bf16[24,4352]{1,0:T(8,128)(2,1)S(1)} %get-tuple-element.68), channel_id=1, source_target_pairs={{0,1},{1,0},{2,3},{3,2},{4,5},{5,4},{6,7},{7,6},{8,9},{9,8},{10,11... | collective-permute-start | bytes 626696 | tf_op jit(solution)/shard_map/ppermute | solution.py:1264
  7.8 7.3 %collective-permute-start.1 = (bf16[24,4352]{1,0:T(8,128)(2,1)S(1)}, bf16[24,4352]{1,0:T(8,128)(2,1)S(1)}, u32[]{:S(2)}, u32[]{:S(2)}) collective-permute-start(bf16[24,4352]{1,0:T(8,128)(2,1)S(1)} %get-tuple-element.75), channel_id=1, source_target_pairs={{0,2},{1,3},{2,0},{3,1},{4,6},{5,7},{6,4},{7,5},{8,10},{9,11},{10,... | collective-permute-start | bytes 626696 | tf_op jit(solution)/shard_map/ppermute | solution.py:1264
  15.1 2.8 %collective-permute-start.3 = (bf16[24,4352]{1,0:T(8,128)(2,1)S(1)}, bf16[24,4352]{1,0:T(8,128)(2,1)S(1)}, u32[]{:S(2)}, u32[]{:S(2)}) collective-permute-start(bf16[24,4352]{1,0:T(8,128)(2,1)S(1)} %collective-permute-done.1.s2.e2), channel_id=1, source_target_pairs={{0,1},{1,0},{2,3},{3,2},{4,5},{5,4},{6,7},{7,6},{8,9},{9,8},{10,11... | collective-permute-start | bytes 626696 | tf_op jit(solution)/shard_map/ppermute | solution.py:1264
  15.1 13.6 %collective-permute-start.4 = (bf16[24,5120]{1,0:T(8,128)(2,1)S(1)}, bf16[24,5120]{1,0:T(8,128)(2,1)S(1)}, u32[]{:S(2)}, u32[]{:S(2)}) collective-permute-start(bf16[24,5120]{1,0:T(8,128)(2,1)S(1)} %get-tuple-element.85), channel_id=1, source_target_pairs={{0,1},{1,0},{2,3},{3,2},{4,5},{5,4},{6,7},{7,6},{8,9},{9,8},{10,11... | collective-permute-start | bytes 737288 | tf_op jit(solution)/shard_map/ppermute | solution.py:1264
  15.6 13.1 %collective-permute-start.5 = (bf16[24,5120]{1,0:T(8,128)(2,1)S(1)}, bf16[24,5120]{1,0:T(8,128)(2,1)S(1)}, u32[]{:S(2)}, u32[]{:S(2)}) collective-permute-start(bf16[24,5120]{1,0:T(8,128)(2,1)S(1)} %get-tuple-element.86), channel_id=1, source_target_pairs={{0,2},{1,3},{2,0},{3,1},{4,6},{5,7},{6,4},{7,5},{8,10},{9,11},{10,... | collective-permute-start | bytes 737288 | tf_op jit(solution)/shard_map/ppermute | solution.py:1264
  17.9 10.9 %collective-permute-start.6 = (bf16[24,5120]{1,0:T(8,128)(2,1)S(1)}, bf16[24,5120]{1,0:T(8,128)(2,1)S(1)}, u32[]{:S(2)}, u32[]{:S(2)}) collective-permute-start(bf16[24,5120]{1,0:T(8,128)(2,1)S(1)} %get-tuple-element.87), channel_id=1, source_target_pairs={{0,3},{1,2},{2,1},{3,0},{4,7},{5,6},{6,5},{7,4},{8,11},{9,10},{10,... | collective-permute-start | bytes 737288 | tf_op jit(solution)/shard_map/ppermute | solution.py:1264
  22.4 16.9 %all-to-all-start = ((bf16[32,8,512]{2,1,0:T(8,128)(2,1)}), bf16[32,8,512]{2,1,0:T(8,128)(2,1)S(1)}, u32[]{:S(2)}, u32[]{:S(2)}) async-start(bf16[32,8,512]{2,1,0:T(8,128)(2,1)} %bitcast.3), calls=%async_computation | async-start | bytes 524288 | tf_op jit(solution)/shard_map/all_to_all | solution.py:1300
  42.9 22.9 %copy-start.5 = (f32[2,64,256]{2,1,0:T(8,128)S(1)}, f32[2,64,256]{2,1,0:T(8,128)}, u32[]{:S(2)}) copy-start(f32[2,64,256]{2,1,0:T(8,128)} %rest_1_.3) | copy-start | bytes 393220
  42.9 22.9 %copy-start.6 = (f32[2,64,256]{2,1,0:T(8,128)S(1)}, f32[2,64,256]{2,1,0:T(8,128)}, u32[]{:S(2)}) copy-start(f32[2,64,256]{2,1,0:T(8,128)} %rest_6_.3) | copy-start | bytes 393220
  42.9 22.9 %copy-start.7 = (f32[2,64,256]{2,1,0:T(8,128)S(1)}, f32[2,64,256]{2,1,0:T(8,128)}, u32[]{:S(2)}) copy-start(f32[2,64,256]{2,1,0:T(8,128)} %w2.1) | copy-start | bytes 393220
  42.9 22.9 %copy-start.8 = (f32[2,25,256]{2,0,1:T(2,128)S(1)}, f32[2,25,256]{2,0,1:T(2,128)}, u32[]{:S(2)}) copy-start(f32[2,25,256]{2,0,1:T(2,128)} %param.44) | copy-start | bytes 153604
  42.9 22.9 %copy-start.9 = (f32[2,25,256]{2,0,1:T(2,128)S(1)}, f32[2,25,256]{2,0,1:T(2,128)}, u32[]{:S(2)}) copy-start(f32[2,25,256]{2,0,1:T(2,128)} %param.49) | copy-start | bytes 153604
  42.9 22.9 %copy-start.10 = (f32[2,25,256]{2,0,1:T(2,128)S(1)}, f32[2,25,256]{2,0,1:T(2,128)}, u32[]{:S(2)}) copy-start(f32[2,25,256]{2,0,1:T(2,128)} %param.39) | copy-start | bytes 153604
  42.9 22.9 %copy-start.11 = (f32[2,64,47]{1,0,2:T(2,128)S(1)}, f32[2,64,47]{1,0,2:T(2,128)}, u32[]{:S(2)}) copy-start(f32[2,64,47]{1,0,2:T(2,128)} %param.46) | copy-start | bytes 72196
  43.0 22.9 %copy-start.12 = (f32[2,64,47]{1,0,2:T(2,128)S(1)}, f32[2,64,47]{1,0,2:T(2,128)}, u32[]{:S(2)}) copy-start(f32[2,64,47]{1,0,2:T(2,128)} %param.51) | copy-start | bytes 72196
  43.0 22.9 %copy-start.13 = (f32[2,64,47]{1,0,2:T(2,128)S(1)}, f32[2,64,47]{1,0,2:T(2,128)}, u32[]{:S(2)}) copy-start(f32[2,64,47]{1,0,2:T(2,128)} %param.41) | copy-start | bytes 72196
  43.0 22.9 %copy-start.16 = (f32[2,64]{1,0:T(2,128)S(1)}, f32[2,64]{1,0:T(2,128)}, u32[]{:S(2)}) copy-start(f32[2,64]{1,0:T(2,128)} %rest_3_.3) | copy-start | bytes 1540
  43.0 22.9 %copy-start.17 = (f32[2,64]{1,0:T(2,128)S(1)}, f32[2,64]{1,0:T(2,128)}, u32[]{:S(2)}) copy-start(f32[2,64]{1,0:T(2,128)} %rest_8_.3) | copy-start | bytes 1540
  43.0 22.9 %copy-start.18 = (f32[2,64]{1,0:T(2,128)S(1)}, f32[2,64]{1,0:T(2,128)}, u32[]{:S(2)}) copy-start(f32[2,64]{1,0:T(2,128)} %wh.1) | copy-start | bytes 1540
  43.0 22.9 %copy-start.19 = (f32[47]{0:T(128)S(1)}, f32[47]{0:T(128)}, u32[]{:S(2)}) copy-start(f32[47]{0:T(128)} %param.48) | copy-start | bytes 568
  43.0 22.9 %copy-start.20 = (f32[47]{0:T(128)S(1)}, f32[47]{0:T(128)}, u32[]{:S(2)}) copy-start(f32[47]{0:T(128)} %param.53) | copy-start | bytes 568
  43.0 22.9 %copy-start.21 = (f32[47]{0:T(128)S(1)}, f32[47]{0:T(128)}, u32[]{:S(2)}) copy-start(f32[47]{0:T(128)} %param.43) | copy-start | bytes 568
  43.1 1.5 %collective-permute-start.7 = (bf16[832,128]{1,0:T(8,128)(2,1)S(1)}, bf16[832,128]{1,0:T(8,128)(2,1)S(1)}, u32[]{:S(2)}, u32[]{:S(2)}) collective-permute-start(bf16[832,128]{1,0:T(8,128)(2,1)S(1)} %get-tuple-element.89), channel_id=1, source_target_pairs={{0,1},{1,0},{2,3},{3,2},{4,5},{5,4},{6,7},{7,6},{8,9},{9,8},{10,11... | collective-permute-start | bytes 638984 | tf_op jit(solution)/shard_map/ppermute | solution.py:1264
  44.7 6.3 %collective-permute-start.10 = (bf16[416,128]{1,0:T(8,128)(2,1)S(1)}, bf16[416,128]{1,0:T(8,128)(2,1)S(1)}, u32[]{:S(2)}, u32[]{:S(2)}) collective-permute-start(bf16[416,128]{1,0:T(8,128)(2,1)S(1)} %get-tuple-element.115), channel_id=1, source_target_pairs={{0,6},{1,7},{2,4},{3,5},{4,2},{5,3},{6,0},{7,1},{8,14},{9,15},{10,... | collective-permute-start | bytes 319496 | tf_op jit(solution)/shard_map/ppermute | solution.py:1308
  47.4 5.8 %collective-permute-start.8 = (bf16[416,128]{1,0:T(8,128)(2,1)S(1)}, bf16[416,128]{1,0:T(8,128)(2,1)S(1)}, u32[]{:S(2)}, u32[]{:S(2)}) collective-permute-start(bf16[416,128]{1,0:T(8,128)(2,1)S(1)} %get-tuple-element.115), channel_id=1, source_target_pairs={{0,2},{1,3},{2,0},{3,1},{4,6},{5,7},{6,4},{7,5},{8,10},{9,11},{10,... | collective-permute-start | bytes 319496 | tf_op jit(solution)/shard_map/ppermute | solution.py:1264
  47.8 5.6 %collective-permute-start.9 = (bf16[416,128]{1,0:T(8,128)(2,1)S(1)}, bf16[416,128]{1,0:T(8,128)(2,1)S(1)}, u32[]{:S(2)}, u32[]{:S(2)}) collective-permute-start(bf16[416,128]{1,0:T(8,128)(2,1)S(1)} %get-tuple-element.114), channel_id=1, source_target_pairs={{0,4},{4,0},{8,12},{12,8},{16,20},{20,16},{24,28},{28,24},{1,5},{5... | collective-permute-start | bytes 319496 | tf_op jit(solution)/shard_map/ppermute | solution.py:1264
  53.5 4.8 %collective-permute-start.11 = (bf16[416,128]{1,0:T(8,128)(2,1)S(1)}, bf16[416,128]{1,0:T(8,128)(2,1)S(1)}, u32[]{:S(2)}, u32[]{:S(2)}) collective-permute-start(bf16[416,128]{1,0:T(8,128)(2,1)S(1)} %fusion.1), channel_id=1, source_target_pairs={{0,8},{4,12},{8,0},{12,4},{16,24},{20,28},{24,16},{28,20},{1,9},{5... | collective-permute-start | bytes 319496 | tf_op jit(solution)/shard_map/ppermute | solution.py:1264
  58.3 7.4 %collective-permute-start.12 = (bf16[416,128]{1,0:T(8,128)(2,1)S(1)}, bf16[416,128]{1,0:T(8,128)(2,1)S(1)}, u32[]{:S(2)}, u32[]{:S(2)}) collective-permute-start(bf16[416,128]{1,0:T(8,128)(2,1)S(1)} %fusion), channel_id=1, source_target_pairs={{0,16},{4,20},{8,24},{12,28},{16,0},{20,4},{24,8},{28,12},{1,17},{... | collective-permute-start | bytes 319496 | tf_op jit(solution)/shard_map/ppermute | solution.py:1264
  66.7 1.2 %collective-permute-start.13 = (f32[8,128]{1,0:T(8,128)S(1)}, f32[8,128]{1,0:T(8,128)S(1)}, u32[]{:S(2)}, u32[]{:S(2)}) collective-permute-start(f32[8,128]{1,0:T(8,128)S(1)} %get-tuple-element.91), channel_id=1, source_target_pairs={{0,1},{1,0},{2,3},{3,2},{4,5},{5,4},{6,7},{7,6},{8,9},{9,8},{10,11... | collective-permute-start | bytes 12296 | tf_op jit(solution)/shard_map/ppermute | solution.py:1264
  67.9 3.6 %collective-permute-start.14 = (f32[8,128]{1,0:T(8,128)S(1)}, f32[8,128]{1,0:T(8,128)S(1)}, u32[]{:S(2)}, u32[]{:S(2)}) collective-permute-start(f32[8,128]{1,0:T(8,128)S(1)} %add.31.own), channel_id=1, source_target_pairs={{0,2},{1,3},{2,0},{3,1},{4,6},{5,7},{6,4},{7,5},{8,10},{9,11},{10,... | collective-permute-start | bytes 12296 | tf_op jit(solution)/shard_map/ppermute | solution.py:1264
  (6 other events, 42.8 us)
